TPU v7x, 32 devices: a whole 2x2x4 slice. The times are simulated.
32 devices in a mesh: parts: 2 (over x), group: 8 (over z, y), tensor: 2 (over core).
Axes of the slice: x: 2, y: 2, z: 4, core: 2. Of those that a mesh axis runs over, the one named last changes fastest.
Arguments:
- normed_inputs: bfloat16 [2048, 8192], P(('parts', 'group'), 'tensor'), parts along dimension 0, may hold values from -6 to 6
- value_matrix: bfloat16 [8192, 1024], P('group', 'tensor'), may hold values from -0.0625 to 0.0625
- adapter_down_weight: bfloat16 [16, 16, 8192], P('group'), may hold values from -0.0625 to 0.0625
- adapter_up_weight: bfloat16 [16, 16, 1024], P('group', None, 'tensor'), may hold values from -1.5 to 1.5
- adapter_position: int32 [16], replicated, may hold values from 0 to 15, each once
- span_adapter_index: int32 [32], P('parts'), parts along dimension 0, may hold values from 0 to 15
- queries: bfloat16 [2048, 8192], P(('parts', 'group'), 'tensor'), parts along dimension 0, may hold values from -150 to 150, as said below
- incoming_keys: bfloat16 [2048, 1024], P(('parts', 'group'), 'tensor'), parts along dimension 0, may hold values from -6 to 6
- stored_keys: bfloat16 [32, 2048, 1024], P(('parts', 'group'), None, 'tensor'), parts along dimension 0, may hold values from -5 to 5
- stored_values: bfloat16 [32, 2048, 1024], P(('parts', 'group'), None, 'tensor'), parts along dimension 0, may hold values from -6 to 6
- cache_length: int32 [32], P(('parts', 'group')), parts along dimension 0, may hold values from 256 to 2048, as said below
Outputs:
- attended: bfloat16 [2048, 8192], P(('parts', 'group'), 'tensor'), parts along dimension 0
- incoming_values: bfloat16 [2048, 1024], P(('parts', 'group'), 'tensor'), parts along dimension 0
There are 2 independent parts, one for each index of `parts`. A program takes and returns all parts, laid end to end along the dimension named above; an argument that names none is the same for every part. Nothing has to cross between parts.
Inputs may be any that keep to these rules, and one draw needn't show every extreme that they name: `queries`: in the shown draw twice a truncated standard normal. `cache_length`: some span has a full cache in every draw.
All inputs are finite; a program needn't handle non-finite values.
Results may differ from a plain program's by a relative error of at most 0.014.
Values may be sent and summed in bfloat16 or wider, within the bound.
No kernel may reach another device: no remote copies, remote signals or barrier semaphores. Data moves between devices by JAX's collectives and lax.ppermute only.
A program may use at most 128 MiB of HBM per device.

v0:
```python
import functools
import math

import jax
import jax.numpy as jnp
from jax import lax
from jax.experimental import pallas as pl
from jax.experimental.pallas import tpu as pltpu
from jax.sharding import PartitionSpec as P

HD = 128
RANK = 16
SPAN = 64
CHUNK = 512
ADAPTER_SCALE = 2.0
EXP2_SCALE = math.log2(math.e) / math.sqrt(HD)
DEAD = -1e30
BOTH = ("group", "tensor")
VMEM_LIMIT = 56 * 1024 * 1024


def dot_last(a, b):
    return lax.dot_general(a, b, (((1,), (1,)), ((), ())), preferred_element_type=jnp.float32)


def dot(a, b):
    return jnp.dot(a, b, preferred_element_type=jnp.float32)


def cache_kernel(kv_heads, group_size, lens, q_ref, fk_ref, k_ref, v_ref, out_ref, pf_ref, qs, m_s, l_s, acc):
    span, step = pl.program_id(0), pl.program_id(1)
    length = lens[span]
    rows = group_size * SPAN
    chunk = k_ref.shape[1]

    def fresh_scores(k):
        s = dot_last(fk_ref[:, k * HD : (k + 1) * HD], qs[k])
        key = lax.broadcasted_iota(jnp.int32, (SPAN, rows), 0)
        token = lax.broadcasted_iota(jnp.int32, (SPAN, rows), 1) % SPAN
        return jnp.where(key <= token, s, DEAD)

    @pl.when(step == 0)
    def _():
        for k in range(kv_heads):
            for h in range(group_size):
                col = (k * group_size + h) * HD
                qs[k, h * SPAN : (h + 1) * SPAN, :] = q_ref[:, col : col + HD]
            s = fresh_scores(k)
            top = jnp.max(s, axis=0, keepdims=True)
            m_s[k] = top
            l_s[k] = jnp.sum(jnp.exp2((s - top) * EXP2_SCALE), axis=0, keepdims=True)
            acc[k] = jnp.zeros((HD, rows), jnp.float32)

    def add_chunk(masked):
        for k in range(kv_heads):
            s = dot_last(k_ref[0, :, k * HD : (k + 1) * HD], qs[k])
            if masked:
                slot = step * chunk + lax.broadcasted_iota(jnp.int32, (chunk, rows), 0)
                s = jnp.where(slot < length, s, DEAD)
            before = m_s[k]
            top = jnp.maximum(before, jnp.max(s, axis=0, keepdims=True))
            alpha = jnp.exp2((before - top) * EXP2_SCALE)
            p = jnp.exp2((s - top) * EXP2_SCALE)
            m_s[k] = top
            l_s[k] = l_s[k] * alpha + jnp.sum(p, axis=0, keepdims=True)
            values = v_ref[0, :, k * HD : (k + 1) * HD].T
            acc[k] = acc[k] * alpha + dot(values, p.astype(jnp.bfloat16))

    @pl.when((step + 1) * chunk <= length)
    def _():
        add_chunk(False)

    @pl.when((step * chunk < length) & ((step + 1) * chunk > length))
    def _():
        add_chunk(True)

    @pl.when(step == pl.num_programs(1) - 1)
    def _():
        for k in range(kv_heads):
            inverse = 1.0 / l_s[k]
            p = jnp.exp2((fresh_scores(k) - m_s[k]) * EXP2_SCALE) * inverse
            pf_ref[k * rows : (k + 1) * rows, :] = p.T.astype(jnp.bfloat16)
            mixed = (acc[k] * inverse).T
            for h in range(group_size):
                col = (k * group_size + h) * HD
                out_ref[:, col : col + HD] = mixed[h * SPAN : (h + 1) * SPAN, :]


def cache_attention(queries, fresh_keys, keys, values, lengths):
    spans, slots, width = keys.shape
    kv_heads = width // HD
    q_width = queries.shape[1]
    group_size = q_width // width
    rows = group_size * SPAN
    chunk = min(CHUNK, slots)
    steps = slots // chunk

    def kv_index(s, i, lens):
        return (s, jnp.minimum(i, (lens[s] - 1) // chunk), 0)

    return pl.pallas_call(
        functools.partial(cache_kernel, kv_heads, group_size),
        grid_spec=pltpu.PrefetchScalarGridSpec(
            num_scalar_prefetch=1,
            grid=(spans, steps),
            in_specs=[
                pl.BlockSpec((SPAN, q_width), lambda s, i, lens: (s, 0)),
                pl.BlockSpec((SPAN, width), lambda s, i, lens: (s, 0)),
                pl.BlockSpec((1, chunk, width), kv_index),
                pl.BlockSpec((1, chunk, width), kv_index),
            ],
            out_specs=[
                pl.BlockSpec((SPAN, q_width), lambda s, i, lens: (s, 0)),
                pl.BlockSpec((kv_heads * rows, SPAN), lambda s, i, lens: (s, 0)),
            ],
            scratch_shapes=[
                pltpu.VMEM((kv_heads, rows, HD), jnp.bfloat16),
                pltpu.VMEM((kv_heads, 1, rows), jnp.float32),
                pltpu.VMEM((kv_heads, 1, rows), jnp.float32),
                pltpu.VMEM((kv_heads, HD, rows), jnp.float32),
            ],
        ),
        out_shape=[
            jax.ShapeDtypeStruct((spans * SPAN, q_width), jnp.float32),
            jax.ShapeDtypeStruct((spans * kv_heads * rows, SPAN), jnp.bfloat16),
        ],
        compiler_params=pltpu.CompilerParams(vmem_limit_bytes=VMEM_LIMIT),
        cost_estimate=pl.CostEstimate(
            flops=4 * spans * kv_heads * rows * slots * HD,
            bytes_accessed=2 * spans * slots * width * 2,
            transcendentals=spans * kv_heads * rows * slots,
        ),
        name="cache_attention",
    )(lengths, queries, fresh_keys, keys, values)


def pack_kernel(x_ref, x_other, d_ref, u_ref, u_other, out):
    core = lax.axis_index("tensor")
    groups, _, width = out.shape
    half = groups // 2
    cols = u_ref.shape[1]
    mine = pl.ds(pl.multiple_of(core * RANK, RANK), RANK)
    for piece in range(half):
        here = slice(piece * width, (piece + 1) * width)
        out[core * half + piece, :SPAN, :] = x_ref[pl.ds(pl.multiple_of(core * SPAN, SPAN), SPAN), here]
        out[(1 - core) * half + piece, :SPAN, :] = x_other[:, here]
    for g in range(groups):
        out[g, SPAN : SPAN + RANK, :] = d_ref[mine, g * width : (g + 1) * width]
        for side, ups in ((core, u_ref), (1 - core, u_other)):
            for begin in range(0, cols, min(cols, width)):
                place = side * cols + begin
                row = pl.multiple_of(SPAN + RANK + place // width * RANK, RANK)
                column = pl.multiple_of(place % width, min(cols, width))
                out[g, pl.ds(row, RANK), pl.ds(column, min(cols, width))] = ups[mine, begin : begin + min(cols, width)]


def pack(tokens, tokens_other, downs, ups, ups_other, width, groups):
    vmem = pl.BlockSpec(memory_space=pltpu.VMEM)
    pieces = 2 * ups.shape[1] // width
    return pl.pallas_call(
        pack_kernel,
        in_specs=[vmem] * 5,
        out_specs=vmem,
        out_shape=jax.ShapeDtypeStruct((groups, SPAN + (1 + pieces) * RANK, width), jnp.bfloat16),
        compiler_params=pltpu.CompilerParams(vmem_limit_bytes=VMEM_LIMIT),
        name="pack_tokens",
    )(tokens, tokens_other, downs, ups, ups_other)


def slice_kernel(position, adapter, got, maps_other, own_ref, other_ref, out, xs, ds, us):
    core = lax.axis_index("tensor")
    groups, _, width = got.shape
    cols = own_ref.shape[1]
    ranks = ds.shape[0]
    for g in range(groups):
        xs[g * SPAN : (g + 1) * SPAN, :] = got[g, :SPAN, :]
        mine = pl.ds(pl.multiple_of((2 * g + core) * RANK, RANK), RANK)
        theirs = pl.ds(pl.multiple_of((2 * g + 1 - core) * RANK, RANK), RANK)
        ds[mine, :] = got[g, SPAN : SPAN + RANK, :]
        ds[theirs, :] = maps_other[g, :RANK, :]
        for i in range(2 * cols // width):
            here = slice(i * width, (i + 1) * width)
            us[mine, here] = got[g, SPAN + (1 + i) * RANK : SPAN + (2 + i) * RANK, :]
            us[theirs, here] = maps_other[g, (1 + i) * RANK : (2 + i) * RANK, :]
    shrink = dot_last(xs[...], ds[...])
    which = lax.broadcasted_iota(jnp.int32, (SPAN, ranks), 1) // RANK
    masked = [
        jnp.where(which == position[adapter[2 * g + core]], shrink[g * SPAN : (g + 1) * SPAN, :], 0.0)
        for g in range(groups)
    ]
    shrink = (jnp.concatenate(masked, axis=0) * ADAPTER_SCALE).astype(jnp.bfloat16)
    for side, weights in ((core, own_ref), (1 - core, other_ref)):
        up = us[:, pl.ds(pl.multiple_of(side * cols, cols), cols)]
        product = (dot(xs[...], weights[...]) + dot(shrink, up)).astype(jnp.bfloat16)
        for g in range(groups):
            out[2 * g + side] = product[g * SPAN : (g + 1) * SPAN, :]


def slice_products(got, maps_other, own, other, position, adapter):
    groups, _, width = got.shape
    cols = own.shape[1]
    ranks = groups * 2 * RANK
    vmem = pl.BlockSpec(memory_space=pltpu.VMEM)
    smem = pl.BlockSpec(memory_space=pltpu.SMEM)
    return pl.pallas_call(
        slice_kernel,
        in_specs=[smem, smem] + [vmem] * 4,
        out_specs=vmem,
        out_shape=jax.ShapeDtypeStruct((2 * groups, SPAN, cols), jnp.bfloat16),
        scratch_shapes=[
            pltpu.VMEM((groups * SPAN, width), jnp.bfloat16),
            pltpu.VMEM((ranks, width), jnp.bfloat16),
            pltpu.VMEM((ranks, 2 * cols), jnp.bfloat16),
        ],
        compiler_params=pltpu.CompilerParams(vmem_limit_bytes=VMEM_LIMIT),
        name="slice_products",
    )(position, adapter, got, maps_other, own, other)


def finish_kernel(mixed_ref, pf_ref, parts, out_ref, values_ref, vals):
    span, kv = pl.program_id(0), pl.program_id(1)
    rows = pf_ref.shape[0]

    @pl.when((span == 0) & (kv == 0))
    def _():
        for u in range(2):
            total = parts[u].astype(jnp.float32)
            for g in range(1, parts.shape[0] // 2):
                total = total + parts[2 * g + u].astype(jnp.float32)
            total = total.astype(jnp.bfloat16)
            values_ref[u * SPAN : (u + 1) * SPAN, :] = total
            for k in range(total.shape[1] // HD):
                vals[u, k] = total[:, k * HD : (k + 1) * HD]

    fresh = dot(pf_ref[...], vals[span, kv])
    for h in range(rows // SPAN):
        cols = slice(h * HD, (h + 1) * HD)
        out_ref[:, cols] = (mixed_ref[:, cols] + fresh[h * SPAN : (h + 1) * SPAN, :]).astype(jnp.bfloat16)


def finish(mixed, fresh_probs, parts):
    cols = parts.shape[2]
    kv_heads = cols // HD
    tokens, q_width = mixed.shape
    spans = tokens // SPAN
    rows = fresh_probs.shape[0] // (spans * kv_heads)
    head_width = q_width // kv_heads
    return pl.pallas_call(
        finish_kernel,
        grid=(spans, kv_heads),
        in_specs=[
            pl.BlockSpec((SPAN, head_width), lambda s, k: (s, k)),
            pl.BlockSpec((rows, SPAN), lambda s, k: (s * kv_heads + k, 0)),
            pl.BlockSpec(parts.shape, lambda s, k: (0, 0, 0)),
        ],
        out_specs=[
            pl.BlockSpec((SPAN, head_width), lambda s, k: (s, k)),
            pl.BlockSpec((tokens, cols), lambda s, k: (0, 0)),
        ],
        out_shape=[
            jax.ShapeDtypeStruct((tokens, q_width), jnp.bfloat16),
            jax.ShapeDtypeStruct((tokens, cols), jnp.bfloat16),
        ],
        scratch_shapes=[pltpu.VMEM((spans, kv_heads, SPAN, HD), jnp.bfloat16)],
        compiler_params=pltpu.CompilerParams(vmem_limit_bytes=VMEM_LIMIT),
        name="finish_attention",
    )(mixed, fresh_probs, parts)


def on_device(
    normed_inputs,
    value_matrix,
    adapter_down_weight,
    adapter_up_weight,
    adapter_position,
    span_adapter_index,
    queries,
    incoming_keys,
    stored_keys,
    stored_values,
    cache_length,
):
    groups = lax.axis_size("group")
    core = lax.axis_index("tensor")
    width, cols = value_matrix.shape
    downs = adapter_down_weight.reshape(-1, adapter_down_weight.shape[2])
    ups = adapter_up_weight.reshape(-1, cols)
    swap = [(0, 1), (1, 0)]

    leaving = lax.dynamic_slice_in_dim(normed_inputs, (1 - core) * SPAN, SPAN, 0)
    tokens_other = lax.ppermute(leaving, "tensor", swap)
    ups_other = lax.ppermute(ups, "tensor", swap)
    other = lax.ppermute(value_matrix, "tensor", swap)
    sent = pack(normed_inputs, tokens_other, downs, ups, ups_other, width, groups)
    got = lax.all_to_all(sent, "group", 0, 0)
    maps_other = lax.ppermute(got[:, SPAN:], "tensor", swap)
    mixed, fresh_probs = cache_attention(queries, incoming_keys, stored_keys, stored_values, cache_length)
    products = slice_products(got, maps_other, value_matrix, other, adapter_position, span_adapter_index)
    parts = lax.all_to_all(products, BOTH, 0, 0)
    attended, incoming_values = finish(mixed, fresh_probs, parts)
    return (attended, incoming_values)


def solution(mesh):
    in_specs = (
        P(("parts", "group"), "tensor"),
        P("group", "tensor"),
        P("group", None, None),
        P("group", None, "tensor"),
        P(),
        P("parts"),
        P(("parts", "group"), "tensor"),
        P(("parts", "group"), "tensor"),
        P(("parts", "group"), None, "tensor"),
        P(("parts", "group"), None, "tensor"),
        P(("parts", "group")),
    )
    out_specs = (P(("parts", "group"), "tensor"), P(("parts", "group"), "tensor"))
    return jax.shard_map(
        on_device, mesh=mesh, in_specs=in_specs, out_specs=out_specs, check_vma=False
    )
```

profile of v0, /device:TPU:0, one launch (start us, length us, event | category | flops | bytes accessed | tf_op | source)
XLA Modules:
  0.0 94.5 jit_solution(5275995729070020040)
XLA Ops:
  0.6 1.1 %constant_dynamic-slice_fusion = bf16[64,4096]{1,0:T(8,128)(2,1)S(1)} fusion(bf16[128,4096]{1,0:T(8,128)(2,1)} %x_ref.1, s32[]{:T(128)S(6)} %select_n.3), kind=kLoop, calls=%fused_computation | loop fusion | bytes 1048580 | tf_op jit(solution)/shard_map/dynamic_slice | solution.py:290
  1.7 0.5 collective-permute-start
  2.2 0.1 collective-permute-start.1
  2.3 1.7 %collective-permute-done.1.u_other = bf16[32,512]{1,0:T(8,128)(2,1)S(1)} collective-permute-done((bf16[32,512]{1,0:T(8,128)(2,1)}, bf16[32,512]{1,0:T(8,128)(2,1)S(1)}, u32[]{:S(2)}, u32[]{:S(2)}) %collective-permute-start.1) | collective-permute-done | bytes 32800 | tf_op jit(solution)/shard_map/ppermute | solution.py:292
  4.0 0.0 copy-start.5
  4.0 0.0 collective-permute-done.x_other
  4.0 0.0 copy-start.3
  4.0 0.6 copy-done.5
  4.6 0.2 copy-done.3
  4.8 2.8 %pack_tokens.1 = bf16[8,96,1024]{2,1,0:T(8,128)(2,1)} custom-call(bf16[128,4096]{1,0:T(8,128)(2,1)} %x_ref.1, bf16[64,4096]{1,0:T(8,128)(2,1)} %copy-done.3, bf16[32,8192]{1,0:T(8,128)(2,1)} %bitcast.2, bf16[32,512]{1,0:T(8,128)(2,1)} %bitcast.4, bf16[32,512]{1,0:T(8,128)(2,1)} %copy-done.5), custom_call_target="tpu_custom_call" | custom-call | tf_op jit(solution)/shard_map/pack_tokens/pallas_call | solution.py:160
  7.6 0.0 copy-start.2
  7.6 7.3 %all-to-all-start = ((bf16[8,96,1024]{2,1,0:T(8,128)(2,1)}), bf16[8,96,1024]{2,1,0:T(8,128)(2,1)S(1)}, u32[]{:S(2)}, u32[]{:S(2)}) async-start(bf16[8,96,1024]{2,1,0:T(8,128)(2,1)} %pack_tokens.1), calls=%async_computation | async-start | bytes 3145728 | tf_op jit(solution)/shard_map/all_to_all | solution.py:295
  15.0 0.0 copy-done.2
  15.0 0.1 collective-permute-start.3
  15.1 37.2 %all-to-all-done.got = bf16[8,96,1024]{2,1,0:T(8,128)(2,1)S(1)} async-done(((bf16[8,96,1024]{2,1,0:T(8,128)(2,1)}), bf16[8,96,1024]{2,1,0:T(8,128)(2,1)S(1)}, u32[]{:S(2)}, u32[]{:S(2)}) %all-to-all-start) | async-done | bytes 1572896 | tf_op jit(solution)/shard_map/all_to_all | solution.py:295
  52.3 0.0 copy-start
  52.3 0.1 collective-permute-start.2
  52.4 0.0 collective-permute-done.3.other_ref
  52.4 1.9 %collective-permute-done.2.maps_other = bf16[8,32,1024]{2,1,0:T(8,128)(2,1)S(1)} collective-permute-done((bf16[8,32,1024]{2,1,0:T(8,128)(2,1)S(1)}, bf16[8,32,1024]{2,1,0:T(8,128)(2,1)S(1)}, u32[]{:S(2)}, u32[]{:S(2)}) %collective-permute-start.2) | collective-permute-done | bytes 524320 | tf_op jit(solution)/shard_map/ppermute | solution.py:296
  54.3 0.0 copy-done
  54.3 0.0 copy-start.4
  54.3 0.8 copy-done.4
  55.1 5.0 %slice_products.1 = bf16[16,64,512]{2,1,0:T(8,128)(2,1)} custom-call(s32[16]{0:T(128)} %position.1, s32[16]{0:T(128)} %adapter.1, bf16[8,96,1024]{2,1,0:T(8,128)(2,1)} %copy-done, bf16[8,32,1024]{2,1,0:T(8,128)(2,1)} %copy-done.4, bf16[1024,512]{1,0:T(8,128)(2,1)} %own_ref.1, bf16[1024,512]{1,0:T(8,128)(2,1)} %collective-permute-done.3.other_ref), custom_call_target="tpu_custom_call" | custom-call | tf_op jit(solution)/shard_map/slice_products/pallas_call | solution.py:205
  60.1 3.7 %all-to-all-start.1 = ((bf16[16,64,512]{2,1,0:T(8,128)(2,1)}), bf16[16,64,512]{2,1,0:T(8,128)(2,1)S(1)}, u32[]{:S(2)}, u32[]{:S(2)}) async-start(bf16[16,64,512]{2,1,0:T(8,128)(2,1)} %slice_products.1), calls=%async_computation.1 | async-start | bytes 2097152 | tf_op jit(solution)/shard_map/all_to_all | solution.py:299
  63.9 16.0 %cache_attention.1 = (f32[128,4096]{1,0:T(8,128)}, bf16[4096,64]{1,0:T(8,128)(2,1)}) custom-call(s32[2]{0:T(128)} %lens.1, bf16[128,4096]{1,0:T(8,128)(2,1)} %q_ref.1, bf16[128,512]{1,0:T(8,128)(2,1)} %fk_ref.1, bf16[2,2048,512]{2,1,0:T(8,128)(2,1)} %k_ref.1, bf16[2,2048,512]{2,1,0:T(8,128)(2,1)} %v_ref.1), custom_call_target="tpu_custom_call" | custom-call | flops 4294967296 | bytes 8388608 | tf_op jit(solution)/shard_map/cache_attention/pallas_call | solution.py:101
  79.9 6.9 %all-to-all-done.1.parts = bf16[16,64,512]{2,1,0:T(8,128)(2,1)S(1)} async-done(((bf16[16,64,512]{2,1,0:T(8,128)(2,1)}), bf16[16,64,512]{2,1,0:T(8,128)(2,1)S(1)}, u32[]{:S(2)}, u32[]{:S(2)}) %all-to-all-start.1) | async-done | bytes 1048608 | tf_op jit(solution)/shard_map/all_to_all | solution.py:299
  86.8 0.0 copy-start.1
  86.8 1.0 %copy-done.1 = bf16[16,64,512]{2,1,0:T(8,128)(2,1)} copy-done((bf16[16,64,512]{2,1,0:T(8,128)(2,1)}, bf16[16,64,512]{2,1,0:T(8,128)(2,1)S(1)}, u32[]{:S(2)}) %copy-start.1) | copy-done | bytes 1048600
  87.8 6.7 %finish_attention.1 = (bf16[128,4096]{1,0:T(8,128)(2,1)}, bf16[128,512]{1,0:T(8,128)(2,1)}) custom-call(f32[128,4096]{1,0:T(8,128)} %get-tuple-element.4.mixed_ref, bf16[4096,64]{1,0:T(8,128)(2,1)} %get-tuple-element.5.pf_ref, bf16[16,64,512]{2,1,0:T(8,128)(2,1)} %copy-done.1), custom_call_target="tpu_custom_call" | custom-call | tf_op jit(solution)/shard_map/finish_attention/pallas_call | solution.py:248
  (1 shorter events, 0.0 us)
Async XLA Ops:
  1.7 2.3 %collective-permute-start = (bf16[64,4096]{1,0:T(8,128)(2,1)S(1)}, bf16[64,4096]{1,0:T(8,128)(2,1)S(1)}, u32[]{:S(2)}, u32[]{:S(2)}) collective-permute-start(bf16[64,4096]{1,0:T(8,128)(2,1)S(1)} %constant_dynamic-slice_fusion), channel_id=1, source_target_pairs={{0,1},{1,0},{2,3},{3,2},{4,5},{5,4},{6,7},{7,6},{8,9},{9,8},{10,11... | collective-permute-start | bytes 1572872 | tf_op jit(solution)/shard_map/ppermute | solution.py:291
  2.2 1.8 %collective-permute-start.1 = (bf16[32,512]{1,0:T(8,128)(2,1)}, bf16[32,512]{1,0:T(8,128)(2,1)S(1)}, u32[]{:S(2)}, u32[]{:S(2)}) collective-permute-start(bf16[32,512]{1,0:T(8,128)(2,1)} %bitcast.3), channel_id=1, source_target_pairs={{0,1},{1,0},{2,3},{3,2},{4,5},{5,4},{6,7},{7,6},{8,9},{9,8},{10,11... | collective-permute-start | bytes 98312 | tf_op jit(solution)/shard_map/ppermute | solution.py:292
  4.0 0.6 copy-start.5
  4.0 0.8 copy-start.3
  7.6 7.3 %copy-start.2 = (bf16[1024,512]{1,0:T(8,128)(2,1)S(1)}, bf16[1024,512]{1,0:T(8,128)(2,1)}, u32[]{:S(2)}) copy-start(bf16[1024,512]{1,0:T(8,128)(2,1)} %own_ref.1) | copy-start | bytes 3145732
  7.6 44.6 %all-to-all-start = ((bf16[8,96,1024]{2,1,0:T(8,128)(2,1)}), bf16[8,96,1024]{2,1,0:T(8,128)(2,1)S(1)}, u32[]{:S(2)}, u32[]{:S(2)}) async-start(bf16[8,96,1024]{2,1,0:T(8,128)(2,1)} %pack_tokens.1), calls=%async_computation | async-start | bytes 3145728 | tf_op jit(solution)/shard_map/all_to_all | solution.py:295
  15.0 37.4 %collective-permute-start.3 = (bf16[1024,512]{1,0:T(8,128)(2,1)S(1)}, bf16[1024,512]{1,0:T(8,128)(2,1)}, u32[]{:S(2)}, u32[]{:S(2)}) collective-permute-start(bf16[1024,512]{1,0:T(8,128)(2,1)S(1)} %copy-done.2), channel_id=1, source_target_pairs={{0,1},{1,0},{2,3},{3,2},{4,5},{5,4},{6,7},{7,6},{8,9},{9,8},{10,11... | collective-permute-start | bytes 3145736 | tf_op jit(solution)/shard_map/ppermute | solution.py:293
  52.3 2.0 %copy-start = (bf16[8,96,1024]{2,1,0:T(8,128)(2,1)}, bf16[8,96,1024]{2,1,0:T(8,128)(2,1)S(1)}, u32[]{:S(2)}) copy-start(bf16[8,96,1024]{2,1,0:T(8,128)(2,1)S(1)} %all-to-all-done.got) | copy-start | bytes 4718596
  52.3 2.0 %collective-permute-start.2 = (bf16[8,32,1024]{2,1,0:T(8,128)(2,1)S(1)}, bf16[8,32,1024]{2,1,0:T(8,128)(2,1)S(1)}, u32[]{:S(2)}, u32[]{:S(2)}) collective-permute-start(bf16[8,32,1024]{2,1,0:T(8,128)(2,1)S(1)} %slice.4), channel_id=1, source_target_pairs={{0,1},{1,0},{2,3},{3,2},{4,5},{5,4},{6,7},{7,6},{8,9},{9,8},{10,11... | collective-permute-start | bytes 1572872 | tf_op jit(solution)/shard_map/ppermute | solution.py:296
  54.3 0.8 copy-start.4
  60.1 26.7 %all-to-all-start.1 = ((bf16[16,64,512]{2,1,0:T(8,128)(2,1)}), bf16[16,64,512]{2,1,0:T(8,128)(2,1)S(1)}, u32[]{:S(2)}, u32[]{:S(2)}) async-start(bf16[16,64,512]{2,1,0:T(8,128)(2,1)} %slice_products.1), calls=%async_computation.1 | async-start | bytes 2097152 | tf_op jit(solution)/shard_map/all_to_all | solution.py:299
  86.8 1.0 %copy-start.1 = (bf16[16,64,512]{2,1,0:T(8,128)(2,1)}, bf16[16,64,512]{2,1,0:T(8,128)(2,1)S(1)}, u32[]{:S(2)}) copy-start(bf16[16,64,512]{2,1,0:T(8,128)(2,1)S(1)} %all-to-all-done.1.parts) | copy-start | bytes 3145732
where the time goes:
time: 96.2 us; the launch traced here: 94.5 us
  waiting for transfers between devices  47.7 us (50%)
  Pallas kernels  30.6 us (32%)
  starting transfers between devices  11.8 us (12%)
  local copies, waits for them, and re-layouts  3.71 us (4%)
    all_to_all x1, waiting for transfers between devices, on_device(): got = lax.all_to_all(sent, 'group', 0, 0)  37.2 us
    pallas_call x1, Pallas kernels, cache_attention(): pl.pallas_call(functools.partial(cache_kernel, kv_heads, group_size), gri...  16 us
    all_to_all x1, starting transfers between devices, on_device(): got = lax.all_to_all(sent, 'group', 0, 0)  7.33 us
    all_to_all x1, waiting for transfers between devices, on_device(): parts = lax.all_to_all(products, BOTH, 0, 0)  6.9 us
    pallas_call x1, Pallas kernels, finish(): pl.pallas_call(finish_kernel, grid=(spans, kv_heads), in_specs=[pl.BlockS...  6.69 us
    pallas_call x1, Pallas kernels, slice_products(): pl.pallas_call(slice_kernel, in_specs=[smem, smem] + [vmem] * 4, out_spec...  5.04 us
    all_to_all x1, starting transfers between devices, on_device(): parts = lax.all_to_all(products, BOTH, 0, 0)  3.74 us
    pallas_call x1, Pallas kernels, pack(): pl.pallas_call(pack_kernel, in_specs=[vmem] * 5, out_specs=vmem, out_shap...  2.81 us
  transfers between devices with their start and end apart: 6, of which 4 were waited for; matrix products, arithmetic and copies ran while one was open for 0% of the time, Pallas kernels for 17%

commit v1 on v0

v1 whole, which is shorter than its diff:
```python
import functools
import math

import jax
import jax.numpy as jnp
from jax import lax
from jax.experimental import pallas as pl
from jax.experimental.pallas import tpu as pltpu
from jax.sharding import Mesh
from jax.sharding import PartitionSpec as P

HD = 128
RANK = 16
SPAN = 64
CHUNK = 512
CHUNKS = 2
ADAPTER_SCALE = 2.0
EXP2_SCALE = math.log2(math.e) / math.sqrt(HD)
DEAD = -1e30
MIB = 1024 * 1024
SWAP = [(0, 1), (1, 0)]


def dot_last(a, b):
    return lax.dot_general(a, b, (((1,), (1,)), ((), ())), preferred_element_type=jnp.float32)


def dot(a, b):
    return jnp.dot(a, b, preferred_element_type=jnp.float32)


def cache_kernel(span, kv_heads, group_size, lens, q_ref, fk_ref, k_ref, v_ref, out_ref, pf_ref, qs, m_s, l_s, acc):
    step = pl.program_id(0)
    length = lens[span]
    rows = group_size * SPAN
    chunk = k_ref.shape[1]

    def fresh_scores(k):
        s = dot_last(fk_ref[:, k * HD : (k + 1) * HD], qs[k])
        key = lax.broadcasted_iota(jnp.int32, (SPAN, rows), 0)
        token = lax.broadcasted_iota(jnp.int32, (SPAN, rows), 1) % SPAN
        return jnp.where(key <= token, s, DEAD)

    @pl.when(step == 0)
    def _():
        for k in range(kv_heads):
            for h in range(group_size):
                col = (k * group_size + h) * HD
                qs[k, h * SPAN : (h + 1) * SPAN, :] = q_ref[:, col : col + HD]
            s = fresh_scores(k)
            top = jnp.max(s, axis=0, keepdims=True)
            m_s[k] = top
            l_s[k] = jnp.sum(jnp.exp2((s - top) * EXP2_SCALE), axis=0, keepdims=True)
            acc[k] = jnp.zeros((HD, rows), jnp.float32)

    def add_chunk(masked):
        for k in range(kv_heads):
            s = dot_last(k_ref[0, :, k * HD : (k + 1) * HD], qs[k])
            if masked:
                slot = step * chunk + lax.broadcasted_iota(jnp.int32, (chunk, rows), 0)
                s = jnp.where(slot < length, s, DEAD)
            before = m_s[k]
            top = jnp.maximum(before, jnp.max(s, axis=0, keepdims=True))
            alpha = jnp.exp2((before - top) * EXP2_SCALE)
            p = jnp.exp2((s - top) * EXP2_SCALE)
            m_s[k] = top
            l_s[k] = l_s[k] * alpha + jnp.sum(p, axis=0, keepdims=True)
            values = v_ref[0, :, k * HD : (k + 1) * HD].T
            acc[k] = acc[k] * alpha + dot(values, p.astype(jnp.bfloat16))

    @pl.when((step + 1) * chunk <= length)
    def _():
        add_chunk(False)

    @pl.when((step * chunk < length) & ((step + 1) * chunk > length))
    def _():
        add_chunk(True)

    @pl.when(step == pl.num_programs(0) - 1)
    def _():
        for k in range(kv_heads):
            inverse = 1.0 / l_s[k]
            p = jnp.exp2((fresh_scores(k) - m_s[k]) * EXP2_SCALE) * inverse
            pf_ref[k * rows : (k + 1) * rows, :] = p.T.astype(jnp.bfloat16)
            mixed = (acc[k] * inverse).T
            for h in range(group_size):
                col = (k * group_size + h) * HD
                out_ref[:, col : col + HD] = mixed[h * SPAN : (h + 1) * SPAN, :]


def cache_attention(span, queries, fresh_keys, keys, values, lengths):
    _, slots, width = keys.shape
    kv_heads = width // HD
    q_width = queries.shape[1]
    group_size = q_width // width
    rows = group_size * SPAN
    chunk = min(CHUNK, slots)
    steps = slots // chunk

    def kv_index(i, lens):
        return (span, jnp.minimum(i, (lens[span] - 1) // chunk), 0)

    return pl.pallas_call(
        functools.partial(cache_kernel, span, kv_heads, group_size),
        grid_spec=pltpu.PrefetchScalarGridSpec(
            num_scalar_prefetch=1,
            grid=(steps,),
            in_specs=[
                pl.BlockSpec((SPAN, q_width), lambda i, lens: (span, 0)),
                pl.BlockSpec((SPAN, width), lambda i, lens: (span, 0)),
                pl.BlockSpec((1, chunk, width), kv_index),
                pl.BlockSpec((1, chunk, width), kv_index),
            ],
            out_specs=[
                pl.BlockSpec((SPAN, q_width), lambda i, lens: (0, 0)),
                pl.BlockSpec((kv_heads * rows, SPAN), lambda i, lens: (0, 0)),
            ],
            scratch_shapes=[
                pltpu.VMEM((kv_heads, rows, HD), jnp.bfloat16),
                pltpu.VMEM((kv_heads, 1, rows), jnp.float32),
                pltpu.VMEM((kv_heads, 1, rows), jnp.float32),
                pltpu.VMEM((kv_heads, HD, rows), jnp.float32),
            ],
        ),
        out_shape=[
            jax.ShapeDtypeStruct((SPAN, q_width), jnp.float32),
            jax.ShapeDtypeStruct((kv_heads * rows, SPAN), jnp.bfloat16),
        ],
        compiler_params=pltpu.CompilerParams(vmem_limit_bytes=32 * MIB),
        cost_estimate=pl.CostEstimate(
            flops=4 * kv_heads * rows * slots * HD,
            bytes_accessed=2 * slots * width * 2,
            transcendentals=kv_heads * rows * slots,
        ),
        name="cache_attention",
    )(lengths, queries, fresh_keys, keys, values)


def rows_kernel(w_ref, *refs):
    outs, sems = refs[:-1], refs[-1]
    chunk = outs[0].shape[0]
    first = lax.axis_index("parts") % 2 * (chunk * len(outs))
    copies = []
    for i, out in enumerate(outs):
        begin = pl.multiple_of(first + i * chunk, chunk)
        copies.append(pltpu.make_async_copy(w_ref.at[pl.ds(begin, chunk), :], out, sems.at[i]))
    for copy in copies:
        copy.start()
    for copy in copies:
        copy.wait()


def rows_to_send(weights, chunks):
    width, cols = weights.shape
    anywhere = pl.BlockSpec(memory_space=pl.ANY)
    return pl.pallas_call(
        rows_kernel,
        in_specs=[anywhere],
        out_specs=[anywhere] * chunks,
        out_shape=[jax.ShapeDtypeStruct((width // 2 // chunks, cols), weights.dtype)] * chunks,
        scratch_shapes=[pltpu.SemaphoreType.DMA((chunks,))],
        name="rows_to_send",
    )(weights)


def pack_kernel(x_ref, d_ref, u_ref, xs, du):
    part, core = lax.axis_index("parts") % 2, lax.axis_index("tensor")
    quads, _, width = xs.shape
    groups, _, sub = du.shape
    cols = u_ref.shape[1]
    mine = pl.ds(pl.multiple_of(part * RANK, RANK), RANK)
    downs = width // sub
    for j in range(quads):
        xs[j] = x_ref[:, j * width : (j + 1) * width]
        begin = core * (quads * width) + j * width
        for wing in range(2):
            g = wing * quads + j
            for i in range(downs):
                piece = pl.ds(pl.multiple_of(begin + i * sub, sub), sub)
                du[g, i * RANK : (i + 1) * RANK, :] = d_ref[mine, piece]
            for i in range(cols // sub):
                row = (downs + i) * RANK
                du[g, row : row + RANK, :] = u_ref[mine, i * sub : (i + 1) * sub]


def pack(tokens, downs, ups, width, quads):
    vmem = pl.BlockSpec(memory_space=pltpu.VMEM)
    cols = ups.shape[1]
    sub = min(width, cols)
    rows = RANK * (width // sub + cols // sub)
    return pl.pallas_call(
        pack_kernel,
        in_specs=[vmem] * 3,
        out_specs=[vmem] * 2,
        out_shape=[
            jax.ShapeDtypeStruct((quads, tokens.shape[0], width), tokens.dtype),
            jax.ShapeDtypeStruct((2 * quads, rows, sub), downs.dtype),
        ],
        compiler_params=pltpu.CompilerParams(vmem_limit_bytes=8 * MIB),
        name="pack_tokens",
    )(tokens, downs, ups)


def near_kernel(position, adapter, x_mine, x_theirs, own_ref, du_a, du_b, du_c, du_d, out, ds, us):
    part, core, wing = lax.axis_index("parts") % 2, lax.axis_index("tensor"), lax.axis_index("wing")
    quads, tokens, width = x_mine.shape
    groups, _, sub = du_a.shape
    cols = own_ref.shape[1]
    ranks = us.shape[0]
    downs = width // sub
    for g in range(groups):
        for parity, mine, theirs in ((part, du_a, du_c), (1 - part, du_b, du_d)):
            rows = pl.ds(pl.multiple_of((2 * g + parity) * RANK, RANK), RANK)
            for i in range(downs):
                here = slice(i * sub, (i + 1) * sub)
                ds[0, rows, here] = mine[g, i * RANK : (i + 1) * RANK, :]
                ds[1, rows, here] = theirs[g, i * RANK : (i + 1) * RANK, :]
            for i in range(cols // sub):
                row = (downs + i) * RANK
                us[rows, i * sub : (i + 1) * sub] = mine[g, row : row + RANK, :]
    flat = (quads * tokens, width)
    shrink = dot_last(x_mine[...].reshape(flat), ds[0]) + dot_last(x_theirs[...].reshape(flat), ds[1])
    which = lax.broadcasted_iota(jnp.int32, (SPAN, ranks), 1) // RANK
    spans = tokens // SPAN
    masked = []
    for i in range(quads * spans):
        slot = position[adapter[wing * (quads * spans) + i]]
        masked.append(jnp.where(which == slot, shrink[i * SPAN : (i + 1) * SPAN, :], 0.0))
    shrink = (jnp.concatenate(masked, axis=0) * ADAPTER_SCALE).astype(jnp.bfloat16)
    out[...] = dot(shrink, us[...])

    @pl.when(core == wing)
    def _():
        out[...] += dot(x_mine[...].reshape(flat), own_ref[...])

    @pl.when(core != wing)
    def _():
        out[...] += dot(x_theirs[...].reshape(flat), own_ref[...])


def near_products(x_mine, x_theirs, own, maps, position, adapter):
    quads, tokens, width = x_mine.shape
    cols = own.shape[1]
    ranks = 2 * maps[0].shape[0] * RANK
    vmem = pl.BlockSpec(memory_space=pltpu.VMEM)
    smem = pl.BlockSpec(memory_space=pltpu.SMEM)
    return pl.pallas_call(
        near_kernel,
        in_specs=[smem, smem] + [vmem] * 7,
        out_specs=vmem,
        out_shape=jax.ShapeDtypeStruct((quads * tokens, cols), jnp.float32),
        scratch_shapes=[
            pltpu.VMEM((2, ranks, width), jnp.bfloat16),
            pltpu.VMEM((ranks, cols), jnp.bfloat16),
        ],
        compiler_params=pltpu.CompilerParams(vmem_limit_bytes=48 * MIB if quads > 4 else 24 * MIB),
        cost_estimate=pl.CostEstimate(
            flops=2 * quads * tokens * width * (cols + 2 * ranks), bytes_accessed=6 * MIB, transcendentals=0
        ),
        name="near_products",
    )(position, adapter, x_mine, x_theirs, own, *maps)


def far_kernel(x_mine, x_theirs, near, *refs):
    weights, out, whole = refs[:-2], refs[-2], refs[-1]
    part, core, wing = lax.axis_index("parts") % 2, lax.axis_index("tensor"), lax.axis_index("wing")
    quads, tokens, width = x_mine.shape
    flat = (quads * tokens, width)
    chunk = weights[0].shape[0]
    chunks = len(weights) // 2
    for side in range(2):
        first = (part if side == 0 else 1 - part) * (chunks * chunk)
        for i in range(chunks):
            begin = pl.multiple_of(first + i * chunk, chunk)
            whole[pl.ds(begin, chunk), :] = weights[side * chunks + i][...]

    def store(x):
        out[...] = (near[...] + dot(x[...].reshape(flat), whole[...])).astype(jnp.bfloat16).reshape(out.shape)

    @pl.when(core == wing)
    def _():
        store(x_theirs)

    @pl.when(core != wing)
    def _():
        store(x_mine)


def far_products(x_mine, x_theirs, near, weights):
    quads, tokens, width = x_mine.shape
    cols = near.shape[1]
    vmem = pl.BlockSpec(memory_space=pltpu.VMEM)
    return pl.pallas_call(
        far_kernel,
        in_specs=[vmem] * (3 + len(weights)),
        out_specs=vmem,
        out_shape=jax.ShapeDtypeStruct((quads, tokens, cols), jnp.bfloat16),
        scratch_shapes=[pltpu.VMEM((width, cols), jnp.bfloat16)],
        compiler_params=pltpu.CompilerParams(vmem_limit_bytes=48 * MIB if quads > 4 else 16 * MIB),
        cost_estimate=pl.CostEstimate(
            flops=2 * quads * tokens * width * cols, bytes_accessed=5 * MIB, transcendentals=0
        ),
        name="far_products",
    )(x_mine, x_theirs, near, *weights)


def finish_kernel(spans, parts, *refs):
    mixed, probs, (out_ref, values_ref) = refs[:spans], refs[spans : 2 * spans], refs[2 * spans :]
    total = parts[0].astype(jnp.float32)
    for j in range(1, parts.shape[0]):
        total = total + parts[j].astype(jnp.float32)
    total = total.astype(jnp.bfloat16)
    values_ref[...] = total
    kv_heads = total.shape[1] // HD
    for span in range(spans):
        rows = slice(span * SPAN, (span + 1) * SPAN)
        count = probs[span].shape[0] // kv_heads
        for k in range(kv_heads):
            fresh = dot(probs[span][k * count : (k + 1) * count, :], total[rows, k * HD : (k + 1) * HD])
            for h in range(count // SPAN):
                col = (k * (count // SPAN) + h) * HD
                out_ref[rows, col : col + HD] = (
                    mixed[span][:, col : col + HD] + fresh[h * SPAN : (h + 1) * SPAN, :]
                ).astype(jnp.bfloat16)


def finish(mixed, fresh_probs, parts):
    _, tokens, cols = parts.shape
    vmem = pl.BlockSpec(memory_space=pltpu.VMEM)
    return pl.pallas_call(
        functools.partial(finish_kernel, len(mixed)),
        in_specs=[vmem] * (1 + 2 * len(mixed)),
        out_specs=[vmem] * 2,
        out_shape=[
            jax.ShapeDtypeStruct((tokens, mixed[0].shape[1]), jnp.bfloat16),
            jax.ShapeDtypeStruct((tokens, cols), jnp.bfloat16),
        ],
        compiler_params=pltpu.CompilerParams(vmem_limit_bytes=16 * MIB),
        name="finish_attention",
    )(parts, *mixed, *fresh_probs)


def on_device(
    normed_inputs,
    value_matrix,
    adapter_down_weight,
    adapter_up_weight,
    adapter_position,
    span_adapter_index,
    queries,
    incoming_keys,
    stored_keys,
    stored_values,
    cache_length,
):
    quads = lax.axis_size("quad")
    parts_swap = [(i, i ^ 1) for i in range(lax.axis_size("parts"))]
    width, cols = value_matrix.shape
    downs = adapter_down_weight.reshape(-1, adapter_down_weight.shape[2])
    ups = adapter_up_weight.reshape(-1, cols)

    def attention(span, lengths):
        return cache_attention(span, queries, incoming_keys, stored_keys, stored_values, lengths)

    leaving = rows_to_send(value_matrix, CHUNKS)
    far = [lax.ppermute(rows, "wing", SWAP) for rows in leaving]
    xs, du = pack(normed_inputs, downs, ups, width, quads)
    x_mine = lax.all_to_all(xs, "quad", 0, 0)
    maps_a = lax.all_to_all(du, ("wing", "quad"), 0, 0)

    lengths, _ = lax.optimization_barrier((cache_length, du))
    first = attention(0, lengths)
    x_mine, maps_a, far_0, _ = lax.optimization_barrier((x_mine, maps_a, far[0], first[1]))
    x_theirs = lax.ppermute(x_mine, "tensor", SWAP)
    maps_b = lax.ppermute(maps_a, "parts", parts_swap)
    maps_c = lax.ppermute(maps_a, "tensor", SWAP)
    far_0_other = lax.ppermute(far_0, "parts", parts_swap)

    lengths, _ = lax.optimization_barrier((cache_length, maps_a))
    second = attention(1, lengths)
    far_1, maps_b, _ = lax.optimization_barrier((far[1], maps_b, second[1]))
    far_1_other = lax.ppermute(far_1, "parts", parts_swap)
    maps_d = lax.ppermute(maps_b, "tensor", SWAP)

    near = near_products(
        x_mine, x_theirs, value_matrix, (maps_a, maps_b, maps_c, maps_d), adapter_position, span_adapter_index
    )
    products = far_products(x_mine, x_theirs, near, (far_0, far_1, far_0_other, far_1_other))
    parts = lax.all_to_all(products, "quad", 0, 0)
    mixed, fresh_probs = zip(first, second)
    attended, incoming_values = finish(mixed, fresh_probs, parts)
    return (attended, incoming_values)


def solution(mesh):
    sizes = mesh.devices.shape
    cut = Mesh(
        mesh.devices.reshape(sizes[0], 2, sizes[1] // 2, sizes[2]), ("parts", "wing", "quad", "tensor")
    )
    group = ("wing", "quad")
    home = ("parts", "wing", "quad")
    in_specs = (
        P(home, "tensor"),
        P(group, "tensor"),
        P(group, None, None),
        P(group, None, "tensor"),
        P(),
        P("parts"),
        P(home, "tensor"),
        P(home, "tensor"),
        P(home, None, "tensor"),
        P(home, None, "tensor"),
        P(home),
    )
    out_specs = (P(home, "tensor"), P(home, "tensor"))
    return jax.shard_map(
        on_device, mesh=cut, in_specs=in_specs, out_specs=out_specs, check_vma=False
    )
```

time: 96.2 us -> 109 us (1.13)
  waiting for transfers between devices: 47.7 us -> 9.62 us
  blocking collectives: 0 us -> 29.8 us
  Pallas kernels: 30.6 us -> 43 us
  local copies, waits for them, and re-layouts: 3.71 us -> 14.5 us
  starting transfers between devices: 11.8 us -> 10.6 us
    all_to_all x2 -> x1, waiting for transfers between devices: 44.1 us -> 0.01 us  [on_device(): x_mine = lax.all_to_all(xs, 'quad', 0, 0)]
    all_to_all x0 -> x2, blocking collectives: none -> 29.8 us  [the longest x1 19.2 us: on_device(): maps_a = lax.all_to_all(du, ('wing', 'quad'), 0, 0)]
    pallas_call x4 -> x7, Pallas kernels: 30.6 us -> 43 us  [the longest x2 19.3 us: cache_attention(): pl.pallas_call(functools.partial(cache_kernel, span, kv_heads, group_size...]
    unnamed x12 -> x32, local copies, waits for them, and re-layouts: 2.59 us -> 14.5 us
    all_to_all x2 -> x1, starting transfers between devices: 11.1 us -> 3.52 us  [on_device(): x_mine = lax.all_to_all(xs, 'quad', 0, 0)]
    ppermute x4 -> x8, starting transfers between devices: 0.74 us -> 7.12 us  [the longest x2 4.44 us: on_device(): far = [lax.ppermute(rows, 'wing', SWAP) for rows in leaving]]
    ppermute x4 -> x8, waiting for transfers between devices: 3.61 us -> 9.62 us  [the longest x1 4.85 us: on_device(): far_0_other = lax.ppermute(far_0, 'parts', parts_swap)]
  transfers between devices with their start and end apart: 6 -> 9, of which waited for: 4 -> 2; matrix products, arithmetic and copies ran while one was open for 0% -> 0% of each run, Pallas kernels for 17% -> 36%
where the time goes in v1:
time: 109 us; the launch traced here: 108 us
  Pallas kernels  43 us (39%)
  blocking collectives  29.8 us (27%)
  local copies, waits for them, and re-layouts  14.5 us (13%)
  starting transfers between devices  10.6 us (10%)
  waiting for transfers between devices  9.62 us (9%)
    pallas_call x2, Pallas kernels, cache_attention(): pl.pallas_call(functools.partial(cache_kernel, span, kv_heads, group_size...  19.3 us
    all_to_all x1, blocking collectives, on_device(): maps_a = lax.all_to_all(du, ('wing', 'quad'), 0, 0)  19.2 us
    pallas_call x1, Pallas kernels, rows_to_send(): pl.pallas_call(rows_kernel, in_specs=[anywhere], out_specs=[anywhere] * c...  17 us
    unnamed x32, local copies, waits for them, and re-layouts  14.5 us
    all_to_all x1, blocking collectives, on_device(): parts = lax.all_to_all(products, 'quad', 0, 0)  10.6 us
    ppermute x1, waiting for transfers between devices, on_device(): far_0_other = lax.ppermute(far_0, 'parts', parts_swap)  4.85 us
    ppermute x1, waiting for transfers between devices, on_device(): far_1_other = lax.ppermute(far_1, 'parts', parts_swap)  4.75 us
    ppermute x2, starting transfers between devices, on_device(): far = [lax.ppermute(rows, 'wing', SWAP) for rows in leaving]  4.44 us
  transfers between devices with their start and end apart: 9, of which 2 were waited for; matrix products, arithmetic and copies ran while one was open for 0% of the time, Pallas kernels for 36%

profile of v1, /device:TPU:0, one launch (start us, length us, event | category | flops | bytes accessed | tf_op | source)
XLA Modules:
  0.0 108.3 jit_solution(14576447583979221716)
XLA Ops:
  0.6 0.0 copy-start.4
  0.6 0.0 copy-start.6
  0.7 1.3 %copy-done.6 = bf16[128,4096]{1,0:T(8,128)(2,1)S(1)} copy-done((bf16[128,4096]{1,0:T(8,128)(2,1)S(1)}, bf16[128,4096]{1,0:T(8,128)(2,1)}, u32[]{:S(2)}) %copy-start.6) | copy-done | bytes 1048600
  2.0 1.0 copy-done.9
  3.0 0.8 copy-done.12
  3.8 1.1 pack_tokens.1
  4.8 19.2 %all_to_all.15.du_a = bf16[8,48,512]{2,1,0:T(8,128)(2,1)S(1)} all-to-all(bf16[8,48,512]{2,1,0:T(8,128)(2,1)S(1)} %get-tuple-element.18), channel_id=1, replica_groups=mesh['parts'=2,'wing'=2,'quad'=4,'tensor'=2] {'wing','quad'}, dimensions={0} | all-to-all | bytes 786432 | tf_op jit(solution)/shard_map/all_to_all | solution.py:369
  24.0 3.5 %all-to-all-start = ((bf16[4,128,1024]{2,1,0:T(8,128)(2,1)}), bf16[4,128,1024]{2,1,0:T(8,128)(2,1)S(1)}, u32[]{:S(2)}, u32[]{:S(2)}) async-start(bf16[4,128,1024]{2,1,0:T(8,128)(2,1)} %get-tuple-element.17), calls=%async_computation | async-start | bytes 2097152 | tf_op jit(solution)/shard_map/all_to_all | solution.py:368
  27.5 17.0 %rows_to_send.1 = (bf16[256,512]{1,0:T(8,128)(2,1)}, bf16[256,512]{1,0:T(8,128)(2,1)}) custom-call(bf16[1024,512]{1,0:T(8,128)(2,1)} %own_ref.1), custom_call_target="tpu_custom_call" | custom-call | tf_op jit(solution)/shard_map/rows_to_send/pallas_call | solution.py:156
  44.5 0.9 collective-permute-start
  45.5 0.0 copy-done.4
  45.5 0.0 copy-done.13
  45.5 2.2 %copy-done = bf16[2,2048,512]{2,1,0:T(8,128)(2,1)S(1)} copy-done((bf16[2,2048,512]{2,1,0:T(8,128)(2,1)S(1)}, bf16[2,2048,512]{2,1,0:T(8,128)(2,1)}, u32[]{:S(2)}) %copy-start) | copy-done | bytes 4194328
  47.7 2.2 %copy-done.2 = bf16[2,2048,512]{2,1,0:T(8,128)(2,1)S(1)} copy-done((bf16[2,2048,512]{2,1,0:T(8,128)(2,1)S(1)}, bf16[2,2048,512]{2,1,0:T(8,128)(2,1)}, u32[]{:S(2)}) %copy-start.2) | copy-done | bytes 4194328
  49.9 0.9 copy-done.7
  50.8 8.5 %cache_attention.2 = (f32[64,4096]{1,0:T(8,128)S(1)}, bf16[2048,64]{1,0:T(8,128)(2,1)S(1)}) custom-call(s32[2]{0:T(128)S(1)} %copy-done.13, bf16[128,4096]{1,0:T(8,128)(2,1)S(1)} %copy-done.4, bf16[128,512]{1,0:T(8,128)(2,1)S(1)} %copy-done.7, bf16[2,2048,512]{2,1,0:T(8,128)(2,1)S(1)} %copy-done, bf16[2,2048,512]{2,1,0:T(8,128)(2,1)S(1)} %copy-done.2), custom_call_target="tpu_custom_call" | custom-call | flops 2147483648 | bytes 4194304 | tf_op jit(solution)/shard_map/cache_attention/pallas_call | solution.py:103
  59.3 0.0 copy-start.10
  59.3 0.8 copy-done.10
  60.1 0.0 collective-permute-done.refs_0_
  60.1 0.0 all-to-all-done.x_mine
  60.1 0.0 collective-permute-start.1
  60.1 0.1 collective-permute-start.3
  60.2 0.0 copy-start.14
  60.2 0.0 copy-start.15
  60.2 3.5 %collective-permute-start.2 = (bf16[256,512]{1,0:T(8,128)(2,1)}, bf16[256,512]{1,0:T(8,128)(2,1)S(1)}, u32[]{:S(2)}, u32[]{:S(2)}) collective-permute-start(bf16[256,512]{1,0:T(8,128)(2,1)} %get-tuple-element.24), channel_id=1, source_target_pairs={{0,8},{8,0},{1,9},{9,1},{2,10},{10,2},{3,11},{11,3},{4,12},{12,4},... | collective-permute-start | bytes 786440 | tf_op jit(solution)/shard_map/ppermute | solution.py:366
  63.7 0.0 collective-permute-start.4
  63.7 2.2 %copy-done.1 = bf16[2,2048,512]{2,1,0:T(8,128)(2,1)S(1)} copy-done((bf16[2,2048,512]{2,1,0:T(8,128)(2,1)S(1)}, bf16[2,2048,512]{2,1,0:T(8,128)(2,1)}, u32[]{:S(2)}) %copy-start.1) | copy-done | bytes 4194328
  65.9 2.2 %copy-done.3 = bf16[2,2048,512]{2,1,0:T(8,128)(2,1)S(1)} copy-done((bf16[2,2048,512]{2,1,0:T(8,128)(2,1)S(1)}, bf16[2,2048,512]{2,1,0:T(8,128)(2,1)}, u32[]{:S(2)}) %copy-start.3) | copy-done | bytes 4194328
  68.1 0.9 copy-done.8
  69.0 10.8 %cache_attention.3 = (f32[64,4096]{1,0:T(8,128)S(1)}, bf16[2048,64]{1,0:T(8,128)(2,1)S(1)}) custom-call(s32[2]{0:T(128)S(1)} %copy-done.13, bf16[128,4096]{1,0:T(8,128)(2,1)S(1)} %copy-done.4, bf16[128,512]{1,0:T(8,128)(2,1)S(1)} %copy-done.8, bf16[2,2048,512]{2,1,0:T(8,128)(2,1)S(1)} %copy-done.1, bf16[2,2048,512]{2,1,0:T(8,128)(2,1)S(1)} %copy-done.3), custom_call_target="tpu_custom_call" | custom-call | flops 2147483648 | bytes 4194304 | tf_op jit(solution)/shard_map/cache_attention/pallas_call | solution.py:103
  79.8 0.0 collective-permute-done.2.refs_1_
  79.8 0.0 collective-permute-done.3.du_b
  79.8 0.6 collective-permute-start.5
  80.4 0.0 collective-permute-start.6
  80.4 2.0 %collective-permute-start.7 = (bf16[256,512]{1,0:T(8,128)(2,1)S(1)}, bf16[256,512]{1,0:T(8,128)(2,1)S(1)}, u32[]{:S(2)}, u32[]{:S(2)}) collective-permute-start(bf16[256,512]{1,0:T(8,128)(2,1)S(1)} %collective-permute-done.2.refs_1_), channel_id=1, source_target_pairs={{0,16},{16,0},{1,17},{17,1},{2,18},{18,2},{3,19},{19,3},{4,20},{20... | collective-permute-start | bytes 786440 | tf_op jit(solution)/shard_map/ppermute | solution.py:382
  82.4 0.0 collective-permute-done.4.du_c
  82.4 0.0 collective-permute-done.5.du_d
  82.5 0.0 collective-permute-done.1.x_theirs
  82.5 0.0 copy-done.14
  82.5 0.0 copy-done.15
  82.5 0.0 copy-done.5
  82.5 2.4 %near_products.1.near = f32[512,512]{1,0:T(8,128)S(1)} custom-call(s32[16]{0:T(128)S(1)} %copy-done.14, s32[16]{0:T(128)S(1)} %copy-done.15, bf16[4,128,1024]{2,1,0:T(8,128)(2,1)S(1)} %all-to-all-done.x_mine, bf16[4,128,1024]{2,1,0:T(8,128)(2,1)S(1)} %collective-permute-done.1.x_theirs, bf16[1024,512]{1,0:T(8,128)(2,1)S(1)} %copy-done.5, ...), custom_call_target="tpu_custom_call" | custom-call | flops 1073741824 | bytes 6291456 | tf_op jit(solution)/shard_map/near_products/pallas_call | solution.py:247
  84.9 0.0 copy-start.11
  84.9 4.9 %collective-permute-done.6.refs_2_ = bf16[256,512]{1,0:T(8,128)(2,1)S(1)} collective-permute-done((bf16[256,512]{1,0:T(8,128)(2,1)}, bf16[256,512]{1,0:T(8,128)(2,1)S(1)}, u32[]{:S(2)}, u32[]{:S(2)}) %collective-permute-start.6) | collective-permute-done | bytes 262176 | tf_op jit(solution)/shard_map/ppermute | solution.py:377
  89.8 4.7 %collective-permute-done.7.refs_3_ = bf16[256,512]{1,0:T(8,128)(2,1)S(1)} collective-permute-done((bf16[256,512]{1,0:T(8,128)(2,1)S(1)}, bf16[256,512]{1,0:T(8,128)(2,1)S(1)}, u32[]{:S(2)}, u32[]{:S(2)}) %collective-permute-start.7) | collective-permute-done | bytes 262176 | tf_op jit(solution)/shard_map/ppermute | solution.py:382
  94.5 1.7 %far_products.1 = bf16[4,128,512]{2,1,0:T(8,128)(2,1)S(1)} custom-call(bf16[4,128,1024]{2,1,0:T(8,128)(2,1)S(1)} %all-to-all-done.x_mine, bf16[4,128,1024]{2,1,0:T(8,128)(2,1)S(1)} %collective-permute-done.1.x_theirs, f32[512,512]{1,0:T(8,128)S(1)} %near_products.1.near, bf16[256,512]{1,0:T(8,128)(2,1)} %collective-permute-done.refs_0_, ...), custom_call_target="tpu_custom_call" | custom-call | flops 536870912 | bytes 5242880 | tf_op jit(solution)/shard_map/far_products/pallas_call | solution.py:293
  96.3 10.6 %all_to_all.16.parts = bf16[4,128,512]{2,1,0:T(8,128)(2,1)S(1)} all-to-all(bf16[4,128,512]{2,1,0:T(8,128)(2,1)S(1)} %far_products.1), channel_id=1, replica_groups=mesh['parts'=2,'wing'=2,'quad'=4,'tensor'=2] {'quad'}, dimensions={0} | all-to-all | bytes 1048576 | tf_op jit(solution)/shard_map/all_to_all | solution.py:389
  106.9 1.4 %finish_attention.1 = (bf16[128,4096]{1,0:T(8,128)(2,1)}, bf16[128,512]{1,0:T(8,128)(2,1)}) custom-call(bf16[4,128,512]{2,1,0:T(8,128)(2,1)S(1)} %all_to_all.16.parts, f32[64,4096]{1,0:T(8,128)S(1)} %get-tuple-element.30.refs_0_, f32[64,4096]{1,0:T(8,128)S(1)} %get-tuple-element.31.refs_1_, bf16[2048,64]{1,0:T(8,128)(2,1)S(1)} %copy-done.11, ...), custom_call_target="tpu_custom_call" | custom-call | tf_op jit(solution)/shard_map/finish_attention/pallas_call | solution.py:330
  (11 shorter events, 0.0 us)
Async XLA Ops:
  0.6 44.8 %copy-start.4 = (bf16[128,4096]{1,0:T(8,128)(2,1)S(1)}, bf16[128,4096]{1,0:T(8,128)(2,1)}, u32[]{:S(2)}) copy-start(bf16[128,4096]{1,0:T(8,128)(2,1)} %q_ref.3) | copy-start | bytes 3145732
  0.6 1.3 %copy-start.6 = (bf16[128,4096]{1,0:T(8,128)(2,1)S(1)}, bf16[128,4096]{1,0:T(8,128)(2,1)}, u32[]{:S(2)}) copy-start(bf16[128,4096]{1,0:T(8,128)(2,1)} %x_ref.1) | copy-start | bytes 3145732
  2.0 1.0 copy-start.9
  3.0 0.8 copy-start.12
  3.8 41.7 %copy-start.13 = (s32[2]{0:T(128)S(1)}, s32[2]{0:T(128)}, u32[]{:S(2)}) copy-start(s32[2]{0:T(128)} %lens.1) | copy-start | bytes 28
  24.0 36.1 %all-to-all-start = ((bf16[4,128,1024]{2,1,0:T(8,128)(2,1)}), bf16[4,128,1024]{2,1,0:T(8,128)(2,1)S(1)}, u32[]{:S(2)}, u32[]{:S(2)}) async-start(bf16[4,128,1024]{2,1,0:T(8,128)(2,1)} %get-tuple-element.17), calls=%async_computation | async-start | bytes 2097152 | tf_op jit(solution)/shard_map/all_to_all | solution.py:368
  44.5 15.6 %collective-permute-start = (bf16[256,512]{1,0:T(8,128)(2,1)}, bf16[256,512]{1,0:T(8,128)(2,1)}, u32[]{:S(2)}, u32[]{:S(2)}) collective-permute-start(bf16[256,512]{1,0:T(8,128)(2,1)} %get-tuple-element.19), channel_id=1, source_target_pairs={{0,8},{8,0},{1,9},{9,1},{2,10},{10,2},{3,11},{11,3},{4,12},{12,4},... | collective-permute-start | bytes 786440 | tf_op jit(solution)/shard_map/ppermute | solution.py:366
  45.5 2.2 %copy-start = (bf16[2,2048,512]{2,1,0:T(8,128)(2,1)S(1)}, bf16[2,2048,512]{2,1,0:T(8,128)(2,1)}, u32[]{:S(2)}) copy-start(bf16[2,2048,512]{2,1,0:T(8,128)(2,1)} %k_ref.3) | copy-start | bytes 12582916
  47.7 2.2 %copy-start.2 = (bf16[2,2048,512]{2,1,0:T(8,128)(2,1)S(1)}, bf16[2,2048,512]{2,1,0:T(8,128)(2,1)}, u32[]{:S(2)}) copy-start(bf16[2,2048,512]{2,1,0:T(8,128)(2,1)} %v_ref.3) | copy-start | bytes 12582916
  49.8 0.9 copy-start.7
  59.3 0.8 copy-start.10
  60.1 22.3 %collective-permute-start.1 = (bf16[4,128,1024]{2,1,0:T(8,128)(2,1)S(1)}, bf16[4,128,1024]{2,1,0:T(8,128)(2,1)S(1)}, u32[]{:S(2)}, u32[]{:S(2)}) collective-permute-start(bf16[4,128,1024]{2,1,0:T(8,128)(2,1)S(1)} %all-to-all-done.x_mine), channel_id=1, source_target_pairs={{0,1},{1,0},{2,3},{3,2},{4,5},{5,4},{6,7},{7,6},{8,9},{9,8},{10,11... | collective-permute-start | bytes 3145736 | tf_op jit(solution)/shard_map/ppermute | solution.py:374
  60.1 19.7 %collective-permute-start.3 = (bf16[8,48,512]{2,1,0:T(8,128)(2,1)S(1)}, bf16[8,48,512]{2,1,0:T(8,128)(2,1)S(1)}, u32[]{:S(2)}, u32[]{:S(2)}) collective-permute-start(bf16[8,48,512]{2,1,0:T(8,128)(2,1)S(1)} %all_to_all.15.du_a), channel_id=1, source_target_pairs={{0,16},{16,0},{1,17},{17,1},{2,18},{18,2},{3,19},{19,3},{4,20},{20... | collective-permute-start | bytes 1179656 | tf_op jit(solution)/shard_map/ppermute | solution.py:375
  60.2 22.2 %copy-start.14 = (s32[16]{0:T(128)S(1)}, s32[16]{0:T(128)}, u32[]{:S(2)}) copy-start(s32[16]{0:T(128)} %position.1) | copy-start | bytes 196
  60.2 22.2 %copy-start.15 = (s32[16]{0:T(128)S(1)}, s32[16]{0:T(128)}, u32[]{:S(2)}) copy-start(s32[16]{0:T(128)} %adapter.1) | copy-start | bytes 196
  60.2 19.6 %collective-permute-start.2 = (bf16[256,512]{1,0:T(8,128)(2,1)}, bf16[256,512]{1,0:T(8,128)(2,1)S(1)}, u32[]{:S(2)}, u32[]{:S(2)}) collective-permute-start(bf16[256,512]{1,0:T(8,128)(2,1)} %get-tuple-element.24), channel_id=1, source_target_pairs={{0,8},{8,0},{1,9},{9,1},{2,10},{10,2},{3,11},{11,3},{4,12},{12,4},... | collective-permute-start | bytes 786440 | tf_op jit(solution)/shard_map/ppermute | solution.py:366
  63.7 18.7 %collective-permute-start.4 = (bf16[8,48,512]{2,1,0:T(8,128)(2,1)S(1)}, bf16[8,48,512]{2,1,0:T(8,128)(2,1)S(1)}, u32[]{:S(2)}, u32[]{:S(2)}) collective-permute-start(bf16[8,48,512]{2,1,0:T(8,128)(2,1)S(1)} %all_to_all.15.du_a), channel_id=1, source_target_pairs={{0,1},{1,0},{2,3},{3,2},{4,5},{5,4},{6,7},{7,6},{8,9},{9,8},{10,11... | collective-permute-start | bytes 1179656 | tf_op jit(solution)/shard_map/ppermute | solution.py:376
  63.7 2.2 %copy-start.1 = (bf16[2,2048,512]{2,1,0:T(8,128)(2,1)S(1)}, bf16[2,2048,512]{2,1,0:T(8,128)(2,1)}, u32[]{:S(2)}) copy-start(bf16[2,2048,512]{2,1,0:T(8,128)(2,1)} %k_ref.3) | copy-start | bytes 12582916
  65.9 2.2 %copy-start.3 = (bf16[2,2048,512]{2,1,0:T(8,128)(2,1)S(1)}, bf16[2,2048,512]{2,1,0:T(8,128)(2,1)}, u32[]{:S(2)}) copy-start(bf16[2,2048,512]{2,1,0:T(8,128)(2,1)} %v_ref.3) | copy-start | bytes 12582916
  68.1 0.9 copy-start.8
  69.0 13.5 %copy-start.5 = (bf16[1024,512]{1,0:T(8,128)(2,1)S(1)}, bf16[1024,512]{1,0:T(8,128)(2,1)}, u32[]{:S(2)}) copy-start(bf16[1024,512]{1,0:T(8,128)(2,1)} %own_ref.1) | copy-start | bytes 3145732
  79.8 2.6 %collective-permute-start.5 = (bf16[8,48,512]{2,1,0:T(8,128)(2,1)S(1)}, bf16[8,48,512]{2,1,0:T(8,128)(2,1)S(1)}, u32[]{:S(2)}, u32[]{:S(2)}) collective-permute-start(bf16[8,48,512]{2,1,0:T(8,128)(2,1)S(1)} %collective-permute-done.3.du_b), channel_id=1, source_target_pairs={{0,1},{1,0},{2,3},{3,2},{4,5},{5,4},{6,7},{7,6},{8,9},{9,8},{10,11... | collective-permute-start | bytes 1179656 | tf_op jit(solution)/shard_map/ppermute | solution.py:383
  80.4 9.4 %collective-permute-start.6 = (bf16[256,512]{1,0:T(8,128)(2,1)}, bf16[256,512]{1,0:T(8,128)(2,1)S(1)}, u32[]{:S(2)}, u32[]{:S(2)}) collective-permute-start(bf16[256,512]{1,0:T(8,128)(2,1)} %collective-permute-done.refs_0_), channel_id=1, source_target_pairs={{0,16},{16,0},{1,17},{17,1},{2,18},{18,2},{3,19},{19,3},{4,20},{20... | collective-permute-start | bytes 786440 | tf_op jit(solution)/shard_map/ppermute | solution.py:377
  80.4 14.1 %collective-permute-start.7 = (bf16[256,512]{1,0:T(8,128)(2,1)S(1)}, bf16[256,512]{1,0:T(8,128)(2,1)S(1)}, u32[]{:S(2)}, u32[]{:S(2)}) collective-permute-start(bf16[256,512]{1,0:T(8,128)(2,1)S(1)} %collective-permute-done.2.refs_1_), channel_id=1, source_target_pairs={{0,16},{16,0},{1,17},{17,1},{2,18},{18,2},{3,19},{19,3},{4,20},{20... | collective-permute-start | bytes 786440 | tf_op jit(solution)/shard_map/ppermute | solution.py:382
  84.9 22.0 %copy-start.11 = (bf16[2048,64]{1,0:T(8,128)(2,1)S(1)}, bf16[2048,64]{1,0:T(8,128)(2,1)}, u32[]{:S(2)}) copy-start(bf16[2048,64]{1,0:T(8,128)(2,1)} %copy-done.10) | copy-start | bytes 786436

commit v2 on v1

v2 whole, which is shorter than its diff:
```python
import functools
import math

import jax
import jax.numpy as jnp
from jax import lax
from jax.experimental import pallas as pl
from jax.experimental.pallas import tpu as pltpu
from jax.sharding import Mesh
from jax.sharding import PartitionSpec as P

HD = 128
RANK = 16
SPAN = 64
CHUNK = 512
CHUNKS = 2
ADAPTER_SCALE = 2.0
EXP2_SCALE = math.log2(math.e) / math.sqrt(HD)
DEAD = -1e30
MIB = 1024 * 1024
SWAP = [(0, 1), (1, 0)]


def dot_last(a, b):
    return lax.dot_general(a, b, (((1,), (1,)), ((), ())), preferred_element_type=jnp.float32)


def dot(a, b):
    return jnp.dot(a, b, preferred_element_type=jnp.float32)


def cache_kernel(span, kv_heads, group_size, lens, q_ref, fk_ref, k_hbm, v_hbm, out_ref, pf_ref, qs, ks, vs, m_s, l_s, acc, sems):
    length = lens[span]
    rows = group_size * SPAN
    chunks, chunk, _ = ks.shape

    def copies(i):
        live = pl.ds(pl.multiple_of(i * chunk, chunk), chunk)
        return (
            pltpu.make_async_copy(k_hbm.at[span, live, :], ks.at[i], sems.at[0, i]),
            pltpu.make_async_copy(v_hbm.at[span, live, :], vs.at[i], sems.at[1, i]),
        )

    for i in range(chunks):

        @pl.when(i * chunk < length)
        def _():
            for copy in copies(i):
                copy.start()

    def fresh_scores(k):
        s = dot_last(fk_ref[span * SPAN : (span + 1) * SPAN, k * HD : (k + 1) * HD], qs[k])
        key = lax.broadcasted_iota(jnp.int32, (SPAN, rows), 0)
        token = lax.broadcasted_iota(jnp.int32, (SPAN, rows), 1) % SPAN
        return jnp.where(key <= token, s, DEAD)

    for k in range(kv_heads):
        for h in range(group_size):
            col = (k * group_size + h) * HD
            qs[k, h * SPAN : (h + 1) * SPAN, :] = q_ref[span * SPAN : (span + 1) * SPAN, col : col + HD]
        s = fresh_scores(k)
        top = jnp.max(s, axis=0, keepdims=True)
        m_s[k] = top
        l_s[k] = jnp.sum(jnp.exp2((s - top) * EXP2_SCALE), axis=0, keepdims=True)
        acc[k] = jnp.zeros((HD, rows), jnp.float32)

    def add_chunk(i, masked):
        for copy in copies(i):
            copy.wait()
        for k in range(kv_heads):
            s = dot_last(ks[i, :, k * HD : (k + 1) * HD], qs[k])
            if masked:
                slot = i * chunk + lax.broadcasted_iota(jnp.int32, (chunk, rows), 0)
                s = jnp.where(slot < length, s, DEAD)
            before = m_s[k]
            top = jnp.maximum(before, jnp.max(s, axis=0, keepdims=True))
            alpha = jnp.exp2((before - top) * EXP2_SCALE)
            p = jnp.exp2((s - top) * EXP2_SCALE)
            m_s[k] = top
            l_s[k] = l_s[k] * alpha + jnp.sum(p, axis=0, keepdims=True)
            values = vs[i, :, k * HD : (k + 1) * HD].T
            acc[k] = acc[k] * alpha + dot(values, p.astype(jnp.bfloat16))

    @pl.loop(0, length // chunk)
    def _(i):
        add_chunk(i, False)

    @pl.when(length % chunk != 0)
    def _():
        add_chunk(length // chunk, True)

    for k in range(kv_heads):
        inverse = 1.0 / l_s[k]
        p = jnp.exp2((fresh_scores(k) - m_s[k]) * EXP2_SCALE) * inverse
        pf_ref[k * rows : (k + 1) * rows, :] = p.T.astype(jnp.bfloat16)
        mixed = (acc[k] * inverse).T
        for h in range(group_size):
            col = (k * group_size + h) * HD
            out_ref[:, col : col + HD] = mixed[h * SPAN : (h + 1) * SPAN, :]


def cache_attention(span, queries, fresh_keys, keys, values, lengths):
    _, slots, width = keys.shape
    kv_heads = width // HD
    q_width = queries.shape[1]
    group_size = q_width // width
    rows = group_size * SPAN
    chunk = min(CHUNK, slots)
    chunks = slots // chunk
    vmem = pl.BlockSpec(memory_space=pltpu.VMEM)
    hbm = pl.BlockSpec(memory_space=pltpu.HBM)
    return pl.pallas_call(
        functools.partial(cache_kernel, span, kv_heads, group_size),
        in_specs=[pl.BlockSpec(memory_space=pltpu.SMEM), vmem, vmem, hbm, hbm],
        out_specs=[vmem, vmem],
        scratch_shapes=[
            pltpu.VMEM((kv_heads, rows, HD), jnp.bfloat16),
            pltpu.VMEM((chunks, chunk, width), jnp.bfloat16),
            pltpu.VMEM((chunks, chunk, width), jnp.bfloat16),
            pltpu.VMEM((kv_heads, 1, rows), jnp.float32),
            pltpu.VMEM((kv_heads, 1, rows), jnp.float32),
            pltpu.VMEM((kv_heads, HD, rows), jnp.float32),
            pltpu.SemaphoreType.DMA((2, chunks)),
        ],
        out_shape=[
            jax.ShapeDtypeStruct((SPAN, q_width), jnp.float32),
            jax.ShapeDtypeStruct((kv_heads * rows, SPAN), jnp.bfloat16),
        ],
        compiler_params=pltpu.CompilerParams(vmem_limit_bytes=57 * MIB),
        name="cache_attention",
    )(lengths, queries, fresh_keys, keys, values)


def cross_kernel(w_ref, d_ref, u_ref, maps, *outs):
    part, core = lax.axis_index("parts") % 2, lax.axis_index("tensor")
    chunk = outs[0].shape[0]
    cols = u_ref.shape[1]
    width = maps.shape[1] - cols
    first = part * (chunk * len(outs))
    maps[:, :width] = d_ref[:, pl.ds(pl.multiple_of(core * width, width), width)]
    maps[:, width:] = u_ref[...]
    for i, out in enumerate(outs):
        out[...] = w_ref[pl.ds(pl.multiple_of(first + i * chunk, chunk), chunk), :]


def cross_pack(weights, downs, ups, chunks):
    width, cols = weights.shape
    vmem = pl.BlockSpec(memory_space=pltpu.VMEM)
    rows = jax.ShapeDtypeStruct((width // 2 // chunks, cols), weights.dtype)
    maps = jax.ShapeDtypeStruct((downs.shape[0], downs.shape[1] // 2 + cols), downs.dtype)
    return pl.pallas_call(
        cross_kernel,
        in_specs=[vmem] * 3,
        out_specs=[vmem] * (1 + chunks),
        out_shape=[maps] + [rows] * chunks,
        compiler_params=pltpu.CompilerParams(vmem_limit_bytes=8 * MIB),
        name="cross_pack",
    )(weights, downs, ups)


def quad_kernel(x_ref, d_ref, u_ref, maps, out):
    core = lax.axis_index("tensor")
    quads, _, width = out.shape
    tokens, features = x_ref.shape
    ranks, cols = u_ref.shape
    sub = min(width, cols)
    for j in range(quads):
        here = slice(j * width, (j + 1) * width)
        out[j, :tokens, :] = x_ref[:, here]
        begin = pl.multiple_of(core * features + j * width, width)
        out[j, tokens : tokens + ranks, :] = d_ref[:, pl.ds(begin, width)]
        out[j, tokens + ranks : tokens + 2 * ranks, :] = maps[:, here]
        for side in range(2):
            for first in range(0, cols, sub):
                row = tokens + (2 + (side * cols + first) // width) * ranks
                col = (side * cols + first) % width
                up = u_ref[:, first : first + sub] if side == 0 else maps[:, features + first : features + first + sub]
                out[j, row : row + ranks, col : col + sub] = up


def quad_pack(tokens, downs, ups, maps, width, quads):
    vmem = pl.BlockSpec(memory_space=pltpu.VMEM)
    ranks, cols = ups.shape
    rows = tokens.shape[0] + ranks * (2 + 2 * cols // width)
    return pl.pallas_call(
        quad_kernel,
        in_specs=[vmem] * 4,
        out_specs=vmem,
        out_shape=jax.ShapeDtypeStruct((quads, rows, width), tokens.dtype),
        compiler_params=pltpu.CompilerParams(vmem_limit_bytes=8 * MIB),
        name="quad_pack",
    )(tokens, downs, ups, maps)


def near_kernel(tokens, position, adapter, mine, theirs, own_ref, out, ds, us):
    core, wing = lax.axis_index("tensor"), lax.axis_index("wing")
    quads, _, width = mine.shape
    cols = own_ref.shape[1]
    ranks = us.shape[0] // (2 * quads)
    for side in range(2):
        for j in range(quads):
            rows = slice((side * quads + j) * ranks, (side * quads + j + 1) * ranks)
            row = tokens + side * ranks
            ds[0, rows, :] = mine[j, row : row + ranks, :]
            ds[1, rows, :] = theirs[j, row : row + ranks, :]
            sub = min(width, cols)
            for first in range(0, cols, sub):
                row = tokens + (2 + (side * cols + first) // width) * ranks
                col = (side * cols + first) % width
                us[rows, first : first + sub] = mine[j, row : row + ranks, col : col + sub]

    def product(x, weights):
        return dot(x[:, :tokens, :].reshape(quads * tokens, width), weights)

    shrink = dot_last(mine[:, :tokens, :].reshape(quads * tokens, width), ds[0])
    shrink += dot_last(theirs[:, :tokens, :].reshape(quads * tokens, width), ds[1])
    slots = us.shape[0] // RANK
    which = lax.broadcasted_iota(jnp.int32, (SPAN, slots * RANK), 1) // RANK + wing * (slots // 2)
    which = jnp.where(which >= slots, which - slots, which)
    spans = quads * tokens // SPAN
    masked = []
    for i in range(spans):
        slot = position[adapter[wing * spans + i]]
        masked.append(jnp.where(which == slot, shrink[i * SPAN : (i + 1) * SPAN, :], 0.0))
    shrink = (jnp.concatenate(masked, axis=0) * ADAPTER_SCALE).astype(jnp.bfloat16)
    out[...] = dot(shrink, us[...])

    @pl.when(core == wing)
    def _():
        out[...] += product(mine, own_ref[...])

    @pl.when(core != wing)
    def _():
        out[...] += product(theirs, own_ref[...])


def near_products(mine, theirs, own, position, adapter, tokens, ranks):
    quads, _, width = mine.shape
    cols = own.shape[1]
    vmem = pl.BlockSpec(memory_space=pltpu.VMEM)
    smem = pl.BlockSpec(memory_space=pltpu.SMEM)
    return pl.pallas_call(
        functools.partial(near_kernel, tokens),
        in_specs=[smem, smem] + [vmem] * 3,
        out_specs=vmem,
        out_shape=jax.ShapeDtypeStruct((quads * tokens, cols), jnp.float32),
        scratch_shapes=[
            pltpu.VMEM((2, 2 * quads * ranks, width), jnp.bfloat16),
            pltpu.VMEM((2 * quads * ranks, cols), jnp.bfloat16),
        ],
        compiler_params=pltpu.CompilerParams(vmem_limit_bytes=48 * MIB if quads > 4 else 24 * MIB),
        name="near_products",
    )(position, adapter, mine, theirs, own)


def far_kernel(tokens, mine, theirs, near, *refs):
    weights, out, whole = refs[:-2], refs[-2], refs[-1]
    part, core, wing = lax.axis_index("parts") % 2, lax.axis_index("tensor"), lax.axis_index("wing")
    quads, _, width = mine.shape
    chunk = weights[0].shape[0]
    chunks = len(weights) // 2
    for side in range(2):
        first = (part if side == 0 else 1 - part) * (chunks * chunk)
        for i in range(chunks):
            begin = pl.multiple_of(first + i * chunk, chunk)
            whole[pl.ds(begin, chunk), :] = weights[side * chunks + i][...]

    def store(x):
        product = dot(x[:, :tokens, :].reshape(quads * tokens, width), whole[...])
        out[...] = (near[...] + product).astype(jnp.bfloat16).reshape(out.shape)

    @pl.when(core == wing)
    def _():
        store(theirs)

    @pl.when(core != wing)
    def _():
        store(mine)


def far_products(mine, theirs, near, weights, tokens):
    quads, _, width = mine.shape
    cols = near.shape[1]
    vmem = pl.BlockSpec(memory_space=pltpu.VMEM)
    return pl.pallas_call(
        functools.partial(far_kernel, tokens),
        in_specs=[vmem] * (3 + len(weights)),
        out_specs=vmem,
        out_shape=jax.ShapeDtypeStruct((quads, tokens, cols), jnp.bfloat16),
        scratch_shapes=[pltpu.VMEM((width, cols), jnp.bfloat16)],
        compiler_params=pltpu.CompilerParams(vmem_limit_bytes=48 * MIB if quads > 4 else 16 * MIB),
        name="far_products",
    )(mine, theirs, near, *weights)


def finish_kernel(spans, parts, *refs):
    mixed, probs, (out_ref, values_ref) = refs[:spans], refs[spans : 2 * spans], refs[2 * spans :]
    total = parts[0].astype(jnp.float32)
    for j in range(1, parts.shape[0]):
        total = total + parts[j].astype(jnp.float32)
    total = total.astype(jnp.bfloat16)
    values_ref[...] = total
    kv_heads = total.shape[1] // HD
    for span in range(spans):
        rows = slice(span * SPAN, (span + 1) * SPAN)
        count = probs[span].shape[0] // kv_heads
        for k in range(kv_heads):
            fresh = dot(probs[span][k * count : (k + 1) * count, :], total[rows, k * HD : (k + 1) * HD])
            for h in range(count // SPAN):
                col = (k * (count // SPAN) + h) * HD
                out_ref[rows, col : col + HD] = (
                    mixed[span][:, col : col + HD] + fresh[h * SPAN : (h + 1) * SPAN, :]
                ).astype(jnp.bfloat16)


def finish(mixed, fresh_probs, parts):
    _, tokens, cols = parts.shape
    vmem = pl.BlockSpec(memory_space=pltpu.VMEM)
    return pl.pallas_call(
        functools.partial(finish_kernel, len(mixed)),
        in_specs=[vmem] * (1 + 2 * len(mixed)),
        out_specs=[vmem] * 2,
        out_shape=[
            jax.ShapeDtypeStruct((tokens, mixed[0].shape[1]), jnp.bfloat16),
            jax.ShapeDtypeStruct((tokens, cols), jnp.bfloat16),
        ],
        compiler_params=pltpu.CompilerParams(vmem_limit_bytes=16 * MIB),
        name="finish_attention",
    )(parts, *mixed, *fresh_probs)


def on_device(
    normed_inputs,
    value_matrix,
    adapter_down_weight,
    adapter_up_weight,
    adapter_position,
    span_adapter_index,
    queries,
    incoming_keys,
    stored_keys,
    stored_values,
    cache_length,
):
    quads = lax.axis_size("quad")
    parts_swap = [(i, i ^ 1) for i in range(lax.axis_size("parts"))]
    width, cols = value_matrix.shape
    downs = adapter_down_weight.reshape(-1, adapter_down_weight.shape[2])
    ups = adapter_up_weight.reshape(-1, cols)

    def attention(span, lengths):
        return cache_attention(span, queries, incoming_keys, stored_keys, stored_values, lengths)

    maps, *leaving = cross_pack(value_matrix, downs, ups, CHUNKS)
    maps = lax.ppermute(maps, "wing", SWAP)
    far = [lax.ppermute(rows, "wing", SWAP) for rows in leaving]
    message = quad_pack(normed_inputs, downs, ups, maps, width, quads)
    mine = lax.all_to_all(message, "quad", 0, 0)

    lengths, _ = lax.optimization_barrier((cache_length, message))
    first = attention(0, lengths)
    far_0, _ = lax.optimization_barrier((far[0], first[1]))
    far_0_other = lax.ppermute(far_0, "parts", parts_swap)

    lengths, _ = lax.optimization_barrier((cache_length, far_0))
    second = attention(1, lengths)
    mine, far_1, _ = lax.optimization_barrier((mine, far[1], second[1]))
    theirs = lax.ppermute(mine, "tensor", SWAP)
    far_1_other = lax.ppermute(far_1, "parts", parts_swap)

    tokens = normed_inputs.shape[0]
    near = near_products(
        mine, theirs, value_matrix, adapter_position, span_adapter_index, tokens, downs.shape[0]
    )
    products = far_products(mine, theirs, near, (far_0, far_1, far_0_other, far_1_other), tokens)
    parts = lax.all_to_all(products, "quad", 0, 0)
    mixed, fresh_probs = zip(first, second)
    attended, incoming_values = finish(mixed, fresh_probs, parts)
    return (attended, incoming_values)


def solution(mesh):
    sizes = mesh.devices.shape
    cut = Mesh(
        mesh.devices.reshape(sizes[0], 2, sizes[1] // 2, sizes[2]), ("parts", "wing", "quad", "tensor")
    )
    group = ("wing", "quad")
    home = ("parts", "wing", "quad")
    in_specs = (
        P(home, "tensor"),
        P(group, "tensor"),
        P(group, None, None),
        P(group, None, "tensor"),
        P(),
        P("parts"),
        P(home, "tensor"),
        P(home, "tensor"),
        P(home, None, "tensor"),
        P(home, None, "tensor"),
        P(home),
    )
    out_specs = (P(home, "tensor"), P(home, "tensor"))
    return jax.shard_map(
        on_device, mesh=cut, in_specs=in_specs, out_specs=out_specs, check_vma=False
    )
```

time: 109 us -> 99.3 us (0.911)
  waiting for transfers between devices: 9.62 us -> 38 us
  Pallas kernels: 43 us -> 27.6 us
  blocking collectives: 29.8 us -> 15.3 us
  local copies, waits for them, and re-layouts: 14.5 us -> 4.32 us
  starting transfers between devices: 10.6 us -> 12.8 us
    all_to_all x1 -> x0, blocking collectives: 19.2 us -> none  [on_device(): maps_a = lax.all_to_all(du, ('wing', 'quad'), 0, 0)]
    pallas_call x4, Pallas kernels: 22.2 us -> 4.04 us  [the longest x1 2.37 us: near_products(): pl.pallas_call(functools.partial(near_kernel, tokens), in_specs=[smem, sm...]
    ppermute x4 -> x2, waiting for transfers between devices: 0.01 us -> 15 us  [the longest x1 13.3 us: on_device(): maps = lax.ppermute(maps, 'wing', SWAP)]
    ppermute x2, waiting for transfers between devices: 0.01 us -> 14.9 us  [on_device(): far = [lax.ppermute(rows, 'wing', SWAP) for rows in leaving]]
    unnamed x32 -> x26, local copies, waits for them, and re-layouts: 14.5 us -> 4.32 us
    all_to_all x1, blocking collectives: 10.6 us -> 15.3 us  [on_device(): parts = lax.all_to_all(products, 'quad', 0, 0)]
    ppermute x4 -> x2, starting transfers between devices: 0.65 us -> 4.11 us  [the longest x1 4.04 us: on_device(): maps = lax.ppermute(maps, 'wing', SWAP)]
    pallas_call x2, Pallas kernels: 19.3 us -> 22.2 us  [cache_attention(): pl.pallas_call(functools.partial(cache_kernel, span, kv_heads, group_size...]
  transfers between devices with their start and end apart: 9 -> 7, of which waited for: 2 -> 5; matrix products, arithmetic and copies ran while one was open for 0% -> 0% of each run, Pallas kernels for 36% -> 25%
where the time goes in v2:
time: 99.3 us; the launch traced here: 98.8 us
  waiting for transfers between devices  38 us (38%)
  Pallas kernels  27.6 us (28%)
  blocking collectives  15.3 us (15%)
  starting transfers between devices  12.8 us (13%)
  local copies, waits for them, and re-layouts  4.32 us (4%)
    pallas_call x2, Pallas kernels, cache_attention(): pl.pallas_call(functools.partial(cache_kernel, span, kv_heads, group_size...  22.2 us
    all_to_all x1, blocking collectives, on_device(): parts = lax.all_to_all(products, 'quad', 0, 0)  15.3 us
    ppermute x2, waiting for transfers between devices, on_device(): far = [lax.ppermute(rows, 'wing', SWAP) for rows in leaving]  14.9 us
    ppermute x1, waiting for transfers between devices, on_device(): maps = lax.ppermute(maps, 'wing', SWAP)  13.3 us
    ppermute x1, waiting for transfers between devices, on_device(): far_1_other = lax.ppermute(far_1, 'parts', parts_swap)  5.17 us
    unnamed x26, local copies, waits for them, and re-layouts  4.32 us
    ppermute x1, starting transfers between devices, on_device(): maps = lax.ppermute(maps, 'wing', SWAP)  4.04 us
    all_to_all x1, starting transfers between devices, on_device(): mine = lax.all_to_all(message, 'quad', 0, 0)  3.58 us
  transfers between devices with their start and end apart: 7, of which 5 were waited for; matrix products, arithmetic and copies ran while one was open for 0% of the time, Pallas kernels for 25%

profile of v2, /device:TPU:0, one launch (start us, length us, event | category | flops | bytes accessed | tf_op | source)
XLA Modules:
  0.0 98.8 jit_solution(8790590689066248029)
XLA Ops:
  0.6 0.0 copy-start.1
  0.6 1.2 %copy-done.1 = bf16[1024,512]{1,0:T(8,128)(2,1)S(1)} copy-done((bf16[1024,512]{1,0:T(8,128)(2,1)S(1)}, bf16[1024,512]{1,0:T(8,128)(2,1)}, u32[]{:S(2)}) %copy-start.1) | copy-done | bytes 1048600
  1.9 0.0 copy-start.3
  1.9 1.0 %copy-done.3 = bf16[2,16,8192]{2,1,0:T(8,128)(2,1)S(1)} copy-done((bf16[2,16,8192]{2,1,0:T(8,128)(2,1)S(1)}, bf16[2,16,8192]{2,1,0:T(8,128)(2,1)}, u32[]{:S(2)}) %copy-start.3) | copy-done | bytes 524312
  2.9 0.0 copy-start.10
  2.9 0.8 copy-done.10
  3.7 0.0 copy-start.4
  3.7 0.0 copy-start.5
  3.7 0.8 cross_pack.1
  4.4 4.0 %collective-permute-start = (bf16[32,4608]{1,0:T(8,128)(2,1)S(1)}, bf16[32,4608]{1,0:T(8,128)(2,1)S(1)}, u32[]{:S(2)}, u32[]{:S(2)}) collective-permute-start(bf16[32,4608]{1,0:T(8,128)(2,1)S(1)} %get-tuple-element.14), channel_id=1, source_target_pairs={{0,8},{8,0},{1,9},{9,1},{2,10},{10,2},{3,11},{11,3},{4,12},{12,4},... | collective-permute-start | bytes 884744 | tf_op jit(solution)/shard_map/ppermute | solution.py:355
  8.5 13.3 %collective-permute-done.maps = bf16[32,4608]{1,0:T(8,128)(2,1)S(1)} collective-permute-done((bf16[32,4608]{1,0:T(8,128)(2,1)S(1)}, bf16[32,4608]{1,0:T(8,128)(2,1)S(1)}, u32[]{:S(2)}, u32[]{:S(2)}) %collective-permute-start) | collective-permute-done | bytes 294944 | tf_op jit(solution)/shard_map/ppermute | solution.py:355
  21.8 0.0 copy-done.4
  21.8 0.0 copy-done.5
  21.8 0.1 quad_pack.1
  21.9 0.0 copy-start
  21.9 1.3 %copy-done = bf16[4,224,1024]{2,1,0:T(8,128)(2,1)} copy-done((bf16[4,224,1024]{2,1,0:T(8,128)(2,1)}, bf16[4,224,1024]{2,1,0:T(8,128)(2,1)S(1)}, u32[]{:S(2)}) %copy-start) | copy-done | bytes 1835032
  23.2 3.6 %all-to-all-start = ((bf16[4,224,1024]{2,1,0:T(8,128)(2,1)}), bf16[4,224,1024]{2,1,0:T(8,128)(2,1)S(1)}, u32[]{:S(2)}, u32[]{:S(2)}) async-start(bf16[4,224,1024]{2,1,0:T(8,128)(2,1)} %copy-done), calls=%async_computation | async-start | bytes 3670016 | tf_op jit(solution)/shard_map/all_to_all | solution.py:358
  26.8 2.7 %collective-permute-start.2 = (bf16[256,512]{1,0:T(8,128)(2,1)S(1)}, bf16[256,512]{1,0:T(8,128)(2,1)S(1)}, u32[]{:S(2)}, u32[]{:S(2)}) collective-permute-start(bf16[256,512]{1,0:T(8,128)(2,1)S(1)} %get-tuple-element.16), channel_id=1, source_target_pairs={{0,8},{8,0},{1,9},{9,1},{2,10},{10,2},{3,11},{11,3},{4,12},{12,4},... | collective-permute-start | bytes 786440 | tf_op jit(solution)/shard_map/ppermute | solution.py:356
  29.5 0.3 collective-permute-start.1
  29.8 8.8 %cache_attention.2 = (f32[64,4096]{1,0:T(8,128)}, bf16[2048,64]{1,0:T(8,128)(2,1)}) custom-call(s32[2]{0:T(128)} %lens.1, bf16[128,4096]{1,0:T(8,128)(2,1)} %q_ref.3, bf16[128,512]{1,0:T(8,128)(2,1)} %fk_ref.3, bf16[2,2048,512]{2,1,0:T(8,128)(2,1)} %k_hbm.3, bf16[2,2048,512]{2,1,0:T(8,128)(2,1)} %v_hbm.3), custom_call_target="tpu_custom_call" | custom-call | tf_op jit(solution)/shard_map/cache_attention/pallas_call | solution.py:112
  38.6 14.9 %collective-permute-done.2.refs_0_ = bf16[256,512]{1,0:T(8,128)(2,1)S(1)} collective-permute-done((bf16[256,512]{1,0:T(8,128)(2,1)S(1)}, bf16[256,512]{1,0:T(8,128)(2,1)S(1)}, u32[]{:S(2)}, u32[]{:S(2)}) %collective-permute-start.2) | collective-permute-done | bytes 262176 | tf_op jit(solution)/shard_map/ppermute | solution.py:356
  53.4 0.0 copy-start.2
  53.4 0.0 copy-start.11
  53.4 0.0 copy-start.12
  53.4 13.4 %cache_attention.3 = (f32[64,4096]{1,0:T(8,128)}, bf16[2048,64]{1,0:T(8,128)(2,1)}) custom-call(s32[2]{0:T(128)} %lens.1, bf16[128,4096]{1,0:T(8,128)(2,1)} %q_ref.3, bf16[128,512]{1,0:T(8,128)(2,1)} %fk_ref.3, bf16[2,2048,512]{2,1,0:T(8,128)(2,1)} %k_hbm.3, bf16[2,2048,512]{2,1,0:T(8,128)(2,1)} %v_hbm.3), custom_call_target="tpu_custom_call" | custom-call | tf_op jit(solution)/shard_map/cache_attention/pallas_call | solution.py:112
  66.8 0.0 collective-permute-done.1.refs_1_
  66.8 0.0 all-to-all-done.mine
  66.8 0.1 collective-permute-start.3
  66.9 0.1 collective-permute-start.4
  67.0 2.0 %collective-permute-start.5 = (bf16[256,512]{1,0:T(8,128)(2,1)S(1)}, bf16[256,512]{1,0:T(8,128)(2,1)S(1)}, u32[]{:S(2)}, u32[]{:S(2)}) collective-permute-start(bf16[256,512]{1,0:T(8,128)(2,1)S(1)} %collective-permute-done.1.refs_1_), channel_id=1, source_target_pairs={{0,16},{16,0},{1,17},{17,1},{2,18},{18,2},{3,19},{19,3},{4,20},{20... | collective-permute-start | bytes 786440 | tf_op jit(solution)/shard_map/ppermute | solution.py:369
  69.0 1.7 %collective-permute-done.3.theirs = bf16[4,224,1024]{2,1,0:T(8,128)(2,1)S(1)} collective-permute-done((bf16[4,224,1024]{2,1,0:T(8,128)(2,1)S(1)}, bf16[4,224,1024]{2,1,0:T(8,128)(2,1)S(1)}, u32[]{:S(2)}, u32[]{:S(2)}) %collective-permute-start.3) | collective-permute-done | bytes 1835040 | tf_op jit(solution)/shard_map/ppermute | solution.py:368
  70.7 0.0 copy-done.2
  70.7 0.0 copy-done.11
  70.7 0.0 copy-done.12
  70.7 2.4 %near_products.1.near = f32[512,512]{1,0:T(8,128)S(1)} custom-call(s32[16]{0:T(128)S(1)} %copy-done.11, s32[16]{0:T(128)S(1)} %copy-done.12, bf16[4,224,1024]{2,1,0:T(8,128)(2,1)S(1)} %all-to-all-done.mine, bf16[4,224,1024]{2,1,0:T(8,128)(2,1)S(1)} %collective-permute-done.3.theirs, bf16[1024,512]{1,0:T(8,128)(2,1)S(1)} %copy-done.2), custom_call_target="tpu_custom_call" | custom-call | tf_op jit(solution)/shard_map/near_products/pallas_call | solution.py:242
  73.1 0.0 copy-start.6
  73.1 0.0 copy-start.7
  73.1 0.0 copy-start.8
  73.1 0.0 copy-start.9
  73.1 3.0 %collective-permute-done.4.refs_2_ = bf16[256,512]{1,0:T(8,128)(2,1)S(1)} collective-permute-done((bf16[256,512]{1,0:T(8,128)(2,1)S(1)}, bf16[256,512]{1,0:T(8,128)(2,1)S(1)}, u32[]{:S(2)}, u32[]{:S(2)}) %collective-permute-start.4) | collective-permute-done | bytes 262176 | tf_op jit(solution)/shard_map/ppermute | solution.py:363
  76.1 5.2 %collective-permute-done.5.refs_3_ = bf16[256,512]{1,0:T(8,128)(2,1)S(1)} collective-permute-done((bf16[256,512]{1,0:T(8,128)(2,1)S(1)}, bf16[256,512]{1,0:T(8,128)(2,1)S(1)}, u32[]{:S(2)}, u32[]{:S(2)}) %collective-permute-start.5) | collective-permute-done | bytes 262176 | tf_op jit(solution)/shard_map/ppermute | solution.py:369
  81.2 0.8 far_products.1
  82.0 15.3 %all_to_all.10.parts = bf16[4,128,512]{2,1,0:T(8,128)(2,1)S(1)} all-to-all(bf16[4,128,512]{2,1,0:T(8,128)(2,1)S(1)} %far_products.1), channel_id=1, replica_groups=mesh['parts'=2,'wing'=2,'quad'=4,'tensor'=2] {'quad'}, dimensions={0} | all-to-all | bytes 1048576 | tf_op jit(solution)/shard_map/all_to_all | solution.py:376
  97.3 0.0 copy-done.6
  97.4 0.0 copy-done.7
  97.4 0.0 copy-done.8
  97.4 0.0 copy-done.9
  97.4 1.4 %finish_attention.1 = (bf16[128,4096]{1,0:T(8,128)(2,1)}, bf16[128,512]{1,0:T(8,128)(2,1)}) custom-call(bf16[4,128,512]{2,1,0:T(8,128)(2,1)S(1)} %all_to_all.10.parts, f32[64,4096]{1,0:T(8,128)S(1)} %copy-done.6, f32[64,4096]{1,0:T(8,128)S(1)} %copy-done.7, bf16[2048,64]{1,0:T(8,128)(2,1)S(1)} %copy-done.8, bf16[2048,64]{1,0:T(8,128)(2,1)S(1)} %copy-done.9), custom_call_target="tpu_custom_call" | custom-call | tf_op jit(solution)/shard_map/finish_attention/pallas_call | solution.py:319
Async XLA Ops:
  0.6 1.2 %copy-start.1 = (bf16[1024,512]{1,0:T(8,128)(2,1)S(1)}, bf16[1024,512]{1,0:T(8,128)(2,1)}, u32[]{:S(2)}) copy-start(bf16[1024,512]{1,0:T(8,128)(2,1)} %own_ref.1) | copy-start | bytes 3145732
  1.9 1.0 %copy-start.3 = (bf16[2,16,8192]{2,1,0:T(8,128)(2,1)S(1)}, bf16[2,16,8192]{2,1,0:T(8,128)(2,1)}, u32[]{:S(2)}) copy-start(bf16[2,16,8192]{2,1,0:T(8,128)(2,1)} %param.13) | copy-start | bytes 1572868
  2.9 0.8 copy-start.10
  3.7 18.1 %copy-start.4 = (bf16[2,16,8192]{2,1,0:T(8,128)(2,1)S(1)}, bf16[2,16,8192]{2,1,0:T(8,128)(2,1)}, u32[]{:S(2)}) copy-start(bf16[2,16,8192]{2,1,0:T(8,128)(2,1)} %param.13) | copy-start | bytes 1572868
  3.7 18.1 %copy-start.5 = (bf16[128,4096]{1,0:T(8,128)(2,1)S(1)}, bf16[128,4096]{1,0:T(8,128)(2,1)}, u32[]{:S(2)}) copy-start(bf16[128,4096]{1,0:T(8,128)(2,1)} %x_ref.1) | copy-start | bytes 3145732
  4.4 17.4 %collective-permute-start = (bf16[32,4608]{1,0:T(8,128)(2,1)S(1)}, bf16[32,4608]{1,0:T(8,128)(2,1)S(1)}, u32[]{:S(2)}, u32[]{:S(2)}) collective-permute-start(bf16[32,4608]{1,0:T(8,128)(2,1)S(1)} %get-tuple-element.14), channel_id=1, source_target_pairs={{0,8},{8,0},{1,9},{9,1},{2,10},{10,2},{3,11},{11,3},{4,12},{12,4},... | collective-permute-start | bytes 884744 | tf_op jit(solution)/shard_map/ppermute | solution.py:355
  21.9 1.3 %copy-start = (bf16[4,224,1024]{2,1,0:T(8,128)(2,1)}, bf16[4,224,1024]{2,1,0:T(8,128)(2,1)S(1)}, u32[]{:S(2)}) copy-start(bf16[4,224,1024]{2,1,0:T(8,128)(2,1)S(1)} %quad_pack.1) | copy-start | bytes 5505028
  23.2 43.6 %all-to-all-start = ((bf16[4,224,1024]{2,1,0:T(8,128)(2,1)}), bf16[4,224,1024]{2,1,0:T(8,128)(2,1)S(1)}, u32[]{:S(2)}, u32[]{:S(2)}) async-start(bf16[4,224,1024]{2,1,0:T(8,128)(2,1)} %copy-done), calls=%async_computation | async-start | bytes 3670016 | tf_op jit(solution)/shard_map/all_to_all | solution.py:358
  26.8 26.7 %collective-permute-start.2 = (bf16[256,512]{1,0:T(8,128)(2,1)S(1)}, bf16[256,512]{1,0:T(8,128)(2,1)S(1)}, u32[]{:S(2)}, u32[]{:S(2)}) collective-permute-start(bf16[256,512]{1,0:T(8,128)(2,1)S(1)} %get-tuple-element.16), channel_id=1, source_target_pairs={{0,8},{8,0},{1,9},{9,1},{2,10},{10,2},{3,11},{11,3},{4,12},{12,4},... | collective-permute-start | bytes 786440 | tf_op jit(solution)/shard_map/ppermute | solution.py:356
  29.5 37.3 %collective-permute-start.1 = (bf16[256,512]{1,0:T(8,128)(2,1)}, bf16[256,512]{1,0:T(8,128)(2,1)S(1)}, u32[]{:S(2)}, u32[]{:S(2)}) collective-permute-start(bf16[256,512]{1,0:T(8,128)(2,1)} %get-tuple-element.15), channel_id=1, source_target_pairs={{0,8},{8,0},{1,9},{9,1},{2,10},{10,2},{3,11},{11,3},{4,12},{12,4},... | collective-permute-start | bytes 786440 | tf_op jit(solution)/shard_map/ppermute | solution.py:356
  53.4 17.3 %copy-start.2 = (bf16[1024,512]{1,0:T(8,128)(2,1)S(1)}, bf16[1024,512]{1,0:T(8,128)(2,1)}, u32[]{:S(2)}) copy-start(bf16[1024,512]{1,0:T(8,128)(2,1)} %own_ref.1) | copy-start | bytes 3145732
  53.4 17.3 %copy-start.11 = (s32[16]{0:T(128)S(1)}, s32[16]{0:T(128)}, u32[]{:S(2)}) copy-start(s32[16]{0:T(128)} %position.1) | copy-start | bytes 196
  53.4 17.3 %copy-start.12 = (s32[16]{0:T(128)S(1)}, s32[16]{0:T(128)}, u32[]{:S(2)}) copy-start(s32[16]{0:T(128)} %adapter.1) | copy-start | bytes 196
  66.8 3.9 %collective-permute-start.3 = (bf16[4,224,1024]{2,1,0:T(8,128)(2,1)S(1)}, bf16[4,224,1024]{2,1,0:T(8,128)(2,1)S(1)}, u32[]{:S(2)}, u32[]{:S(2)}) collective-permute-start(bf16[4,224,1024]{2,1,0:T(8,128)(2,1)S(1)} %all-to-all-done.mine), channel_id=1, source_target_pairs={{0,1},{1,0},{2,3},{3,2},{4,5},{5,4},{6,7},{7,6},{8,9},{9,8},{10,11... | collective-permute-start | bytes 5505032 | tf_op jit(solution)/shard_map/ppermute | solution.py:368
  66.9 9.2 %collective-permute-start.4 = (bf16[256,512]{1,0:T(8,128)(2,1)S(1)}, bf16[256,512]{1,0:T(8,128)(2,1)S(1)}, u32[]{:S(2)}, u32[]{:S(2)}) collective-permute-start(bf16[256,512]{1,0:T(8,128)(2,1)S(1)} %collective-permute-done.2.refs_0_), channel_id=1, source_target_pairs={{0,16},{16,0},{1,17},{17,1},{2,18},{18,2},{3,19},{19,3},{4,20},{20... | collective-permute-start | bytes 786440 | tf_op jit(solution)/shard_map/ppermute | solution.py:363
  67.0 14.3 %collective-permute-start.5 = (bf16[256,512]{1,0:T(8,128)(2,1)S(1)}, bf16[256,512]{1,0:T(8,128)(2,1)S(1)}, u32[]{:S(2)}, u32[]{:S(2)}) collective-permute-start(bf16[256,512]{1,0:T(8,128)(2,1)S(1)} %collective-permute-done.1.refs_1_), channel_id=1, source_target_pairs={{0,16},{16,0},{1,17},{17,1},{2,18},{18,2},{3,19},{19,3},{4,20},{20... | collective-permute-start | bytes 786440 | tf_op jit(solution)/shard_map/ppermute | solution.py:369
  73.1 24.3 %copy-start.6 = (f32[64,4096]{1,0:T(8,128)S(1)}, f32[64,4096]{1,0:T(8,128)}, u32[]{:S(2)}) copy-start(f32[64,4096]{1,0:T(8,128)} %get-tuple-element.24.refs_0_) | copy-start | bytes 3145732
  73.1 24.3 %copy-start.7 = (f32[64,4096]{1,0:T(8,128)S(1)}, f32[64,4096]{1,0:T(8,128)}, u32[]{:S(2)}) copy-start(f32[64,4096]{1,0:T(8,128)} %get-tuple-element.25.refs_1_) | copy-start | bytes 3145732
  73.1 24.3 %copy-start.8 = (bf16[2048,64]{1,0:T(8,128)(2,1)S(1)}, bf16[2048,64]{1,0:T(8,128)(2,1)}, u32[]{:S(2)}) copy-start(bf16[2048,64]{1,0:T(8,128)(2,1)} %get-tuple-element.18.refs_2_) | copy-start | bytes 786436
  73.1 24.3 %copy-start.9 = (bf16[2048,64]{1,0:T(8,128)(2,1)S(1)}, bf16[2048,64]{1,0:T(8,128)(2,1)}, u32[]{:S(2)}) copy-start(bf16[2048,64]{1,0:T(8,128)(2,1)} %get-tuple-element.21.refs_3_) | copy-start | bytes 786436

commit v3 on v2

v3 whole, which is shorter than its diff:
```python
import functools
import math

import jax
import jax.numpy as jnp
from jax import lax
from jax.experimental import pallas as pl
from jax.experimental.pallas import tpu as pltpu
from jax.sharding import Mesh
from jax.sharding import PartitionSpec as P

HD = 128
RANK = 16
SPAN = 64
CHUNK = 512
EARLY = 2
ONES = 16
ADAPTER_SCALE = 2.0
EXP2_SCALE = math.log2(math.e) / math.sqrt(HD)
DEAD = -1e30
MIB = 1024 * 1024
SWAP = [(0, 1), (1, 0)]
FREE = pl.CostEstimate(flops=1, bytes_accessed=1, transcendentals=0)


def dot_last(a, b):
    return lax.dot_general(a, b, (((1,), (1,)), ((), ())), preferred_element_type=jnp.float32)


def dot(a, b):
    return jnp.dot(a, b, preferred_element_type=jnp.float32)


def cache_kernel(span, first_head, kv_heads, group_size, lens, q_ref, fk_ref, k_hbm, v_hbm, out_ref, pf_ref, qs, ks, vs, m_s, acc, sems):
    length = lens[span]
    rows = group_size * SPAN
    chunks, chunk, width = ks.shape
    heads = slice(first_head * HD, first_head * HD + width)

    def copies(i):
        live = pl.ds(pl.multiple_of(i * chunk, chunk), chunk)
        return (
            pltpu.make_async_copy(k_hbm.at[span, live, heads], ks.at[i], sems.at[0, i]),
            pltpu.make_async_copy(v_hbm.at[span, live, heads], vs.at[i], sems.at[1, i]),
        )

    for i in range(chunks):

        @pl.when(i * chunk < length)
        def _():
            for copy in copies(i):
                copy.start()

    def fresh_scores(k):
        s = dot_last(fk_ref[span * SPAN : (span + 1) * SPAN, (first_head + k) * HD : (first_head + k + 1) * HD], qs[k])
        key = lax.broadcasted_iota(jnp.int32, (SPAN, rows), 0)
        token = lax.broadcasted_iota(jnp.int32, (SPAN, rows), 1) % SPAN
        return jnp.where(key <= token, s, DEAD)

    for k in range(kv_heads):
        for h in range(group_size):
            col = ((first_head + k) * group_size + h) * HD
            qs[k, h * SPAN : (h + 1) * SPAN, :] = q_ref[span * SPAN : (span + 1) * SPAN, col : col + HD]
        m_s[k] = jnp.max(fresh_scores(k), axis=0, keepdims=True)
        acc[k] = jnp.zeros((HD + ONES, rows), jnp.float32)

    ones = jnp.ones((ONES, chunk), jnp.bfloat16)

    def add_chunk(i, masked):
        for copy in copies(i):
            copy.wait()

        def scores(k):
            s = dot_last(ks[i, :, k * HD : (k + 1) * HD], qs[k])
            if masked:
                slot = i * chunk + lax.broadcasted_iota(jnp.int32, (chunk, rows), 0)
                s = jnp.where(slot < length, s, DEAD)
            return s

        s = scores(0)
        for k in range(kv_heads):
            later = scores(k + 1) if k + 1 < kv_heads else None
            before = m_s[k]
            top = jnp.maximum(before, jnp.max(s, axis=0, keepdims=True))
            m_s[k] = top
            p = jnp.exp2((s - top) * EXP2_SCALE).astype(jnp.bfloat16)
            alpha = jnp.exp2((before - top) * EXP2_SCALE)
            values = jnp.concatenate([vs[i, :, k * HD : (k + 1) * HD].T, ones], axis=0)
            acc[k] = acc[k] * alpha + dot(values, p)
            s = later

    @pl.loop(0, length // chunk)
    def _(i):
        add_chunk(i, False)

    @pl.when(length % chunk != 0)
    def _():
        add_chunk(length // chunk, True)

    for k in range(kv_heads):
        p = jnp.exp2((fresh_scores(k) - m_s[k]) * EXP2_SCALE)
        inverse = 1.0 / (acc[k, HD : HD + 1, :] + jnp.sum(p, axis=0, keepdims=True))
        pf_ref[k * rows : (k + 1) * rows, :] = (p * inverse).T.astype(jnp.bfloat16)
        mixed = (acc[k, :HD, :] * inverse).T
        for h in range(group_size):
            col = (k * group_size + h) * HD
            out_ref[:, col : col + HD] = mixed[h * SPAN : (h + 1) * SPAN, :]


def cache_attention(span, first_head, kv_heads, hides, queries, fresh_keys, keys, values, lengths):
    slots = keys.shape[1]
    group_size = queries.shape[1] // keys.shape[2]
    width = kv_heads * HD
    rows = group_size * SPAN
    chunk = min(CHUNK, slots)
    chunks = slots // chunk
    vmem = pl.BlockSpec(memory_space=pltpu.VMEM)
    hbm = pl.BlockSpec(memory_space=pltpu.HBM)
    return pl.pallas_call(
        functools.partial(cache_kernel, span, first_head, kv_heads, group_size),
        in_specs=[pl.BlockSpec(memory_space=pltpu.SMEM), vmem, vmem, hbm, hbm],
        out_specs=[vmem, vmem],
        scratch_shapes=[
            pltpu.VMEM((kv_heads, rows, HD), jnp.bfloat16),
            pltpu.VMEM((chunks, chunk, width), jnp.bfloat16),
            pltpu.VMEM((chunks, chunk, width), jnp.bfloat16),
            pltpu.VMEM((kv_heads, 1, rows), jnp.float32),
            pltpu.VMEM((kv_heads, HD + ONES, rows), jnp.float32),
            pltpu.SemaphoreType.DMA((2, chunks)),
        ],
        out_shape=[
            jax.ShapeDtypeStruct((SPAN, group_size * width), jnp.float32),
            jax.ShapeDtypeStruct((kv_heads * rows, SPAN), jnp.bfloat16),
        ],
        compiler_params=pltpu.CompilerParams(vmem_limit_bytes=57 * MIB),
        cost_estimate=pl.CostEstimate(
            flops=4 * rows * slots * width, bytes_accessed=4 * slots * width, transcendentals=0
        )
        if hides
        else FREE,
        name="cache_attention",
    )(lengths, queries, fresh_keys, keys, values)


def run_copies(copies, sems):
    copies = [pltpu.make_async_copy(src, dst, sems.at[i]) for i, (src, dst) in enumerate(copies)]
    for copy in copies:
        copy.start()
    for copy in copies:
        copy.wait()


def cross_kernel(w_hbm, d_hbm, u_hbm, early, late, sems):
    part, core = lax.axis_index("parts") % 2, lax.axis_index("tensor")
    cols = u_hbm.shape[1]
    features = d_hbm.shape[1] // 2
    pieces = features // cols
    ranks = d_hbm.shape[0]
    head = early.shape[0] - (pieces + 1) * ranks
    begin = part * (head + late.shape[0])
    copies = []
    for i in range(pieces):
        here = pl.ds(pl.multiple_of(core * features + i * cols, cols), cols)
        copies.append((d_hbm.at[:, here], early.at[head + i * ranks : head + (i + 1) * ranks, :]))
    copies.append((u_hbm, early.at[head + pieces * ranks :, :]))
    copies.append((w_hbm.at[pl.ds(pl.multiple_of(begin, head), head), :], early.at[:head, :]))
    rest = pl.ds(pl.multiple_of(begin + head, head), late.shape[0])
    copies.append((w_hbm.at[rest, :], late))
    run_copies(copies, sems)


def cross_pack(weights, downs, ups):
    width, cols = weights.shape
    head = width // 2 // EARLY
    pieces = downs.shape[1] // 2 // cols
    vmem = pl.BlockSpec(memory_space=pltpu.VMEM)
    hbm = pl.BlockSpec(memory_space=pltpu.HBM)
    return pl.pallas_call(
        cross_kernel,
        in_specs=[hbm] * 3,
        out_specs=[vmem] * 2,
        out_shape=[
            jax.ShapeDtypeStruct((head + (pieces + 1) * downs.shape[0], cols), weights.dtype),
            jax.ShapeDtypeStruct((width // 2 - head, cols), weights.dtype),
        ],
        scratch_shapes=[pltpu.SemaphoreType.DMA((pieces + 3,))],
        compiler_params=pltpu.CompilerParams(vmem_limit_bytes=57 * MIB),
        cost_estimate=FREE,
        name="cross_pack",
    )(weights, downs, ups)


def up_places(cols, width):
    step = min(cols, width)
    return [
        (slot, first, (slot * cols + first) // width * RANK, (slot * cols + first) % width)
        for slot in range(2)
        for first in range(0, cols, step)
    ]


def quad_kernel(x_hbm, d_hbm, u_hbm, out, sems):
    core = lax.axis_index("tensor")
    quads, _, width = out.shape
    tokens, features = x_hbm.shape
    ranks, cols = u_hbm.shape
    step = min(cols, width)
    copies = []
    for j in range(quads):
        begin = pl.multiple_of(core * features + j * width, width)
        copies.append((x_hbm.at[:, j * width : (j + 1) * width], out.at[j, :tokens, :]))
        copies.append((d_hbm.at[:, pl.ds(begin, width)], out.at[j, tokens : tokens + ranks, :]))
        for slot, first, row, col in up_places(cols, width):
            row += tokens + ranks
            copies.append(
                (
                    u_hbm.at[slot * RANK : (slot + 1) * RANK, first : first + step],
                    out.at[j, row : row + RANK, col : col + step],
                )
            )
    run_copies(copies, sems)


def quad_pack(tokens, downs, ups, width, quads):
    vmem = pl.BlockSpec(memory_space=pltpu.VMEM)
    hbm = pl.BlockSpec(memory_space=pltpu.HBM)
    ranks, cols = ups.shape
    rows = tokens.shape[0] + ranks + RANK * (2 * cols // width)
    count = quads * (2 + len(up_places(cols, width)))
    return pl.pallas_call(
        quad_kernel,
        in_specs=[hbm] * 3,
        out_specs=vmem,
        out_shape=jax.ShapeDtypeStruct((quads, rows, width), tokens.dtype),
        scratch_shapes=[pltpu.SemaphoreType.DMA((count,))],
        compiler_params=pltpu.CompilerParams(vmem_limit_bytes=57 * MIB),
        cost_estimate=FREE,
        name="quad_pack",
    )(tokens, downs, ups)


def maps_kernel(here, rows_out, *outs):
    quad = lax.axis_index("quad")
    width = outs[0].shape[1]
    cols = here.shape[1]
    ranks = 2 * RANK
    step = min(cols, width)
    head = rows_out.shape[0]
    last = here.shape[0] - ranks
    rows_out[...] = here[:head, :]
    for q, out in enumerate(outs):
        for first in range(0, width, step):
            place = (quad ^ q) * width + first
            row = pl.multiple_of(head + place // cols * ranks, RANK)
            col = pl.multiple_of(place % cols, step)
            out[:ranks, first : first + step] = here[pl.ds(row, ranks), pl.ds(col, step)]
        for slot, first, row, col in up_places(cols, width):
            up = here[last + slot * RANK : last + (slot + 1) * RANK, first : first + step]
            out[ranks + row : ranks + row + RANK, col : col + step] = up


def maps_pack(here, width, quads):
    vmem = pl.BlockSpec(memory_space=pltpu.VMEM)
    rows, cols = here.shape
    head = rows - (quads * width // cols + 1) * 2 * RANK
    maps = jax.ShapeDtypeStruct((RANK * (2 + 2 * cols // width), width), here.dtype)
    return pl.pallas_call(
        maps_kernel,
        in_specs=[vmem],
        out_specs=[vmem] * (1 + quads),
        out_shape=[jax.ShapeDtypeStruct((head, cols), here.dtype)] + [maps] * quads,
        compiler_params=pltpu.CompilerParams(vmem_limit_bytes=4 * MIB),
        cost_estimate=FREE,
        name="maps_pack",
    )(here)


def near_kernel(tokens, position, adapter, mine, theirs, maps_mine, maps_theirs, own_ref, out, ds, us):
    core, wing, quad = lax.axis_index("tensor"), lax.axis_index("wing"), lax.axis_index("quad")
    quads, _, width = mine.shape
    cols = own_ref.shape[1]
    ranks = 2 * RANK
    step = min(cols, width)
    for j in range(quads):
        for side, here, there, base, index in (
            (0, mine.at[j], theirs.at[j], tokens, j),
            (1, maps_mine.at[j], maps_theirs.at[j], 0, quad ^ j),
        ):
            first_row = (side * quads + index) * ranks
            rows = pl.ds(pl.multiple_of(first_row, ranks), ranks)
            ds[0, rows, :] = here[base : base + ranks, :]
            ds[1, rows, :] = there[base : base + ranks, :]
            for slot, first, row, col in up_places(cols, width):
                row += base + ranks
                place = pl.ds(pl.multiple_of(first_row + slot * RANK, RANK), RANK)
                us[place, first : first + step] = here[row : row + RANK, col : col + step]

    x_mine = mine[:, :tokens, :].reshape(quads * tokens, width)
    x_theirs = theirs[:, :tokens, :].reshape(quads * tokens, width)
    shrink = dot_last(x_mine, ds[0]) + dot_last(x_theirs, ds[1])
    slots = us.shape[0] // RANK
    which = lax.broadcasted_iota(jnp.int32, (SPAN, slots * RANK), 1) // RANK + wing * (slots // 2)
    which = jnp.where(which >= slots, which - slots, which)
    spans = quads * tokens // SPAN
    masked = []
    for i in range(spans):
        slot = position[adapter[wing * spans + i]]
        masked.append(jnp.where(which == slot, shrink[i * SPAN : (i + 1) * SPAN, :], 0.0))
    shrink = (jnp.concatenate(masked, axis=0) * ADAPTER_SCALE).astype(jnp.bfloat16)
    out[...] = dot(shrink, us[...])

    @pl.when(core == wing)
    def _():
        out[...] += dot(x_mine, own_ref[...])

    @pl.when(core != wing)
    def _():
        out[...] += dot(x_theirs, own_ref[...])


def near_products(mine, theirs, maps_mine, maps_theirs, own, position, adapter, tokens):
    quads, _, width = mine.shape
    cols = own.shape[1]
    ranks = 4 * quads * RANK
    vmem = pl.BlockSpec(memory_space=pltpu.VMEM)
    smem = pl.BlockSpec(memory_space=pltpu.SMEM)
    return pl.pallas_call(
        functools.partial(near_kernel, tokens),
        in_specs=[smem, smem] + [vmem] * 5,
        out_specs=vmem,
        out_shape=jax.ShapeDtypeStruct((quads * tokens, cols), jnp.float32),
        scratch_shapes=[
            pltpu.VMEM((2, ranks, width), jnp.bfloat16),
            pltpu.VMEM((ranks, cols), jnp.bfloat16),
        ],
        compiler_params=pltpu.CompilerParams(vmem_limit_bytes=48 * MIB if quads > 4 else 24 * MIB),
        cost_estimate=FREE,
        name="near_products",
    )(position, adapter, mine, theirs, maps_mine, maps_theirs, own)


def far_kernel(tokens, mine, theirs, near, *refs):
    quads, _, width = mine.shape
    outs, (whole, total) = refs[-2 - quads : -2], refs[-2:]
    weights = refs[:4]
    part, core, wing = lax.axis_index("parts") % 2, lax.axis_index("tensor"), lax.axis_index("wing")
    quad = lax.axis_index("quad")
    late = weights[1].shape[0]
    head = width // 2 - late
    for side in range(2):
        begin = (part if side == 0 else 1 - part) * (width // 2)
        whole[pl.ds(pl.multiple_of(begin, head), head), :] = weights[2 * side][...]
        whole[pl.ds(pl.multiple_of(begin + head, head), late), :] = weights[2 * side + 1][...]

    def store(x):
        product = dot(x[:, :tokens, :].reshape(quads * tokens, width), whole[...])
        total[...] = (near[...] + product).astype(jnp.bfloat16).reshape(total.shape)

    @pl.when(core == wing)
    def _():
        store(theirs)

    @pl.when(core != wing)
    def _():
        store(mine)

    for q in range(quads):
        outs[q][...] = total[quad ^ q]


def far_products(mine, theirs, near, weights, tokens):
    quads, _, width = mine.shape
    cols = near.shape[1]
    vmem = pl.BlockSpec(memory_space=pltpu.VMEM)
    return pl.pallas_call(
        functools.partial(far_kernel, tokens),
        in_specs=[vmem] * (3 + len(weights)),
        out_specs=[vmem] * quads,
        out_shape=[jax.ShapeDtypeStruct((tokens, cols), jnp.bfloat16)] * quads,
        scratch_shapes=[
            pltpu.VMEM((width, cols), jnp.bfloat16),
            pltpu.VMEM((quads, tokens, cols), jnp.bfloat16),
        ],
        compiler_params=pltpu.CompilerParams(vmem_limit_bytes=48 * MIB if quads > 4 else 16 * MIB),
        cost_estimate=FREE,
        name="far_products",
    )(mine, theirs, near, *weights)


def finish_kernel(places, *refs):
    count = len(places)
    out_ref, values_ref = refs[-2:]
    mixed, probs, parts = refs[:count], refs[count : 2 * count], refs[2 * count : -2]
    total = parts[0][...].astype(jnp.float32)
    for part in parts[1:]:
        total = total + part[...].astype(jnp.float32)
    total = total.astype(jnp.bfloat16)
    values_ref[...] = total
    for (span, head), mix, prob in zip(places, mixed, probs):
        rows = slice(span * SPAN, (span + 1) * SPAN)
        group_size = out_ref.shape[1] // total.shape[1]
        queries = group_size * SPAN
        for k in range(prob.shape[0] // queries):
            values = total[rows, (head + k) * HD : (head + k + 1) * HD]
            fresh = dot(prob[k * queries : (k + 1) * queries, :], values)
            for h in range(group_size):
                here = slice((k * group_size + h) * HD, (k * group_size + h + 1) * HD)
                col = ((head + k) * group_size + h) * HD
                out_ref[rows, col : col + HD] = (
                    mix[:, here] + fresh[h * SPAN : (h + 1) * SPAN, :]
                ).astype(jnp.bfloat16)


def finish(places, mixed, fresh_probs, parts, q_width):
    tokens, cols = parts[0].shape
    vmem = pl.BlockSpec(memory_space=pltpu.VMEM)
    return pl.pallas_call(
        functools.partial(finish_kernel, places),
        in_specs=[vmem] * (len(parts) + 2 * len(mixed)),
        out_specs=[vmem] * 2,
        out_shape=[
            jax.ShapeDtypeStruct((tokens, q_width), jnp.bfloat16),
            jax.ShapeDtypeStruct((tokens, cols), jnp.bfloat16),
        ],
        compiler_params=pltpu.CompilerParams(vmem_limit_bytes=16 * MIB),
        cost_estimate=FREE,
        name="finish_attention",
    )(*mixed, *fresh_probs, *parts)


def on_device(
    normed_inputs,
    value_matrix,
    adapter_down_weight,
    adapter_up_weight,
    adapter_position,
    span_adapter_index,
    queries,
    incoming_keys,
    stored_keys,
    stored_values,
    cache_length,
):
    quads = lax.axis_size("quad")
    parts_swap = [(i, i ^ 1) for i in range(lax.axis_size("parts"))]
    width, cols = value_matrix.shape
    downs = adapter_down_weight.reshape(-1, adapter_down_weight.shape[2])
    ups = adapter_up_weight.reshape(-1, cols)

    kv_heads = cols // HD
    places = [(span, head) for span in range(2) for head in range(0, kv_heads, kv_heads // 2)]

    def attention(place, lengths):
        span, head = places[place]
        return cache_attention(
            span, head, kv_heads // 2, place > 1, queries, incoming_keys, stored_keys, stored_values, lengths
        )

    def after(value, *others):
        return lax.optimization_barrier((value, *others))[0]

    def to_quad(value, q):
        return lax.ppermute(value, "quad", [(j, j ^ q) for j in range(quads)])

    early, late = cross_pack(value_matrix, downs, ups)
    message = quad_pack(after(normed_inputs, early), downs, ups, width, quads)
    early = lax.ppermute(early, "wing", SWAP)
    mine = lax.all_to_all(message, "quad", 0, 0)

    attn = [attention(0, after(cache_length, message))]
    attn.append(attention(1, after(cache_length, attn[0][1])))
    early = after(early, attn[1][1])
    late = lax.ppermute(after(late, early), "wing", SWAP)
    early, *passed = maps_pack(early, width, quads)
    early_other = lax.ppermute(early, "parts", parts_swap)
    passed_on = [to_quad(passed[q], q) for q in range(1, quads)]

    attn.append(attention(2, after(cache_length, early)))
    maps_mine = jnp.stack([passed[0]] + [after(maps, attn[2][1]) for maps in passed_on])
    theirs = lax.ppermute(after(mine, early), "tensor", SWAP)
    maps_theirs = lax.ppermute(maps_mine, "tensor", SWAP)
    late_other = lax.ppermute(after(late, attn[2][1]), "parts", parts_swap)

    tokens, q_width = queries.shape
    near = near_products(
        mine, theirs, maps_mine, maps_theirs, value_matrix, adapter_position, span_adapter_index, tokens
    )
    products = far_products(mine, theirs, near, (early, late, early_other, late_other), tokens)
    parts = [to_quad(products[q], q) for q in range(1, quads)]
    attn.append(attention(3, after(cache_length, products[0])))
    parts = [products[0]] + [after(part, attn[3][1]) for part in parts]
    mixed, fresh_probs = zip(*attn)
    attended, incoming_values = finish(places, mixed, fresh_probs, parts, q_width)
    return (attended, incoming_values)


def solution(mesh):
    sizes = mesh.devices.shape
    cut = Mesh(
        mesh.devices.reshape(sizes[0], 2, sizes[1] // 2, sizes[2]), ("parts", "wing", "quad", "tensor")
    )
    group = ("wing", "quad")
    home = ("parts", "wing", "quad")
    in_specs = (
        P(home, "tensor"),
        P(group, "tensor"),
        P(group, None, None),
        P(group, None, "tensor"),
        P(),
        P("parts"),
        P(home, "tensor"),
        P(home, "tensor"),
        P(home, None, "tensor"),
        P(home, None, "tensor"),
        P(home),
    )
    out_specs = (P(home, "tensor"), P(home, "tensor"))
    return jax.shard_map(
        on_device, mesh=cut, in_specs=in_specs, out_specs=out_specs, check_vma=False
    )
```

time: 99.3 us -> 85 us (0.86)
  blocking collectives: 15.3 us -> 0 us
  waiting for transfers between devices: 38 us -> 27.3 us
  Pallas kernels: 27.6 us -> 34.5 us
  starting transfers between devices: 12.8 us -> 19.6 us
  local copies, waits for them, and re-layouts: 4.32 us -> 2.03 us
    all_to_all x1 -> x0, blocking collectives: 15.3 us -> none  [on_device(): parts = lax.all_to_all(products, 'quad', 0, 0)]
    ppermute x6 -> x12, waiting for transfers between devices: 38 us -> 25.2 us  [the longest x1 15.6 us: on_device(): early = lax.ppermute(early, 'wing', SWAP)]
    pallas_call x5 -> x8, Pallas kernels: 24.5 us -> 31.2 us  [the longest x4 24.9 us: cache_attention(): pl.pallas_call(functools.partial(cache_kernel, span, first_head, kv_heads...]
    ppermute x6 -> x12, starting transfers between devices: 9.18 us -> 14.2 us  [the longest x6 7.85 us: to_quad(): return lax.ppermute(value, 'quad', [(j, j ^ q) for j in range(quads)])]
    unnamed x26, local copies, waits for them, and re-layouts: 4.32 us -> 2.03 us
    all_to_all x1, waiting for transfers between devices: 0.01 us -> 2.08 us  [on_device(): mine = lax.all_to_all(message, 'quad', 0, 0)]
    all_to_all x1, starting transfers between devices: 3.58 us -> 5.39 us  [on_device(): mine = lax.all_to_all(message, 'quad', 0, 0)]
  transfers between devices with their start and end apart: 7 -> 13, of which waited for: 5 -> 5; matrix products, arithmetic and copies ran while one was open for 0% -> 0% of each run, Pallas kernels for 25% -> 33%
where the time goes in v3:
time: 85 us; the launch traced here: 84.3 us
  Pallas kernels  34.5 us (41%)
  waiting for transfers between devices  27.3 us (32%)
  starting transfers between devices  19.6 us (23%)
  local copies, waits for them, and re-layouts  2.03 us (2%)
  between operations  0.89 us (1%)
    pallas_call x4, Pallas kernels, cache_attention(): pl.pallas_call(functools.partial(cache_kernel, span, first_head, kv_heads...  24.9 us
    ppermute x1, waiting for transfers between devices, on_device(): early = lax.ppermute(early, 'wing', SWAP)  15.6 us
    ppermute x6, starting transfers between devices, to_quad(): return lax.ppermute(value, 'quad', [(j, j ^ q) for j in range(quads)])  7.85 us
    all_to_all x1, starting transfers between devices, on_device(): mine = lax.all_to_all(message, 'quad', 0, 0)  5.39 us
    ppermute x1, waiting for transfers between devices, on_device(): late_other = lax.ppermute(after(late, attn[2][1]), 'parts', parts_swap)  5.17 us
    ppermute x1, waiting for transfers between devices, on_device(): early_other = lax.ppermute(early, 'parts', parts_swap)  2.81 us
    pallas_call x1, Pallas kernels, quad_pack(): pl.pallas_call(quad_kernel, in_specs=[hbm] * 3, out_specs=vmem, out_shape...  2.62 us
    ppermute x1, starting transfers between devices, on_device(): early = lax.ppermute(early, 'wing', SWAP)  2.59 us
  transfers between devices with their start and end apart: 13, of which 5 were waited for; matrix products, arithmetic and copies ran while one was open for 0% of the time, Pallas kernels for 33%

profile of v3, /device:TPU:0, one launch (start us, length us, event | category | flops | bytes accessed | tf_op | source)
XLA Modules:
  0.0 84.3 jit_solution(8009960561961083898)
XLA Ops:
  0.6 2.2 %cross_pack.1 = (bf16[544,512]{1,0:T(8,128)(2,1)}, bf16[256,512]{1,0:T(8,128)(2,1)}) custom-call(bf16[1024,512]{1,0:T(8,128)(2,1)} %own_ref.1, bf16[32,8192]{1,0:T(8,128)(2,1)} %bitcast.7, bf16[32,512]{1,0:T(8,128)(2,1)} %bitcast.9), custom_call_target="tpu_custom_call" | custom-call | flops 1 | bytes 1 | tf_op jit(solution)/shard_map/cross_pack/pallas_call | solution.py:178
  2.8 2.6 %quad_pack.1 = bf16[4,176,1024]{2,1,0:T(8,128)(2,1)} custom-call(bf16[128,4096]{1,0:T(8,128)(2,1)} %x_hbm, bf16[32,8192]{1,0:T(8,128)(2,1)} %bitcast.8, bf16[32,512]{1,0:T(8,128)(2,1)} %bitcast.10), custom_call_target="tpu_custom_call" | custom-call | flops 1 | bytes 1 | tf_op jit(solution)/shard_map/quad_pack/pallas_call | solution.py:230
  5.5 0.0 copy-start.11
  5.5 5.4 %all-to-all-start = ((bf16[4,176,1024]{2,1,0:T(8,128)(2,1)}), bf16[4,176,1024]{2,1,0:T(8,128)(2,1)S(1)}, u32[]{:S(2)}, u32[]{:S(2)}) async-start(bf16[4,176,1024]{2,1,0:T(8,128)(2,1)} %quad_pack.1), calls=%async_computation | async-start | bytes 2883584 | tf_op jit(solution)/shard_map/all_to_all | solution.py:468
  10.9 2.6 %collective-permute-start = (bf16[544,512]{1,0:T(8,128)(2,1)S(1)}, bf16[544,512]{1,0:T(8,128)(2,1)S(1)}, u32[]{:S(2)}, u32[]{:S(2)}) collective-permute-start(bf16[544,512]{1,0:T(8,128)(2,1)S(1)} %copy-done.11), channel_id=1, source_target_pairs={{0,8},{8,0},{1,9},{9,1},{2,10},{10,2},{3,11},{11,3},{4,12},{12,4},... | collective-permute-start | bytes 1671176 | tf_op jit(solution)/shard_map/ppermute | solution.py:467
  13.5 4.7 %cache_attention.4 = (f32[64,2048]{1,0:T(8,128)}, bf16[1024,64]{1,0:T(8,128)(2,1)}) custom-call(s32[2]{0:T(128)} %lens.3, bf16[128,4096]{1,0:T(8,128)(2,1)} %q_ref.7, bf16[128,512]{1,0:T(8,128)(2,1)} %fk_ref.7, bf16[2,2048,512]{2,1,0:T(8,128)(2,1)} %k_hbm.7, bf16[2,2048,512]{2,1,0:T(8,128)(2,1)} %v_hbm.7), custom_call_target="tpu_custom_call" | custom-call | flops 1 | bytes 1 | tf_op jit(solution)/shard_map/cache_attention/pallas_call | solution.py:119
  18.2 4.7 %cache_attention.5 = (f32[64,2048]{1,0:T(8,128)}, bf16[1024,64]{1,0:T(8,128)(2,1)}) custom-call(s32[2]{0:T(128)} %lens.3, bf16[128,4096]{1,0:T(8,128)(2,1)} %q_ref.7, bf16[128,512]{1,0:T(8,128)(2,1)} %fk_ref.7, bf16[2,2048,512]{2,1,0:T(8,128)(2,1)} %k_hbm.7, bf16[2,2048,512]{2,1,0:T(8,128)(2,1)} %v_hbm.7), custom_call_target="tpu_custom_call" | custom-call | flops 1 | bytes 1 | tf_op jit(solution)/shard_map/cache_attention/pallas_call | solution.py:119
  22.9 15.6 %collective-permute-done.here = bf16[544,512]{1,0:T(8,128)(2,1)S(1)} collective-permute-done((bf16[544,512]{1,0:T(8,128)(2,1)S(1)}, bf16[544,512]{1,0:T(8,128)(2,1)S(1)}, u32[]{:S(2)}, u32[]{:S(2)}) %collective-permute-start) | collective-permute-done | bytes 557088 | tf_op jit(solution)/shard_map/ppermute | solution.py:467
  38.5 0.1 maps_pack.1
  38.5 2.1 %all-to-all-done.mine = bf16[4,176,1024]{2,1,0:T(8,128)(2,1)S(1)} async-done(((bf16[4,176,1024]{2,1,0:T(8,128)(2,1)}), bf16[4,176,1024]{2,1,0:T(8,128)(2,1)S(1)}, u32[]{:S(2)}, u32[]{:S(2)}) %all-to-all-start) | async-done | bytes 1441824 | tf_op jit(solution)/shard_map/all_to_all | solution.py:468
  40.6 0.0 collective-permute-start.1
  40.6 1.5 %collective-permute-start.6 = (bf16[256,512]{1,0:T(8,128)(2,1)S(1)}, bf16[256,512]{1,0:T(8,128)(2,1)S(1)}, u32[]{:S(2)}, u32[]{:S(2)}) collective-permute-start(bf16[256,512]{1,0:T(8,128)(2,1)S(1)} %copy-done.12), channel_id=1, source_target_pairs={{0,8},{8,0},{1,9},{9,1},{2,10},{10,2},{3,11},{11,3},{4,12},{12,4},... | collective-permute-start | bytes 786440 | tf_op jit(solution)/shard_map/ppermute | solution.py:473
  42.1 1.7 %collective-permute-start.2 = (bf16[48,1024]{1,0:T(8,128)(2,1)S(1)}, bf16[48,1024]{1,0:T(8,128)(2,1)S(1)}, u32[]{:S(2)}, u32[]{:S(2)}) collective-permute-start(bf16[48,1024]{1,0:T(8,128)(2,1)S(1)} %get-tuple-element.50), channel_id=1, source_target_pairs={{0,2},{2,0},{4,6},{6,4},{1,3},{3,1},{5,7},{7,5},{8,10},{10,8},{12,... | collective-permute-start | bytes 294920 | tf_op jit(solution)/shard_map/ppermute | solution.py:463
  43.8 1.4 %collective-permute-start.3 = (bf16[48,1024]{1,0:T(8,128)(2,1)S(1)}, bf16[48,1024]{1,0:T(8,128)(2,1)S(1)}, u32[]{:S(2)}, u32[]{:S(2)}) collective-permute-start(bf16[48,1024]{1,0:T(8,128)(2,1)S(1)} %get-tuple-element.53), channel_id=1, source_target_pairs={{0,4},{2,6},{4,0},{6,2},{1,5},{3,7},{5,1},{7,3},{8,12},{10,14},{12... | collective-permute-start | bytes 294920 | tf_op jit(solution)/shard_map/ppermute | solution.py:463
  45.3 0.3 collective-permute-start.4
  45.6 7.7 %cache_attention.6 = (f32[64,2048]{1,0:T(8,128)}, bf16[1024,64]{1,0:T(8,128)(2,1)}) custom-call(s32[2]{0:T(128)} %lens.3, bf16[128,4096]{1,0:T(8,128)(2,1)} %q_ref.7, bf16[128,512]{1,0:T(8,128)(2,1)} %fk_ref.7, bf16[2,2048,512]{2,1,0:T(8,128)(2,1)} %k_hbm.7, bf16[2,2048,512]{2,1,0:T(8,128)(2,1)} %v_hbm.7), custom_call_target="tpu_custom_call" | custom-call | flops 1073741824 | bytes 2097152 | tf_op jit(solution)/shard_map/cache_attention/pallas_call | solution.py:119
  53.3 0.0 collective-permute-done.4
  53.3 0.0 collective-permute-done.3
  53.3 0.0 collective-permute-done.2
  53.3 0.1 pad_maximum_fusion.maps_mine
  53.4 0.1 collective-permute-start.5
  53.5 0.7 collective-permute-start.7
  54.2 1.6 %collective-permute-done.6.refs_1_ = bf16[256,512]{1,0:T(8,128)(2,1)S(1)} collective-permute-done((bf16[256,512]{1,0:T(8,128)(2,1)S(1)}, bf16[256,512]{1,0:T(8,128)(2,1)S(1)}, u32[]{:S(2)}, u32[]{:S(2)}) %collective-permute-start.6) | collective-permute-done | bytes 262176 | tf_op jit(solution)/shard_map/ppermute | solution.py:473
  55.9 1.5 %collective-permute-start.8 = (bf16[256,512]{1,0:T(8,128)(2,1)S(1)}, bf16[256,512]{1,0:T(8,128)(2,1)S(1)}, u32[]{:S(2)}, u32[]{:S(2)}) collective-permute-start(bf16[256,512]{1,0:T(8,128)(2,1)S(1)} %collective-permute-done.6.refs_1_), channel_id=1, source_target_pairs={{0,16},{16,0},{1,17},{17,1},{2,18},{18,2},{3,19},{19,3},{4,20},{20... | collective-permute-start | bytes 786440 | tf_op jit(solution)/shard_map/ppermute | solution.py:482
  57.4 0.0 collective-permute-done.5.maps_theirs
  57.4 0.0 collective-permute-done.1.theirs
  57.4 0.0 copy-done.9
  57.4 0.0 copy-done.10
  57.4 0.0 copy-done
  57.4 2.5 %near_products.1.near = f32[512,512]{1,0:T(8,128)S(1)} custom-call(s32[16]{0:T(128)S(1)} %copy-done.9, s32[16]{0:T(128)S(1)} %copy-done.10, bf16[4,176,1024]{2,1,0:T(8,128)(2,1)S(1)} %all-to-all-done.mine, bf16[4,176,1024]{2,1,0:T(8,128)(2,1)S(1)} %collective-permute-done.1.theirs, bf16[4,48,1024]{2,1,0:T(8,128)(2,1)S(1)} %pad_maximum_fusion.maps_mine, ...), custom_call_target="tpu_custom_call" | custom-call | flops 1 | bytes 1 | tf_op jit(solution)/shard_map/near_products/pallas_call | solution.py:327
  59.8 2.8 %collective-permute-done.7.refs_2_ = bf16[256,512]{1,0:T(8,128)(2,1)S(1)} collective-permute-done((bf16[256,512]{1,0:T(8,128)(2,1)S(1)}, bf16[256,512]{1,0:T(8,128)(2,1)S(1)}, u32[]{:S(2)}, u32[]{:S(2)}) %collective-permute-start.7) | collective-permute-done | bytes 262176 | tf_op jit(solution)/shard_map/ppermute | solution.py:475
  62.7 5.2 %collective-permute-done.8.refs_3_ = bf16[256,512]{1,0:T(8,128)(2,1)S(1)} collective-permute-done((bf16[256,512]{1,0:T(8,128)(2,1)S(1)}, bf16[256,512]{1,0:T(8,128)(2,1)S(1)}, u32[]{:S(2)}, u32[]{:S(2)}) %collective-permute-start.8) | collective-permute-done | bytes 262176 | tf_op jit(solution)/shard_map/ppermute | solution.py:482
  67.8 0.8 far_products.1
  68.7 2.6 %collective-permute-start.11 = (bf16[128,512]{1,0:T(8,128)(2,1)S(1)}, bf16[128,512]{1,0:T(8,128)(2,1)S(1)}, u32[]{:S(2)}, u32[]{:S(2)}) collective-permute-start(bf16[128,512]{1,0:T(8,128)(2,1)S(1)} %get-tuple-element.68), channel_id=1, source_target_pairs={{0,6},{2,4},{4,2},{6,0},{1,7},{3,5},{5,3},{7,1},{8,14},{10,12},{12... | collective-permute-start | bytes 393224 | tf_op jit(solution)/shard_map/ppermute | solution.py:463
  71.3 0.4 collective-permute-start.10
  71.7 1.4 %collective-permute-start.9 = (bf16[128,512]{1,0:T(8,128)(2,1)S(1)}, bf16[128,512]{1,0:T(8,128)(2,1)S(1)}, u32[]{:S(2)}, u32[]{:S(2)}) collective-permute-start(bf16[128,512]{1,0:T(8,128)(2,1)S(1)} %get-tuple-element.64), channel_id=1, source_target_pairs={{0,2},{2,0},{4,6},{6,4},{1,3},{3,1},{5,7},{7,5},{8,10},{10,8},{12,... | collective-permute-start | bytes 393224 | tf_op jit(solution)/shard_map/ppermute | solution.py:463
  73.1 7.8 %cache_attention.7 = (f32[64,2048]{1,0:T(8,128)}, bf16[1024,64]{1,0:T(8,128)(2,1)}) custom-call(s32[2]{0:T(128)} %lens.3, bf16[128,4096]{1,0:T(8,128)(2,1)} %q_ref.7, bf16[128,512]{1,0:T(8,128)(2,1)} %fk_ref.7, bf16[2,2048,512]{2,1,0:T(8,128)(2,1)} %k_hbm.7, bf16[2,2048,512]{2,1,0:T(8,128)(2,1)} %v_hbm.7), custom_call_target="tpu_custom_call" | custom-call | flops 1073741824 | bytes 2097152 | tf_op jit(solution)/shard_map/cache_attention/pallas_call | solution.py:119
  80.8 0.0 collective-permute-done.11.refs_11_
  80.9 0.0 collective-permute-done.10.refs_10_
  80.9 0.0 collective-permute-done.9.refs_9_
  80.9 0.0 copy-done.1
  80.9 0.0 copy-done.2
  80.9 0.0 copy-done.3
  80.9 0.0 copy-done.5
  80.9 0.0 copy-done.6
  80.9 1.0 %copy-done.4 = f32[64,2048]{1,0:T(8,128)S(1)} copy-done((f32[64,2048]{1,0:T(8,128)S(1)}, f32[64,2048]{1,0:T(8,128)}, u32[]{:S(2)}) %copy-start.4) | copy-done | bytes 524312
  82.0 0.9 %copy-done.8 = bf16[1024,64]{1,0:T(8,128)(2,1)S(1)} copy-done((bf16[1024,64]{1,0:T(8,128)(2,1)S(1)}, bf16[1024,64]{1,0:T(8,128)(2,1)}, u32[]{:S(2)}) %copy-start.8) | copy-done | bytes 131096
  82.9 1.4 %finish_attention.1 = (bf16[128,4096]{1,0:T(8,128)(2,1)}, bf16[128,512]{1,0:T(8,128)(2,1)}) custom-call(f32[64,2048]{1,0:T(8,128)S(1)} %copy-done.1, f32[64,2048]{1,0:T(8,128)S(1)} %copy-done.2, f32[64,2048]{1,0:T(8,128)S(1)} %copy-done.3, f32[64,2048]{1,0:T(8,128)S(1)} %copy-done.4, bf16[1024,64]{1,0:T(8,128)(2,1)S(1)} %copy-done.5, ...), custom_call_target="tpu_custom_call" | custom-call | flops 1 | bytes 1 | tf_op jit(solution)/shard_map/finish_attention/pallas_call | solution.py:417
  (15 shorter events, 0.0 us)
Async XLA Ops:
  5.5 5.4 %copy-start.11 = (bf16[544,512]{1,0:T(8,128)(2,1)S(1)}, bf16[544,512]{1,0:T(8,128)(2,1)}, u32[]{:S(2)}) copy-start(bf16[544,512]{1,0:T(8,128)(2,1)} %get-tuple-element.36) | copy-start | bytes 1671172
  5.5 35.1 %all-to-all-start = ((bf16[4,176,1024]{2,1,0:T(8,128)(2,1)}), bf16[4,176,1024]{2,1,0:T(8,128)(2,1)S(1)}, u32[]{:S(2)}, u32[]{:S(2)}) async-start(bf16[4,176,1024]{2,1,0:T(8,128)(2,1)} %quad_pack.1), calls=%async_computation | async-start | bytes 2883584 | tf_op jit(solution)/shard_map/all_to_all | solution.py:468
  10.9 27.6 %collective-permute-start = (bf16[544,512]{1,0:T(8,128)(2,1)S(1)}, bf16[544,512]{1,0:T(8,128)(2,1)S(1)}, u32[]{:S(2)}, u32[]{:S(2)}) collective-permute-start(bf16[544,512]{1,0:T(8,128)(2,1)S(1)} %copy-done.11), channel_id=1, source_target_pairs={{0,8},{8,0},{1,9},{9,1},{2,10},{10,2},{3,11},{11,3},{4,12},{12,4},... | collective-permute-start | bytes 1671176 | tf_op jit(solution)/shard_map/ppermute | solution.py:467
  18.2 22.5 %copy-start.12 = (bf16[256,512]{1,0:T(8,128)(2,1)S(1)}, bf16[256,512]{1,0:T(8,128)(2,1)}, u32[]{:S(2)}) copy-start(bf16[256,512]{1,0:T(8,128)(2,1)} %get-tuple-element.58) | copy-start | bytes 786436
  40.6 16.7 %collective-permute-start.1 = (bf16[4,176,1024]{2,1,0:T(8,128)(2,1)S(1)}, bf16[4,176,1024]{2,1,0:T(8,128)(2,1)S(1)}, u32[]{:S(2)}, u32[]{:S(2)}) collective-permute-start(bf16[4,176,1024]{2,1,0:T(8,128)(2,1)S(1)} %all-to-all-done.mine), channel_id=1, source_target_pairs={{0,1},{1,0},{2,3},{3,2},{4,5},{5,4},{6,7},{7,6},{8,9},{9,8},{10,11... | collective-permute-start | bytes 4325384 | tf_op jit(solution)/shard_map/ppermute | solution.py:480
  40.6 15.2 %collective-permute-start.6 = (bf16[256,512]{1,0:T(8,128)(2,1)S(1)}, bf16[256,512]{1,0:T(8,128)(2,1)S(1)}, u32[]{:S(2)}, u32[]{:S(2)}) collective-permute-start(bf16[256,512]{1,0:T(8,128)(2,1)S(1)} %copy-done.12), channel_id=1, source_target_pairs={{0,8},{8,0},{1,9},{9,1},{2,10},{10,2},{3,11},{11,3},{4,12},{12,4},... | collective-permute-start | bytes 786440 | tf_op jit(solution)/shard_map/ppermute | solution.py:473
  42.1 11.2 %collective-permute-start.2 = (bf16[48,1024]{1,0:T(8,128)(2,1)S(1)}, bf16[48,1024]{1,0:T(8,128)(2,1)S(1)}, u32[]{:S(2)}, u32[]{:S(2)}) collective-permute-start(bf16[48,1024]{1,0:T(8,128)(2,1)S(1)} %get-tuple-element.50), channel_id=1, source_target_pairs={{0,2},{2,0},{4,6},{6,4},{1,3},{3,1},{5,7},{7,5},{8,10},{10,8},{12,... | collective-permute-start | bytes 294920 | tf_op jit(solution)/shard_map/ppermute | solution.py:463
  43.8 9.5 %collective-permute-start.3 = (bf16[48,1024]{1,0:T(8,128)(2,1)S(1)}, bf16[48,1024]{1,0:T(8,128)(2,1)S(1)}, u32[]{:S(2)}, u32[]{:S(2)}) collective-permute-start(bf16[48,1024]{1,0:T(8,128)(2,1)S(1)} %get-tuple-element.53), channel_id=1, source_target_pairs={{0,4},{2,6},{4,0},{6,2},{1,5},{3,7},{5,1},{7,3},{8,12},{10,14},{12... | collective-permute-start | bytes 294920 | tf_op jit(solution)/shard_map/ppermute | solution.py:463
  45.3 12.1 %copy-start.9 = (s32[16]{0:T(128)S(1)}, s32[16]{0:T(128)}, u32[]{:S(2)}) copy-start(s32[16]{0:T(128)} %position.1) | copy-start | bytes 196
  45.3 12.1 %copy-start.10 = (s32[16]{0:T(128)S(1)}, s32[16]{0:T(128)}, u32[]{:S(2)}) copy-start(s32[16]{0:T(128)} %adapter.1) | copy-start | bytes 196
  45.3 8.0 %collective-permute-start.4 = (bf16[48,1024]{1,0:T(8,128)(2,1)S(1)}, bf16[48,1024]{1,0:T(8,128)(2,1)S(1)}, u32[]{:S(2)}, u32[]{:S(2)}) collective-permute-start(bf16[48,1024]{1,0:T(8,128)(2,1)S(1)} %get-tuple-element.55), channel_id=1, source_target_pairs={{0,6},{2,4},{4,2},{6,0},{1,7},{3,5},{5,3},{7,1},{8,14},{10,12},{12... | collective-permute-start | bytes 294920 | tf_op jit(solution)/shard_map/ppermute | solution.py:463
  45.6 11.8 %copy-start = (bf16[1024,512]{1,0:T(8,128)(2,1)S(1)}, bf16[1024,512]{1,0:T(8,128)(2,1)}, u32[]{:S(2)}) copy-start(bf16[1024,512]{1,0:T(8,128)(2,1)} %own_ref.1) | copy-start | bytes 3145732
  53.4 4.0 %collective-permute-start.5 = (bf16[4,48,1024]{2,1,0:T(8,128)(2,1)S(1)}, bf16[4,48,1024]{2,1,0:T(8,128)(2,1)S(1)}, u32[]{:S(2)}, u32[]{:S(2)}) collective-permute-start(bf16[4,48,1024]{2,1,0:T(8,128)(2,1)S(1)} %pad_maximum_fusion.maps_mine), channel_id=1, source_target_pairs={{0,1},{1,0},{2,3},{3,2},{4,5},{5,4},{6,7},{7,6},{8,9},{9,8},{10,11... | collective-permute-start | bytes 1179656 | tf_op jit(solution)/shard_map/ppermute | solution.py:481
  53.5 9.2 %collective-permute-start.7 = (bf16[256,512]{1,0:T(8,128)(2,1)S(1)}, bf16[256,512]{1,0:T(8,128)(2,1)S(1)}, u32[]{:S(2)}, u32[]{:S(2)}) collective-permute-start(bf16[256,512]{1,0:T(8,128)(2,1)S(1)} %get-tuple-element.45.refs_0_), channel_id=1, source_target_pairs={{0,16},{16,0},{1,17},{17,1},{2,18},{18,2},{3,19},{19,3},{4,20},{20... | collective-permute-start | bytes 786440 | tf_op jit(solution)/shard_map/ppermute | solution.py:475
  55.9 12.0 %collective-permute-start.8 = (bf16[256,512]{1,0:T(8,128)(2,1)S(1)}, bf16[256,512]{1,0:T(8,128)(2,1)S(1)}, u32[]{:S(2)}, u32[]{:S(2)}) collective-permute-start(bf16[256,512]{1,0:T(8,128)(2,1)S(1)} %collective-permute-done.6.refs_1_), channel_id=1, source_target_pairs={{0,16},{16,0},{1,17},{17,1},{2,18},{18,2},{3,19},{19,3},{4,20},{20... | collective-permute-start | bytes 786440 | tf_op jit(solution)/shard_map/ppermute | solution.py:482
  68.7 12.2 %collective-permute-start.11 = (bf16[128,512]{1,0:T(8,128)(2,1)S(1)}, bf16[128,512]{1,0:T(8,128)(2,1)S(1)}, u32[]{:S(2)}, u32[]{:S(2)}) collective-permute-start(bf16[128,512]{1,0:T(8,128)(2,1)S(1)} %get-tuple-element.68), channel_id=1, source_target_pairs={{0,6},{2,4},{4,2},{6,0},{1,7},{3,5},{5,3},{7,1},{8,14},{10,12},{12... | collective-permute-start | bytes 393224 | tf_op jit(solution)/shard_map/ppermute | solution.py:463
  71.3 9.6 %collective-permute-start.10 = (bf16[128,512]{1,0:T(8,128)(2,1)S(1)}, bf16[128,512]{1,0:T(8,128)(2,1)S(1)}, u32[]{:S(2)}, u32[]{:S(2)}) collective-permute-start(bf16[128,512]{1,0:T(8,128)(2,1)S(1)} %get-tuple-element.66), channel_id=1, source_target_pairs={{0,4},{2,6},{4,0},{6,2},{1,5},{3,7},{5,1},{7,3},{8,12},{10,14},{12... | collective-permute-start | bytes 393224 | tf_op jit(solution)/shard_map/ppermute | solution.py:463
  71.7 9.2 %collective-permute-start.9 = (bf16[128,512]{1,0:T(8,128)(2,1)S(1)}, bf16[128,512]{1,0:T(8,128)(2,1)S(1)}, u32[]{:S(2)}, u32[]{:S(2)}) collective-permute-start(bf16[128,512]{1,0:T(8,128)(2,1)S(1)} %get-tuple-element.64), channel_id=1, source_target_pairs={{0,2},{2,0},{4,6},{6,4},{1,3},{3,1},{5,7},{7,5},{8,10},{10,8},{12,... | collective-permute-start | bytes 393224 | tf_op jit(solution)/shard_map/ppermute | solution.py:463
  73.0 7.9 %copy-start.1 = (f32[64,2048]{1,0:T(8,128)S(1)}, f32[64,2048]{1,0:T(8,128)}, u32[]{:S(2)}) copy-start(f32[64,2048]{1,0:T(8,128)} %get-tuple-element.39.refs_0_) | copy-start | bytes 1572868
  73.0 7.9 %copy-start.2 = (f32[64,2048]{1,0:T(8,128)S(1)}, f32[64,2048]{1,0:T(8,128)}, u32[]{:S(2)}) copy-start(f32[64,2048]{1,0:T(8,128)} %get-tuple-element.42.refs_1_) | copy-start | bytes 1572868
  73.0 7.9 %copy-start.3 = (f32[64,2048]{1,0:T(8,128)S(1)}, f32[64,2048]{1,0:T(8,128)}, u32[]{:S(2)}) copy-start(f32[64,2048]{1,0:T(8,128)} %get-tuple-element.47.refs_2_) | copy-start | bytes 1572868
  73.0 7.9 %copy-start.5 = (bf16[1024,64]{1,0:T(8,128)(2,1)S(1)}, bf16[1024,64]{1,0:T(8,128)(2,1)}, u32[]{:S(2)}) copy-start(bf16[1024,64]{1,0:T(8,128)(2,1)} %get-tuple-element.40.refs_4_) | copy-start | bytes 393220
  73.0 7.9 %copy-start.6 = (bf16[1024,64]{1,0:T(8,128)(2,1)S(1)}, bf16[1024,64]{1,0:T(8,128)(2,1)}, u32[]{:S(2)}) copy-start(bf16[1024,64]{1,0:T(8,128)(2,1)} %get-tuple-element.43.refs_5_) | copy-start | bytes 393220
  73.0 7.9 %copy-start.7 = (bf16[1024,64]{1,0:T(8,128)(2,1)S(1)}, bf16[1024,64]{1,0:T(8,128)(2,1)}, u32[]{:S(2)}) copy-start(bf16[1024,64]{1,0:T(8,128)(2,1)} %get-tuple-element.51.refs_6_) | copy-start | bytes 393220
  80.9 1.0 %copy-start.4 = (f32[64,2048]{1,0:T(8,128)S(1)}, f32[64,2048]{1,0:T(8,128)}, u32[]{:S(2)}) copy-start(f32[64,2048]{1,0:T(8,128)} %get-tuple-element.62.refs_3_) | copy-start | bytes 1572868
  82.0 0.9 %copy-start.8 = (bf16[1024,64]{1,0:T(8,128)(2,1)S(1)}, bf16[1024,64]{1,0:T(8,128)(2,1)}, u32[]{:S(2)}) copy-start(bf16[1024,64]{1,0:T(8,128)(2,1)} %get-tuple-element.63.refs_7_) | copy-start | bytes 393220

commit v4 on v3

--- a/solution.py
+++ b/solution.py
@@ -448,12 +448,9 @@
     ups = adapter_up_weight.reshape(-1, cols)
 
     kv_heads = cols // HD
-    places = [(span, head) for span in range(2) for head in range(0, kv_heads, kv_heads // 2)]
-
-    def attention(place, lengths):
-        span, head = places[place]
+    def attention(span, lengths):
         return cache_attention(
-            span, head, kv_heads // 2, place > 1, queries, incoming_keys, stored_keys, stored_values, lengths
+            span, 0, cols // HD, False, queries, incoming_keys, stored_keys, stored_values, lengths
         )
 
     def after(value, *others):
@@ -475,22 +472,19 @@
     early_other = lax.ppermute(early, "parts", parts_swap)
     passed_on = [to_quad(passed[q], q) for q in range(1, quads)]
 
-    attn.append(attention(2, after(cache_length, early)))
-    maps_mine = jnp.stack([passed[0]] + [after(maps, attn[2][1]) for maps in passed_on])
+    maps_mine = jnp.stack([passed[0]] + passed_on)
     theirs = lax.ppermute(after(mine, early), "tensor", SWAP)
-    maps_theirs = lax.ppermute(maps_mine, "tensor", SWAP)
-    late_other = lax.ppermute(after(late, attn[2][1]), "parts", parts_swap)
+    maps_theirs = lax.ppermute(after(maps_mine, early_other, late), "tensor", SWAP)
+    late_other = lax.ppermute(late, "parts", parts_swap)
 
     tokens, q_width = queries.shape
     near = near_products(
         mine, theirs, maps_mine, maps_theirs, value_matrix, adapter_position, span_adapter_index, tokens
     )
     products = far_products(mine, theirs, near, (early, late, early_other, late_other), tokens)
-    parts = [to_quad(products[q], q) for q in range(1, quads)]
-    attn.append(attention(3, after(cache_length, products[0])))
-    parts = [products[0]] + [after(part, attn[3][1]) for part in parts]
+    parts = [products[0]] + [to_quad(products[q], q) for q in range(1, quads)]
     mixed, fresh_probs = zip(*attn)
-    attended, incoming_values = finish(places, mixed, fresh_probs, parts, q_width)
+    attended, incoming_values = finish([(0, 0), (1, 0)], mixed, fresh_probs, parts, q_width)
     return (attended, incoming_values)
 
 

time: 85 us -> 79.8 us (0.939)
  Pallas kernels: 34.5 us -> 32 us
  local copies, waits for them, and re-layouts: 2.03 us -> 0.05 us
    ppermute x6, waiting for transfers between devices: 0.02 us -> 13.1 us  [to_quad(): return lax.ppermute(value, 'quad', [(j, j ^ q) for j in range(quads)])]
    ppermute x1, waiting for transfers between devices: 15.6 us -> 2.55 us  [on_device(): early = lax.ppermute(early, 'wing', SWAP)]
    ppermute x1, waiting for transfers between devices: 2.81 us -> 0.01 us  [on_device(): early_other = lax.ppermute(early, 'parts', parts_swap)]
    ppermute x1, waiting for transfers between devices: 1.63 us -> 4.41 us  [on_device(): late = lax.ppermute(after(late, early), 'wing', SWAP)]
    pallas_call x4 -> x2, Pallas kernels: 24.9 us -> 22.4 us  [cache_attention(): pl.pallas_call(functools.partial(cache_kernel, span, first_head, kv_heads...]
    unnamed x26 -> x18, local copies, waits for them, and re-layouts: 2.03 us -> 0.05 us
    ppermute x1, starting transfers between devices: 1.46 us -> 0.32 us  [on_device(): late = lax.ppermute(after(late, early), 'wing', SWAP)]
  transfers between devices with their start and end apart: 13 -> 13, of which waited for: 5 -> 10; matrix products, arithmetic and copies ran while one was open for 0% -> 0% of each run, Pallas kernels for 33% -> 31%
where the time goes in v4:
time: 79.8 us; the launch traced here: 79.5 us
  Pallas kernels  32 us (40%)
  waiting for transfers between devices  27.1 us (34%)
  starting transfers between devices  19.5 us (24%)
  between operations  0.81 us (1%)
    pallas_call x2, Pallas kernels, cache_attention(): pl.pallas_call(functools.partial(cache_kernel, span, first_head, kv_heads...  22.4 us
    ppermute x6, waiting for transfers between devices, to_quad(): return lax.ppermute(value, 'quad', [(j, j ^ q) for j in range(quads)])  13.1 us
    ppermute x6, starting transfers between devices, to_quad(): return lax.ppermute(value, 'quad', [(j, j ^ q) for j in range(quads)])  8.45 us
    all_to_all x1, starting transfers between devices, on_device(): mine = lax.all_to_all(message, 'quad', 0, 0)  5.39 us
    ppermute x1, waiting for transfers between devices, on_device(): late_other = lax.ppermute(late, 'parts', parts_swap)  4.48 us
    ppermute x1, waiting for transfers between devices, on_device(): late = lax.ppermute(after(late, early), 'wing', SWAP)  4.41 us
    pallas_call x1, Pallas kernels, quad_pack(): pl.pallas_call(quad_kernel, in_specs=[hbm] * 3, out_specs=vmem, out_shape...  2.63 us
    ppermute x1, starting transfers between devices, on_device(): early = lax.ppermute(early, 'wing', SWAP)  2.59 us
  transfers between devices with their start and end apart: 13, of which 10 were waited for; matrix products, arithmetic and copies ran while one was open for 0% of the time, Pallas kernels for 31%

profile of v4, /device:TPU:0, one launch (start us, length us, event | category | flops | bytes accessed | tf_op | source)
XLA Modules:
  0.0 79.5 jit_solution(10039629159114602248)
XLA Ops:
  0.6 2.2 %cross_pack.1 = (bf16[544,512]{1,0:T(8,128)(2,1)}, bf16[256,512]{1,0:T(8,128)(2,1)}) custom-call(bf16[1024,512]{1,0:T(8,128)(2,1)} %own_ref.1, bf16[32,8192]{1,0:T(8,128)(2,1)} %bitcast.7, bf16[32,512]{1,0:T(8,128)(2,1)} %bitcast.9), custom_call_target="tpu_custom_call" | custom-call | flops 1 | bytes 1 | tf_op jit(solution)/shard_map/cross_pack/pallas_call | solution.py:178
  2.8 2.6 %quad_pack.1 = bf16[4,176,1024]{2,1,0:T(8,128)(2,1)} custom-call(bf16[128,4096]{1,0:T(8,128)(2,1)} %x_hbm, bf16[32,8192]{1,0:T(8,128)(2,1)} %bitcast.8, bf16[32,512]{1,0:T(8,128)(2,1)} %bitcast.10), custom_call_target="tpu_custom_call" | custom-call | flops 1 | bytes 1 | tf_op jit(solution)/shard_map/quad_pack/pallas_call | solution.py:230
  5.5 0.0 copy-start.7
  5.5 5.4 %all-to-all-start = ((bf16[4,176,1024]{2,1,0:T(8,128)(2,1)}), bf16[4,176,1024]{2,1,0:T(8,128)(2,1)S(1)}, u32[]{:S(2)}, u32[]{:S(2)}) async-start(bf16[4,176,1024]{2,1,0:T(8,128)(2,1)} %quad_pack.1), calls=%async_computation | async-start | bytes 2883584 | tf_op jit(solution)/shard_map/all_to_all | solution.py:465
  10.9 0.0 copy-done.7
  10.9 2.6 %collective-permute-start = (bf16[544,512]{1,0:T(8,128)(2,1)S(1)}, bf16[544,512]{1,0:T(8,128)(2,1)S(1)}, u32[]{:S(2)}, u32[]{:S(2)}) collective-permute-start(bf16[544,512]{1,0:T(8,128)(2,1)S(1)} %copy-done.7), channel_id=1, source_target_pairs={{0,8},{8,0},{1,9},{9,1},{2,10},{10,2},{3,11},{11,3},{4,12},{12,4},... | collective-permute-start | bytes 1671176 | tf_op jit(solution)/shard_map/ppermute | solution.py:464
  13.5 11.2 %cache_attention.2 = (f32[64,4096]{1,0:T(8,128)}, bf16[2048,64]{1,0:T(8,128)(2,1)}) custom-call(s32[2]{0:T(128)} %lens.1, bf16[128,4096]{1,0:T(8,128)(2,1)} %q_ref.3, bf16[128,512]{1,0:T(8,128)(2,1)} %fk_ref.3, bf16[2,2048,512]{2,1,0:T(8,128)(2,1)} %k_hbm.3, bf16[2,2048,512]{2,1,0:T(8,128)(2,1)} %v_hbm.3), custom_call_target="tpu_custom_call" | custom-call | flops 1 | bytes 1 | tf_op jit(solution)/shard_map/cache_attention/pallas_call | solution.py:119
  24.6 0.0 copy-start.8
  24.6 0.0 copy-start.5
  24.7 0.0 copy-start.6
  24.7 11.2 %cache_attention.3 = (f32[64,4096]{1,0:T(8,128)}, bf16[2048,64]{1,0:T(8,128)(2,1)}) custom-call(s32[2]{0:T(128)} %lens.1, bf16[128,4096]{1,0:T(8,128)(2,1)} %q_ref.3, bf16[128,512]{1,0:T(8,128)(2,1)} %fk_ref.3, bf16[2,2048,512]{2,1,0:T(8,128)(2,1)} %k_hbm.3, bf16[2,2048,512]{2,1,0:T(8,128)(2,1)} %v_hbm.3), custom_call_target="tpu_custom_call" | custom-call | flops 1 | bytes 1 | tf_op jit(solution)/shard_map/cache_attention/pallas_call | solution.py:119
  35.9 0.0 copy-start
  35.9 2.6 %collective-permute-done.here = bf16[544,512]{1,0:T(8,128)(2,1)S(1)} collective-permute-done((bf16[544,512]{1,0:T(8,128)(2,1)S(1)}, bf16[544,512]{1,0:T(8,128)(2,1)S(1)}, u32[]{:S(2)}, u32[]{:S(2)}) %collective-permute-start) | collective-permute-done | bytes 557088 | tf_op jit(solution)/shard_map/ppermute | solution.py:464
  38.5 0.1 maps_pack.1
  38.5 2.1 %all-to-all-done.mine = bf16[4,176,1024]{2,1,0:T(8,128)(2,1)S(1)} async-done(((bf16[4,176,1024]{2,1,0:T(8,128)(2,1)}), bf16[4,176,1024]{2,1,0:T(8,128)(2,1)S(1)}, u32[]{:S(2)}, u32[]{:S(2)}) %all-to-all-start) | async-done | bytes 1441824 | tf_op jit(solution)/shard_map/all_to_all | solution.py:465
  40.6 0.0 collective-permute-start.1
  40.6 3.8 %collective-permute-start.4 = (bf16[48,1024]{1,0:T(8,128)(2,1)S(1)}, bf16[48,1024]{1,0:T(8,128)(2,1)S(1)}, u32[]{:S(2)}, u32[]{:S(2)}) collective-permute-start(bf16[48,1024]{1,0:T(8,128)(2,1)S(1)} %get-tuple-element.38), channel_id=1, source_target_pairs={{0,6},{2,4},{4,2},{6,0},{1,7},{3,5},{5,3},{7,1},{8,14},{10,12},{12... | collective-permute-start | bytes 294920 | tf_op jit(solution)/shard_map/ppermute | solution.py:460
  44.4 1.5 %collective-permute-start.5 = (bf16[256,512]{1,0:T(8,128)(2,1)S(1)}, bf16[256,512]{1,0:T(8,128)(2,1)S(1)}, u32[]{:S(2)}, u32[]{:S(2)}) collective-permute-start(bf16[256,512]{1,0:T(8,128)(2,1)S(1)} %get-tuple-element.33.refs_0_), channel_id=1, source_target_pairs={{0,16},{16,0},{1,17},{17,1},{2,18},{18,2},{3,19},{19,3},{4,20},{20... | collective-permute-start | bytes 786440 | tf_op jit(solution)/shard_map/ppermute | solution.py:472
  45.9 0.0 copy-done.8
  45.9 0.3 collective-permute-start.6
  46.2 0.6 collective-permute-start.3
  46.8 1.0 %collective-permute-done.4 = bf16[48,1024]{1,0:T(8,128)(2,1)S(1)} collective-permute-done((bf16[48,1024]{1,0:T(8,128)(2,1)S(1)}, bf16[48,1024]{1,0:T(8,128)(2,1)S(1)}, u32[]{:S(2)}, u32[]{:S(2)}) %collective-permute-start.4) | collective-permute-done | bytes 98336 | tf_op jit(solution)/shard_map/ppermute | solution.py:460
  47.8 0.6 collective-permute-start.2
  48.3 6.5 %collective-permute-done.3 = bf16[48,1024]{1,0:T(8,128)(2,1)S(1)} collective-permute-done((bf16[48,1024]{1,0:T(8,128)(2,1)S(1)}, bf16[48,1024]{1,0:T(8,128)(2,1)S(1)}, u32[]{:S(2)}, u32[]{:S(2)}) %collective-permute-start.3) | collective-permute-done | bytes 98336 | tf_op jit(solution)/shard_map/ppermute | solution.py:460
  54.8 0.0 collective-permute-done.2
  54.8 0.1 pad_maximum_fusion.maps_mine
  54.9 0.0 collective-permute-done.5.refs_2_
  54.9 4.4 %collective-permute-done.6.refs_1_ = bf16[256,512]{1,0:T(8,128)(2,1)S(1)} collective-permute-done((bf16[256,512]{1,0:T(8,128)(2,1)S(1)}, bf16[256,512]{1,0:T(8,128)(2,1)S(1)}, u32[]{:S(2)}, u32[]{:S(2)}) %collective-permute-start.6) | collective-permute-done | bytes 262176 | tf_op jit(solution)/shard_map/ppermute | solution.py:470
  59.3 0.0 collective-permute-start.7
  59.3 1.3 %collective-permute-start.8 = (bf16[256,512]{1,0:T(8,128)(2,1)S(1)}, bf16[256,512]{1,0:T(8,128)(2,1)S(1)}, u32[]{:S(2)}, u32[]{:S(2)}) collective-permute-start(bf16[256,512]{1,0:T(8,128)(2,1)S(1)} %collective-permute-done.6.refs_1_), channel_id=1, source_target_pairs={{0,16},{16,0},{1,17},{17,1},{2,18},{18,2},{3,19},{19,3},{4,20},{20... | collective-permute-start | bytes 786440 | tf_op jit(solution)/shard_map/ppermute | solution.py:478
  60.6 0.4 collective-permute-done.7.maps_theirs
  61.0 0.0 collective-permute-done.1.theirs
  61.0 0.0 copy-done.5
  61.0 0.0 copy-done.6
  61.0 0.0 copy-done
  61.0 2.4 %near_products.1.near = f32[512,512]{1,0:T(8,128)S(1)} custom-call(s32[16]{0:T(128)S(1)} %copy-done.5, s32[16]{0:T(128)S(1)} %copy-done.6, bf16[4,176,1024]{2,1,0:T(8,128)(2,1)S(1)} %all-to-all-done.mine, bf16[4,176,1024]{2,1,0:T(8,128)(2,1)S(1)} %collective-permute-done.1.theirs, bf16[4,48,1024]{2,1,0:T(8,128)(2,1)S(1)} %pad_maximum_fusion.maps_mine, ...), custom_call_target="tpu_custom_call" | custom-call | flops 1 | bytes 1 | tf_op jit(solution)/shard_map/near_products/pallas_call | solution.py:327
  63.5 0.0 copy-start.1
  63.5 0.0 copy-start.2
  63.5 4.5 %collective-permute-done.8.refs_3_ = bf16[256,512]{1,0:T(8,128)(2,1)S(1)} collective-permute-done((bf16[256,512]{1,0:T(8,128)(2,1)S(1)}, bf16[256,512]{1,0:T(8,128)(2,1)S(1)}, u32[]{:S(2)}, u32[]{:S(2)}) %collective-permute-start.8) | collective-permute-done | bytes 262176 | tf_op jit(solution)/shard_map/ppermute | solution.py:478
  68.0 0.8 %far_products.1 = (bf16[128,512]{1,0:T(8,128)(2,1)S(1)}, bf16[128,512]{1,0:T(8,128)(2,1)S(1)}, bf16[128,512]{1,0:T(8,128)(2,1)S(1)}, bf16[128,512]{1,0:T(8,128)(2,1)S(1)}) custom-call(bf16[4,176,1024]{2,1,0:T(8,128)(2,1)S(1)} %all-to-all-done.mine, bf16[4,176,1024]{2,1,0:T(8,128)(2,1)S(1)} %collective-permute-done.1.theirs, ...), custom_call_target="tpu_custom_call" | custom-call | flops 1 | bytes 1 | tf_op jit(solution)/shard_map/far_products/pallas_call | solution.py:375
  68.9 1.5 %collective-permute-start.9 = (bf16[128,512]{1,0:T(8,128)(2,1)S(1)}, bf16[128,512]{1,0:T(8,128)(2,1)S(1)}, u32[]{:S(2)}, u32[]{:S(2)}) collective-permute-start(bf16[128,512]{1,0:T(8,128)(2,1)S(1)} %get-tuple-element.43), channel_id=1, source_target_pairs={{0,2},{2,0},{4,6},{6,4},{1,3},{3,1},{5,7},{7,5},{8,10},{10,8},{12,... | collective-permute-start | bytes 393224 | tf_op jit(solution)/shard_map/ppermute | solution.py:460
  70.4 0.0 collective-permute-start.10
  70.4 2.0 %collective-permute-start.11 = (bf16[128,512]{1,0:T(8,128)(2,1)S(1)}, bf16[128,512]{1,0:T(8,128)(2,1)S(1)}, u32[]{:S(2)}, u32[]{:S(2)}) collective-permute-start(bf16[128,512]{1,0:T(8,128)(2,1)S(1)} %get-tuple-element.45), channel_id=1, source_target_pairs={{0,6},{2,4},{4,2},{6,0},{1,7},{3,5},{5,3},{7,1},{8,14},{10,12},{12... | collective-permute-start | bytes 393224 | tf_op jit(solution)/shard_map/ppermute | solution.py:460
  72.4 2.0 %collective-permute-done.9.refs_5_ = bf16[128,512]{1,0:T(8,128)(2,1)S(1)} collective-permute-done((bf16[128,512]{1,0:T(8,128)(2,1)S(1)}, bf16[128,512]{1,0:T(8,128)(2,1)S(1)}, u32[]{:S(2)}, u32[]{:S(2)}) %collective-permute-start.9) | collective-permute-done | bytes 131104 | tf_op jit(solution)/shard_map/ppermute | solution.py:460
  74.5 2.2 %collective-permute-done.10.refs_6_ = bf16[128,512]{1,0:T(8,128)(2,1)S(1)} collective-permute-done((bf16[128,512]{1,0:T(8,128)(2,1)S(1)}, bf16[128,512]{1,0:T(8,128)(2,1)S(1)}, u32[]{:S(2)}, u32[]{:S(2)}) %collective-permute-start.10) | collective-permute-done | bytes 131104 | tf_op jit(solution)/shard_map/ppermute | solution.py:460
  76.6 1.4 %collective-permute-done.11.refs_7_ = bf16[128,512]{1,0:T(8,128)(2,1)S(1)} collective-permute-done((bf16[128,512]{1,0:T(8,128)(2,1)S(1)}, bf16[128,512]{1,0:T(8,128)(2,1)S(1)}, u32[]{:S(2)}, u32[]{:S(2)}) %collective-permute-start.11) | collective-permute-done | bytes 131104 | tf_op jit(solution)/shard_map/ppermute | solution.py:460
  78.0 0.0 copy-done.2
  78.0 1.4 %finish_attention.1 = (bf16[128,4096]{1,0:T(8,128)(2,1)}, bf16[128,512]{1,0:T(8,128)(2,1)}) custom-call(f32[64,4096]{1,0:T(8,128)S(1)} %copy-done.1, f32[64,4096]{1,0:T(8,128)S(1)} %copy-done.2, bf16[2048,64]{1,0:T(8,128)(2,1)S(1)} %copy-done.3, bf16[2048,64]{1,0:T(8,128)(2,1)S(1)} %copy-done.4, bf16[128,512]{1,0:T(8,128)(2,1)S(1)} %get-tuple-element.42.refs_4_, ...), custom_call_target="tpu_custom_call" | custom-call | flops 1 | bytes 1 | tf_op jit(solution)/shard_map/finish_attention/pallas_call | solution.py:417
  (5 shorter events, 0.0 us)
Async XLA Ops:
  5.5 5.4 %copy-start.7 = (bf16[544,512]{1,0:T(8,128)(2,1)S(1)}, bf16[544,512]{1,0:T(8,128)(2,1)}, u32[]{:S(2)}) copy-start(bf16[544,512]{1,0:T(8,128)(2,1)} %get-tuple-element.24) | copy-start | bytes 1671172
  5.5 35.1 %all-to-all-start = ((bf16[4,176,1024]{2,1,0:T(8,128)(2,1)}), bf16[4,176,1024]{2,1,0:T(8,128)(2,1)S(1)}, u32[]{:S(2)}, u32[]{:S(2)}) async-start(bf16[4,176,1024]{2,1,0:T(8,128)(2,1)} %quad_pack.1), calls=%async_computation | async-start | bytes 2883584 | tf_op jit(solution)/shard_map/all_to_all | solution.py:465
  10.9 27.6 %collective-permute-start = (bf16[544,512]{1,0:T(8,128)(2,1)S(1)}, bf16[544,512]{1,0:T(8,128)(2,1)S(1)}, u32[]{:S(2)}, u32[]{:S(2)}) collective-permute-start(bf16[544,512]{1,0:T(8,128)(2,1)S(1)} %copy-done.7), channel_id=1, source_target_pairs={{0,8},{8,0},{1,9},{9,1},{2,10},{10,2},{3,11},{11,3},{4,12},{12,4},... | collective-permute-start | bytes 1671176 | tf_op jit(solution)/shard_map/ppermute | solution.py:464
  24.6 21.3 %copy-start.8 = (bf16[256,512]{1,0:T(8,128)(2,1)S(1)}, bf16[256,512]{1,0:T(8,128)(2,1)}, u32[]{:S(2)}) copy-start(bf16[256,512]{1,0:T(8,128)(2,1)} %get-tuple-element.40) | copy-start | bytes 786436
  24.6 36.4 %copy-start.5 = (s32[16]{0:T(128)S(1)}, s32[16]{0:T(128)}, u32[]{:S(2)}) copy-start(s32[16]{0:T(128)} %position.1) | copy-start | bytes 196
  24.7 36.4 %copy-start.6 = (s32[16]{0:T(128)S(1)}, s32[16]{0:T(128)}, u32[]{:S(2)}) copy-start(s32[16]{0:T(128)} %adapter.1) | copy-start | bytes 196
  35.9 25.1 %copy-start = (bf16[1024,512]{1,0:T(8,128)(2,1)S(1)}, bf16[1024,512]{1,0:T(8,128)(2,1)}, u32[]{:S(2)}) copy-start(bf16[1024,512]{1,0:T(8,128)(2,1)} %own_ref.1) | copy-start | bytes 3145732
  40.6 20.4 %collective-permute-start.1 = (bf16[4,176,1024]{2,1,0:T(8,128)(2,1)S(1)}, bf16[4,176,1024]{2,1,0:T(8,128)(2,1)S(1)}, u32[]{:S(2)}, u32[]{:S(2)}) collective-permute-start(bf16[4,176,1024]{2,1,0:T(8,128)(2,1)S(1)} %all-to-all-done.mine), channel_id=1, source_target_pairs={{0,1},{1,0},{2,3},{3,2},{4,5},{5,4},{6,7},{7,6},{8,9},{9,8},{10,11... | collective-permute-start | bytes 4325384 | tf_op jit(solution)/shard_map/ppermute | solution.py:476
  40.6 7.2 %collective-permute-start.4 = (bf16[48,1024]{1,0:T(8,128)(2,1)S(1)}, bf16[48,1024]{1,0:T(8,128)(2,1)S(1)}, u32[]{:S(2)}, u32[]{:S(2)}) collective-permute-start(bf16[48,1024]{1,0:T(8,128)(2,1)S(1)} %get-tuple-element.38), channel_id=1, source_target_pairs={{0,6},{2,4},{4,2},{6,0},{1,7},{3,5},{5,3},{7,1},{8,14},{10,12},{12... | collective-permute-start | bytes 294920 | tf_op jit(solution)/shard_map/ppermute | solution.py:460
  44.4 10.5 %collective-permute-start.5 = (bf16[256,512]{1,0:T(8,128)(2,1)S(1)}, bf16[256,512]{1,0:T(8,128)(2,1)S(1)}, u32[]{:S(2)}, u32[]{:S(2)}) collective-permute-start(bf16[256,512]{1,0:T(8,128)(2,1)S(1)} %get-tuple-element.33.refs_0_), channel_id=1, source_target_pairs={{0,16},{16,0},{1,17},{17,1},{2,18},{18,2},{3,19},{19,3},{4,20},{20... | collective-permute-start | bytes 786440 | tf_op jit(solution)/shard_map/ppermute | solution.py:472
  45.9 13.4 %collective-permute-start.6 = (bf16[256,512]{1,0:T(8,128)(2,1)S(1)}, bf16[256,512]{1,0:T(8,128)(2,1)S(1)}, u32[]{:S(2)}, u32[]{:S(2)}) collective-permute-start(bf16[256,512]{1,0:T(8,128)(2,1)S(1)} %copy-done.8), channel_id=1, source_target_pairs={{0,8},{8,0},{1,9},{9,1},{2,10},{10,2},{3,11},{11,3},{4,12},{12,4},... | collective-permute-start | bytes 786440 | tf_op jit(solution)/shard_map/ppermute | solution.py:470
  46.2 8.6 %collective-permute-start.3 = (bf16[48,1024]{1,0:T(8,128)(2,1)S(1)}, bf16[48,1024]{1,0:T(8,128)(2,1)S(1)}, u32[]{:S(2)}, u32[]{:S(2)}) collective-permute-start(bf16[48,1024]{1,0:T(8,128)(2,1)S(1)} %get-tuple-element.37), channel_id=1, source_target_pairs={{0,4},{2,6},{4,0},{6,2},{1,5},{3,7},{5,1},{7,3},{8,12},{10,14},{12... | collective-permute-start | bytes 294920 | tf_op jit(solution)/shard_map/ppermute | solution.py:460
  47.8 7.0 %collective-permute-start.2 = (bf16[48,1024]{1,0:T(8,128)(2,1)S(1)}, bf16[48,1024]{1,0:T(8,128)(2,1)S(1)}, u32[]{:S(2)}, u32[]{:S(2)}) collective-permute-start(bf16[48,1024]{1,0:T(8,128)(2,1)S(1)} %get-tuple-element.36), channel_id=1, source_target_pairs={{0,2},{2,0},{4,6},{6,4},{1,3},{3,1},{5,7},{7,5},{8,10},{10,8},{12,... | collective-permute-start | bytes 294920 | tf_op jit(solution)/shard_map/ppermute | solution.py:460
  59.3 1.7 %collective-permute-start.7 = (bf16[4,48,1024]{2,1,0:T(8,128)(2,1)S(1)}, bf16[4,48,1024]{2,1,0:T(8,128)(2,1)S(1)}, u32[]{:S(2)}, u32[]{:S(2)}) collective-permute-start(bf16[4,48,1024]{2,1,0:T(8,128)(2,1)S(1)} %pad_maximum_fusion.maps_mine), channel_id=1, source_target_pairs={{0,1},{1,0},{2,3},{3,2},{4,5},{5,4},{6,7},{7,6},{8,9},{9,8},{10,11... | collective-permute-start | bytes 1179656 | tf_op jit(solution)/shard_map/ppermute | solution.py:477
  59.3 8.7 %collective-permute-start.8 = (bf16[256,512]{1,0:T(8,128)(2,1)S(1)}, bf16[256,512]{1,0:T(8,128)(2,1)S(1)}, u32[]{:S(2)}, u32[]{:S(2)}) collective-permute-start(bf16[256,512]{1,0:T(8,128)(2,1)S(1)} %collective-permute-done.6.refs_1_), channel_id=1, source_target_pairs={{0,16},{16,0},{1,17},{17,1},{2,18},{18,2},{3,19},{19,3},{4,20},{20... | collective-permute-start | bytes 786440 | tf_op jit(solution)/shard_map/ppermute | solution.py:478
  63.5 14.5 %copy-start.1 = (f32[64,4096]{1,0:T(8,128)S(1)}, f32[64,4096]{1,0:T(8,128)}, u32[]{:S(2)}) copy-start(f32[64,4096]{1,0:T(8,128)} %get-tuple-element.27.refs_0_) | copy-start | bytes 3145732
  63.5 14.5 %copy-start.2 = (f32[64,4096]{1,0:T(8,128)S(1)}, f32[64,4096]{1,0:T(8,128)}, u32[]{:S(2)}) copy-start(f32[64,4096]{1,0:T(8,128)} %get-tuple-element.30.refs_1_) | copy-start | bytes 3145732
  63.5 14.5 %copy-start.3 = (bf16[2048,64]{1,0:T(8,128)(2,1)S(1)}, bf16[2048,64]{1,0:T(8,128)(2,1)}, u32[]{:S(2)}) copy-start(bf16[2048,64]{1,0:T(8,128)(2,1)} %get-tuple-element.28.refs_2_) | copy-start | bytes 786436
  63.5 14.5 %copy-start.4 = (bf16[2048,64]{1,0:T(8,128)(2,1)S(1)}, bf16[2048,64]{1,0:T(8,128)(2,1)}, u32[]{:S(2)}) copy-start(bf16[2048,64]{1,0:T(8,128)(2,1)} %get-tuple-element.31.refs_3_) | copy-start | bytes 786436
  68.9 5.6 %collective-permute-start.9 = (bf16[128,512]{1,0:T(8,128)(2,1)S(1)}, bf16[128,512]{1,0:T(8,128)(2,1)S(1)}, u32[]{:S(2)}, u32[]{:S(2)}) collective-permute-start(bf16[128,512]{1,0:T(8,128)(2,1)S(1)} %get-tuple-element.43), channel_id=1, source_target_pairs={{0,2},{2,0},{4,6},{6,4},{1,3},{3,1},{5,7},{7,5},{8,10},{10,8},{12,... | collective-permute-start | bytes 393224 | tf_op jit(solution)/shard_map/ppermute | solution.py:460
  70.4 6.2 %collective-permute-start.10 = (bf16[128,512]{1,0:T(8,128)(2,1)S(1)}, bf16[128,512]{1,0:T(8,128)(2,1)S(1)}, u32[]{:S(2)}, u32[]{:S(2)}) collective-permute-start(bf16[128,512]{1,0:T(8,128)(2,1)S(1)} %get-tuple-element.44), channel_id=1, source_target_pairs={{0,4},{2,6},{4,0},{6,2},{1,5},{3,7},{5,1},{7,3},{8,12},{10,14},{12... | collective-permute-start | bytes 393224 | tf_op jit(solution)/shard_map/ppermute | solution.py:460
  70.4 7.6 %collective-permute-start.11 = (bf16[128,512]{1,0:T(8,128)(2,1)S(1)}, bf16[128,512]{1,0:T(8,128)(2,1)S(1)}, u32[]{:S(2)}, u32[]{:S(2)}) collective-permute-start(bf16[128,512]{1,0:T(8,128)(2,1)S(1)} %get-tuple-element.45), channel_id=1, source_target_pairs={{0,6},{2,4},{4,2},{6,0},{1,7},{3,5},{5,3},{7,1},{8,14},{10,12},{12... | collective-permute-start | bytes 393224 | tf_op jit(solution)/shard_map/ppermute | solution.py:460

commit v5 on v4

--- a/solution.py
+++ b/solution.py
@@ -13,7 +13,7 @@
 RANK = 16
 SPAN = 64
 CHUNK = 512
-EARLY = 2
+CHUNKS = 1
 ONES = 16
 ADAPTER_SCALE = 2.0
 EXP2_SCALE = math.log2(math.e) / math.sqrt(HD)
@@ -150,46 +150,6 @@
         copy.wait()
 
 
-def cross_kernel(w_hbm, d_hbm, u_hbm, early, late, sems):
-    part, core = lax.axis_index("parts") % 2, lax.axis_index("tensor")
-    cols = u_hbm.shape[1]
-    features = d_hbm.shape[1] // 2
-    pieces = features // cols
-    ranks = d_hbm.shape[0]
-    head = early.shape[0] - (pieces + 1) * ranks
-    begin = part * (head + late.shape[0])
-    copies = []
-    for i in range(pieces):
-        here = pl.ds(pl.multiple_of(core * features + i * cols, cols), cols)
-        copies.append((d_hbm.at[:, here], early.at[head + i * ranks : head + (i + 1) * ranks, :]))
-    copies.append((u_hbm, early.at[head + pieces * ranks :, :]))
-    copies.append((w_hbm.at[pl.ds(pl.multiple_of(begin, head), head), :], early.at[:head, :]))
-    rest = pl.ds(pl.multiple_of(begin + head, head), late.shape[0])
-    copies.append((w_hbm.at[rest, :], late))
-    run_copies(copies, sems)
-
-
-def cross_pack(weights, downs, ups):
-    width, cols = weights.shape
-    head = width // 2 // EARLY
-    pieces = downs.shape[1] // 2 // cols
-    vmem = pl.BlockSpec(memory_space=pltpu.VMEM)
-    hbm = pl.BlockSpec(memory_space=pltpu.HBM)
-    return pl.pallas_call(
-        cross_kernel,
-        in_specs=[hbm] * 3,
-        out_specs=[vmem] * 2,
-        out_shape=[
-            jax.ShapeDtypeStruct((head + (pieces + 1) * downs.shape[0], cols), weights.dtype),
-            jax.ShapeDtypeStruct((width // 2 - head, cols), weights.dtype),
-        ],
-        scratch_shapes=[pltpu.SemaphoreType.DMA((pieces + 3,))],
-        compiler_params=pltpu.CompilerParams(vmem_limit_bytes=57 * MIB),
-        cost_estimate=FREE,
-        name="cross_pack",
-    )(weights, downs, ups)
-
-
 def up_places(cols, width):
     step = min(cols, width)
     return [
@@ -199,17 +159,25 @@
     ]
 
 
-def quad_kernel(x_hbm, d_hbm, u_hbm, out, sems):
-    core = lax.axis_index("tensor")
+def pack_kernel(x_hbm, d_hbm, u_hbm, w_hbm, out, maps, *refs):
+    rows, sems = refs[:-1], refs[-1]
+    part, core = lax.axis_index("parts") % 2, lax.axis_index("tensor")
     quads, _, width = out.shape
     tokens, features = x_hbm.shape
     ranks, cols = u_hbm.shape
     step = min(cols, width)
+    begin = part * (w_hbm.shape[0] // 2)
     copies = []
+    for piece in rows:
+        size = piece.shape[0]
+        copies.append((w_hbm.at[pl.ds(pl.multiple_of(begin, size), size), :], piece))
+        begin = begin + size
+    copies.append((d_hbm.at[:, pl.ds(pl.multiple_of(core * features, features), features)], maps.at[:, :features]))
+    copies.append((u_hbm, maps.at[:, features:]))
     for j in range(quads):
-        begin = pl.multiple_of(core * features + j * width, width)
+        first = pl.multiple_of(core * features + j * width, width)
         copies.append((x_hbm.at[:, j * width : (j + 1) * width], out.at[j, :tokens, :]))
-        copies.append((d_hbm.at[:, pl.ds(begin, width)], out.at[j, tokens : tokens + ranks, :]))
+        copies.append((d_hbm.at[:, pl.ds(first, width)], out.at[j, tokens : tokens + ranks, :]))
         for slot, first, row, col in up_places(cols, width):
             row += tokens + ranks
             copies.append(
@@ -221,54 +189,53 @@
     run_copies(copies, sems)
 
 
-def quad_pack(tokens, downs, ups, width, quads):
+def pack(tokens, downs, ups, weights, quads):
     vmem = pl.BlockSpec(memory_space=pltpu.VMEM)
     hbm = pl.BlockSpec(memory_space=pltpu.HBM)
     ranks, cols = ups.shape
+    width = weights.shape[0]
     rows = tokens.shape[0] + ranks + RANK * (2 * cols // width)
-    count = quads * (2 + len(up_places(cols, width)))
-    return pl.pallas_call(
-        quad_kernel,
-        in_specs=[hbm] * 3,
-        out_specs=vmem,
-        out_shape=jax.ShapeDtypeStruct((quads, rows, width), tokens.dtype),
+    count = CHUNKS + 2 + quads * (2 + len(up_places(cols, width)))
+    piece = jax.ShapeDtypeStruct((width // 2 // CHUNKS, cols), weights.dtype)
+    return pl.pallas_call(
+        pack_kernel,
+        in_specs=[hbm] * 4,
+        out_specs=[vmem] * (2 + CHUNKS),
+        out_shape=[
+            jax.ShapeDtypeStruct((quads, rows, width), tokens.dtype),
+            jax.ShapeDtypeStruct((ranks, tokens.shape[1] + cols), downs.dtype),
+        ]
+        + [piece] * CHUNKS,
         scratch_shapes=[pltpu.SemaphoreType.DMA((count,))],
         compiler_params=pltpu.CompilerParams(vmem_limit_bytes=57 * MIB),
         cost_estimate=FREE,
-        name="quad_pack",
-    )(tokens, downs, ups)
-
-
-def maps_kernel(here, rows_out, *outs):
+        name="pack",
+    )(tokens, downs, ups, weights)
+
+
+def maps_kernel(here, *outs):
     quad = lax.axis_index("quad")
     width = outs[0].shape[1]
-    cols = here.shape[1]
-    ranks = 2 * RANK
+    ranks = here.shape[0]
+    features = len(outs) * width
+    cols = here.shape[1] - features
     step = min(cols, width)
-    head = rows_out.shape[0]
-    last = here.shape[0] - ranks
-    rows_out[...] = here[:head, :]
     for q, out in enumerate(outs):
-        for first in range(0, width, step):
-            place = (quad ^ q) * width + first
-            row = pl.multiple_of(head + place // cols * ranks, RANK)
-            col = pl.multiple_of(place % cols, step)
-            out[:ranks, first : first + step] = here[pl.ds(row, ranks), pl.ds(col, step)]
+        out[:ranks, :] = here[:, pl.ds(pl.multiple_of((quad ^ q) * width, width), width)]
         for slot, first, row, col in up_places(cols, width):
-            up = here[last + slot * RANK : last + (slot + 1) * RANK, first : first + step]
+            up = here[slot * RANK : (slot + 1) * RANK, features + first : features + first + step]
             out[ranks + row : ranks + row + RANK, col : col + step] = up
 
 
 def maps_pack(here, width, quads):
     vmem = pl.BlockSpec(memory_space=pltpu.VMEM)
-    rows, cols = here.shape
-    head = rows - (quads * width // cols + 1) * 2 * RANK
+    cols = here.shape[1] - quads * width
     maps = jax.ShapeDtypeStruct((RANK * (2 + 2 * cols // width), width), here.dtype)
     return pl.pallas_call(
         maps_kernel,
         in_specs=[vmem],
-        out_specs=[vmem] * (1 + quads),
-        out_shape=[jax.ShapeDtypeStruct((head, cols), here.dtype)] + [maps] * quads,
+        out_specs=[vmem] * quads,
+        out_shape=[maps] * quads,
         compiler_params=pltpu.CompilerParams(vmem_limit_bytes=4 * MIB),
         cost_estimate=FREE,
         name="maps_pack",
@@ -342,15 +309,16 @@
 def far_kernel(tokens, mine, theirs, near, *refs):
     quads, _, width = mine.shape
     outs, (whole, total) = refs[-2 - quads : -2], refs[-2:]
-    weights = refs[:4]
+    weights = refs[: -2 - quads]
     part, core, wing = lax.axis_index("parts") % 2, lax.axis_index("tensor"), lax.axis_index("wing")
     quad = lax.axis_index("quad")
-    late = weights[1].shape[0]
-    head = width // 2 - late
+    chunk = weights[0].shape[0]
+    chunks = len(weights) // 2
     for side in range(2):
         begin = (part if side == 0 else 1 - part) * (width // 2)
-        whole[pl.ds(pl.multiple_of(begin, head), head), :] = weights[2 * side][...]
-        whole[pl.ds(pl.multiple_of(begin + head, head), late), :] = weights[2 * side + 1][...]
+        for i in range(chunks):
+            row = pl.multiple_of(begin + i * chunk, chunk)
+            whole[pl.ds(row, chunk), :] = weights[side * chunks + i][...]
 
     def store(x):
         product = dot(x[:, :tokens, :].reshape(quads * tokens, width), whole[...])
@@ -459,29 +427,27 @@
     def to_quad(value, q):
         return lax.ppermute(value, "quad", [(j, j ^ q) for j in range(quads)])
 
-    early, late = cross_pack(value_matrix, downs, ups)
-    message = quad_pack(after(normed_inputs, early), downs, ups, width, quads)
-    early = lax.ppermute(early, "wing", SWAP)
+    message, maps, *rows = pack(normed_inputs, downs, ups, value_matrix, quads)
     mine = lax.all_to_all(message, "quad", 0, 0)
+    maps = lax.ppermute(maps, "wing", SWAP)
+    rows = [lax.ppermute(piece, "wing", SWAP) for piece in rows]
 
     attn = [attention(0, after(cache_length, message))]
     attn.append(attention(1, after(cache_length, attn[0][1])))
-    early = after(early, attn[1][1])
-    late = lax.ppermute(after(late, early), "wing", SWAP)
-    early, *passed = maps_pack(early, width, quads)
-    early_other = lax.ppermute(early, "parts", parts_swap)
+    maps, *rows = lax.optimization_barrier((maps, *rows, attn[1][1]))[:-1]
+    passed = maps_pack(maps, width, quads)
     passed_on = [to_quad(passed[q], q) for q in range(1, quads)]
+    rows_other = [lax.ppermute(piece, "parts", parts_swap) for piece in rows]
 
     maps_mine = jnp.stack([passed[0]] + passed_on)
-    theirs = lax.ppermute(after(mine, early), "tensor", SWAP)
-    maps_theirs = lax.ppermute(after(maps_mine, early_other, late), "tensor", SWAP)
-    late_other = lax.ppermute(late, "parts", parts_swap)
+    theirs = lax.ppermute(after(mine, rows[0]), "tensor", SWAP)
+    maps_theirs = lax.ppermute(maps_mine, "tensor", SWAP)
 
     tokens, q_width = queries.shape
     near = near_products(
         mine, theirs, maps_mine, maps_theirs, value_matrix, adapter_position, span_adapter_index, tokens
     )
-    products = far_products(mine, theirs, near, (early, late, early_other, late_other), tokens)
+    products = far_products(mine, theirs, near, (*rows, *rows_other), tokens)
     parts = [products[0]] + [to_quad(products[q], q) for q in range(1, quads)]
     mixed, fresh_probs = zip(*attn)
     attended, incoming_values = finish([(0, 0), (1, 0)], mixed, fresh_probs, parts, q_width)

time: 79.8 us -> 75.6 us (0.947)
  Pallas kernels: 32 us -> 26.8 us
  waiting for transfers between devices: 27.1 us -> 30.7 us
  starting transfers between devices: 19.5 us -> 16.9 us
    ppermute x6 -> x5, waiting for transfers between devices: 11.9 us -> 22.4 us  [the longest x1 16.5 us: on_device(): maps = lax.ppermute(maps, 'wing', SWAP)]
    ppermute x6, waiting for transfers between devices: 13.1 us -> 8.29 us  [to_quad(): return lax.ppermute(value, 'quad', [(j, j ^ q) for j in range(quads)])]
    pallas_call x2, Pallas kernels: 22.4 us -> 19 us  [cache_attention(): pl.pallas_call(functools.partial(cache_kernel, span, first_head, kv_heads...]
    all_to_all x1, waiting for transfers between devices: 2.08 us -> 0.01 us  [on_device(): mine = lax.all_to_all(message, 'quad', 0, 0)]
    pallas_call x3 -> x2, Pallas kernels: 4.9 us -> 3.16 us  [the longest x1 3.12 us: pack(): pl.pallas_call(pack_kernel, in_specs=[hbm] * 4, out_specs=[vmem] * (2 + C...]
    ppermute x6, starting transfers between devices: 8.45 us -> 7.11 us  [to_quad(): return lax.ppermute(value, 'quad', [(j, j ^ q) for j in range(quads)])]
    ppermute x6 -> x5, starting transfers between devices: 5.69 us -> 4.54 us  [the longest x1 2.59 us: on_device(): rows = [lax.ppermute(piece, 'wing', SWAP) for piece in rows]]
  transfers between devices with their start and end apart: 13 -> 12, of which waited for: 10 -> 8; matrix products, arithmetic and copies ran while one was open for 0% -> 0% of each run, Pallas kernels for 31% -> 28%
where the time goes in v5:
time: 75.6 us; the launch traced here: 75.3 us
  waiting for transfers between devices  30.7 us (41%)
  Pallas kernels  26.8 us (35%)
  starting transfers between devices  16.9 us (22%)
  between operations  0.79 us (1%)
    pallas_call x2, Pallas kernels, cache_attention(): pl.pallas_call(functools.partial(cache_kernel, span, first_head, kv_heads...  19 us
    ppermute x1, waiting for transfers between devices, on_device(): maps = lax.ppermute(maps, 'wing', SWAP)  16.5 us
    ppermute x6, waiting for transfers between devices, to_quad(): return lax.ppermute(value, 'quad', [(j, j ^ q) for j in range(quads)])  8.29 us
    ppermute x6, starting transfers between devices, to_quad(): return lax.ppermute(value, 'quad', [(j, j ^ q) for j in range(quads)])  7.11 us
    all_to_all x1, starting transfers between devices, on_device(): mine = lax.all_to_all(message, 'quad', 0, 0)  5.26 us
    ppermute x1, waiting for transfers between devices, on_device(): rows_other = [lax.ppermute(piece, 'parts', parts_swap) for piece in rows]  4.17 us
    pallas_call x1, Pallas kernels, pack(): pl.pallas_call(pack_kernel, in_specs=[hbm] * 4, out_specs=[vmem] * (2 + C...  3.12 us
    ppermute x1, starting transfers between devices, on_device(): rows = [lax.ppermute(piece, 'wing', SWAP) for piece in rows]  2.59 us
  transfers between devices with their start and end apart: 12, of which 8 were waited for; matrix products, arithmetic and copies ran while one was open for 0% of the time, Pallas kernels for 28%

profile of v5, /device:TPU:0, one launch (start us, length us, event | category | flops | bytes accessed | tf_op | source)
XLA Modules:
  0.0 75.3 jit_solution(15004288350426524192)
XLA Ops:
  0.6 3.1 %pack.1 = (bf16[4,176,1024]{2,1,0:T(8,128)(2,1)}, bf16[32,4608]{1,0:T(8,128)(2,1)}, bf16[512,512]{1,0:T(8,128)(2,1)}) custom-call(bf16[128,4096]{1,0:T(8,128)(2,1)} %x_hbm.1, bf16[32,8192]{1,0:T(8,128)(2,1)} %bitcast.7, bf16[32,512]{1,0:T(8,128)(2,1)} %bitcast.11, bf16[1024,512]{1,0:T(8,128)(2,1)} %own_ref.1), custom_call_target="tpu_custom_call" | custom-call | flops 1 | bytes 1 | tf_op jit(solution)/shard_map/pack/pallas_call | solution.py:200
  3.8 5.3 %all-to-all-start = ((bf16[4,176,1024]{2,1,0:T(8,128)(2,1)}), bf16[4,176,1024]{2,1,0:T(8,128)(2,1)S(1)}, u32[]{:S(2)}, u32[]{:S(2)}) async-start(bf16[4,176,1024]{2,1,0:T(8,128)(2,1)} %get-tuple-element.22), calls=%async_computation | async-start | bytes 2883584 | tf_op jit(solution)/shard_map/all_to_all | solution.py:431
  9.0 2.6 %collective-permute-start.1 = (bf16[512,512]{1,0:T(8,128)(2,1)}, bf16[512,512]{1,0:T(8,128)(2,1)S(1)}, u32[]{:S(2)}, u32[]{:S(2)}) collective-permute-start(bf16[512,512]{1,0:T(8,128)(2,1)} %get-tuple-element.30), channel_id=1, source_target_pairs={{0,8},{8,0},{1,9},{9,1},{2,10},{10,2},{3,11},{11,3},{4,12},{12,4},... | collective-permute-start | bytes 1572872 | tf_op jit(solution)/shard_map/ppermute | solution.py:433
  11.6 0.3 collective-permute-start
  11.9 11.2 %cache_attention.2 = (f32[64,4096]{1,0:T(8,128)}, bf16[2048,64]{1,0:T(8,128)(2,1)}) custom-call(s32[2]{0:T(128)} %lens.1, bf16[128,4096]{1,0:T(8,128)(2,1)} %q_ref.3, bf16[128,512]{1,0:T(8,128)(2,1)} %fk_ref.3, bf16[2,2048,512]{2,1,0:T(8,128)(2,1)} %k_hbm.3, bf16[2,2048,512]{2,1,0:T(8,128)(2,1)} %v_hbm.3), custom_call_target="tpu_custom_call" | custom-call | flops 1 | bytes 1 | tf_op jit(solution)/shard_map/cache_attention/pallas_call | solution.py:119
  23.1 0.0 copy-start.5
  23.1 0.0 copy-start.6
  23.2 7.8 %cache_attention.3 = (f32[64,4096]{1,0:T(8,128)}, bf16[2048,64]{1,0:T(8,128)(2,1)}) custom-call(s32[2]{0:T(128)} %lens.1, bf16[128,4096]{1,0:T(8,128)(2,1)} %q_ref.3, bf16[128,512]{1,0:T(8,128)(2,1)} %fk_ref.3, bf16[2,2048,512]{2,1,0:T(8,128)(2,1)} %k_hbm.3, bf16[2,2048,512]{2,1,0:T(8,128)(2,1)} %v_hbm.3), custom_call_target="tpu_custom_call" | custom-call | flops 1 | bytes 1 | tf_op jit(solution)/shard_map/cache_attention/pallas_call | solution.py:119
  31.0 0.0 copy-start
  31.0 16.5 %collective-permute-done.here = bf16[32,4608]{1,0:T(8,128)(2,1)S(1)} collective-permute-done((bf16[32,4608]{1,0:T(8,128)(2,1)}, bf16[32,4608]{1,0:T(8,128)(2,1)S(1)}, u32[]{:S(2)}, u32[]{:S(2)}) %collective-permute-start) | collective-permute-done | bytes 294944 | tf_op jit(solution)/shard_map/ppermute | solution.py:432
  47.5 0.0 collective-permute-done.1.refs_0_
  47.5 0.0 all-to-all-done.mine
  47.5 0.0 collective-permute-start.2
  47.5 2.0 %collective-permute-start.5 = (bf16[48,1024]{1,0:T(8,128)(2,1)S(1)}, bf16[48,1024]{1,0:T(8,128)(2,1)S(1)}, u32[]{:S(2)}, u32[]{:S(2)}) collective-permute-start(bf16[48,1024]{1,0:T(8,128)(2,1)S(1)} %get-tuple-element.37), channel_id=1, source_target_pairs={{0,6},{2,4},{4,2},{6,0},{1,7},{3,5},{5,3},{7,1},{8,14},{10,12},{12... | collective-permute-start | bytes 294920 | tf_op jit(solution)/shard_map/ppermute | solution.py:428
  49.5 1.2 %collective-permute-start.4 = (bf16[48,1024]{1,0:T(8,128)(2,1)S(1)}, bf16[48,1024]{1,0:T(8,128)(2,1)S(1)}, u32[]{:S(2)}, u32[]{:S(2)}) collective-permute-start(bf16[48,1024]{1,0:T(8,128)(2,1)S(1)} %get-tuple-element.36), channel_id=1, source_target_pairs={{0,4},{2,6},{4,0},{6,2},{1,5},{3,7},{5,1},{7,3},{8,12},{10,14},{12... | collective-permute-start | bytes 294920 | tf_op jit(solution)/shard_map/ppermute | solution.py:428
  50.8 0.3 collective-permute-start.3
  51.1 1.5 %collective-permute-start.7 = (bf16[512,512]{1,0:T(8,128)(2,1)S(1)}, bf16[512,512]{1,0:T(8,128)(2,1)S(1)}, u32[]{:S(2)}, u32[]{:S(2)}) collective-permute-start(bf16[512,512]{1,0:T(8,128)(2,1)S(1)} %collective-permute-done.1.refs_0_), channel_id=1, source_target_pairs={{0,16},{16,0},{1,17},{17,1},{2,18},{18,2},{3,19},{19,3},{4,20},{20... | collective-permute-start | bytes 1572872 | tf_op jit(solution)/shard_map/ppermute | solution.py:440
  52.6 1.5 %collective-permute-done.5 = bf16[48,1024]{1,0:T(8,128)(2,1)S(1)} collective-permute-done((bf16[48,1024]{1,0:T(8,128)(2,1)S(1)}, bf16[48,1024]{1,0:T(8,128)(2,1)S(1)}, u32[]{:S(2)}, u32[]{:S(2)}) %collective-permute-start.5) | collective-permute-done | bytes 98336 | tf_op jit(solution)/shard_map/ppermute | solution.py:428
  54.1 1.9 %collective-permute-done.4 = bf16[48,1024]{1,0:T(8,128)(2,1)S(1)} collective-permute-done((bf16[48,1024]{1,0:T(8,128)(2,1)S(1)}, bf16[48,1024]{1,0:T(8,128)(2,1)S(1)}, u32[]{:S(2)}, u32[]{:S(2)}) %collective-permute-start.4) | collective-permute-done | bytes 98336 | tf_op jit(solution)/shard_map/ppermute | solution.py:428
  56.0 0.0 collective-permute-done.3
  56.0 0.1 pad_maximum_fusion.maps_mine
  56.1 0.1 collective-permute-start.6
  56.2 1.7 %collective-permute-done.6.maps_theirs = bf16[4,48,1024]{2,1,0:T(8,128)(2,1)S(1)} collective-permute-done((bf16[4,48,1024]{2,1,0:T(8,128)(2,1)S(1)}, bf16[4,48,1024]{2,1,0:T(8,128)(2,1)S(1)}, u32[]{:S(2)}, u32[]{:S(2)}) %collective-permute-start.6) | collective-permute-done | bytes 393248 | tf_op jit(solution)/shard_map/ppermute | solution.py:444
  57.9 0.0 collective-permute-done.2.theirs
  57.9 0.0 copy-done.5
  57.9 0.0 copy-done.6
  57.9 0.0 copy-done
  57.9 2.5 %near_products.1.near = f32[512,512]{1,0:T(8,128)S(1)} custom-call(s32[16]{0:T(128)S(1)} %copy-done.5, s32[16]{0:T(128)S(1)} %copy-done.6, bf16[4,176,1024]{2,1,0:T(8,128)(2,1)S(1)} %all-to-all-done.mine, bf16[4,176,1024]{2,1,0:T(8,128)(2,1)S(1)} %collective-permute-done.2.theirs, bf16[4,48,1024]{2,1,0:T(8,128)(2,1)S(1)} %pad_maximum_fusion.maps_mine, ...), custom_call_target="tpu_custom_call" | custom-call | flops 1 | bytes 1 | tf_op jit(solution)/shard_map/near_products/pallas_call | solution.py:294
  60.4 0.0 copy-start.1
  60.4 0.0 copy-start.2
  60.4 0.0 copy-start.3
  60.4 0.0 copy-start.4
  60.4 4.2 %collective-permute-done.7.refs_1_ = bf16[512,512]{1,0:T(8,128)(2,1)S(1)} collective-permute-done((bf16[512,512]{1,0:T(8,128)(2,1)S(1)}, bf16[512,512]{1,0:T(8,128)(2,1)S(1)}, u32[]{:S(2)}, u32[]{:S(2)}) %collective-permute-start.7) | collective-permute-done | bytes 524320 | tf_op jit(solution)/shard_map/ppermute | solution.py:440
  64.6 0.8 %far_products.1 = (bf16[128,512]{1,0:T(8,128)(2,1)S(1)}, bf16[128,512]{1,0:T(8,128)(2,1)S(1)}, bf16[128,512]{1,0:T(8,128)(2,1)S(1)}, bf16[128,512]{1,0:T(8,128)(2,1)S(1)}) custom-call(bf16[4,176,1024]{2,1,0:T(8,128)(2,1)S(1)} %all-to-all-done.mine, bf16[4,176,1024]{2,1,0:T(8,128)(2,1)S(1)} %collective-permute-done.2.theirs, ...), custom_call_target="tpu_custom_call" | custom-call | flops 1 | bytes 1 | tf_op jit(solution)/shard_map/far_products/pallas_call | solution.py:343
  65.4 1.8 %collective-permute-start.8 = (bf16[128,512]{1,0:T(8,128)(2,1)S(1)}, bf16[128,512]{1,0:T(8,128)(2,1)S(1)}, u32[]{:S(2)}, u32[]{:S(2)}) collective-permute-start(bf16[128,512]{1,0:T(8,128)(2,1)S(1)} %get-tuple-element.39), channel_id=1, source_target_pairs={{0,2},{2,0},{4,6},{6,4},{1,3},{3,1},{5,7},{7,5},{8,10},{10,8},{12,... | collective-permute-start | bytes 393224 | tf_op jit(solution)/shard_map/ppermute | solution.py:428
  67.2 0.8 %collective-permute-start.9 = (bf16[128,512]{1,0:T(8,128)(2,1)S(1)}, bf16[128,512]{1,0:T(8,128)(2,1)S(1)}, u32[]{:S(2)}, u32[]{:S(2)}) collective-permute-start(bf16[128,512]{1,0:T(8,128)(2,1)S(1)} %get-tuple-element.40), channel_id=1, source_target_pairs={{0,4},{2,6},{4,0},{6,2},{1,5},{3,7},{5,1},{7,3},{8,12},{10,14},{12... | collective-permute-start | bytes 393224 | tf_op jit(solution)/shard_map/ppermute | solution.py:428
  68.0 1.0 %collective-permute-start.10 = (bf16[128,512]{1,0:T(8,128)(2,1)S(1)}, bf16[128,512]{1,0:T(8,128)(2,1)S(1)}, u32[]{:S(2)}, u32[]{:S(2)}) collective-permute-start(bf16[128,512]{1,0:T(8,128)(2,1)S(1)} %get-tuple-element.41), channel_id=1, source_target_pairs={{0,6},{2,4},{4,2},{6,0},{1,7},{3,5},{5,3},{7,1},{8,14},{10,12},{12... | collective-permute-start | bytes 393224 | tf_op jit(solution)/shard_map/ppermute | solution.py:428
  69.0 2.9 %collective-permute-done.8.refs_5_ = bf16[128,512]{1,0:T(8,128)(2,1)S(1)} collective-permute-done((bf16[128,512]{1,0:T(8,128)(2,1)S(1)}, bf16[128,512]{1,0:T(8,128)(2,1)S(1)}, u32[]{:S(2)}, u32[]{:S(2)}) %collective-permute-start.8) | collective-permute-done | bytes 131104 | tf_op jit(solution)/shard_map/ppermute | solution.py:428
  71.9 0.6 collective-permute-done.9.refs_6_
  72.5 1.4 %collective-permute-done.10.refs_7_ = bf16[128,512]{1,0:T(8,128)(2,1)S(1)} collective-permute-done((bf16[128,512]{1,0:T(8,128)(2,1)S(1)}, bf16[128,512]{1,0:T(8,128)(2,1)S(1)}, u32[]{:S(2)}, u32[]{:S(2)}) %collective-permute-start.10) | collective-permute-done | bytes 131104 | tf_op jit(solution)/shard_map/ppermute | solution.py:428
  73.9 0.0 copy-done.1
  73.9 0.0 copy-done.2
  73.9 0.0 copy-done.3
  73.9 0.0 copy-done.4
  73.9 1.4 %finish_attention.1 = (bf16[128,4096]{1,0:T(8,128)(2,1)}, bf16[128,512]{1,0:T(8,128)(2,1)}) custom-call(f32[64,4096]{1,0:T(8,128)S(1)} %copy-done.1, f32[64,4096]{1,0:T(8,128)S(1)} %copy-done.2, bf16[2048,64]{1,0:T(8,128)(2,1)S(1)} %copy-done.3, bf16[2048,64]{1,0:T(8,128)(2,1)S(1)} %copy-done.4, bf16[128,512]{1,0:T(8,128)(2,1)S(1)} %get-tuple-element.38.refs_4_, ...), custom_call_target="tpu_custom_call" | custom-call | flops 1 | bytes 1 | tf_op jit(solution)/shard_map/finish_attention/pallas_call | solution.py:385
  (1 shorter events, 0.0 us)
Async XLA Ops:
  3.8 43.7 %all-to-all-start = ((bf16[4,176,1024]{2,1,0:T(8,128)(2,1)}), bf16[4,176,1024]{2,1,0:T(8,128)(2,1)S(1)}, u32[]{:S(2)}, u32[]{:S(2)}) async-start(bf16[4,176,1024]{2,1,0:T(8,128)(2,1)} %get-tuple-element.22), calls=%async_computation | async-start | bytes 2883584 | tf_op jit(solution)/shard_map/all_to_all | solution.py:431
  9.0 38.5 %collective-permute-start.1 = (bf16[512,512]{1,0:T(8,128)(2,1)}, bf16[512,512]{1,0:T(8,128)(2,1)S(1)}, u32[]{:S(2)}, u32[]{:S(2)}) collective-permute-start(bf16[512,512]{1,0:T(8,128)(2,1)} %get-tuple-element.30), channel_id=1, source_target_pairs={{0,8},{8,0},{1,9},{9,1},{2,10},{10,2},{3,11},{11,3},{4,12},{12,4},... | collective-permute-start | bytes 1572872 | tf_op jit(solution)/shard_map/ppermute | solution.py:433
  11.6 35.9 %collective-permute-start = (bf16[32,4608]{1,0:T(8,128)(2,1)}, bf16[32,4608]{1,0:T(8,128)(2,1)S(1)}, u32[]{:S(2)}, u32[]{:S(2)}) collective-permute-start(bf16[32,4608]{1,0:T(8,128)(2,1)} %get-tuple-element.29), channel_id=1, source_target_pairs={{0,8},{8,0},{1,9},{9,1},{2,10},{10,2},{3,11},{11,3},{4,12},{12,4},... | collective-permute-start | bytes 884744 | tf_op jit(solution)/shard_map/ppermute | solution.py:432
  23.1 34.8 %copy-start.5 = (s32[16]{0:T(128)S(1)}, s32[16]{0:T(128)}, u32[]{:S(2)}) copy-start(s32[16]{0:T(128)} %position.1) | copy-start | bytes 196
  23.1 34.7 %copy-start.6 = (s32[16]{0:T(128)S(1)}, s32[16]{0:T(128)}, u32[]{:S(2)}) copy-start(s32[16]{0:T(128)} %adapter.1) | copy-start | bytes 196
  31.0 26.9 %copy-start = (bf16[1024,512]{1,0:T(8,128)(2,1)S(1)}, bf16[1024,512]{1,0:T(8,128)(2,1)}, u32[]{:S(2)}) copy-start(bf16[1024,512]{1,0:T(8,128)(2,1)} %own_ref.1) | copy-start | bytes 3145732
  47.5 10.4 %collective-permute-start.2 = (bf16[4,176,1024]{2,1,0:T(8,128)(2,1)S(1)}, bf16[4,176,1024]{2,1,0:T(8,128)(2,1)S(1)}, u32[]{:S(2)}, u32[]{:S(2)}) collective-permute-start(bf16[4,176,1024]{2,1,0:T(8,128)(2,1)S(1)} %all-to-all-done.mine), channel_id=1, source_target_pairs={{0,1},{1,0},{2,3},{3,2},{4,5},{5,4},{6,7},{7,6},{8,9},{9,8},{10,11... | collective-permute-start | bytes 4325384 | tf_op jit(solution)/shard_map/ppermute | solution.py:443
  47.5 6.6 %collective-permute-start.5 = (bf16[48,1024]{1,0:T(8,128)(2,1)S(1)}, bf16[48,1024]{1,0:T(8,128)(2,1)S(1)}, u32[]{:S(2)}, u32[]{:S(2)}) collective-permute-start(bf16[48,1024]{1,0:T(8,128)(2,1)S(1)} %get-tuple-element.37), channel_id=1, source_target_pairs={{0,6},{2,4},{4,2},{6,0},{1,7},{3,5},{5,3},{7,1},{8,14},{10,12},{12... | collective-permute-start | bytes 294920 | tf_op jit(solution)/shard_map/ppermute | solution.py:428
  49.5 6.5 %collective-permute-start.4 = (bf16[48,1024]{1,0:T(8,128)(2,1)S(1)}, bf16[48,1024]{1,0:T(8,128)(2,1)S(1)}, u32[]{:S(2)}, u32[]{:S(2)}) collective-permute-start(bf16[48,1024]{1,0:T(8,128)(2,1)S(1)} %get-tuple-element.36), channel_id=1, source_target_pairs={{0,4},{2,6},{4,0},{6,2},{1,5},{3,7},{5,1},{7,3},{8,12},{10,14},{12... | collective-permute-start | bytes 294920 | tf_op jit(solution)/shard_map/ppermute | solution.py:428
  50.8 5.3 %collective-permute-start.3 = (bf16[48,1024]{1,0:T(8,128)(2,1)S(1)}, bf16[48,1024]{1,0:T(8,128)(2,1)S(1)}, u32[]{:S(2)}, u32[]{:S(2)}) collective-permute-start(bf16[48,1024]{1,0:T(8,128)(2,1)S(1)} %get-tuple-element.35), channel_id=1, source_target_pairs={{0,2},{2,0},{4,6},{6,4},{1,3},{3,1},{5,7},{7,5},{8,10},{10,8},{12,... | collective-permute-start | bytes 294920 | tf_op jit(solution)/shard_map/ppermute | solution.py:428
  51.1 13.5 %collective-permute-start.7 = (bf16[512,512]{1,0:T(8,128)(2,1)S(1)}, bf16[512,512]{1,0:T(8,128)(2,1)S(1)}, u32[]{:S(2)}, u32[]{:S(2)}) collective-permute-start(bf16[512,512]{1,0:T(8,128)(2,1)S(1)} %collective-permute-done.1.refs_0_), channel_id=1, source_target_pairs={{0,16},{16,0},{1,17},{17,1},{2,18},{18,2},{3,19},{19,3},{4,20},{20... | collective-permute-start | bytes 1572872 | tf_op jit(solution)/shard_map/ppermute | solution.py:440
  56.1 1.8 %collective-permute-start.6 = (bf16[4,48,1024]{2,1,0:T(8,128)(2,1)S(1)}, bf16[4,48,1024]{2,1,0:T(8,128)(2,1)S(1)}, u32[]{:S(2)}, u32[]{:S(2)}) collective-permute-start(bf16[4,48,1024]{2,1,0:T(8,128)(2,1)S(1)} %pad_maximum_fusion.maps_mine), channel_id=1, source_target_pairs={{0,1},{1,0},{2,3},{3,2},{4,5},{5,4},{6,7},{7,6},{8,9},{9,8},{10,11... | collective-permute-start | bytes 1179656 | tf_op jit(solution)/shard_map/ppermute | solution.py:444
  60.4 13.5 %copy-start.1 = (f32[64,4096]{1,0:T(8,128)S(1)}, f32[64,4096]{1,0:T(8,128)}, u32[]{:S(2)}) copy-start(f32[64,4096]{1,0:T(8,128)} %get-tuple-element.24.refs_0_) | copy-start | bytes 3145732
  60.4 13.5 %copy-start.2 = (f32[64,4096]{1,0:T(8,128)S(1)}, f32[64,4096]{1,0:T(8,128)}, u32[]{:S(2)}) copy-start(f32[64,4096]{1,0:T(8,128)} %get-tuple-element.27.refs_1_) | copy-start | bytes 3145732
  60.4 13.5 %copy-start.3 = (bf16[2048,64]{1,0:T(8,128)(2,1)S(1)}, bf16[2048,64]{1,0:T(8,128)(2,1)}, u32[]{:S(2)}) copy-start(bf16[2048,64]{1,0:T(8,128)(2,1)} %get-tuple-element.25.refs_2_) | copy-start | bytes 786436
  60.4 13.5 %copy-start.4 = (bf16[2048,64]{1,0:T(8,128)(2,1)S(1)}, bf16[2048,64]{1,0:T(8,128)(2,1)}, u32[]{:S(2)}) copy-start(bf16[2048,64]{1,0:T(8,128)(2,1)} %get-tuple-element.28.refs_3_) | copy-start | bytes 786436
  65.4 6.4 %collective-permute-start.8 = (bf16[128,512]{1,0:T(8,128)(2,1)S(1)}, bf16[128,512]{1,0:T(8,128)(2,1)S(1)}, u32[]{:S(2)}, u32[]{:S(2)}) collective-permute-start(bf16[128,512]{1,0:T(8,128)(2,1)S(1)} %get-tuple-element.39), channel_id=1, source_target_pairs={{0,2},{2,0},{4,6},{6,4},{1,3},{3,1},{5,7},{7,5},{8,10},{10,8},{12,... | collective-permute-start | bytes 393224 | tf_op jit(solution)/shard_map/ppermute | solution.py:428
  67.2 5.3 %collective-permute-start.9 = (bf16[128,512]{1,0:T(8,128)(2,1)S(1)}, bf16[128,512]{1,0:T(8,128)(2,1)S(1)}, u32[]{:S(2)}, u32[]{:S(2)}) collective-permute-start(bf16[128,512]{1,0:T(8,128)(2,1)S(1)} %get-tuple-element.40), channel_id=1, source_target_pairs={{0,4},{2,6},{4,0},{6,2},{1,5},{3,7},{5,1},{7,3},{8,12},{10,14},{12... | collective-permute-start | bytes 393224 | tf_op jit(solution)/shard_map/ppermute | solution.py:428
  68.0 5.9 %collective-permute-start.10 = (bf16[128,512]{1,0:T(8,128)(2,1)S(1)}, bf16[128,512]{1,0:T(8,128)(2,1)S(1)}, u32[]{:S(2)}, u32[]{:S(2)}) collective-permute-start(bf16[128,512]{1,0:T(8,128)(2,1)S(1)} %get-tuple-element.41), channel_id=1, source_target_pairs={{0,6},{2,4},{4,2},{6,0},{1,7},{3,5},{5,3},{7,1},{8,14},{10,12},{12... | collective-permute-start | bytes 393224 | tf_op jit(solution)/shard_map/ppermute | solution.py:428

commit v6 on v5

--- a/solution.py
+++ b/solution.py
@@ -13,7 +13,6 @@
 RANK = 16
 SPAN = 64
 CHUNK = 512
-CHUNKS = 1
 ONES = 16
 ADAPTER_SCALE = 2.0
 EXP2_SCALE = math.log2(math.e) / math.sqrt(HD)
@@ -159,25 +158,52 @@
     ]
 
 
-def pack_kernel(x_hbm, d_hbm, u_hbm, w_hbm, out, maps, *refs):
+def cross_kernel(w_hbm, d_hbm, u_hbm, maps, *refs):
     rows, sems = refs[:-1], refs[-1]
     part, core = lax.axis_index("parts") % 2, lax.axis_index("tensor")
+    cols = u_hbm.shape[1]
+    features = maps.shape[1] - cols
+    mine = pl.ds(pl.multiple_of(part * RANK, RANK), RANK)
+    here = pl.ds(pl.multiple_of(core * features, features), features)
+    copies = [(d_hbm.at[mine, here], maps.at[:, :features]), (u_hbm.at[mine, :], maps.at[:, features:])]
+    begin = part * (w_hbm.shape[0] // 2)
+    for piece in rows:
+        size = piece.shape[0]
+        copies.append((w_hbm.at[pl.ds(pl.multiple_of(begin, RANK), size), :], piece))
+        begin = begin + size
+    run_copies(copies, sems)
+
+
+def cross_pack(weights, downs, ups):
+    width, cols = weights.shape
+    vmem = pl.BlockSpec(memory_space=pltpu.VMEM)
+    hbm = pl.BlockSpec(memory_space=pltpu.HBM)
+    maps = jax.ShapeDtypeStruct((RANK, downs.shape[1] // 2 + cols), downs.dtype)
+    first = width // 2 * 3 // 8
+    rows = [jax.ShapeDtypeStruct((size, cols), weights.dtype) for size in (first, width // 2 - first)]
+    return pl.pallas_call(
+        cross_kernel,
+        in_specs=[hbm] * 3,
+        out_specs=[vmem] * 3,
+        out_shape=[maps] + rows,
+        scratch_shapes=[pltpu.SemaphoreType.DMA((4,))],
+        compiler_params=pltpu.CompilerParams(vmem_limit_bytes=57 * MIB),
+        cost_estimate=FREE,
+        name="cross_pack",
+    )(weights, downs, ups)
+
+
+def quad_kernel(x_hbm, d_hbm, u_hbm, out, sems):
+    core = lax.axis_index("tensor")
     quads, _, width = out.shape
     tokens, features = x_hbm.shape
     ranks, cols = u_hbm.shape
     step = min(cols, width)
-    begin = part * (w_hbm.shape[0] // 2)
     copies = []
-    for piece in rows:
-        size = piece.shape[0]
-        copies.append((w_hbm.at[pl.ds(pl.multiple_of(begin, size), size), :], piece))
-        begin = begin + size
-    copies.append((d_hbm.at[:, pl.ds(pl.multiple_of(core * features, features), features)], maps.at[:, :features]))
-    copies.append((u_hbm, maps.at[:, features:]))
     for j in range(quads):
-        first = pl.multiple_of(core * features + j * width, width)
+        begin = pl.multiple_of(core * features + j * width, width)
         copies.append((x_hbm.at[:, j * width : (j + 1) * width], out.at[j, :tokens, :]))
-        copies.append((d_hbm.at[:, pl.ds(first, width)], out.at[j, tokens : tokens + ranks, :]))
+        copies.append((d_hbm.at[:, pl.ds(begin, width)], out.at[j, tokens : tokens + ranks, :]))
         for slot, first, row, col in up_places(cols, width):
             row += tokens + ranks
             copies.append(
@@ -189,57 +215,54 @@
     run_copies(copies, sems)
 
 
-def pack(tokens, downs, ups, weights, quads):
+def quad_pack(tokens, downs, ups, width, quads):
     vmem = pl.BlockSpec(memory_space=pltpu.VMEM)
     hbm = pl.BlockSpec(memory_space=pltpu.HBM)
     ranks, cols = ups.shape
-    width = weights.shape[0]
     rows = tokens.shape[0] + ranks + RANK * (2 * cols // width)
-    count = CHUNKS + 2 + quads * (2 + len(up_places(cols, width)))
-    piece = jax.ShapeDtypeStruct((width // 2 // CHUNKS, cols), weights.dtype)
-    return pl.pallas_call(
-        pack_kernel,
-        in_specs=[hbm] * 4,
-        out_specs=[vmem] * (2 + CHUNKS),
-        out_shape=[
-            jax.ShapeDtypeStruct((quads, rows, width), tokens.dtype),
-            jax.ShapeDtypeStruct((ranks, tokens.shape[1] + cols), downs.dtype),
-        ]
-        + [piece] * CHUNKS,
+    count = quads * (2 + len(up_places(cols, width)))
+    return pl.pallas_call(
+        quad_kernel,
+        in_specs=[hbm] * 3,
+        out_specs=vmem,
+        out_shape=jax.ShapeDtypeStruct((quads, rows, width), tokens.dtype),
         scratch_shapes=[pltpu.SemaphoreType.DMA((count,))],
         compiler_params=pltpu.CompilerParams(vmem_limit_bytes=57 * MIB),
         cost_estimate=FREE,
-        name="pack",
-    )(tokens, downs, ups, weights)
-
-
-def maps_kernel(here, *outs):
-    quad = lax.axis_index("quad")
+        name="quad_pack",
+    )(tokens, downs, ups)
+
+
+def maps_kernel(here, there, *outs):
+    part, quad = lax.axis_index("parts") % 2, lax.axis_index("quad")
     width = outs[0].shape[1]
-    ranks = here.shape[0]
     features = len(outs) * width
     cols = here.shape[1] - features
     step = min(cols, width)
     for q, out in enumerate(outs):
-        out[:ranks, :] = here[:, pl.ds(pl.multiple_of((quad ^ q) * width, width), width)]
-        for slot, first, row, col in up_places(cols, width):
-            up = here[slot * RANK : (slot + 1) * RANK, features + first : features + first + step]
-            out[ranks + row : ranks + row + RANK, col : col + step] = up
-
-
-def maps_pack(here, width, quads):
+        column = pl.ds(pl.multiple_of((quad ^ q) * width, width), width)
+        for slot, maps in ((part, here), (1 - part, there)):
+            out[pl.ds(pl.multiple_of(slot * RANK, RANK), RANK), :] = maps[:, column]
+            for first in range(0, cols, step):
+                place = slot * cols + first
+                row = pl.multiple_of((2 + place // width) * RANK, RANK)
+                col = pl.multiple_of(place % width, step)
+                out[pl.ds(row, RANK), pl.ds(col, step)] = maps[:, features + first : features + first + step]
+
+
+def maps_pack(here, there, width, quads):
     vmem = pl.BlockSpec(memory_space=pltpu.VMEM)
     cols = here.shape[1] - quads * width
     maps = jax.ShapeDtypeStruct((RANK * (2 + 2 * cols // width), width), here.dtype)
     return pl.pallas_call(
         maps_kernel,
-        in_specs=[vmem],
+        in_specs=[vmem] * 2,
         out_specs=[vmem] * quads,
         out_shape=[maps] * quads,
         compiler_params=pltpu.CompilerParams(vmem_limit_bytes=4 * MIB),
         cost_estimate=FREE,
         name="maps_pack",
-    )(here)
+    )(here, there)
 
 
 def near_kernel(tokens, position, adapter, mine, theirs, maps_mine, maps_theirs, own_ref, out, ds, us):
@@ -312,13 +335,11 @@
     weights = refs[: -2 - quads]
     part, core, wing = lax.axis_index("parts") % 2, lax.axis_index("tensor"), lax.axis_index("wing")
     quad = lax.axis_index("quad")
-    chunk = weights[0].shape[0]
-    chunks = len(weights) // 2
     for side in range(2):
         begin = (part if side == 0 else 1 - part) * (width // 2)
-        for i in range(chunks):
-            row = pl.multiple_of(begin + i * chunk, chunk)
-            whole[pl.ds(row, chunk), :] = weights[side * chunks + i][...]
+        for piece in weights[2 * side : 2 * side + 2]:
+            whole[pl.ds(pl.multiple_of(begin, RANK), piece.shape[0]), :] = piece[...]
+            begin = begin + piece.shape[0]
 
     def store(x):
         product = dot(x[:, :tokens, :].reshape(quads * tokens, width), whole[...])
@@ -416,9 +437,12 @@
     ups = adapter_up_weight.reshape(-1, cols)
 
     kv_heads = cols // HD
-    def attention(span, lengths):
+    kv_heads = cols // HD
+    pieces = [(0, 0, 1), (0, 1, 1), (0, 2, kv_heads - 2), (1, 0, kv_heads // 2), (1, kv_heads // 2, kv_heads // 2)]
+
+    def attention(piece, lengths):
         return cache_attention(
-            span, 0, cols // HD, False, queries, incoming_keys, stored_keys, stored_values, lengths
+            *pieces[piece], False, queries, incoming_keys, stored_keys, stored_values, lengths
         )
 
     def after(value, *others):
@@ -427,21 +451,36 @@
     def to_quad(value, q):
         return lax.ppermute(value, "quad", [(j, j ^ q) for j in range(quads)])
 
-    message, maps, *rows = pack(normed_inputs, downs, ups, value_matrix, quads)
+    leaving, *rows = cross_pack(value_matrix, downs, ups)
+    maps = lax.ppermute(leaving, "wing", SWAP)
+    rows = [lax.ppermute(piece, "wing", SWAP) for piece in rows]
+
+    attn = [attention(0, after(cache_length, leaving))]
+    message = quad_pack(after(normed_inputs, attn[0][1]), downs, ups, width, quads)
     mine = lax.all_to_all(message, "quad", 0, 0)
-    maps = lax.ppermute(maps, "wing", SWAP)
-    rows = [lax.ppermute(piece, "wing", SWAP) for piece in rows]
-
-    attn = [attention(0, after(cache_length, message))]
-    attn.append(attention(1, after(cache_length, attn[0][1])))
-    maps, *rows = lax.optimization_barrier((maps, *rows, attn[1][1]))[:-1]
-    passed = maps_pack(maps, width, quads)
+    maps = after(maps, message)
+    maps_other = lax.ppermute(maps, "parts", parts_swap)
+
+    attn.append(attention(1, after(cache_length, maps)))
+    maps_other, rows[0] = lax.optimization_barrier((maps_other, rows[0], attn[1][1]))[:-1]
+    rows_other = [lax.ppermute(rows[0], "parts", parts_swap)]
+    passed = maps_pack(maps, maps_other, width, quads)
     passed_on = [to_quad(passed[q], q) for q in range(1, quads)]
-    rows_other = [lax.ppermute(piece, "parts", parts_swap) for piece in rows]
-
+
+    attn.append(attention(2, after(cache_length, passed[0])))
+    attn.append(attention(3, after(cache_length, attn[2][1])))
+    rows[1], rows_other[0], mine, *passed_on = lax.optimization_barrier(
+        (rows[1], rows_other[0], mine, *passed_on, attn[3][1])
+    )[:-1]
+    rows_other.append(lax.ppermute(rows[1], "parts", parts_swap))
+    theirs = lax.ppermute(mine, "tensor", SWAP)
     maps_mine = jnp.stack([passed[0]] + passed_on)
-    theirs = lax.ppermute(after(mine, rows[0]), "tensor", SWAP)
     maps_theirs = lax.ppermute(maps_mine, "tensor", SWAP)
+
+    attn.append(attention(4, after(cache_length, rows[1], mine, maps_mine)))
+    theirs, maps_theirs, rows_other[1] = lax.optimization_barrier(
+        (theirs, maps_theirs, rows_other[1], attn[4][1])
+    )[:-1]
 
     tokens, q_width = queries.shape
     near = near_products(
@@ -450,7 +489,7 @@
     products = far_products(mine, theirs, near, (*rows, *rows_other), tokens)
     parts = [products[0]] + [to_quad(products[q], q) for q in range(1, quads)]
     mixed, fresh_probs = zip(*attn)
-    attended, incoming_values = finish([(0, 0), (1, 0)], mixed, fresh_probs, parts, q_width)
+    attended, incoming_values = finish([piece[:2] for piece in pieces], mixed, fresh_probs, parts, q_width)
     return (attended, incoming_values)
 
 

time: 75.6 us -> 91.4 us (1.21)
  Pallas kernels: 26.8 us -> 39.6 us
  starting transfers between devices: 16.9 us -> 27.9 us
  waiting for transfers between devices: 30.7 us -> 23 us
    pallas_call x2 -> x5, Pallas kernels: 19 us -> 30.2 us  [cache_attention(): pl.pallas_call(functools.partial(cache_kernel, span, first_head, kv_heads...]
    ppermute x3 -> x5, starting transfers between devices: 1.88 us -> 9 us  [the longest x1 3.07 us: on_device(): maps = lax.ppermute(leaving, 'wing', SWAP)]
    ppermute x3 -> x5, waiting for transfers between devices: 20.7 us -> 17.2 us  [the longest x1 16.8 us: on_device(): maps = lax.ppermute(leaving, 'wing', SWAP)]
    ppermute x6, waiting for transfers between devices: 8.29 us -> 5.78 us  [to_quad(): return lax.ppermute(value, 'quad', [(j, j ^ q) for j in range(quads)])]
    ppermute x6, starting transfers between devices: 7.11 us -> 8.82 us  [to_quad(): return lax.ppermute(value, 'quad', [(j, j ^ q) for j in range(quads)])]
    ppermute x1, waiting for transfers between devices: 1.71 us -> 0.01 us  [on_device(): maps_theirs = lax.ppermute(maps_mine, 'tensor', SWAP)]
    pallas_call x2 -> x3, Pallas kernels: 3.16 us -> 4.72 us  [the longest x1 2.65 us: quad_pack(): pl.pallas_call(quad_kernel, in_specs=[hbm] * 3, out_specs=vmem, out_shape...]
    ppermute x1 -> x2, starting transfers between devices: 2.59 us -> 3.47 us  [on_device(): rows = [lax.ppermute(piece, 'wing', SWAP) for piece in rows]]
  transfers between devices with their start and end apart: 12 -> 15, of which waited for: 8 -> 5; matrix products, arithmetic and copies ran while one was open for 0% -> 0% of each run, Pallas kernels for 28% -> 28%
where the time goes in v6:
time: 91.4 us; the launch traced here: 91.6 us
  Pallas kernels  39.6 us (43%)
  starting transfers between devices  27.9 us (31%)
  waiting for transfers between devices  23 us (25%)
  between operations  1 us (1%)
    pallas_call x5, Pallas kernels, cache_attention(): pl.pallas_call(functools.partial(cache_kernel, span, first_head, kv_heads...  30.2 us
    ppermute x1, waiting for transfers between devices, on_device(): maps = lax.ppermute(leaving, 'wing', SWAP)  16.8 us
    ppermute x6, starting transfers between devices, to_quad(): return lax.ppermute(value, 'quad', [(j, j ^ q) for j in range(quads)])  8.82 us
    all_to_all x1, starting transfers between devices, on_device(): mine = lax.all_to_all(message, 'quad', 0, 0)  6.05 us
    ppermute x6, waiting for transfers between devices, to_quad(): return lax.ppermute(value, 'quad', [(j, j ^ q) for j in range(quads)])  5.78 us
    ppermute x2, starting transfers between devices, on_device(): rows = [lax.ppermute(piece, 'wing', SWAP) for piece in rows]  3.47 us
    ppermute x1, starting transfers between devices, on_device(): maps = lax.ppermute(leaving, 'wing', SWAP)  3.07 us
    ppermute x1, starting transfers between devices, on_device(): rows_other.append(lax.ppermute(rows[1], 'parts', parts_swap))  3.02 us
  transfers between devices with their start and end apart: 15, of which 5 were waited for; matrix products, arithmetic and copies ran while one was open for 0% of the time, Pallas kernels for 28%

profile of v6, /device:TPU:0, one launch (start us, length us, event | category | flops | bytes accessed | tf_op | source)
XLA Modules:
  0.0 91.6 jit_solution(16505021594084599512)
XLA Ops:
  0.6 2.0 %cross_pack.1 = (bf16[16,4608]{1,0:T(8,128)(2,1)}, bf16[192,512]{1,0:T(8,128)(2,1)}, bf16[320,512]{1,0:T(8,128)(2,1)}) custom-call(bf16[1024,512]{1,0:T(8,128)(2,1)} %own_ref.1, bf16[32,8192]{1,0:T(8,128)(2,1)} %bitcast.7, bf16[32,512]{1,0:T(8,128)(2,1)} %bitcast.9), custom_call_target="tpu_custom_call" | custom-call | flops 1 | bytes 1 | tf_op jit(solution)/shard_map/cross_pack/pallas_call | solution.py:184
  2.7 4.7 %cache_attention.5 = (f32[64,1024]{1,0:T(8,128)}, bf16[512,64]{1,0:T(8,128)(2,1)}) custom-call(s32[2]{0:T(128)} %lens.4, bf16[128,4096]{1,0:T(8,128)(2,1)} %q_ref.9, bf16[128,512]{1,0:T(8,128)(2,1)} %fk_ref.9, bf16[2,2048,512]{2,1,0:T(8,128)(2,1)} %k_hbm.9, bf16[2,2048,512]{2,1,0:T(8,128)(2,1)} %v_hbm.9), custom_call_target="tpu_custom_call" | custom-call | flops 1 | bytes 1 | tf_op jit(solution)/shard_map/cache_attention/pallas_call | solution.py:118
  7.4 2.6 %quad_pack.1 = bf16[4,176,1024]{2,1,0:T(8,128)(2,1)} custom-call(bf16[128,4096]{1,0:T(8,128)(2,1)} %x_hbm, bf16[32,8192]{1,0:T(8,128)(2,1)} %bitcast.8, bf16[32,512]{1,0:T(8,128)(2,1)} %bitcast.10), custom_call_target="tpu_custom_call" | custom-call | flops 1 | bytes 1 | tf_op jit(solution)/shard_map/quad_pack/pallas_call | solution.py:224
  10.0 0.0 copy-start.13
  10.0 6.0 %all-to-all-start = ((bf16[4,176,1024]{2,1,0:T(8,128)(2,1)}), bf16[4,176,1024]{2,1,0:T(8,128)(2,1)S(1)}, u32[]{:S(2)}, u32[]{:S(2)}) async-start(bf16[4,176,1024]{2,1,0:T(8,128)(2,1)} %quad_pack.1), calls=%async_computation | async-start | bytes 2883584 | tf_op jit(solution)/shard_map/all_to_all | solution.py:460
  16.1 3.1 %collective-permute-start = (bf16[16,4608]{1,0:T(8,128)(2,1)S(1)}, bf16[16,4608]{1,0:T(8,128)(2,1)S(1)}, u32[]{:S(2)}, u32[]{:S(2)}) collective-permute-start(bf16[16,4608]{1,0:T(8,128)(2,1)S(1)} %copy-done.15), channel_id=1, source_target_pairs={{0,8},{8,0},{1,9},{9,1},{2,10},{10,2},{3,11},{11,3},{4,12},{12,4},... | collective-permute-start | bytes 442376 | tf_op jit(solution)/shard_map/ppermute | solution.py:455
  19.2 0.1 collective-permute-start.2
  19.3 16.8 %collective-permute-done.here = bf16[16,4608]{1,0:T(8,128)(2,1)S(1)} collective-permute-done((bf16[16,4608]{1,0:T(8,128)(2,1)S(1)}, bf16[16,4608]{1,0:T(8,128)(2,1)S(1)}, u32[]{:S(2)}, u32[]{:S(2)}) %collective-permute-start) | collective-permute-done | bytes 147488 | tf_op jit(solution)/shard_map/ppermute | solution.py:455
  36.1 2.1 %collective-permute-start.1 = (bf16[16,4608]{1,0:T(8,128)(2,1)S(1)}, bf16[16,4608]{1,0:T(8,128)(2,1)S(1)}, u32[]{:S(2)}, u32[]{:S(2)}) collective-permute-start(bf16[16,4608]{1,0:T(8,128)(2,1)S(1)} %collective-permute-done.here), channel_id=1, source_target_pairs={{0,16},{16,0},{1,17},{17,1},{2,18},{18,2},{3,19},{19,3},{4,20},{20... | collective-permute-start | bytes 442376 | tf_op jit(solution)/shard_map/ppermute | solution.py:462
  38.2 3.4 %collective-permute-start.3 = (bf16[320,512]{1,0:T(8,128)(2,1)S(1)}, bf16[320,512]{1,0:T(8,128)(2,1)S(1)}, u32[]{:S(2)}, u32[]{:S(2)}) collective-permute-start(bf16[320,512]{1,0:T(8,128)(2,1)S(1)} %copy-done.13), channel_id=1, source_target_pairs={{0,8},{8,0},{1,9},{9,1},{2,10},{10,2},{3,11},{11,3},{4,12},{12,4},... | collective-permute-start | bytes 983048 | tf_op jit(solution)/shard_map/ppermute | solution.py:456
  41.6 4.7 %cache_attention.6 = (f32[64,1024]{1,0:T(8,128)}, bf16[512,64]{1,0:T(8,128)(2,1)}) custom-call(s32[2]{0:T(128)} %lens.4, bf16[128,4096]{1,0:T(8,128)(2,1)} %q_ref.9, bf16[128,512]{1,0:T(8,128)(2,1)} %fk_ref.9, bf16[2,2048,512]{2,1,0:T(8,128)(2,1)} %k_hbm.9, bf16[2,2048,512]{2,1,0:T(8,128)(2,1)} %v_hbm.9), custom_call_target="tpu_custom_call" | custom-call | flops 1 | bytes 1 | tf_op jit(solution)/shard_map/cache_attention/pallas_call | solution.py:118
  46.3 0.0 collective-permute-done.2.refs_0_
  46.3 0.0 collective-permute-done.1.there
  46.3 0.7 collective-permute-start.4
  47.0 2.8 %collective-permute-start.5 = (bf16[48,1024]{1,0:T(8,128)(2,1)S(1)}, bf16[48,1024]{1,0:T(8,128)(2,1)S(1)}, u32[]{:S(2)}, u32[]{:S(2)}) collective-permute-start(bf16[48,1024]{1,0:T(8,128)(2,1)S(1)} %get-tuple-element.60), channel_id=1, source_target_pairs={{0,2},{2,0},{4,6},{6,4},{1,3},{3,1},{5,7},{7,5},{8,10},{10,8},{12,... | collective-permute-start | bytes 294920 | tf_op jit(solution)/shard_map/ppermute | solution.py:452
  49.8 1.4 %collective-permute-start.6 = (bf16[48,1024]{1,0:T(8,128)(2,1)S(1)}, bf16[48,1024]{1,0:T(8,128)(2,1)S(1)}, u32[]{:S(2)}, u32[]{:S(2)}) collective-permute-start(bf16[48,1024]{1,0:T(8,128)(2,1)S(1)} %get-tuple-element.61), channel_id=1, source_target_pairs={{0,4},{2,6},{4,0},{6,2},{1,5},{3,7},{5,1},{7,3},{8,12},{10,14},{12... | collective-permute-start | bytes 294920 | tf_op jit(solution)/shard_map/ppermute | solution.py:452
  51.2 0.2 collective-permute-start.7
  51.4 5.7 %cache_attention.7 = (f32[64,2048]{1,0:T(8,128)}, bf16[1024,64]{1,0:T(8,128)(2,1)}) custom-call(s32[2]{0:T(128)} %lens.4, bf16[128,4096]{1,0:T(8,128)(2,1)} %q_ref.9, bf16[128,512]{1,0:T(8,128)(2,1)} %fk_ref.9, bf16[2,2048,512]{2,1,0:T(8,128)(2,1)} %k_hbm.9, bf16[2,2048,512]{2,1,0:T(8,128)(2,1)} %v_hbm.9), custom_call_target="tpu_custom_call" | custom-call | flops 1 | bytes 1 | tf_op jit(solution)/shard_map/cache_attention/pallas_call | solution.py:118
  57.1 7.6 %cache_attention.8 = (f32[64,2048]{1,0:T(8,128)}, bf16[1024,64]{1,0:T(8,128)(2,1)}) custom-call(s32[2]{0:T(128)} %lens.4, bf16[128,4096]{1,0:T(8,128)(2,1)} %q_ref.9, bf16[128,512]{1,0:T(8,128)(2,1)} %fk_ref.9, bf16[2,2048,512]{2,1,0:T(8,128)(2,1)} %k_hbm.9, bf16[2,2048,512]{2,1,0:T(8,128)(2,1)} %v_hbm.9), custom_call_target="tpu_custom_call" | custom-call | flops 1 | bytes 1 | tf_op jit(solution)/shard_map/cache_attention/pallas_call | solution.py:118
  64.6 0.0 collective-permute-done.3.refs_1_
  64.7 0.0 collective-permute-done.5
  64.7 0.0 collective-permute-done.6
  64.7 0.0 collective-permute-done.7
  64.7 0.0 collective-permute-done.4.refs_2_
  64.7 0.0 all-to-all-done.mine
  64.7 0.1 collective-permute-start.8
  64.8 0.1 pad_maximum_fusion.maps_mine
  64.8 0.0 copy-start
  64.9 0.0 copy-start.11
  64.9 0.0 copy-start.12
  64.9 0.6 collective-permute-start.9
  65.4 3.0 %collective-permute-start.10 = (bf16[320,512]{1,0:T(8,128)(2,1)S(1)}, bf16[320,512]{1,0:T(8,128)(2,1)S(1)}, u32[]{:S(2)}, u32[]{:S(2)}) collective-permute-start(bf16[320,512]{1,0:T(8,128)(2,1)S(1)} %collective-permute-done.3.refs_1_), channel_id=1, source_target_pairs={{0,16},{16,0},{1,17},{17,1},{2,18},{18,2},{3,19},{19,3},{4,20},{20... | collective-permute-start | bytes 983048 | tf_op jit(solution)/shard_map/ppermute | solution.py:475
  68.5 7.6 %cache_attention.9 = (f32[64,2048]{1,0:T(8,128)}, bf16[1024,64]{1,0:T(8,128)(2,1)}) custom-call(s32[2]{0:T(128)} %lens.4, bf16[128,4096]{1,0:T(8,128)(2,1)} %q_ref.9, bf16[128,512]{1,0:T(8,128)(2,1)} %fk_ref.9, bf16[2,2048,512]{2,1,0:T(8,128)(2,1)} %k_hbm.9, bf16[2,2048,512]{2,1,0:T(8,128)(2,1)} %v_hbm.9), custom_call_target="tpu_custom_call" | custom-call | flops 1 | bytes 1 | tf_op jit(solution)/shard_map/cache_attention/pallas_call | solution.py:118
  76.0 0.4 collective-permute-done.10.refs_3_
  76.4 0.0 collective-permute-done.9.maps_theirs
  76.4 0.0 collective-permute-done.8.theirs
  76.4 2.5 %near_products.1.near = f32[512,512]{1,0:T(8,128)S(1)} custom-call(s32[16]{0:T(128)S(1)} %copy-done.11, s32[16]{0:T(128)S(1)} %copy-done.12, bf16[4,176,1024]{2,1,0:T(8,128)(2,1)S(1)} %all-to-all-done.mine, bf16[4,176,1024]{2,1,0:T(8,128)(2,1)S(1)} %collective-permute-done.8.theirs, bf16[4,48,1024]{2,1,0:T(8,128)(2,1)S(1)} %pad_maximum_fusion.maps_mine, ...), custom_call_target="tpu_custom_call" | custom-call | flops 1 | bytes 1 | tf_op jit(solution)/shard_map/near_products/pallas_call | solution.py:317
  78.9 0.0 copy-start.1
  79.0 0.0 copy-start.9
  79.0 0.0 copy-start.10
  79.0 0.8 far_products.1
  79.9 2.9 %collective-permute-start.11 = (bf16[128,512]{1,0:T(8,128)(2,1)S(1)}, bf16[128,512]{1,0:T(8,128)(2,1)S(1)}, u32[]{:S(2)}, u32[]{:S(2)}) collective-permute-start(bf16[128,512]{1,0:T(8,128)(2,1)S(1)} %get-tuple-element.77), channel_id=1, source_target_pairs={{0,2},{2,0},{4,6},{6,4},{1,3},{3,1},{5,7},{7,5},{8,10},{10,8},{12,... | collective-permute-start | bytes 393224 | tf_op jit(solution)/shard_map/ppermute | solution.py:452
  82.8 0.0 collective-permute-start.12
  82.8 1.5 %collective-permute-start.13 = (bf16[128,512]{1,0:T(8,128)(2,1)S(1)}, bf16[128,512]{1,0:T(8,128)(2,1)S(1)}, u32[]{:S(2)}, u32[]{:S(2)}) collective-permute-start(bf16[128,512]{1,0:T(8,128)(2,1)S(1)} %get-tuple-element.79), channel_id=1, source_target_pairs={{0,6},{2,4},{4,2},{6,0},{1,7},{3,5},{5,3},{7,1},{8,14},{10,12},{12... | collective-permute-start | bytes 393224 | tf_op jit(solution)/shard_map/ppermute | solution.py:452
  84.3 1.9 %collective-permute-done.11.refs_11_ = bf16[128,512]{1,0:T(8,128)(2,1)S(1)} collective-permute-done((bf16[128,512]{1,0:T(8,128)(2,1)S(1)}, bf16[128,512]{1,0:T(8,128)(2,1)S(1)}, u32[]{:S(2)}, u32[]{:S(2)}) %collective-permute-start.11) | collective-permute-done | bytes 131104 | tf_op jit(solution)/shard_map/ppermute | solution.py:452
  86.2 2.7 %collective-permute-done.12.refs_12_ = bf16[128,512]{1,0:T(8,128)(2,1)S(1)} collective-permute-done((bf16[128,512]{1,0:T(8,128)(2,1)S(1)}, bf16[128,512]{1,0:T(8,128)(2,1)S(1)}, u32[]{:S(2)}, u32[]{:S(2)}) %collective-permute-start.12) | collective-permute-done | bytes 131104 | tf_op jit(solution)/shard_map/ppermute | solution.py:452
  88.9 1.2 %collective-permute-done.13.refs_13_ = bf16[128,512]{1,0:T(8,128)(2,1)S(1)} collective-permute-done((bf16[128,512]{1,0:T(8,128)(2,1)S(1)}, bf16[128,512]{1,0:T(8,128)(2,1)S(1)}, u32[]{:S(2)}, u32[]{:S(2)}) %collective-permute-start.13) | collective-permute-done | bytes 131104 | tf_op jit(solution)/shard_map/ppermute | solution.py:452
  90.2 1.4 %finish_attention.1 = (bf16[128,4096]{1,0:T(8,128)(2,1)}, bf16[128,512]{1,0:T(8,128)(2,1)}) custom-call(f32[64,1024]{1,0:T(8,128)S(1)} %copy-done.4, f32[64,1024]{1,0:T(8,128)S(1)} %copy-done.5, f32[64,2048]{1,0:T(8,128)S(1)} %copy-done.1, f32[64,2048]{1,0:T(8,128)S(1)} %copy-done.2, f32[64,2048]{1,0:T(8,128)S(1)} %copy-done.3, ...), custom_call_target="tpu_custom_call" | custom-call | flops 1 | bytes 1 | tf_op jit(solution)/shard_map/finish_attention/pallas_call | solution.py:406
  (26 shorter events, 0.1 us)
Async XLA Ops:
  10.0 6.1 %copy-start.15 = (bf16[16,4608]{1,0:T(8,128)(2,1)S(1)}, bf16[16,4608]{1,0:T(8,128)(2,1)}, u32[]{:S(2)}) copy-start(bf16[16,4608]{1,0:T(8,128)(2,1)} %get-tuple-element.41) | copy-start | bytes 442372
  10.0 9.1 %copy-start.14 = (bf16[192,512]{1,0:T(8,128)(2,1)S(1)}, bf16[192,512]{1,0:T(8,128)(2,1)}, u32[]{:S(2)}) copy-start(bf16[192,512]{1,0:T(8,128)(2,1)} %get-tuple-element.49) | copy-start | bytes 589828
  10.0 28.2 %copy-start.13 = (bf16[320,512]{1,0:T(8,128)(2,1)S(1)}, bf16[320,512]{1,0:T(8,128)(2,1)}, u32[]{:S(2)}) copy-start(bf16[320,512]{1,0:T(8,128)(2,1)} %get-tuple-element.58) | copy-start | bytes 983044
  10.0 54.7 %all-to-all-start = ((bf16[4,176,1024]{2,1,0:T(8,128)(2,1)}), bf16[4,176,1024]{2,1,0:T(8,128)(2,1)S(1)}, u32[]{:S(2)}, u32[]{:S(2)}) async-start(bf16[4,176,1024]{2,1,0:T(8,128)(2,1)} %quad_pack.1), calls=%async_computation | async-start | bytes 2883584 | tf_op jit(solution)/shard_map/all_to_all | solution.py:460
  16.1 20.0 %collective-permute-start = (bf16[16,4608]{1,0:T(8,128)(2,1)S(1)}, bf16[16,4608]{1,0:T(8,128)(2,1)S(1)}, u32[]{:S(2)}, u32[]{:S(2)}) collective-permute-start(bf16[16,4608]{1,0:T(8,128)(2,1)S(1)} %copy-done.15), channel_id=1, source_target_pairs={{0,8},{8,0},{1,9},{9,1},{2,10},{10,2},{3,11},{11,3},{4,12},{12,4},... | collective-permute-start | bytes 442376 | tf_op jit(solution)/shard_map/ppermute | solution.py:455
  19.2 27.1 %collective-permute-start.2 = (bf16[192,512]{1,0:T(8,128)(2,1)S(1)}, bf16[192,512]{1,0:T(8,128)(2,1)S(1)}, u32[]{:S(2)}, u32[]{:S(2)}) collective-permute-start(bf16[192,512]{1,0:T(8,128)(2,1)S(1)} %copy-done.14), channel_id=1, source_target_pairs={{0,8},{8,0},{1,9},{9,1},{2,10},{10,2},{3,11},{11,3},{4,12},{12,4},... | collective-permute-start | bytes 589832 | tf_op jit(solution)/shard_map/ppermute | solution.py:456
  36.1 10.2 %collective-permute-start.1 = (bf16[16,4608]{1,0:T(8,128)(2,1)S(1)}, bf16[16,4608]{1,0:T(8,128)(2,1)S(1)}, u32[]{:S(2)}, u32[]{:S(2)}) collective-permute-start(bf16[16,4608]{1,0:T(8,128)(2,1)S(1)} %collective-permute-done.here), channel_id=1, source_target_pairs={{0,16},{16,0},{1,17},{17,1},{2,18},{18,2},{3,19},{19,3},{4,20},{20... | collective-permute-start | bytes 442376 | tf_op jit(solution)/shard_map/ppermute | solution.py:462
  38.2 26.5 %collective-permute-start.3 = (bf16[320,512]{1,0:T(8,128)(2,1)S(1)}, bf16[320,512]{1,0:T(8,128)(2,1)S(1)}, u32[]{:S(2)}, u32[]{:S(2)}) collective-permute-start(bf16[320,512]{1,0:T(8,128)(2,1)S(1)} %copy-done.13), channel_id=1, source_target_pairs={{0,8},{8,0},{1,9},{9,1},{2,10},{10,2},{3,11},{11,3},{4,12},{12,4},... | collective-permute-start | bytes 983048 | tf_op jit(solution)/shard_map/ppermute | solution.py:456
  46.3 18.4 %collective-permute-start.4 = (bf16[192,512]{1,0:T(8,128)(2,1)S(1)}, bf16[192,512]{1,0:T(8,128)(2,1)S(1)}, u32[]{:S(2)}, u32[]{:S(2)}) collective-permute-start(bf16[192,512]{1,0:T(8,128)(2,1)S(1)} %collective-permute-done.2.refs_0_), channel_id=1, source_target_pairs={{0,16},{16,0},{1,17},{17,1},{2,18},{18,2},{3,19},{19,3},{4,20},{20... | collective-permute-start | bytes 589832 | tf_op jit(solution)/shard_map/ppermute | solution.py:466
  47.0 17.6 %collective-permute-start.5 = (bf16[48,1024]{1,0:T(8,128)(2,1)S(1)}, bf16[48,1024]{1,0:T(8,128)(2,1)S(1)}, u32[]{:S(2)}, u32[]{:S(2)}) collective-permute-start(bf16[48,1024]{1,0:T(8,128)(2,1)S(1)} %get-tuple-element.60), channel_id=1, source_target_pairs={{0,2},{2,0},{4,6},{6,4},{1,3},{3,1},{5,7},{7,5},{8,10},{10,8},{12,... | collective-permute-start | bytes 294920 | tf_op jit(solution)/shard_map/ppermute | solution.py:452
  49.8 14.8 %collective-permute-start.6 = (bf16[48,1024]{1,0:T(8,128)(2,1)S(1)}, bf16[48,1024]{1,0:T(8,128)(2,1)S(1)}, u32[]{:S(2)}, u32[]{:S(2)}) collective-permute-start(bf16[48,1024]{1,0:T(8,128)(2,1)S(1)} %get-tuple-element.61), channel_id=1, source_target_pairs={{0,4},{2,6},{4,0},{6,2},{1,5},{3,7},{5,1},{7,3},{8,12},{10,14},{12... | collective-permute-start | bytes 294920 | tf_op jit(solution)/shard_map/ppermute | solution.py:452
  51.2 13.5 %collective-permute-start.7 = (bf16[48,1024]{1,0:T(8,128)(2,1)S(1)}, bf16[48,1024]{1,0:T(8,128)(2,1)S(1)}, u32[]{:S(2)}, u32[]{:S(2)}) collective-permute-start(bf16[48,1024]{1,0:T(8,128)(2,1)S(1)} %get-tuple-element.62), channel_id=1, source_target_pairs={{0,6},{2,4},{4,2},{6,0},{1,7},{3,5},{5,3},{7,1},{8,14},{10,12},{12... | collective-permute-start | bytes 294920 | tf_op jit(solution)/shard_map/ppermute | solution.py:452
  64.7 11.7 %collective-permute-start.8 = (bf16[4,176,1024]{2,1,0:T(8,128)(2,1)S(1)}, bf16[4,176,1024]{2,1,0:T(8,128)(2,1)S(1)}, u32[]{:S(2)}, u32[]{:S(2)}) collective-permute-start(bf16[4,176,1024]{2,1,0:T(8,128)(2,1)S(1)} %all-to-all-done.mine), channel_id=1, source_target_pairs={{0,1},{1,0},{2,3},{3,2},{4,5},{5,4},{6,7},{7,6},{8,9},{9,8},{10,11... | collective-permute-start | bytes 4325384 | tf_op jit(solution)/shard_map/ppermute | solution.py:476
  64.8 11.6 %copy-start = (bf16[1024,512]{1,0:T(8,128)(2,1)S(1)}, bf16[1024,512]{1,0:T(8,128)(2,1)}, u32[]{:S(2)}) copy-start(bf16[1024,512]{1,0:T(8,128)(2,1)} %own_ref.1) | copy-start | bytes 3145732
  64.9 11.6 %copy-start.11 = (s32[16]{0:T(128)S(1)}, s32[16]{0:T(128)}, u32[]{:S(2)}) copy-start(s32[16]{0:T(128)} %position.1) | copy-start | bytes 196
  64.9 11.6 %copy-start.12 = (s32[16]{0:T(128)S(1)}, s32[16]{0:T(128)}, u32[]{:S(2)}) copy-start(s32[16]{0:T(128)} %adapter.1) | copy-start | bytes 196
  64.9 11.5 %collective-permute-start.9 = (bf16[4,48,1024]{2,1,0:T(8,128)(2,1)S(1)}, bf16[4,48,1024]{2,1,0:T(8,128)(2,1)S(1)}, u32[]{:S(2)}, u32[]{:S(2)}) collective-permute-start(bf16[4,48,1024]{2,1,0:T(8,128)(2,1)S(1)} %pad_maximum_fusion.maps_mine), channel_id=1, source_target_pairs={{0,1},{1,0},{2,3},{3,2},{4,5},{5,4},{6,7},{7,6},{8,9},{9,8},{10,11... | collective-permute-start | bytes 1179656 | tf_op jit(solution)/shard_map/ppermute | solution.py:478
  65.4 11.0 %collective-permute-start.10 = (bf16[320,512]{1,0:T(8,128)(2,1)S(1)}, bf16[320,512]{1,0:T(8,128)(2,1)S(1)}, u32[]{:S(2)}, u32[]{:S(2)}) collective-permute-start(bf16[320,512]{1,0:T(8,128)(2,1)S(1)} %collective-permute-done.3.refs_1_), channel_id=1, source_target_pairs={{0,16},{16,0},{1,17},{17,1},{2,18},{18,2},{3,19},{19,3},{4,20},{20... | collective-permute-start | bytes 983048 | tf_op jit(solution)/shard_map/ppermute | solution.py:475
  78.9 11.2 %copy-start.1 = (f32[64,2048]{1,0:T(8,128)S(1)}, f32[64,2048]{1,0:T(8,128)}, u32[]{:S(2)}) copy-start(f32[64,2048]{1,0:T(8,128)} %get-tuple-element.54.refs_2_) | copy-start | bytes 1572868
  78.9 11.2 %copy-start.2 = (f32[64,2048]{1,0:T(8,128)S(1)}, f32[64,2048]{1,0:T(8,128)}, u32[]{:S(2)}) copy-start(f32[64,2048]{1,0:T(8,128)} %get-tuple-element.57.refs_3_) | copy-start | bytes 1572868
  78.9 11.2 %copy-start.3 = (f32[64,2048]{1,0:T(8,128)S(1)}, f32[64,2048]{1,0:T(8,128)}, u32[]{:S(2)}) copy-start(f32[64,2048]{1,0:T(8,128)} %get-tuple-element.70.refs_4_) | copy-start | bytes 1572868
  78.9 11.2 %copy-start.4 = (f32[64,1024]{1,0:T(8,128)S(1)}, f32[64,1024]{1,0:T(8,128)}, u32[]{:S(2)}) copy-start(f32[64,1024]{1,0:T(8,128)} %get-tuple-element.43.refs_0_) | copy-start | bytes 786436
  79.0 11.2 %copy-start.5 = (f32[64,1024]{1,0:T(8,128)S(1)}, f32[64,1024]{1,0:T(8,128)}, u32[]{:S(2)}) copy-start(f32[64,1024]{1,0:T(8,128)} %get-tuple-element.48.refs_1_) | copy-start | bytes 786436
  79.0 11.2 %copy-start.6 = (bf16[1024,64]{1,0:T(8,128)(2,1)S(1)}, bf16[1024,64]{1,0:T(8,128)(2,1)}, u32[]{:S(2)}) copy-start(bf16[1024,64]{1,0:T(8,128)(2,1)} %get-tuple-element.55.refs_7_) | copy-start | bytes 393220
  79.0 11.2 %copy-start.7 = (bf16[1024,64]{1,0:T(8,128)(2,1)S(1)}, bf16[1024,64]{1,0:T(8,128)(2,1)}, u32[]{:S(2)}) copy-start(bf16[1024,64]{1,0:T(8,128)(2,1)} %get-tuple-element.63.refs_8_) | copy-start | bytes 393220
  79.0 11.2 %copy-start.8 = (bf16[1024,64]{1,0:T(8,128)(2,1)S(1)}, bf16[1024,64]{1,0:T(8,128)(2,1)}, u32[]{:S(2)}) copy-start(bf16[1024,64]{1,0:T(8,128)(2,1)} %get-tuple-element.71.refs_9_) | copy-start | bytes 393220
  79.0 11.2 %copy-start.9 = (bf16[512,64]{1,0:T(8,128)(2,1)S(1)}, bf16[512,64]{1,0:T(8,128)(2,1)}, u32[]{:S(2)}) copy-start(bf16[512,64]{1,0:T(8,128)(2,1)} %get-tuple-element.44.refs_5_) | copy-start | bytes 196612
  79.0 11.2 %copy-start.10 = (bf16[512,64]{1,0:T(8,128)(2,1)S(1)}, bf16[512,64]{1,0:T(8,128)(2,1)}, u32[]{:S(2)}) copy-start(bf16[512,64]{1,0:T(8,128)(2,1)} %get-tuple-element.50.refs_6_) | copy-start | bytes 196612
  79.9 6.4 %collective-permute-start.11 = (bf16[128,512]{1,0:T(8,128)(2,1)S(1)}, bf16[128,512]{1,0:T(8,128)(2,1)S(1)}, u32[]{:S(2)}, u32[]{:S(2)}) collective-permute-start(bf16[128,512]{1,0:T(8,128)(2,1)S(1)} %get-tuple-element.77), channel_id=1, source_target_pairs={{0,2},{2,0},{4,6},{6,4},{1,3},{3,1},{5,7},{7,5},{8,10},{10,8},{12,... | collective-permute-start | bytes 393224 | tf_op jit(solution)/shard_map/ppermute | solution.py:452
  82.8 6.1 %collective-permute-start.12 = (bf16[128,512]{1,0:T(8,128)(2,1)S(1)}, bf16[128,512]{1,0:T(8,128)(2,1)S(1)}, u32[]{:S(2)}, u32[]{:S(2)}) collective-permute-start(bf16[128,512]{1,0:T(8,128)(2,1)S(1)} %get-tuple-element.78), channel_id=1, source_target_pairs={{0,4},{2,6},{4,0},{6,2},{1,5},{3,7},{5,1},{7,3},{8,12},{10,14},{12... | collective-permute-start | bytes 393224 | tf_op jit(solution)/shard_map/ppermute | solution.py:452
  82.8 7.3 %collective-permute-start.13 = (bf16[128,512]{1,0:T(8,128)(2,1)S(1)}, bf16[128,512]{1,0:T(8,128)(2,1)S(1)}, u32[]{:S(2)}, u32[]{:S(2)}) collective-permute-start(bf16[128,512]{1,0:T(8,128)(2,1)S(1)} %get-tuple-element.79), channel_id=1, source_target_pairs={{0,6},{2,4},{4,2},{6,0},{1,7},{3,5},{5,3},{7,1},{8,14},{10,12},{12... | collective-permute-start | bytes 393224 | tf_op jit(solution)/shard_map/ppermute | solution.py:452

commit v7 on v5

--- a/solution.py
+++ b/solution.py
@@ -13,7 +13,6 @@
 RANK = 16
 SPAN = 64
 CHUNK = 512
-CHUNKS = 1
 ONES = 16
 ADAPTER_SCALE = 2.0
 EXP2_SCALE = math.log2(math.e) / math.sqrt(HD)
@@ -170,7 +169,7 @@
     copies = []
     for piece in rows:
         size = piece.shape[0]
-        copies.append((w_hbm.at[pl.ds(pl.multiple_of(begin, size), size), :], piece))
+        copies.append((w_hbm.at[pl.ds(pl.multiple_of(begin, RANK), size), :], piece))
         begin = begin + size
     copies.append((d_hbm.at[:, pl.ds(pl.multiple_of(core * features, features), features)], maps.at[:, :features]))
     copies.append((u_hbm, maps.at[:, features:]))
@@ -195,17 +194,18 @@
     ranks, cols = ups.shape
     width = weights.shape[0]
     rows = tokens.shape[0] + ranks + RANK * (2 * cols // width)
-    count = CHUNKS + 2 + quads * (2 + len(up_places(cols, width)))
-    piece = jax.ShapeDtypeStruct((width // 2 // CHUNKS, cols), weights.dtype)
+    count = 4 + quads * (2 + len(up_places(cols, width)))
+    first = width // 2 * 3 // 8
+    pieces = [jax.ShapeDtypeStruct((size, cols), weights.dtype) for size in (first, width // 2 - first)]
     return pl.pallas_call(
         pack_kernel,
         in_specs=[hbm] * 4,
-        out_specs=[vmem] * (2 + CHUNKS),
+        out_specs=[vmem] * 4,
         out_shape=[
             jax.ShapeDtypeStruct((quads, rows, width), tokens.dtype),
             jax.ShapeDtypeStruct((ranks, tokens.shape[1] + cols), downs.dtype),
         ]
-        + [piece] * CHUNKS,
+        + pieces,
         scratch_shapes=[pltpu.SemaphoreType.DMA((count,))],
         compiler_params=pltpu.CompilerParams(vmem_limit_bytes=57 * MIB),
         cost_estimate=FREE,
@@ -312,13 +312,11 @@
     weights = refs[: -2 - quads]
     part, core, wing = lax.axis_index("parts") % 2, lax.axis_index("tensor"), lax.axis_index("wing")
     quad = lax.axis_index("quad")
-    chunk = weights[0].shape[0]
-    chunks = len(weights) // 2
     for side in range(2):
         begin = (part if side == 0 else 1 - part) * (width // 2)
-        for i in range(chunks):
-            row = pl.multiple_of(begin + i * chunk, chunk)
-            whole[pl.ds(row, chunk), :] = weights[side * chunks + i][...]
+        for piece in weights[2 * side : 2 * side + 2]:
+            whole[pl.ds(pl.multiple_of(begin, RANK), piece.shape[0]), :] = piece[...]
+            begin = begin + piece.shape[0]
 
     def store(x):
         product = dot(x[:, :tokens, :].reshape(quads * tokens, width), whole[...])
@@ -416,9 +414,12 @@
     ups = adapter_up_weight.reshape(-1, cols)
 
     kv_heads = cols // HD
-    def attention(span, lengths):
+    kv_heads = cols // HD
+    pieces = [(0, 0, kv_heads), (1, 0, kv_heads // 2), (1, kv_heads // 2, kv_heads - kv_heads // 2)]
+
+    def attention(piece, lengths):
         return cache_attention(
-            span, 0, cols // HD, False, queries, incoming_keys, stored_keys, stored_values, lengths
+            *pieces[piece], False, queries, incoming_keys, stored_keys, stored_values, lengths
         )
 
     def after(value, *others):
@@ -433,14 +434,20 @@
     rows = [lax.ppermute(piece, "wing", SWAP) for piece in rows]
 
     attn = [attention(0, after(cache_length, message))]
-    attn.append(attention(1, after(cache_length, attn[0][1])))
-    maps, *rows = lax.optimization_barrier((maps, *rows, attn[1][1]))[:-1]
-    passed = maps_pack(maps, width, quads)
+    passed = maps_pack(after(maps, attn[0][1]), width, quads)
     passed_on = [to_quad(passed[q], q) for q in range(1, quads)]
-    rows_other = [lax.ppermute(piece, "parts", parts_swap) for piece in rows]
-
+
+    attn.append(attention(1, after(cache_length, passed[0])))
+    rows[0], *passed_on = lax.optimization_barrier((rows[0], *passed_on, attn[1][1]))[:-1]
+    rows_other = [lax.ppermute(rows[0], "parts", parts_swap)]
     maps_mine = jnp.stack([passed[0]] + passed_on)
-    theirs = lax.ppermute(after(mine, rows[0]), "tensor", SWAP)
+
+    attn.append(attention(2, after(cache_length, rows[0], maps_mine)))
+    rows[1], rows_other[0], mine, maps_mine = lax.optimization_barrier(
+        (rows[1], rows_other[0], mine, maps_mine, attn[2][1])
+    )[:-1]
+    rows_other.append(lax.ppermute(rows[1], "parts", parts_swap))
+    theirs = lax.ppermute(mine, "tensor", SWAP)
     maps_theirs = lax.ppermute(maps_mine, "tensor", SWAP)
 
     tokens, q_width = queries.shape
@@ -450,7 +457,7 @@
     products = far_products(mine, theirs, near, (*rows, *rows_other), tokens)
     parts = [products[0]] + [to_quad(products[q], q) for q in range(1, quads)]
     mixed, fresh_probs = zip(*attn)
-    attended, incoming_values = finish([(0, 0), (1, 0)], mixed, fresh_probs, parts, q_width)
+    attended, incoming_values = finish([piece[:2] for piece in pieces], mixed, fresh_probs, parts, q_width)
     return (attended, incoming_values)
 
 

time: 75.6 us -> 80.3 us (1.062)
  starting transfers between devices: 16.9 us -> 23.1 us
  waiting for transfers between devices: 30.7 us -> 26.2 us
  Pallas kernels: 26.8 us -> 29 us
    ppermute x1, waiting for transfers between devices: 16.5 us -> 9.87 us  [on_device(): maps = lax.ppermute(maps, 'wing', SWAP)]
    ppermute x6, starting transfers between devices: 7.11 us -> 10.2 us  [to_quad(): return lax.ppermute(value, 'quad', [(j, j ^ q) for j in range(quads)])]
    ppermute x1, starting transfers between devices: 0.34 us -> 2.59 us  [on_device(): maps = lax.ppermute(maps, 'wing', SWAP)]
    pallas_call x2 -> x3, Pallas kernels: 19 us -> 21.1 us  [cache_attention(): pl.pallas_call(functools.partial(cache_kernel, span, first_head, kv_heads...]
    ppermute x1, waiting for transfers between devices: 1.71 us -> 3.27 us  [on_device(): maps_theirs = lax.ppermute(maps_mine, 'tensor', SWAP)]
    ppermute x6, waiting for transfers between devices: 8.29 us -> 9.15 us  [to_quad(): return lax.ppermute(value, 'quad', [(j, j ^ q) for j in range(quads)])]
    ppermute x1 -> x2, starting transfers between devices: 2.59 us -> 2.92 us  [on_device(): rows = [lax.ppermute(piece, 'wing', SWAP) for piece in rows]]
    ppermute x2 -> x3, waiting for transfers between devices: 4.17 us -> 3.87 us  [the longest x1 3.87 us: on_device(): rows_other.append(lax.ppermute(rows[1], 'parts', parts_swap))]
  transfers between devices with their start and end apart: 12 -> 14, of which waited for: 8 -> 8; matrix products, arithmetic and copies ran while one was open for 0% -> 0% of each run, Pallas kernels for 28% -> 30%
where the time goes in v7:
time: 80.3 us; the launch traced here: 79.9 us
  Pallas kernels  29 us (36%)
  waiting for transfers between devices  26.2 us (33%)
  starting transfers between devices  23.1 us (29%)
  between operations  0.87 us (1%)
    pallas_call x3, Pallas kernels, cache_attention(): pl.pallas_call(functools.partial(cache_kernel, span, first_head, kv_heads...  21.1 us
    ppermute x6, starting transfers between devices, to_quad(): return lax.ppermute(value, 'quad', [(j, j ^ q) for j in range(quads)])  10.2 us
    ppermute x1, waiting for transfers between devices, on_device(): maps = lax.ppermute(maps, 'wing', SWAP)  9.87 us
    ppermute x6, waiting for transfers between devices, to_quad(): return lax.ppermute(value, 'quad', [(j, j ^ q) for j in range(quads)])  9.15 us
    all_to_all x1, starting transfers between devices, on_device(): mine = lax.all_to_all(message, 'quad', 0, 0)  5.39 us
    ppermute x1, waiting for transfers between devices, on_device(): rows_other.append(lax.ppermute(rows[1], 'parts', parts_swap))  3.87 us
    ppermute x1, waiting for transfers between devices, on_device(): maps_theirs = lax.ppermute(maps_mine, 'tensor', SWAP)  3.27 us
    pallas_call x1, Pallas kernels, pack(): pl.pallas_call(pack_kernel, in_specs=[hbm] * 4, out_specs=[vmem] * 4, out...  3.16 us
  transfers between devices with their start and end apart: 14, of which 8 were waited for; matrix products, arithmetic and copies ran while one was open for 0% of the time, Pallas kernels for 30%

profile of v7, /device:TPU:0, one launch (start us, length us, event | category | flops | bytes accessed | tf_op | source)
XLA Modules:
  0.0 79.9 jit_solution(6075385484725877744)
XLA Ops:
  0.6 3.2 %pack.1 = (bf16[4,176,1024]{2,1,0:T(8,128)(2,1)}, bf16[32,4608]{1,0:T(8,128)(2,1)}, bf16[192,512]{1,0:T(8,128)(2,1)}, bf16[320,512]{1,0:T(8,128)(2,1)}) custom-call(bf16[128,4096]{1,0:T(8,128)(2,1)} %x_hbm.1, bf16[32,8192]{1,0:T(8,128)(2,1)} %bitcast.7, bf16[32,512]{1,0:T(8,128)(2,1)} %bitcast.11, bf16[1024,512]{1,0:T(8,128)(2,1)} %own_ref.1), custom_call_target="tpu_custom_call" | custom-call | flops 1 | bytes 1 | tf_op jit(solution)/shard_map/pack/pallas_call | solution.py:200
  3.8 0.0 copy-start.11
  3.8 0.0 copy-start.12
  3.8 5.4 %all-to-all-start = ((bf16[4,176,1024]{2,1,0:T(8,128)(2,1)}), bf16[4,176,1024]{2,1,0:T(8,128)(2,1)S(1)}, u32[]{:S(2)}, u32[]{:S(2)}) async-start(bf16[4,176,1024]{2,1,0:T(8,128)(2,1)} %get-tuple-element.32), calls=%async_computation | async-start | bytes 2883584 | tf_op jit(solution)/shard_map/all_to_all | solution.py:432
  9.2 0.0 copy-done.11
  9.2 2.6 %collective-permute-start = (bf16[32,4608]{1,0:T(8,128)(2,1)S(1)}, bf16[32,4608]{1,0:T(8,128)(2,1)S(1)}, u32[]{:S(2)}, u32[]{:S(2)}) collective-permute-start(bf16[32,4608]{1,0:T(8,128)(2,1)S(1)} %copy-done.11), channel_id=1, source_target_pairs={{0,8},{8,0},{1,9},{9,1},{2,10},{10,2},{3,11},{11,3},{4,12},{12,4},... | collective-permute-start | bytes 884744 | tf_op jit(solution)/shard_map/ppermute | solution.py:433
  11.8 0.0 copy-done.12
  11.8 0.3 collective-permute-start.1
  12.1 2.6 %collective-permute-start.5 = (bf16[320,512]{1,0:T(8,128)(2,1)}, bf16[320,512]{1,0:T(8,128)(2,1)S(1)}, u32[]{:S(2)}, u32[]{:S(2)}) collective-permute-start(bf16[320,512]{1,0:T(8,128)(2,1)} %get-tuple-element.53), channel_id=1, source_target_pairs={{0,8},{8,0},{1,9},{9,1},{2,10},{10,2},{3,11},{11,3},{4,12},{12,4},... | collective-permute-start | bytes 983048 | tf_op jit(solution)/shard_map/ppermute | solution.py:434
  14.7 7.8 %cache_attention.3 = (f32[64,4096]{1,0:T(8,128)}, bf16[2048,64]{1,0:T(8,128)(2,1)}) custom-call(s32[2]{0:T(128)} %lens.2, bf16[128,4096]{1,0:T(8,128)(2,1)} %q_ref.5, bf16[128,512]{1,0:T(8,128)(2,1)} %fk_ref.5, bf16[2,2048,512]{2,1,0:T(8,128)(2,1)} %k_hbm.5, bf16[2,2048,512]{2,1,0:T(8,128)(2,1)} %v_hbm.5), custom_call_target="tpu_custom_call" | custom-call | flops 1 | bytes 1 | tf_op jit(solution)/shard_map/cache_attention/pallas_call | solution.py:118
  22.5 9.9 %collective-permute-done.here = bf16[32,4608]{1,0:T(8,128)(2,1)S(1)} collective-permute-done((bf16[32,4608]{1,0:T(8,128)(2,1)S(1)}, bf16[32,4608]{1,0:T(8,128)(2,1)S(1)}, u32[]{:S(2)}, u32[]{:S(2)}) %collective-permute-start) | collective-permute-done | bytes 294944 | tf_op jit(solution)/shard_map/ppermute | solution.py:433
  32.4 2.1 %collective-permute-start.2 = (bf16[48,1024]{1,0:T(8,128)(2,1)S(1)}, bf16[48,1024]{1,0:T(8,128)(2,1)S(1)}, u32[]{:S(2)}, u32[]{:S(2)}) collective-permute-start(bf16[48,1024]{1,0:T(8,128)(2,1)S(1)} %get-tuple-element.42), channel_id=1, source_target_pairs={{0,2},{2,0},{4,6},{6,4},{1,3},{3,1},{5,7},{7,5},{8,10},{10,8},{12,... | collective-permute-start | bytes 294920 | tf_op jit(solution)/shard_map/ppermute | solution.py:429
  34.5 4.5 %collective-permute-start.3 = (bf16[48,1024]{1,0:T(8,128)(2,1)S(1)}, bf16[48,1024]{1,0:T(8,128)(2,1)S(1)}, u32[]{:S(2)}, u32[]{:S(2)}) collective-permute-start(bf16[48,1024]{1,0:T(8,128)(2,1)S(1)} %get-tuple-element.43), channel_id=1, source_target_pairs={{0,4},{2,6},{4,0},{6,2},{1,5},{3,7},{5,1},{7,3},{8,12},{10,14},{12... | collective-permute-start | bytes 294920 | tf_op jit(solution)/shard_map/ppermute | solution.py:429
  39.1 0.0 collective-permute-start.4
  39.1 6.6 %cache_attention.4 = (f32[64,2048]{1,0:T(8,128)}, bf16[1024,64]{1,0:T(8,128)(2,1)}) custom-call(s32[2]{0:T(128)} %lens.2, bf16[128,4096]{1,0:T(8,128)(2,1)} %q_ref.5, bf16[128,512]{1,0:T(8,128)(2,1)} %fk_ref.5, bf16[2,2048,512]{2,1,0:T(8,128)(2,1)} %k_hbm.5, bf16[2,2048,512]{2,1,0:T(8,128)(2,1)} %v_hbm.5), custom_call_target="tpu_custom_call" | custom-call | flops 1 | bytes 1 | tf_op jit(solution)/shard_map/cache_attention/pallas_call | solution.py:118
  45.7 0.0 collective-permute-done.1.refs_0_
  45.7 0.0 collective-permute-done.2
  45.7 1.9 %collective-permute-done.3 = bf16[48,1024]{1,0:T(8,128)(2,1)S(1)} collective-permute-done((bf16[48,1024]{1,0:T(8,128)(2,1)S(1)}, bf16[48,1024]{1,0:T(8,128)(2,1)S(1)}, u32[]{:S(2)}, u32[]{:S(2)}) %collective-permute-start.3) | collective-permute-done | bytes 98336 | tf_op jit(solution)/shard_map/ppermute | solution.py:429
  47.6 2.1 %collective-permute-done.4 = bf16[48,1024]{1,0:T(8,128)(2,1)S(1)} collective-permute-done((bf16[48,1024]{1,0:T(8,128)(2,1)S(1)}, bf16[48,1024]{1,0:T(8,128)(2,1)S(1)}, u32[]{:S(2)}, u32[]{:S(2)}) %collective-permute-start.4) | collective-permute-done | bytes 98336 | tf_op jit(solution)/shard_map/ppermute | solution.py:429
  49.7 1.5 %collective-permute-start.6 = (bf16[192,512]{1,0:T(8,128)(2,1)S(1)}, bf16[192,512]{1,0:T(8,128)(2,1)S(1)}, u32[]{:S(2)}, u32[]{:S(2)}) collective-permute-start(bf16[192,512]{1,0:T(8,128)(2,1)S(1)} %collective-permute-done.1.refs_0_), channel_id=1, source_target_pairs={{0,16},{16,0},{1,17},{17,1},{2,18},{18,2},{3,19},{19,3},{4,20},{20... | collective-permute-start | bytes 589832 | tf_op jit(solution)/shard_map/ppermute | solution.py:442
  51.2 0.1 pad_maximum_fusion.maps_mine
  51.3 0.0 copy-start
  51.3 0.0 copy-start.9
  51.3 0.0 copy-start.10
  51.3 6.7 %cache_attention.5 = (f32[64,2048]{1,0:T(8,128)}, bf16[1024,64]{1,0:T(8,128)(2,1)}) custom-call(s32[2]{0:T(128)} %lens.2, bf16[128,4096]{1,0:T(8,128)(2,1)} %q_ref.5, bf16[128,512]{1,0:T(8,128)(2,1)} %fk_ref.5, bf16[2,2048,512]{2,1,0:T(8,128)(2,1)} %k_hbm.5, bf16[2,2048,512]{2,1,0:T(8,128)(2,1)} %v_hbm.5), custom_call_target="tpu_custom_call" | custom-call | flops 1 | bytes 1 | tf_op jit(solution)/shard_map/cache_attention/pallas_call | solution.py:118
  58.1 0.0 collective-permute-done.5.refs_1_
  58.1 0.0 collective-permute-done.6.refs_2_
  58.1 0.7 copy-done.7
  58.7 0.0 all-to-all-done.mine
  58.8 0.0 collective-permute-start.7
  58.8 0.5 collective-permute-start.8
  59.3 0.0 collective-permute-start.9
  59.3 3.3 %collective-permute-done.8.maps_theirs = bf16[4,48,1024]{2,1,0:T(8,128)(2,1)S(1)} collective-permute-done((bf16[4,48,1024]{2,1,0:T(8,128)(2,1)S(1)}, bf16[4,48,1024]{2,1,0:T(8,128)(2,1)S(1)}, u32[]{:S(2)}, u32[]{:S(2)}) %collective-permute-start.8) | collective-permute-done | bytes 393248 | tf_op jit(solution)/shard_map/ppermute | solution.py:451
  62.5 0.0 collective-permute-done.7.theirs
  62.5 0.0 copy-done
  62.6 2.5 %near_products.1.near = f32[512,512]{1,0:T(8,128)S(1)} custom-call(s32[16]{0:T(128)S(1)} %copy-done.9, s32[16]{0:T(128)S(1)} %copy-done.10, bf16[4,176,1024]{2,1,0:T(8,128)(2,1)S(1)} %all-to-all-done.mine, bf16[4,176,1024]{2,1,0:T(8,128)(2,1)S(1)} %collective-permute-done.7.theirs, bf16[4,48,1024]{2,1,0:T(8,128)(2,1)S(1)} %pad_maximum_fusion.maps_mine, ...), custom_call_target="tpu_custom_call" | custom-call | flops 1 | bytes 1 | tf_op jit(solution)/shard_map/near_products/pallas_call | solution.py:294
  65.0 0.0 copy-start.1
  65.1 3.9 %collective-permute-done.9.refs_3_ = bf16[320,512]{1,0:T(8,128)(2,1)S(1)} collective-permute-done((bf16[320,512]{1,0:T(8,128)(2,1)S(1)}, bf16[320,512]{1,0:T(8,128)(2,1)S(1)}, u32[]{:S(2)}, u32[]{:S(2)}) %collective-permute-start.9) | collective-permute-done | bytes 327712 | tf_op jit(solution)/shard_map/ppermute | solution.py:449
  69.0 0.0 copy-done.8
  69.0 0.8 %far_products.1 = (bf16[128,512]{1,0:T(8,128)(2,1)S(1)}, bf16[128,512]{1,0:T(8,128)(2,1)S(1)}, bf16[128,512]{1,0:T(8,128)(2,1)S(1)}, bf16[128,512]{1,0:T(8,128)(2,1)S(1)}) custom-call(bf16[4,176,1024]{2,1,0:T(8,128)(2,1)S(1)} %all-to-all-done.mine, bf16[4,176,1024]{2,1,0:T(8,128)(2,1)S(1)} %collective-permute-done.7.theirs, ...), custom_call_target="tpu_custom_call" | custom-call | flops 1 | bytes 1 | tf_op jit(solution)/shard_map/far_products/pallas_call | solution.py:341
  69.8 1.6 %collective-permute-start.10 = (bf16[128,512]{1,0:T(8,128)(2,1)S(1)}, bf16[128,512]{1,0:T(8,128)(2,1)S(1)}, u32[]{:S(2)}, u32[]{:S(2)}) collective-permute-start(bf16[128,512]{1,0:T(8,128)(2,1)S(1)} %get-tuple-element.59), channel_id=1, source_target_pairs={{0,2},{2,0},{4,6},{6,4},{1,3},{3,1},{5,7},{7,5},{8,10},{10,8},{12,... | collective-permute-start | bytes 393224 | tf_op jit(solution)/shard_map/ppermute | solution.py:429
  71.4 0.0 collective-permute-start.11
  71.4 1.9 %collective-permute-start.12 = (bf16[128,512]{1,0:T(8,128)(2,1)S(1)}, bf16[128,512]{1,0:T(8,128)(2,1)S(1)}, u32[]{:S(2)}, u32[]{:S(2)}) collective-permute-start(bf16[128,512]{1,0:T(8,128)(2,1)S(1)} %get-tuple-element.61), channel_id=1, source_target_pairs={{0,6},{2,4},{4,2},{6,0},{1,7},{3,5},{5,3},{7,1},{8,14},{10,12},{12... | collective-permute-start | bytes 393224 | tf_op jit(solution)/shard_map/ppermute | solution.py:429
  73.3 2.7 %collective-permute-done.10.refs_7_ = bf16[128,512]{1,0:T(8,128)(2,1)S(1)} collective-permute-done((bf16[128,512]{1,0:T(8,128)(2,1)S(1)}, bf16[128,512]{1,0:T(8,128)(2,1)S(1)}, u32[]{:S(2)}, u32[]{:S(2)}) %collective-permute-start.10) | collective-permute-done | bytes 131104 | tf_op jit(solution)/shard_map/ppermute | solution.py:429
  76.1 1.1 %collective-permute-done.11.refs_8_ = bf16[128,512]{1,0:T(8,128)(2,1)S(1)} collective-permute-done((bf16[128,512]{1,0:T(8,128)(2,1)S(1)}, bf16[128,512]{1,0:T(8,128)(2,1)S(1)}, u32[]{:S(2)}, u32[]{:S(2)}) %collective-permute-start.11) | collective-permute-done | bytes 131104 | tf_op jit(solution)/shard_map/ppermute | solution.py:429
  77.1 1.3 %collective-permute-done.12.refs_9_ = bf16[128,512]{1,0:T(8,128)(2,1)S(1)} collective-permute-done((bf16[128,512]{1,0:T(8,128)(2,1)S(1)}, bf16[128,512]{1,0:T(8,128)(2,1)S(1)}, u32[]{:S(2)}, u32[]{:S(2)}) %collective-permute-start.12) | collective-permute-done | bytes 131104 | tf_op jit(solution)/shard_map/ppermute | solution.py:429
  78.5 0.0 copy-done.2
  78.5 1.4 %finish_attention.1 = (bf16[128,4096]{1,0:T(8,128)(2,1)}, bf16[128,512]{1,0:T(8,128)(2,1)}) custom-call(f32[64,4096]{1,0:T(8,128)S(1)} %copy-done.1, f32[64,2048]{1,0:T(8,128)S(1)} %copy-done.3, f32[64,2048]{1,0:T(8,128)S(1)} %copy-done.4, bf16[2048,64]{1,0:T(8,128)(2,1)S(1)} %copy-done.2, bf16[1024,64]{1,0:T(8,128)(2,1)S(1)} %copy-done.5, ...), custom_call_target="tpu_custom_call" | custom-call | flops 1 | bytes 1 | tf_op jit(solution)/shard_map/finish_attention/pallas_call | solution.py:383
  (15 shorter events, 0.1 us)
Async XLA Ops:
  3.8 5.4 %copy-start.11 = (bf16[32,4608]{1,0:T(8,128)(2,1)S(1)}, bf16[32,4608]{1,0:T(8,128)(2,1)}, u32[]{:S(2)}) copy-start(bf16[32,4608]{1,0:T(8,128)(2,1)} %get-tuple-element.35) | copy-start | bytes 884740
  3.8 8.0 %copy-start.12 = (bf16[192,512]{1,0:T(8,128)(2,1)S(1)}, bf16[192,512]{1,0:T(8,128)(2,1)}, u32[]{:S(2)}) copy-start(bf16[192,512]{1,0:T(8,128)(2,1)} %get-tuple-element.41) | copy-start | bytes 589828
  3.8 54.9 %all-to-all-start = ((bf16[4,176,1024]{2,1,0:T(8,128)(2,1)}), bf16[4,176,1024]{2,1,0:T(8,128)(2,1)S(1)}, u32[]{:S(2)}, u32[]{:S(2)}) async-start(bf16[4,176,1024]{2,1,0:T(8,128)(2,1)} %get-tuple-element.32), calls=%async_computation | async-start | bytes 2883584 | tf_op jit(solution)/shard_map/all_to_all | solution.py:432
  9.2 23.2 %collective-permute-start = (bf16[32,4608]{1,0:T(8,128)(2,1)S(1)}, bf16[32,4608]{1,0:T(8,128)(2,1)S(1)}, u32[]{:S(2)}, u32[]{:S(2)}) collective-permute-start(bf16[32,4608]{1,0:T(8,128)(2,1)S(1)} %copy-done.11), channel_id=1, source_target_pairs={{0,8},{8,0},{1,9},{9,1},{2,10},{10,2},{3,11},{11,3},{4,12},{12,4},... | collective-permute-start | bytes 884744 | tf_op jit(solution)/shard_map/ppermute | solution.py:433
  11.8 33.9 %collective-permute-start.1 = (bf16[192,512]{1,0:T(8,128)(2,1)S(1)}, bf16[192,512]{1,0:T(8,128)(2,1)S(1)}, u32[]{:S(2)}, u32[]{:S(2)}) collective-permute-start(bf16[192,512]{1,0:T(8,128)(2,1)S(1)} %copy-done.12), channel_id=1, source_target_pairs={{0,8},{8,0},{1,9},{9,1},{2,10},{10,2},{3,11},{11,3},{4,12},{12,4},... | collective-permute-start | bytes 589832 | tf_op jit(solution)/shard_map/ppermute | solution.py:434
  12.1 45.9 %collective-permute-start.5 = (bf16[320,512]{1,0:T(8,128)(2,1)}, bf16[320,512]{1,0:T(8,128)(2,1)S(1)}, u32[]{:S(2)}, u32[]{:S(2)}) collective-permute-start(bf16[320,512]{1,0:T(8,128)(2,1)} %get-tuple-element.53), channel_id=1, source_target_pairs={{0,8},{8,0},{1,9},{9,1},{2,10},{10,2},{3,11},{11,3},{4,12},{12,4},... | collective-permute-start | bytes 983048 | tf_op jit(solution)/shard_map/ppermute | solution.py:434
  32.4 13.3 %collective-permute-start.2 = (bf16[48,1024]{1,0:T(8,128)(2,1)S(1)}, bf16[48,1024]{1,0:T(8,128)(2,1)S(1)}, u32[]{:S(2)}, u32[]{:S(2)}) collective-permute-start(bf16[48,1024]{1,0:T(8,128)(2,1)S(1)} %get-tuple-element.42), channel_id=1, source_target_pairs={{0,2},{2,0},{4,6},{6,4},{1,3},{3,1},{5,7},{7,5},{8,10},{10,8},{12,... | collective-permute-start | bytes 294920 | tf_op jit(solution)/shard_map/ppermute | solution.py:429
  34.5 13.1 %collective-permute-start.3 = (bf16[48,1024]{1,0:T(8,128)(2,1)S(1)}, bf16[48,1024]{1,0:T(8,128)(2,1)S(1)}, u32[]{:S(2)}, u32[]{:S(2)}) collective-permute-start(bf16[48,1024]{1,0:T(8,128)(2,1)S(1)} %get-tuple-element.43), channel_id=1, source_target_pairs={{0,4},{2,6},{4,0},{6,2},{1,5},{3,7},{5,1},{7,3},{8,12},{10,14},{12... | collective-permute-start | bytes 294920 | tf_op jit(solution)/shard_map/ppermute | solution.py:429
  39.1 10.7 %collective-permute-start.4 = (bf16[48,1024]{1,0:T(8,128)(2,1)S(1)}, bf16[48,1024]{1,0:T(8,128)(2,1)S(1)}, u32[]{:S(2)}, u32[]{:S(2)}) collective-permute-start(bf16[48,1024]{1,0:T(8,128)(2,1)S(1)} %get-tuple-element.44), channel_id=1, source_target_pairs={{0,6},{2,4},{4,2},{6,0},{1,7},{3,5},{5,3},{7,1},{8,14},{10,12},{12... | collective-permute-start | bytes 294920 | tf_op jit(solution)/shard_map/ppermute | solution.py:429
  49.7 8.3 %collective-permute-start.6 = (bf16[192,512]{1,0:T(8,128)(2,1)S(1)}, bf16[192,512]{1,0:T(8,128)(2,1)S(1)}, u32[]{:S(2)}, u32[]{:S(2)}) collective-permute-start(bf16[192,512]{1,0:T(8,128)(2,1)S(1)} %collective-permute-done.1.refs_0_), channel_id=1, source_target_pairs={{0,16},{16,0},{1,17},{17,1},{2,18},{18,2},{3,19},{19,3},{4,20},{20... | collective-permute-start | bytes 589832 | tf_op jit(solution)/shard_map/ppermute | solution.py:442
  51.3 11.3 %copy-start = (bf16[1024,512]{1,0:T(8,128)(2,1)S(1)}, bf16[1024,512]{1,0:T(8,128)(2,1)}, u32[]{:S(2)}) copy-start(bf16[1024,512]{1,0:T(8,128)(2,1)} %own_ref.1) | copy-start | bytes 3145732
  51.3 11.2 %copy-start.9 = (s32[16]{0:T(128)S(1)}, s32[16]{0:T(128)}, u32[]{:S(2)}) copy-start(s32[16]{0:T(128)} %position.1) | copy-start | bytes 196
  51.3 11.2 %copy-start.10 = (s32[16]{0:T(128)S(1)}, s32[16]{0:T(128)}, u32[]{:S(2)}) copy-start(s32[16]{0:T(128)} %adapter.1) | copy-start | bytes 196
  58.1 0.7 copy-start.7
  58.8 10.2 %copy-start.8 = (bf16[192,512]{1,0:T(8,128)(2,1)S(1)}, bf16[192,512]{1,0:T(8,128)(2,1)}, u32[]{:S(2)}) copy-start(bf16[192,512]{1,0:T(8,128)(2,1)} %copy-done.7) | copy-start | bytes 589828
  58.8 3.8 %collective-permute-start.7 = (bf16[4,176,1024]{2,1,0:T(8,128)(2,1)S(1)}, bf16[4,176,1024]{2,1,0:T(8,128)(2,1)S(1)}, u32[]{:S(2)}, u32[]{:S(2)}) collective-permute-start(bf16[4,176,1024]{2,1,0:T(8,128)(2,1)S(1)} %all-to-all-done.mine), channel_id=1, source_target_pairs={{0,1},{1,0},{2,3},{3,2},{4,5},{5,4},{6,7},{7,6},{8,9},{9,8},{10,11... | collective-permute-start | bytes 4325384 | tf_op jit(solution)/shard_map/ppermute | solution.py:450
  58.8 3.8 %collective-permute-start.8 = (bf16[4,48,1024]{2,1,0:T(8,128)(2,1)S(1)}, bf16[4,48,1024]{2,1,0:T(8,128)(2,1)S(1)}, u32[]{:S(2)}, u32[]{:S(2)}) collective-permute-start(bf16[4,48,1024]{2,1,0:T(8,128)(2,1)S(1)} %pad_maximum_fusion.maps_mine), channel_id=1, source_target_pairs={{0,1},{1,0},{2,3},{3,2},{4,5},{5,4},{6,7},{7,6},{8,9},{9,8},{10,11... | collective-permute-start | bytes 1179656 | tf_op jit(solution)/shard_map/ppermute | solution.py:451
  59.3 9.7 %collective-permute-start.9 = (bf16[320,512]{1,0:T(8,128)(2,1)S(1)}, bf16[320,512]{1,0:T(8,128)(2,1)S(1)}, u32[]{:S(2)}, u32[]{:S(2)}) collective-permute-start(bf16[320,512]{1,0:T(8,128)(2,1)S(1)} %collective-permute-done.5.refs_1_), channel_id=1, source_target_pairs={{0,16},{16,0},{1,17},{17,1},{2,18},{18,2},{3,19},{19,3},{4,20},{20... | collective-permute-start | bytes 983048 | tf_op jit(solution)/shard_map/ppermute | solution.py:449
  65.0 13.5 %copy-start.1 = (f32[64,4096]{1,0:T(8,128)S(1)}, f32[64,4096]{1,0:T(8,128)}, u32[]{:S(2)}) copy-start(f32[64,4096]{1,0:T(8,128)} %get-tuple-element.34.refs_0_) | copy-start | bytes 3145732
  65.0 13.4 %copy-start.2 = (bf16[2048,64]{1,0:T(8,128)(2,1)S(1)}, bf16[2048,64]{1,0:T(8,128)(2,1)}, u32[]{:S(2)}) copy-start(bf16[2048,64]{1,0:T(8,128)(2,1)} %get-tuple-element.36.refs_3_) | copy-start | bytes 786436
  65.0 13.4 %copy-start.3 = (f32[64,2048]{1,0:T(8,128)S(1)}, f32[64,2048]{1,0:T(8,128)}, u32[]{:S(2)}) copy-start(f32[64,2048]{1,0:T(8,128)} %get-tuple-element.40.refs_1_) | copy-start | bytes 1572868
  65.1 13.4 %copy-start.4 = (f32[64,2048]{1,0:T(8,128)S(1)}, f32[64,2048]{1,0:T(8,128)}, u32[]{:S(2)}) copy-start(f32[64,2048]{1,0:T(8,128)} %get-tuple-element.51.refs_2_) | copy-start | bytes 1572868
  65.1 13.4 %copy-start.5 = (bf16[1024,64]{1,0:T(8,128)(2,1)S(1)}, bf16[1024,64]{1,0:T(8,128)(2,1)}, u32[]{:S(2)}) copy-start(bf16[1024,64]{1,0:T(8,128)(2,1)} %get-tuple-element.45.refs_4_) | copy-start | bytes 393220
  65.1 13.4 %copy-start.6 = (bf16[1024,64]{1,0:T(8,128)(2,1)S(1)}, bf16[1024,64]{1,0:T(8,128)(2,1)}, u32[]{:S(2)}) copy-start(bf16[1024,64]{1,0:T(8,128)(2,1)} %get-tuple-element.52.refs_5_) | copy-start | bytes 393220
  69.8 6.3 %collective-permute-start.10 = (bf16[128,512]{1,0:T(8,128)(2,1)S(1)}, bf16[128,512]{1,0:T(8,128)(2,1)S(1)}, u32[]{:S(2)}, u32[]{:S(2)}) collective-permute-start(bf16[128,512]{1,0:T(8,128)(2,1)S(1)} %get-tuple-element.59), channel_id=1, source_target_pairs={{0,2},{2,0},{4,6},{6,4},{1,3},{3,1},{5,7},{7,5},{8,10},{10,8},{12,... | collective-permute-start | bytes 393224 | tf_op jit(solution)/shard_map/ppermute | solution.py:429
  71.4 5.8 %collective-permute-start.11 = (bf16[128,512]{1,0:T(8,128)(2,1)S(1)}, bf16[128,512]{1,0:T(8,128)(2,1)S(1)}, u32[]{:S(2)}, u32[]{:S(2)}) collective-permute-start(bf16[128,512]{1,0:T(8,128)(2,1)S(1)} %get-tuple-element.60), channel_id=1, source_target_pairs={{0,4},{2,6},{4,0},{6,2},{1,5},{3,7},{5,1},{7,3},{8,12},{10,14},{12... | collective-permute-start | bytes 393224 | tf_op jit(solution)/shard_map/ppermute | solution.py:429
  71.4 7.1 %collective-permute-start.12 = (bf16[128,512]{1,0:T(8,128)(2,1)S(1)}, bf16[128,512]{1,0:T(8,128)(2,1)S(1)}, u32[]{:S(2)}, u32[]{:S(2)}) collective-permute-start(bf16[128,512]{1,0:T(8,128)(2,1)S(1)} %get-tuple-element.61), channel_id=1, source_target_pairs={{0,6},{2,4},{4,2},{6,0},{1,7},{3,5},{5,3},{7,1},{8,14},{10,12},{12... | collective-permute-start | bytes 393224 | tf_op jit(solution)/shard_map/ppermute | solution.py:429

commit v8 on v7

--- a/solution.py
+++ b/solution.py
@@ -141,7 +141,38 @@
     )(lengths, queries, fresh_keys, keys, values)
 
 
-def run_copies(copies, sems):
+def pack_kernel(x_hbm, d_hbm, u_hbm, w_hbm, tokens_out, *refs):
+    quads = tokens_out.shape[0]
+    maps_out, rows, sems = refs[:quads], refs[quads:-1], refs[-1]
+    part, core, quad = lax.axis_index("parts") % 2, lax.axis_index("tensor"), lax.axis_index("quad")
+    tokens, features = x_hbm.shape
+    width, cols = w_hbm.shape
+    ranks = d_hbm.shape[0]
+    step = maps_out[0].shape[1]
+    mine = pl.ds(pl.multiple_of(part * RANK, RANK), RANK)
+    copies = []
+    for q, out in enumerate(maps_out):
+        begin = core * features + (quad ^ q) * width
+        for i, first in enumerate(range(0, width, step)):
+            here = pl.ds(pl.multiple_of(begin + first, step), step)
+            copies.append((d_hbm.at[mine, here], out.at[i * RANK : (i + 1) * RANK, :]))
+        for i, first in enumerate(range(0, cols, step)):
+            row = width // step * RANK + i * RANK
+            copies.append((u_hbm.at[mine, first : first + step], out.at[row : row + RANK, :]))
+    begin = part * (width // 2)
+    for piece in rows:
+        size = piece.shape[0]
+        copies.append((w_hbm.at[pl.ds(pl.multiple_of(begin, RANK), size), :], piece))
+        begin = begin + size
+    for j in range(quads):
+        out = tokens_out.at[j]
+        copies.append((x_hbm.at[:, j * width : (j + 1) * width], out.at[:tokens, :]))
+        here = pl.ds(pl.multiple_of(core * features + j * width, width), width)
+        copies.append((d_hbm.at[:, here], out.at[tokens : tokens + ranks, :]))
+        for slot, first, row, col in up_places(cols, width):
+            row += tokens + ranks
+            up = u_hbm.at[slot * RANK : (slot + 1) * RANK, first : first + step]
+            copies.append((up, out.at[row : row + RANK, col : col + step]))
     copies = [pltpu.make_async_copy(src, dst, sems.at[i]) for i, (src, dst) in enumerate(copies)]
     for copy in copies:
         copy.start()
@@ -158,54 +189,23 @@
     ]
 
 
-def pack_kernel(x_hbm, d_hbm, u_hbm, w_hbm, out, maps, *refs):
-    rows, sems = refs[:-1], refs[-1]
-    part, core = lax.axis_index("parts") % 2, lax.axis_index("tensor")
-    quads, _, width = out.shape
-    tokens, features = x_hbm.shape
-    ranks, cols = u_hbm.shape
-    step = min(cols, width)
-    begin = part * (w_hbm.shape[0] // 2)
-    copies = []
-    for piece in rows:
-        size = piece.shape[0]
-        copies.append((w_hbm.at[pl.ds(pl.multiple_of(begin, RANK), size), :], piece))
-        begin = begin + size
-    copies.append((d_hbm.at[:, pl.ds(pl.multiple_of(core * features, features), features)], maps.at[:, :features]))
-    copies.append((u_hbm, maps.at[:, features:]))
-    for j in range(quads):
-        first = pl.multiple_of(core * features + j * width, width)
-        copies.append((x_hbm.at[:, j * width : (j + 1) * width], out.at[j, :tokens, :]))
-        copies.append((d_hbm.at[:, pl.ds(first, width)], out.at[j, tokens : tokens + ranks, :]))
-        for slot, first, row, col in up_places(cols, width):
-            row += tokens + ranks
-            copies.append(
-                (
-                    u_hbm.at[slot * RANK : (slot + 1) * RANK, first : first + step],
-                    out.at[j, row : row + RANK, col : col + step],
-                )
-            )
-    run_copies(copies, sems)
-
-
 def pack(tokens, downs, ups, weights, quads):
     vmem = pl.BlockSpec(memory_space=pltpu.VMEM)
     hbm = pl.BlockSpec(memory_space=pltpu.HBM)
     ranks, cols = ups.shape
     width = weights.shape[0]
-    rows = tokens.shape[0] + ranks + RANK * (2 * cols // width)
-    count = 4 + quads * (2 + len(up_places(cols, width)))
-    first = width // 2 * 3 // 8
-    pieces = [jax.ShapeDtypeStruct((size, cols), weights.dtype) for size in (first, width // 2 - first)]
+    step = min(cols, width)
+    kind = tokens.dtype
+    pieces = (width + cols) // step
+    first = width // 4
+    sizes = [(quads, tokens.shape[0] + ranks + RANK * (2 * cols // width), width)]
+    sizes += [(RANK * pieces, step)] * quads + [(first, cols), (width // 2 - first, cols)]
+    count = quads * (pieces + 2 + len(up_places(cols, width))) + 2
     return pl.pallas_call(
         pack_kernel,
         in_specs=[hbm] * 4,
-        out_specs=[vmem] * 4,
-        out_shape=[
-            jax.ShapeDtypeStruct((quads, rows, width), tokens.dtype),
-            jax.ShapeDtypeStruct((ranks, tokens.shape[1] + cols), downs.dtype),
-        ]
-        + pieces,
+        out_specs=[vmem] * len(sizes),
+        out_shape=[jax.ShapeDtypeStruct(size, kind) for size in sizes],
         scratch_shapes=[pltpu.SemaphoreType.DMA((count,))],
         compiler_params=pltpu.CompilerParams(vmem_limit_bytes=57 * MIB),
         cost_estimate=FREE,
@@ -213,66 +213,48 @@
     )(tokens, downs, ups, weights)
 
 
-def maps_kernel(here, *outs):
-    quad = lax.axis_index("quad")
-    width = outs[0].shape[1]
-    ranks = here.shape[0]
-    features = len(outs) * width
-    cols = here.shape[1] - features
-    step = min(cols, width)
-    for q, out in enumerate(outs):
-        out[:ranks, :] = here[:, pl.ds(pl.multiple_of((quad ^ q) * width, width), width)]
-        for slot, first, row, col in up_places(cols, width):
-            up = here[slot * RANK : (slot + 1) * RANK, features + first : features + first + step]
-            out[ranks + row : ranks + row + RANK, col : col + step] = up
-
-
-def maps_pack(here, width, quads):
-    vmem = pl.BlockSpec(memory_space=pltpu.VMEM)
-    cols = here.shape[1] - quads * width
-    maps = jax.ShapeDtypeStruct((RANK * (2 + 2 * cols // width), width), here.dtype)
-    return pl.pallas_call(
-        maps_kernel,
-        in_specs=[vmem],
-        out_specs=[vmem] * quads,
-        out_shape=[maps] * quads,
-        compiler_params=pltpu.CompilerParams(vmem_limit_bytes=4 * MIB),
-        cost_estimate=FREE,
-        name="maps_pack",
-    )(here)
-
-
-def near_kernel(tokens, position, adapter, mine, theirs, maps_mine, maps_theirs, own_ref, out, ds, us):
-    core, wing, quad = lax.axis_index("tensor"), lax.axis_index("wing"), lax.axis_index("quad")
-    quads, _, width = mine.shape
+def near_kernel(tokens, quads, position, adapter, own_ref, *refs):
+    maps_mine, maps_theirs, refs = refs[:2], refs[2:4], refs[4:]
+    mine, theirs, out, ds, us = refs
+    part, core = lax.axis_index("parts") % 2, lax.axis_index("tensor")
+    wing, quad = lax.axis_index("wing"), lax.axis_index("quad")
+    width = mine.shape[2]
     cols = own_ref.shape[1]
     ranks = 2 * RANK
     step = min(cols, width)
-    for j in range(quads):
-        for side, here, there, base, index in (
-            (0, mine.at[j], theirs.at[j], tokens, j),
-            (1, maps_mine.at[j], maps_theirs.at[j], 0, quad ^ j),
-        ):
-            first_row = (side * quads + index) * ranks
-            rows = pl.ds(pl.multiple_of(first_row, ranks), ranks)
-            ds[0, rows, :] = here[base : base + ranks, :]
-            ds[1, rows, :] = there[base : base + ranks, :]
-            for slot, first, row, col in up_places(cols, width):
-                row += base + ranks
-                place = pl.ds(pl.multiple_of(first_row + slot * RANK, RANK), RANK)
-                us[place, first : first + step] = here[row : row + RANK, col : col + step]
+    for q in range(quads):
+        rows = slice(q * ranks, (q + 1) * ranks)
+        ds[0, rows, :] = mine[q, tokens : tokens + ranks, :]
+        ds[1, rows, :] = theirs[q, tokens : tokens + ranks, :]
+        for slot, first, row, col in up_places(cols, width):
+            row += tokens + ranks
+            place = q * ranks + slot * RANK
+            us[place : place + RANK, first : first + step] = mine[q, row : row + RANK, col : col + step]
+        for side in range(2):
+            place = (quads + q) * ranks + side * RANK
+            for i, first in enumerate(range(0, width, step)):
+                row = i * RANK
+                ds[0, place : place + RANK, first : first + step] = maps_mine[side][q, row : row + RANK, :]
+                ds[1, place : place + RANK, first : first + step] = maps_theirs[side][q, row : row + RANK, :]
+            for i, first in enumerate(range(0, cols, step)):
+                row = (width // step + i) * RANK
+                us[place : place + RANK, first : first + step] = maps_mine[side][q, row : row + RANK, :]
 
     x_mine = mine[:, :tokens, :].reshape(quads * tokens, width)
     x_theirs = theirs[:, :tokens, :].reshape(quads * tokens, width)
     shrink = dot_last(x_mine, ds[0]) + dot_last(x_theirs, ds[1])
-    slots = us.shape[0] // RANK
-    which = lax.broadcasted_iota(jnp.int32, (SPAN, slots * RANK), 1) // RANK + wing * (slots // 2)
-    which = jnp.where(which >= slots, which - slots, which)
-    spans = quads * tokens // SPAN
+    place = lax.broadcasted_iota(jnp.int32, (SPAN, us.shape[0]), 1)
+    far = (place >= quads * ranks).astype(jnp.int32)
+    index = place - far * (quads * ranks)
+    group = (wing ^ far) * quads + ((far * quad) ^ (index >> 5))
+    which = 2 * group + (((index >> 4) & 1) ^ (far * part))
+    spans = tokens // SPAN
     masked = []
-    for i in range(spans):
-        slot = position[adapter[wing * spans + i]]
-        masked.append(jnp.where(which == slot, shrink[i * SPAN : (i + 1) * SPAN, :], 0.0))
+    for q in range(quads):
+        for i in range(spans):
+            slot = position[adapter[(wing * quads + q) * spans + i]]
+            row = (q * spans + i) * SPAN
+            masked.append(jnp.where(which == slot, shrink[row : row + SPAN, :], 0.0))
     shrink = (jnp.concatenate(masked, axis=0) * ADAPTER_SCALE).astype(jnp.bfloat16)
     out[...] = dot(shrink, us[...])
 
@@ -292,8 +274,8 @@
     vmem = pl.BlockSpec(memory_space=pltpu.VMEM)
     smem = pl.BlockSpec(memory_space=pltpu.SMEM)
     return pl.pallas_call(
-        functools.partial(near_kernel, tokens),
-        in_specs=[smem, smem] + [vmem] * 5,
+        functools.partial(near_kernel, tokens, quads),
+        in_specs=[smem, smem] + [vmem] * 7,
         out_specs=vmem,
         out_shape=jax.ShapeDtypeStruct((quads * tokens, cols), jnp.float32),
         scratch_shapes=[
@@ -303,24 +285,24 @@
         compiler_params=pltpu.CompilerParams(vmem_limit_bytes=48 * MIB if quads > 4 else 24 * MIB),
         cost_estimate=FREE,
         name="near_products",
-    )(position, adapter, mine, theirs, maps_mine, maps_theirs, own)
-
-
-def far_kernel(tokens, mine, theirs, near, *refs):
-    quads, _, width = mine.shape
-    outs, (whole, total) = refs[-2 - quads : -2], refs[-2:]
-    weights = refs[: -2 - quads]
+    )(position, adapter, own, *maps_mine, *maps_theirs, mine, theirs)
+
+
+def far_kernel(tokens, quads, near, *refs):
+    weights, (mine, theirs) = refs[:4], refs[4:6]
+    outs, (whole, total) = refs[6:-2], refs[-2:]
+    quad = lax.axis_index("quad")
     part, core, wing = lax.axis_index("parts") % 2, lax.axis_index("tensor"), lax.axis_index("wing")
-    quad = lax.axis_index("quad")
     for side in range(2):
-        begin = (part if side == 0 else 1 - part) * (width // 2)
+        begin = (part if side == 0 else 1 - part) * (whole.shape[0] // 2)
         for piece in weights[2 * side : 2 * side + 2]:
             whole[pl.ds(pl.multiple_of(begin, RANK), piece.shape[0]), :] = piece[...]
             begin = begin + piece.shape[0]
 
-    def store(x):
-        product = dot(x[:, :tokens, :].reshape(quads * tokens, width), whole[...])
-        total[...] = (near[...] + product).astype(jnp.bfloat16).reshape(total.shape)
+    def store(blocks):
+        x = blocks[:, :tokens, :].reshape(near.shape[0], -1)
+        product = (near[...] + dot(x, whole[...])).astype(jnp.bfloat16)
+        total[...] = product.reshape(total.shape)
 
     @pl.when(core == wing)
     def _():
@@ -330,8 +312,8 @@
     def _():
         store(mine)
 
-    for q in range(quads):
-        outs[q][...] = total[quad ^ q]
+    for q, out in enumerate(outs):
+        out[...] = total[quad ^ q]
 
 
 def far_products(mine, theirs, near, weights, tokens):
@@ -339,7 +321,7 @@
     cols = near.shape[1]
     vmem = pl.BlockSpec(memory_space=pltpu.VMEM)
     return pl.pallas_call(
-        functools.partial(far_kernel, tokens),
+        functools.partial(far_kernel, tokens, quads),
         in_specs=[vmem] * (3 + len(weights)),
         out_specs=[vmem] * quads,
         out_shape=[jax.ShapeDtypeStruct((tokens, cols), jnp.bfloat16)] * quads,
@@ -350,7 +332,7 @@
         compiler_params=pltpu.CompilerParams(vmem_limit_bytes=48 * MIB if quads > 4 else 16 * MIB),
         cost_estimate=FREE,
         name="far_products",
-    )(mine, theirs, near, *weights)
+    )(near, *weights, mine, theirs)
 
 
 def finish_kernel(places, *refs):
@@ -415,7 +397,7 @@
 
     kv_heads = cols // HD
     kv_heads = cols // HD
-    pieces = [(0, 0, kv_heads), (1, 0, kv_heads // 2), (1, kv_heads // 2, kv_heads - kv_heads // 2)]
+    pieces = [(0, 0, kv_heads), (1, 0, kv_heads)]
 
     def attention(piece, lengths):
         return cache_attention(
@@ -428,33 +410,34 @@
     def to_quad(value, q):
         return lax.ppermute(value, "quad", [(j, j ^ q) for j in range(quads)])
 
-    message, maps, *rows = pack(normed_inputs, downs, ups, value_matrix, quads)
+    def to_other_wing(value, q):
+        pairs = [(w * quads + j, (1 - w) * quads + (j ^ q)) for w in range(2) for j in range(quads)]
+        return lax.ppermute(value, ("wing", "quad"), pairs)
+
+    message, *maps, early, late = pack(normed_inputs, downs, ups, value_matrix, quads)
     mine = lax.all_to_all(message, "quad", 0, 0)
-    maps = lax.ppermute(maps, "wing", SWAP)
-    rows = [lax.ppermute(piece, "wing", SWAP) for piece in rows]
+    maps = [to_other_wing(each, q) for q, each in enumerate(maps)]
+    early = lax.ppermute(early, "wing", SWAP)
 
     attn = [attention(0, after(cache_length, message))]
-    passed = maps_pack(after(maps, attn[0][1]), width, quads)
-    passed_on = [to_quad(passed[q], q) for q in range(1, quads)]
-
-    attn.append(attention(1, after(cache_length, passed[0])))
-    rows[0], *passed_on = lax.optimization_barrier((rows[0], *passed_on, attn[1][1]))[:-1]
-    rows_other = [lax.ppermute(rows[0], "parts", parts_swap)]
-    maps_mine = jnp.stack([passed[0]] + passed_on)
-
-    attn.append(attention(2, after(cache_length, rows[0], maps_mine)))
-    rows[1], rows_other[0], mine, maps_mine = lax.optimization_barrier(
-        (rows[1], rows_other[0], mine, maps_mine, attn[2][1])
-    )[:-1]
-    rows_other.append(lax.ppermute(rows[1], "parts", parts_swap))
+    attn.append(attention(1, after(cache_length, attn[0][1])))
+    early, *maps = lax.optimization_barrier((early, *maps, attn[1][1]))[:-1]
+    maps = jnp.stack(maps)
+    mine = after(mine, early)
+
+    late = lax.ppermute(after(late, early), "wing", SWAP)
+    early_other = lax.ppermute(early, "parts", parts_swap)
+    late_other = lax.ppermute(late, "parts", parts_swap)
+    maps_other = lax.ppermute(maps, "parts", parts_swap)
+    maps_mine = (maps, maps_other)
+    maps_theirs = [lax.ppermute(each, "tensor", SWAP) for each in maps_mine]
     theirs = lax.ppermute(mine, "tensor", SWAP)
-    maps_theirs = lax.ppermute(maps_mine, "tensor", SWAP)
 
     tokens, q_width = queries.shape
     near = near_products(
         mine, theirs, maps_mine, maps_theirs, value_matrix, adapter_position, span_adapter_index, tokens
     )
-    products = far_products(mine, theirs, near, (*rows, *rows_other), tokens)
+    products = far_products(mine, theirs, near, (early, late, early_other, late_other), tokens)
     parts = [products[0]] + [to_quad(products[q], q) for q in range(1, quads)]
     mixed, fresh_probs = zip(*attn)
     attended, incoming_values = finish([piece[:2] for piece in pieces], mixed, fresh_probs, parts, q_width)

time: 80.3 us -> 74 us (0.922)
  Pallas kernels: 29 us -> 23.5 us
  waiting for transfers between devices: 26.2 us -> 27.1 us
    ppermute x6 -> x3, starting transfers between devices: 10.2 us -> 3.55 us  [to_quad(): return lax.ppermute(value, 'quad', [(j, j ^ q) for j in range(quads)])]
    ppermute x6 -> x11, starting transfers between devices: 7.51 us -> 13.4 us  [the longest x4 7.65 us: to_other_wing(): return lax.ppermute(value, ('wing', 'quad'), pairs)]
    pallas_call x3 -> x2, Pallas kernels: 21.1 us -> 15.6 us  [cache_attention(): pl.pallas_call(functools.partial(cache_kernel, span, first_head, kv_heads...]
    ppermute x6 -> x11, waiting for transfers between devices: 17 us -> 22.2 us  [the longest x1 13 us: on_device(): late = lax.ppermute(after(late, early), 'wing', SWAP)]
    ppermute x6 -> x3, waiting for transfers between devices: 9.15 us -> 4.89 us  [to_quad(): return lax.ppermute(value, 'quad', [(j, j ^ q) for j in range(quads)])]
    pallas_call x4 -> x3, Pallas kernels: 6.47 us -> 6.43 us  [the longest x1 3.21 us: pack(): pl.pallas_call(pack_kernel, in_specs=[hbm] * 4, out_specs=[vmem] * len(si...]
  transfers between devices with their start and end apart: 14 -> 16, of which waited for: 8 -> 8; matrix products, arithmetic and copies ran while one was open for 0% -> 0% of each run, Pallas kernels for 30% -> 24%
where the time goes in v8:
time: 74 us; the launch traced here: 73.9 us
  waiting for transfers between devices  27.1 us (37%)
  Pallas kernels  23.5 us (32%)
  starting transfers between devices  22.4 us (30%)
  between operations  0.84 us (1%)
    pallas_call x2, Pallas kernels, cache_attention(): pl.pallas_call(functools.partial(cache_kernel, span, first_head, kv_heads...  15.6 us
    ppermute x1, waiting for transfers between devices, on_device(): late = lax.ppermute(after(late, early), 'wing', SWAP)  13 us
    ppermute x4, starting transfers between devices, to_other_wing(): return lax.ppermute(value, ('wing', 'quad'), pairs)  7.65 us
    all_to_all x1, starting transfers between devices, on_device(): mine = lax.all_to_all(message, 'quad', 0, 0)  5.39 us
    ppermute x3, waiting for transfers between devices, to_quad(): return lax.ppermute(value, 'quad', [(j, j ^ q) for j in range(quads)])  4.89 us
    ppermute x4, waiting for transfers between devices, to_other_wing(): return lax.ppermute(value, ('wing', 'quad'), pairs)  4.66 us
    ppermute x3, starting transfers between devices, to_quad(): return lax.ppermute(value, 'quad', [(j, j ^ q) for j in range(quads)])  3.55 us
    ppermute x1, waiting for transfers between devices, on_device(): late_other = lax.ppermute(late, 'parts', parts_swap)  3.34 us
  transfers between devices with their start and end apart: 16, of which 8 were waited for; matrix products, arithmetic and copies ran while one was open for 0% of the time, Pallas kernels for 24%

profile of v8, /device:TPU:0, one launch (start us, length us, event | category | flops | bytes accessed | tf_op | source)
XLA Modules:
  0.0 73.9 jit_solution(501434530163698042)
XLA Ops:
  0.6 3.2 %pack.1 = (bf16[4,176,1024]{2,1,0:T(8,128)(2,1)}, bf16[48,512]{1,0:T(8,128)(2,1)}, bf16[48,512]{1,0:T(8,128)(2,1)}, bf16[48,512]{1,0:T(8,128)(2,1)}, bf16[48,512...) custom-call(bf16[128,4096]{1,0:T(8,128)(2,1)} %x_hbm.1, bf16[32,8192]{1,0:T(8,128)(2,1)} %bitcast.6, ...), custom_call_target="tpu_custom_call" | custom-call | flops 1 | bytes 1 | tf_op jit(solution)/shard_map/pack/pallas_call | solution.py:204
  3.9 0.0 copy-start.8
  3.9 0.0 copy-start.9
  3.9 5.4 %all-to-all-start = ((bf16[4,176,1024]{2,1,0:T(8,128)(2,1)}), bf16[4,176,1024]{2,1,0:T(8,128)(2,1)S(1)}, u32[]{:S(2)}, u32[]{:S(2)}) async-start(bf16[4,176,1024]{2,1,0:T(8,128)(2,1)} %get-tuple-element.26), calls=%async_computation | async-start | bytes 2883584 | tf_op jit(solution)/shard_map/all_to_all | solution.py:418
  9.3 0.0 copy-done.8
  9.3 2.6 %collective-permute-start = (bf16[256,512]{1,0:T(8,128)(2,1)S(1)}, bf16[256,512]{1,0:T(8,128)(2,1)S(1)}, u32[]{:S(2)}, u32[]{:S(2)}) collective-permute-start(bf16[256,512]{1,0:T(8,128)(2,1)S(1)} %copy-done.8), channel_id=1, source_target_pairs={{0,8},{8,0},{1,9},{9,1},{2,10},{10,2},{3,11},{11,3},{4,12},{12,4},... | collective-permute-start | bytes 786440 | tf_op jit(solution)/shard_map/ppermute | solution.py:420
  11.9 0.3 collective-permute-start.1
  12.2 4.0 %collective-permute-start.2 = (bf16[48,512]{1,0:T(8,128)(2,1)}, bf16[48,512]{1,0:T(8,128)(2,1)S(1)}, u32[]{:S(2)}, u32[]{:S(2)}) collective-permute-start(bf16[48,512]{1,0:T(8,128)(2,1)} %get-tuple-element.35), channel_id=1, source_target_pairs={{0,10},{2,8},{4,14},{6,12},{8,2},{10,0},{12,6},{14,4},{1,11},{3,9}... | collective-permute-start | bytes 147464 | tf_op jit(solution)/shard_map/ppermute | solution.py:415
  16.2 1.2 %collective-permute-start.3 = (bf16[48,512]{1,0:T(8,128)(2,1)}, bf16[48,512]{1,0:T(8,128)(2,1)S(1)}, u32[]{:S(2)}, u32[]{:S(2)}) collective-permute-start(bf16[48,512]{1,0:T(8,128)(2,1)} %get-tuple-element.36), channel_id=1, source_target_pairs={{0,12},{2,14},{4,8},{6,10},{8,4},{10,6},{12,0},{14,2},{1,13},{3,15... | collective-permute-start | bytes 147464 | tf_op jit(solution)/shard_map/ppermute | solution.py:415
  17.5 0.0 copy-done.9
  17.5 2.0 %collective-permute-start.4 = (bf16[48,512]{1,0:T(8,128)(2,1)S(1)}, bf16[48,512]{1,0:T(8,128)(2,1)S(1)}, u32[]{:S(2)}, u32[]{:S(2)}) collective-permute-start(bf16[48,512]{1,0:T(8,128)(2,1)S(1)} %copy-done.9), channel_id=1, source_target_pairs={{0,14},{2,12},{4,10},{6,8},{8,6},{10,4},{12,2},{14,0},{1,15},{3,13... | collective-permute-start | bytes 147464 | tf_op jit(solution)/shard_map/ppermute | solution.py:415
  19.5 7.8 %cache_attention.2 = (f32[64,4096]{1,0:T(8,128)}, bf16[2048,64]{1,0:T(8,128)(2,1)}) custom-call(s32[2]{0:T(128)} %lens.1, bf16[128,4096]{1,0:T(8,128)(2,1)} %q_ref.3, bf16[128,512]{1,0:T(8,128)(2,1)} %fk_ref.3, bf16[2,2048,512]{2,1,0:T(8,128)(2,1)} %k_hbm.3, bf16[2,2048,512]{2,1,0:T(8,128)(2,1)} %v_hbm.3), custom_call_target="tpu_custom_call" | custom-call | flops 1 | bytes 1 | tf_op jit(solution)/shard_map/cache_attention/pallas_call | solution.py:118
  27.3 0.0 copy-start.7
  27.3 0.0 copy-start
  27.3 0.0 copy-start.5
  27.3 0.0 copy-start.6
  27.3 7.9 %cache_attention.3 = (f32[64,4096]{1,0:T(8,128)}, bf16[2048,64]{1,0:T(8,128)(2,1)}) custom-call(s32[2]{0:T(128)} %lens.1, bf16[128,4096]{1,0:T(8,128)(2,1)} %q_ref.3, bf16[128,512]{1,0:T(8,128)(2,1)} %fk_ref.3, bf16[2,2048,512]{2,1,0:T(8,128)(2,1)} %k_hbm.3, bf16[2,2048,512]{2,1,0:T(8,128)(2,1)} %v_hbm.3), custom_call_target="tpu_custom_call" | custom-call | flops 1 | bytes 1 | tf_op jit(solution)/shard_map/cache_attention/pallas_call | solution.py:118
  35.2 0.0 collective-permute-done.1
  35.2 0.0 collective-permute-done.2
  35.2 3.2 %collective-permute-done.3 = bf16[48,512]{1,0:T(8,128)(2,1)S(1)} collective-permute-done((bf16[48,512]{1,0:T(8,128)(2,1)}, bf16[48,512]{1,0:T(8,128)(2,1)S(1)}, u32[]{:S(2)}, u32[]{:S(2)}) %collective-permute-start.3) | collective-permute-done | bytes 49184 | tf_op jit(solution)/shard_map/ppermute | solution.py:415
  38.4 1.4 %collective-permute-done.4 = bf16[48,512]{1,0:T(8,128)(2,1)S(1)} collective-permute-done((bf16[48,512]{1,0:T(8,128)(2,1)S(1)}, bf16[48,512]{1,0:T(8,128)(2,1)S(1)}, u32[]{:S(2)}, u32[]{:S(2)}) %collective-permute-start.4) | collective-permute-done | bytes 49184 | tf_op jit(solution)/shard_map/ppermute | solution.py:415
  39.9 0.0 collective-permute-done.refs_0_
  39.9 0.0 all-to-all-done.refs_4_
  39.9 0.0 collective-permute-start.8
  39.9 0.1 collective-permute-start.9
  40.0 1.6 %collective-permute-start.5 = (bf16[4,48,512]{2,1,0:T(8,128)(2,1)S(1)}, bf16[4,48,512]{2,1,0:T(8,128)(2,1)S(1)}, u32[]{:S(2)}, u32[]{:S(2)}) collective-permute-start(bf16[4,48,512]{2,1,0:T(8,128)(2,1)S(1)} %pad_maximum_fusion.refs_0_), channel_id=1, source_target_pairs={{0,16},{16,0},{1,17},{17,1},{2,18},{18,2},{3,19},{19,3},{4,20},{20... | collective-permute-start | bytes 589832 | tf_op jit(solution)/shard_map/ppermute | solution.py:431
  41.6 0.5 collective-permute-start.10
  42.1 13.0 %collective-permute-done.9.refs_1_ = bf16[256,512]{1,0:T(8,128)(2,1)S(1)} collective-permute-done((bf16[256,512]{1,0:T(8,128)(2,1)S(1)}, bf16[256,512]{1,0:T(8,128)(2,1)S(1)}, u32[]{:S(2)}, u32[]{:S(2)}) %collective-permute-start.9) | collective-permute-done | bytes 262176 | tf_op jit(solution)/shard_map/ppermute | solution.py:428
  55.1 0.5 collective-permute-start.11
  55.7 0.0 collective-permute-start.6
  55.7 0.0 collective-permute-done.5.refs_1_
  55.7 0.5 collective-permute-start.7
  56.2 0.9 %collective-permute-done.6.refs_2_ = bf16[4,48,512]{2,1,0:T(8,128)(2,1)S(1)} collective-permute-done((bf16[4,48,512]{2,1,0:T(8,128)(2,1)S(1)}, bf16[4,48,512]{2,1,0:T(8,128)(2,1)S(1)}, u32[]{:S(2)}, u32[]{:S(2)}) %collective-permute-start.6) | collective-permute-done | bytes 196640 | tf_op jit(solution)/shard_map/ppermute | solution.py:433
  57.1 0.3 collective-permute-done.7.refs_3_
  57.4 0.0 collective-permute-done.8.refs_5_
  57.4 2.4 %near_products.1.near = f32[512,512]{1,0:T(8,128)S(1)} custom-call(s32[16]{0:T(128)S(1)} %copy-done.5, s32[16]{0:T(128)S(1)} %copy-done.6, bf16[1024,512]{1,0:T(8,128)(2,1)S(1)} %copy-done, bf16[4,48,512]{2,1,0:T(8,128)(2,1)S(1)} %pad_maximum_fusion.refs_0_, bf16[4,48,512]{2,1,0:T(8,128)(2,1)S(1)} %collective-permute-done.5.refs_1_, ...), custom_call_target="tpu_custom_call" | custom-call | flops 1 | bytes 1 | tf_op jit(solution)/shard_map/near_products/pallas_call | solution.py:276
  59.8 0.0 copy-start.1
  59.8 0.0 collective-permute-done.10.refs_2_
  59.8 3.3 %collective-permute-done.11.refs_3_ = bf16[256,512]{1,0:T(8,128)(2,1)S(1)} collective-permute-done((bf16[256,512]{1,0:T(8,128)(2,1)S(1)}, bf16[256,512]{1,0:T(8,128)(2,1)S(1)}, u32[]{:S(2)}, u32[]{:S(2)}) %collective-permute-start.11) | collective-permute-done | bytes 262176 | tf_op jit(solution)/shard_map/ppermute | solution.py:430
  63.2 0.8 %far_products.1 = (bf16[128,512]{1,0:T(8,128)(2,1)S(1)}, bf16[128,512]{1,0:T(8,128)(2,1)S(1)}, bf16[128,512]{1,0:T(8,128)(2,1)S(1)}, bf16[128,512]{1,0:T(8,128)(2,1)S(1)}) custom-call(f32[512,512]{1,0:T(8,128)S(1)} %near_products.1.near, bf16[256,512]{1,0:T(8,128)(2,1)S(1)} %collective-permute-done.refs_0_, ...), custom_call_target="tpu_custom_call" | custom-call | flops 1 | bytes 1 | tf_op jit(solution)/shard_map/far_products/pallas_call | solution.py:323
  64.0 0.2 collective-permute-start.12
  64.2 0.8 %collective-permute-start.13 = (bf16[128,512]{1,0:T(8,128)(2,1)S(1)}, bf16[128,512]{1,0:T(8,128)(2,1)S(1)}, u32[]{:S(2)}, u32[]{:S(2)}) collective-permute-start(bf16[128,512]{1,0:T(8,128)(2,1)S(1)} %get-tuple-element.48), channel_id=1, source_target_pairs={{0,4},{2,6},{4,0},{6,2},{1,5},{3,7},{5,1},{7,3},{8,12},{10,14},{12... | collective-permute-start | bytes 393224 | tf_op jit(solution)/shard_map/ppermute | solution.py:411
  65.0 2.6 %collective-permute-start.14 = (bf16[128,512]{1,0:T(8,128)(2,1)S(1)}, bf16[128,512]{1,0:T(8,128)(2,1)S(1)}, u32[]{:S(2)}, u32[]{:S(2)}) collective-permute-start(bf16[128,512]{1,0:T(8,128)(2,1)S(1)} %get-tuple-element.49), channel_id=1, source_target_pairs={{0,6},{2,4},{4,2},{6,0},{1,7},{3,5},{5,3},{7,1},{8,14},{10,12},{12... | collective-permute-start | bytes 393224 | tf_op jit(solution)/shard_map/ppermute | solution.py:411
  67.6 2.9 %collective-permute-done.12.refs_5_ = bf16[128,512]{1,0:T(8,128)(2,1)S(1)} collective-permute-done((bf16[128,512]{1,0:T(8,128)(2,1)S(1)}, bf16[128,512]{1,0:T(8,128)(2,1)S(1)}, u32[]{:S(2)}, u32[]{:S(2)}) %collective-permute-start.12) | collective-permute-done | bytes 131104 | tf_op jit(solution)/shard_map/ppermute | solution.py:411
  70.5 0.0 collective-permute-done.13.refs_6_
  70.5 2.0 %collective-permute-done.14.refs_7_ = bf16[128,512]{1,0:T(8,128)(2,1)S(1)} collective-permute-done((bf16[128,512]{1,0:T(8,128)(2,1)S(1)}, bf16[128,512]{1,0:T(8,128)(2,1)S(1)}, u32[]{:S(2)}, u32[]{:S(2)}) %collective-permute-start.14) | collective-permute-done | bytes 131104 | tf_op jit(solution)/shard_map/ppermute | solution.py:411
  72.5 0.0 copy-done.1
  72.5 1.4 %finish_attention.1 = (bf16[128,4096]{1,0:T(8,128)(2,1)}, bf16[128,512]{1,0:T(8,128)(2,1)}) custom-call(f32[64,4096]{1,0:T(8,128)S(1)} %copy-done.1, f32[64,4096]{1,0:T(8,128)S(1)} %copy-done.2, bf16[2048,64]{1,0:T(8,128)(2,1)S(1)} %copy-done.3, bf16[2048,64]{1,0:T(8,128)(2,1)S(1)} %copy-done.4, bf16[128,512]{1,0:T(8,128)(2,1)S(1)} %get-tuple-element.46.refs_4_, ...), custom_call_target="tpu_custom_call" | custom-call | flops 1 | bytes 1 | tf_op jit(solution)/shard_map/finish_attention/pallas_call | solution.py:365
  (11 shorter events, 0.0 us)
Async XLA Ops:
  3.9 5.4 %copy-start.8 = (bf16[256,512]{1,0:T(8,128)(2,1)S(1)}, bf16[256,512]{1,0:T(8,128)(2,1)}, u32[]{:S(2)}) copy-start(bf16[256,512]{1,0:T(8,128)(2,1)} %get-tuple-element.33) | copy-start | bytes 786436
  3.9 13.6 %copy-start.9 = (bf16[48,512]{1,0:T(8,128)(2,1)S(1)}, bf16[48,512]{1,0:T(8,128)(2,1)}, u32[]{:S(2)}) copy-start(bf16[48,512]{1,0:T(8,128)(2,1)} %get-tuple-element.37) | copy-start | bytes 147460
  3.9 36.0 %all-to-all-start = ((bf16[4,176,1024]{2,1,0:T(8,128)(2,1)}), bf16[4,176,1024]{2,1,0:T(8,128)(2,1)S(1)}, u32[]{:S(2)}, u32[]{:S(2)}) async-start(bf16[4,176,1024]{2,1,0:T(8,128)(2,1)} %get-tuple-element.26), calls=%async_computation | async-start | bytes 2883584 | tf_op jit(solution)/shard_map/all_to_all | solution.py:418
  9.3 30.6 %collective-permute-start = (bf16[256,512]{1,0:T(8,128)(2,1)S(1)}, bf16[256,512]{1,0:T(8,128)(2,1)S(1)}, u32[]{:S(2)}, u32[]{:S(2)}) collective-permute-start(bf16[256,512]{1,0:T(8,128)(2,1)S(1)} %copy-done.8), channel_id=1, source_target_pairs={{0,8},{8,0},{1,9},{9,1},{2,10},{10,2},{3,11},{11,3},{4,12},{12,4},... | collective-permute-start | bytes 786440 | tf_op jit(solution)/shard_map/ppermute | solution.py:420
  11.9 23.3 %collective-permute-start.1 = (bf16[48,512]{1,0:T(8,128)(2,1)}, bf16[48,512]{1,0:T(8,128)(2,1)S(1)}, u32[]{:S(2)}, u32[]{:S(2)}) collective-permute-start(bf16[48,512]{1,0:T(8,128)(2,1)} %get-tuple-element.34), channel_id=1, source_target_pairs={{0,8},{2,10},{4,12},{6,14},{8,0},{10,2},{12,4},{14,6},{1,9},{3,11}... | collective-permute-start | bytes 147464 | tf_op jit(solution)/shard_map/ppermute | solution.py:415
  12.2 23.0 %collective-permute-start.2 = (bf16[48,512]{1,0:T(8,128)(2,1)}, bf16[48,512]{1,0:T(8,128)(2,1)S(1)}, u32[]{:S(2)}, u32[]{:S(2)}) collective-permute-start(bf16[48,512]{1,0:T(8,128)(2,1)} %get-tuple-element.35), channel_id=1, source_target_pairs={{0,10},{2,8},{4,14},{6,12},{8,2},{10,0},{12,6},{14,4},{1,11},{3,9}... | collective-permute-start | bytes 147464 | tf_op jit(solution)/shard_map/ppermute | solution.py:415
  16.2 22.2 %collective-permute-start.3 = (bf16[48,512]{1,0:T(8,128)(2,1)}, bf16[48,512]{1,0:T(8,128)(2,1)S(1)}, u32[]{:S(2)}, u32[]{:S(2)}) collective-permute-start(bf16[48,512]{1,0:T(8,128)(2,1)} %get-tuple-element.36), channel_id=1, source_target_pairs={{0,12},{2,14},{4,8},{6,10},{8,4},{10,6},{12,0},{14,2},{1,13},{3,15... | collective-permute-start | bytes 147464 | tf_op jit(solution)/shard_map/ppermute | solution.py:415
  17.5 22.4 %collective-permute-start.4 = (bf16[48,512]{1,0:T(8,128)(2,1)S(1)}, bf16[48,512]{1,0:T(8,128)(2,1)S(1)}, u32[]{:S(2)}, u32[]{:S(2)}) collective-permute-start(bf16[48,512]{1,0:T(8,128)(2,1)S(1)} %copy-done.9), channel_id=1, source_target_pairs={{0,14},{2,12},{4,10},{6,8},{8,6},{10,4},{12,2},{14,0},{1,15},{3,13... | collective-permute-start | bytes 147464 | tf_op jit(solution)/shard_map/ppermute | solution.py:415
  27.3 12.6 %copy-start.7 = (bf16[256,512]{1,0:T(8,128)(2,1)S(1)}, bf16[256,512]{1,0:T(8,128)(2,1)}, u32[]{:S(2)}) copy-start(bf16[256,512]{1,0:T(8,128)(2,1)} %get-tuple-element.45) | copy-start | bytes 786436
  27.3 30.1 %copy-start = (bf16[1024,512]{1,0:T(8,128)(2,1)S(1)}, bf16[1024,512]{1,0:T(8,128)(2,1)}, u32[]{:S(2)}) copy-start(bf16[1024,512]{1,0:T(8,128)(2,1)} %own_ref.1) | copy-start | bytes 3145732
  27.3 30.1 %copy-start.5 = (s32[16]{0:T(128)S(1)}, s32[16]{0:T(128)}, u32[]{:S(2)}) copy-start(s32[16]{0:T(128)} %position.1) | copy-start | bytes 196
  27.3 30.1 %copy-start.6 = (s32[16]{0:T(128)S(1)}, s32[16]{0:T(128)}, u32[]{:S(2)}) copy-start(s32[16]{0:T(128)} %adapter.1) | copy-start | bytes 196
  39.9 17.5 %collective-permute-start.8 = (bf16[4,176,1024]{2,1,0:T(8,128)(2,1)S(1)}, bf16[4,176,1024]{2,1,0:T(8,128)(2,1)S(1)}, u32[]{:S(2)}, u32[]{:S(2)}) collective-permute-start(bf16[4,176,1024]{2,1,0:T(8,128)(2,1)S(1)} %all-to-all-done.refs_4_), channel_id=1, source_target_pairs={{0,1},{1,0},{2,3},{3,2},{4,5},{5,4},{6,7},{7,6},{8,9},{9,8},{10,11... | collective-permute-start | bytes 4325384 | tf_op jit(solution)/shard_map/ppermute | solution.py:434
  39.9 15.2 %collective-permute-start.9 = (bf16[256,512]{1,0:T(8,128)(2,1)S(1)}, bf16[256,512]{1,0:T(8,128)(2,1)S(1)}, u32[]{:S(2)}, u32[]{:S(2)}) collective-permute-start(bf16[256,512]{1,0:T(8,128)(2,1)S(1)} %copy-done.7), channel_id=1, source_target_pairs={{0,8},{8,0},{1,9},{9,1},{2,10},{10,2},{3,11},{11,3},{4,12},{12,4},... | collective-permute-start | bytes 786440 | tf_op jit(solution)/shard_map/ppermute | solution.py:428
  40.0 15.6 %collective-permute-start.5 = (bf16[4,48,512]{2,1,0:T(8,128)(2,1)S(1)}, bf16[4,48,512]{2,1,0:T(8,128)(2,1)S(1)}, u32[]{:S(2)}, u32[]{:S(2)}) collective-permute-start(bf16[4,48,512]{2,1,0:T(8,128)(2,1)S(1)} %pad_maximum_fusion.refs_0_), channel_id=1, source_target_pairs={{0,16},{16,0},{1,17},{17,1},{2,18},{18,2},{3,19},{19,3},{4,20},{20... | collective-permute-start | bytes 589832 | tf_op jit(solution)/shard_map/ppermute | solution.py:431
  41.6 18.3 %collective-permute-start.10 = (bf16[256,512]{1,0:T(8,128)(2,1)S(1)}, bf16[256,512]{1,0:T(8,128)(2,1)S(1)}, u32[]{:S(2)}, u32[]{:S(2)}) collective-permute-start(bf16[256,512]{1,0:T(8,128)(2,1)S(1)} %collective-permute-done.refs_0_), channel_id=1, source_target_pairs={{0,16},{16,0},{1,17},{17,1},{2,18},{18,2},{3,19},{19,3},{4,20},{20... | collective-permute-start | bytes 786440 | tf_op jit(solution)/shard_map/ppermute | solution.py:429
  55.1 8.0 %collective-permute-start.11 = (bf16[256,512]{1,0:T(8,128)(2,1)S(1)}, bf16[256,512]{1,0:T(8,128)(2,1)S(1)}, u32[]{:S(2)}, u32[]{:S(2)}) collective-permute-start(bf16[256,512]{1,0:T(8,128)(2,1)S(1)} %collective-permute-done.9.refs_1_), channel_id=1, source_target_pairs={{0,16},{16,0},{1,17},{17,1},{2,18},{18,2},{3,19},{19,3},{4,20},{20... | collective-permute-start | bytes 786440 | tf_op jit(solution)/shard_map/ppermute | solution.py:430
  55.7 1.4 %collective-permute-start.6 = (bf16[4,48,512]{2,1,0:T(8,128)(2,1)S(1)}, bf16[4,48,512]{2,1,0:T(8,128)(2,1)S(1)}, u32[]{:S(2)}, u32[]{:S(2)}) collective-permute-start(bf16[4,48,512]{2,1,0:T(8,128)(2,1)S(1)} %pad_maximum_fusion.refs_0_), channel_id=1, source_target_pairs={{0,1},{1,0},{2,3},{3,2},{4,5},{5,4},{6,7},{7,6},{8,9},{9,8},{10,11... | collective-permute-start | bytes 589832 | tf_op jit(solution)/shard_map/ppermute | solution.py:433
  55.7 1.7 %collective-permute-start.7 = (bf16[4,48,512]{2,1,0:T(8,128)(2,1)S(1)}, bf16[4,48,512]{2,1,0:T(8,128)(2,1)S(1)}, u32[]{:S(2)}, u32[]{:S(2)}) collective-permute-start(bf16[4,48,512]{2,1,0:T(8,128)(2,1)S(1)} %collective-permute-done.5.refs_1_), channel_id=1, source_target_pairs={{0,1},{1,0},{2,3},{3,2},{4,5},{5,4},{6,7},{7,6},{8,9},{9,8},{10,11... | collective-permute-start | bytes 589832 | tf_op jit(solution)/shard_map/ppermute | solution.py:433
  59.8 12.7 %copy-start.1 = (f32[64,4096]{1,0:T(8,128)S(1)}, f32[64,4096]{1,0:T(8,128)}, u32[]{:S(2)}) copy-start(f32[64,4096]{1,0:T(8,128)} %get-tuple-element.28.refs_0_) | copy-start | bytes 3145732
  59.8 12.7 %copy-start.2 = (f32[64,4096]{1,0:T(8,128)S(1)}, f32[64,4096]{1,0:T(8,128)}, u32[]{:S(2)}) copy-start(f32[64,4096]{1,0:T(8,128)} %get-tuple-element.31.refs_1_) | copy-start | bytes 3145732
  59.8 12.7 %copy-start.3 = (bf16[2048,64]{1,0:T(8,128)(2,1)S(1)}, bf16[2048,64]{1,0:T(8,128)(2,1)}, u32[]{:S(2)}) copy-start(bf16[2048,64]{1,0:T(8,128)(2,1)} %get-tuple-element.29.refs_2_) | copy-start | bytes 786436
  59.8 12.7 %copy-start.4 = (bf16[2048,64]{1,0:T(8,128)(2,1)S(1)}, bf16[2048,64]{1,0:T(8,128)(2,1)}, u32[]{:S(2)}) copy-start(bf16[2048,64]{1,0:T(8,128)(2,1)} %get-tuple-element.32.refs_3_) | copy-start | bytes 786436
  64.0 6.4 %collective-permute-start.12 = (bf16[128,512]{1,0:T(8,128)(2,1)S(1)}, bf16[128,512]{1,0:T(8,128)(2,1)S(1)}, u32[]{:S(2)}, u32[]{:S(2)}) collective-permute-start(bf16[128,512]{1,0:T(8,128)(2,1)S(1)} %get-tuple-element.47), channel_id=1, source_target_pairs={{0,2},{2,0},{4,6},{6,4},{1,3},{3,1},{5,7},{7,5},{8,10},{10,8},{12,... | collective-permute-start | bytes 393224 | tf_op jit(solution)/shard_map/ppermute | solution.py:411
  64.2 6.2 %collective-permute-start.13 = (bf16[128,512]{1,0:T(8,128)(2,1)S(1)}, bf16[128,512]{1,0:T(8,128)(2,1)S(1)}, u32[]{:S(2)}, u32[]{:S(2)}) collective-permute-start(bf16[128,512]{1,0:T(8,128)(2,1)S(1)} %get-tuple-element.48), channel_id=1, source_target_pairs={{0,4},{2,6},{4,0},{6,2},{1,5},{3,7},{5,1},{7,3},{8,12},{10,14},{12... | collective-permute-start | bytes 393224 | tf_op jit(solution)/shard_map/ppermute | solution.py:411
  65.0 7.5 %collective-permute-start.14 = (bf16[128,512]{1,0:T(8,128)(2,1)S(1)}, bf16[128,512]{1,0:T(8,128)(2,1)S(1)}, u32[]{:S(2)}, u32[]{:S(2)}) collective-permute-start(bf16[128,512]{1,0:T(8,128)(2,1)S(1)} %get-tuple-element.49), channel_id=1, source_target_pairs={{0,6},{2,4},{4,2},{6,0},{1,7},{3,5},{5,3},{7,1},{8,14},{10,12},{12... | collective-permute-start | bytes 393224 | tf_op jit(solution)/shard_map/ppermute | solution.py:411

commit v9 on v8

--- a/solution.py
+++ b/solution.py
@@ -420,15 +420,17 @@
     early = lax.ppermute(early, "wing", SWAP)
 
     attn = [attention(0, after(cache_length, message))]
-    attn.append(attention(1, after(cache_length, attn[0][1])))
-    early, *maps = lax.optimization_barrier((early, *maps, attn[1][1]))[:-1]
+    early, *maps = lax.optimization_barrier((early, *maps, attn[0][1]))[:-1]
     maps = jnp.stack(maps)
-    mine = after(mine, early)
-
     late = lax.ppermute(after(late, early), "wing", SWAP)
     early_other = lax.ppermute(early, "parts", parts_swap)
+    maps_other = lax.ppermute(maps, "parts", parts_swap)
+
+    attn.append(attention(1, after(cache_length, early, maps)))
+    late, mine, early_other, maps_other = lax.optimization_barrier(
+        (late, mine, early_other, maps_other, attn[1][1])
+    )[:-1]
     late_other = lax.ppermute(late, "parts", parts_swap)
-    maps_other = lax.ppermute(maps, "parts", parts_swap)
     maps_mine = (maps, maps_other)
     maps_theirs = [lax.ppermute(each, "tensor", SWAP) for each in maps_mine]
     theirs = lax.ppermute(mine, "tensor", SWAP)

time: 74 us -> 74.4 us (level)
  waiting for transfers between devices: 27.1 us -> 18.6 us
  Pallas kernels: 23.5 us -> 28.5 us
  starting transfers between devices: 22.4 us -> 25 us
  local copies, waits for them, and re-layouts: 0.05 us -> 1.01 us
    ppermute x1, waiting for transfers between devices: 13 us -> 0.63 us  [on_device(): late = lax.ppermute(after(late, early), 'wing', SWAP)]
    pallas_call x2, Pallas kernels: 15.6 us -> 20.6 us  [cache_attention(): pl.pallas_call(functools.partial(cache_kernel, span, first_head, kv_heads...]
    ppermute x4, waiting for transfers between devices: 4.66 us -> 9.2 us  [to_other_wing(): return lax.ppermute(value, ('wing', 'quad'), pairs)]
    ppermute x1, starting transfers between devices: 0.52 us -> 3.19 us  [on_device(): late_other = lax.ppermute(late, 'parts', parts_swap)]
    ppermute x1, waiting for transfers between devices: 3.34 us -> 1.6 us  [on_device(): late_other = lax.ppermute(late, 'parts', parts_swap)]
    unnamed x20 -> x30, local copies, waits for them, and re-layouts: 0.05 us -> 1.01 us
    ppermute x1, starting transfers between devices: 0.53 us -> 1.49 us  [on_device(): early_other = lax.ppermute(early, 'parts', parts_swap)]
    ppermute x1, starting transfers between devices: 1.56 us -> 0.6 us  [on_device(): maps_other = lax.ppermute(maps, 'parts', parts_swap)]
  transfers between devices with their start and end apart: 16 -> 16, of which waited for: 8 -> 11; matrix products, arithmetic and copies ran while one was open for 0% -> 0% of each run, Pallas kernels for 24% -> 31%
where the time goes in v9:
time: 74.4 us; the launch traced here: 74 us
  Pallas kernels  28.5 us (38%)
  starting transfers between devices  25 us (34%)
  waiting for transfers between devices  18.6 us (25%)
  local copies, waits for them, and re-layouts  1.01 us (1%)
  between operations  0.85 us (1%)
    pallas_call x2, Pallas kernels, cache_attention(): pl.pallas_call(functools.partial(cache_kernel, span, first_head, kv_heads...  20.6 us
    ppermute x4, waiting for transfers between devices, to_other_wing(): return lax.ppermute(value, ('wing', 'quad'), pairs)  9.2 us
    ppermute x4, starting transfers between devices, to_other_wing(): return lax.ppermute(value, ('wing', 'quad'), pairs)  7.65 us
    ppermute x3, waiting for transfers between devices, to_quad(): return lax.ppermute(value, 'quad', [(j, j ^ q) for j in range(quads)])  5.76 us
    all_to_all x1, starting transfers between devices, on_device(): mine = lax.all_to_all(message, 'quad', 0, 0)  5.39 us
    ppermute x3, starting transfers between devices, to_quad(): return lax.ppermute(value, 'quad', [(j, j ^ q) for j in range(quads)])  3.55 us
    pallas_call x1, Pallas kernels, pack(): pl.pallas_call(pack_kernel, in_specs=[hbm] * 4, out_specs=[vmem] * len(si...  3.24 us
    ppermute x1, starting transfers between devices, on_device(): late_other = lax.ppermute(late, 'parts', parts_swap)  3.19 us
  transfers between devices with their start and end apart: 16, of which 11 were waited for; matrix products, arithmetic and copies ran while one was open for 0% of the time, Pallas kernels for 31%

profile of v9, /device:TPU:0, one launch (start us, length us, event | category | flops | bytes accessed | tf_op | source)
XLA Modules:
  0.0 74.0 jit_solution(2151363783314202745)
XLA Ops:
  0.6 3.2 %pack.1 = (bf16[4,176,1024]{2,1,0:T(8,128)(2,1)}, bf16[48,512]{1,0:T(8,128)(2,1)}, bf16[48,512]{1,0:T(8,128)(2,1)}, bf16[48,512]{1,0:T(8,128)(2,1)}, bf16[48,512...) custom-call(bf16[128,4096]{1,0:T(8,128)(2,1)} %x_hbm.1, bf16[32,8192]{1,0:T(8,128)(2,1)} %bitcast.6, ...), custom_call_target="tpu_custom_call" | custom-call | flops 1 | bytes 1 | tf_op jit(solution)/shard_map/pack/pallas_call | solution.py:204
  3.9 0.0 copy-start.10
  3.9 0.0 copy-start.14
  3.9 0.0 copy-start.13
  3.9 0.0 copy-start.12
  3.9 5.4 %all-to-all-start = ((bf16[4,176,1024]{2,1,0:T(8,128)(2,1)}), bf16[4,176,1024]{2,1,0:T(8,128)(2,1)S(1)}, u32[]{:S(2)}, u32[]{:S(2)}) async-start(bf16[4,176,1024]{2,1,0:T(8,128)(2,1)} %get-tuple-element.29), calls=%async_computation | async-start | bytes 2883584 | tf_op jit(solution)/shard_map/all_to_all | solution.py:418
  9.3 2.6 %collective-permute-start = (bf16[256,512]{1,0:T(8,128)(2,1)S(1)}, bf16[256,512]{1,0:T(8,128)(2,1)S(1)}, u32[]{:S(2)}, u32[]{:S(2)}) collective-permute-start(bf16[256,512]{1,0:T(8,128)(2,1)S(1)} %copy-done.10), channel_id=1, source_target_pairs={{0,8},{8,0},{1,9},{9,1},{2,10},{10,2},{3,11},{11,3},{4,12},{12,4},... | collective-permute-start | bytes 786440 | tf_op jit(solution)/shard_map/ppermute | solution.py:420
  11.9 0.3 collective-permute-start.1
  12.3 4.0 %collective-permute-start.2 = (bf16[48,512]{1,0:T(8,128)(2,1)S(1)}, bf16[48,512]{1,0:T(8,128)(2,1)S(1)}, u32[]{:S(2)}, u32[]{:S(2)}) collective-permute-start(bf16[48,512]{1,0:T(8,128)(2,1)S(1)} %copy-done.13), channel_id=1, source_target_pairs={{0,10},{2,8},{4,14},{6,12},{8,2},{10,0},{12,6},{14,4},{1,11},{3,9}... | collective-permute-start | bytes 147464 | tf_op jit(solution)/shard_map/ppermute | solution.py:415
  16.3 1.2 %collective-permute-start.3 = (bf16[48,512]{1,0:T(8,128)(2,1)S(1)}, bf16[48,512]{1,0:T(8,128)(2,1)S(1)}, u32[]{:S(2)}, u32[]{:S(2)}) collective-permute-start(bf16[48,512]{1,0:T(8,128)(2,1)S(1)} %copy-done.12), channel_id=1, source_target_pairs={{0,12},{2,14},{4,8},{6,10},{8,4},{10,6},{12,0},{14,2},{1,13},{3,15... | collective-permute-start | bytes 147464 | tf_op jit(solution)/shard_map/ppermute | solution.py:415
  17.5 2.0 %collective-permute-start.4 = (bf16[48,512]{1,0:T(8,128)(2,1)S(1)}, bf16[48,512]{1,0:T(8,128)(2,1)S(1)}, u32[]{:S(2)}, u32[]{:S(2)}) collective-permute-start(bf16[48,512]{1,0:T(8,128)(2,1)S(1)} %copy-done.11), channel_id=1, source_target_pairs={{0,14},{2,12},{4,10},{6,8},{8,6},{10,4},{12,2},{14,0},{1,15},{3,13... | collective-permute-start | bytes 147464 | tf_op jit(solution)/shard_map/ppermute | solution.py:415
  19.6 11.1 %cache_attention.2 = (f32[64,4096]{1,0:T(8,128)}, bf16[2048,64]{1,0:T(8,128)(2,1)}) custom-call(s32[2]{0:T(128)} %lens.1, bf16[128,4096]{1,0:T(8,128)(2,1)} %q_ref.3, bf16[128,512]{1,0:T(8,128)(2,1)} %fk_ref.3, bf16[2,2048,512]{2,1,0:T(8,128)(2,1)} %k_hbm.3, bf16[2,2048,512]{2,1,0:T(8,128)(2,1)} %v_hbm.3), custom_call_target="tpu_custom_call" | custom-call | flops 1 | bytes 1 | tf_op jit(solution)/shard_map/cache_attention/pallas_call | solution.py:118
  30.7 2.1 %collective-permute-done.1 = bf16[48,512]{1,0:T(8,128)(2,1)S(1)} collective-permute-done((bf16[48,512]{1,0:T(8,128)(2,1)S(1)}, bf16[48,512]{1,0:T(8,128)(2,1)S(1)}, u32[]{:S(2)}, u32[]{:S(2)}) %collective-permute-start.1) | collective-permute-done | bytes 49184 | tf_op jit(solution)/shard_map/ppermute | solution.py:415
  32.8 1.0 %collective-permute-done.2 = bf16[48,512]{1,0:T(8,128)(2,1)S(1)} collective-permute-done((bf16[48,512]{1,0:T(8,128)(2,1)S(1)}, bf16[48,512]{1,0:T(8,128)(2,1)S(1)}, u32[]{:S(2)}, u32[]{:S(2)}) %collective-permute-start.2) | collective-permute-done | bytes 49184 | tf_op jit(solution)/shard_map/ppermute | solution.py:415
  33.7 4.8 %collective-permute-done.3 = bf16[48,512]{1,0:T(8,128)(2,1)S(1)} collective-permute-done((bf16[48,512]{1,0:T(8,128)(2,1)S(1)}, bf16[48,512]{1,0:T(8,128)(2,1)S(1)}, u32[]{:S(2)}, u32[]{:S(2)}) %collective-permute-start.3) | collective-permute-done | bytes 49184 | tf_op jit(solution)/shard_map/ppermute | solution.py:415
  38.5 1.4 %collective-permute-done.4 = bf16[48,512]{1,0:T(8,128)(2,1)S(1)} collective-permute-done((bf16[48,512]{1,0:T(8,128)(2,1)S(1)}, bf16[48,512]{1,0:T(8,128)(2,1)S(1)}, u32[]{:S(2)}, u32[]{:S(2)}) %collective-permute-start.4) | collective-permute-done | bytes 49184 | tf_op jit(solution)/shard_map/ppermute | solution.py:415
  39.9 0.0 collective-permute-done.refs_0_
  39.9 1.5 %collective-permute-start.6 = (bf16[256,512]{1,0:T(8,128)(2,1)S(1)}, bf16[256,512]{1,0:T(8,128)(2,1)S(1)}, u32[]{:S(2)}, u32[]{:S(2)}) collective-permute-start(bf16[256,512]{1,0:T(8,128)(2,1)S(1)} %collective-permute-done.refs_0_), channel_id=1, source_target_pairs={{0,16},{16,0},{1,17},{17,1},{2,18},{18,2},{3,19},{19,3},{4,20},{20... | collective-permute-start | bytes 786440 | tf_op jit(solution)/shard_map/ppermute | solution.py:426
  41.4 0.0 collective-permute-start.5
  41.5 0.0 copy-start
  41.5 0.0 copy-start.7
  41.5 0.0 copy-start.8
  41.5 0.6 collective-permute-start.7
  42.1 9.5 %cache_attention.3 = (f32[64,4096]{1,0:T(8,128)}, bf16[2048,64]{1,0:T(8,128)(2,1)}) custom-call(s32[2]{0:T(128)} %lens.1, bf16[128,4096]{1,0:T(8,128)(2,1)} %q_ref.3, bf16[128,512]{1,0:T(8,128)(2,1)} %fk_ref.3, bf16[2,2048,512]{2,1,0:T(8,128)(2,1)} %k_hbm.3, bf16[2,2048,512]{2,1,0:T(8,128)(2,1)} %v_hbm.3), custom_call_target="tpu_custom_call" | custom-call | flops 1 | bytes 1 | tf_op jit(solution)/shard_map/cache_attention/pallas_call | solution.py:118
  51.6 0.0 collective-permute-done.7.refs_1_
  51.6 0.6 collective-permute-done.5.refs_1_
  52.2 0.0 copy-done.5
  52.3 0.0 collective-permute-done.6.refs_2_
  52.3 0.0 all-to-all-done.refs_4_
  52.3 0.1 collective-permute-start.10
  52.3 3.2 %collective-permute-start.11 = (bf16[256,512]{1,0:T(8,128)(2,1)S(1)}, bf16[256,512]{1,0:T(8,128)(2,1)S(1)}, u32[]{:S(2)}, u32[]{:S(2)}) collective-permute-start(bf16[256,512]{1,0:T(8,128)(2,1)S(1)} %collective-permute-done.5.refs_1_), channel_id=1, source_target_pairs={{0,16},{16,0},{1,17},{17,1},{2,18},{18,2},{3,19},{19,3},{4,20},{20... | collective-permute-start | bytes 786440 | tf_op jit(solution)/shard_map/ppermute | solution.py:433
  55.5 0.2 collective-permute-start.8
  55.7 0.4 collective-permute-start.9
  56.0 0.9 %collective-permute-done.8.refs_2_ = bf16[4,48,512]{2,1,0:T(8,128)(2,1)S(1)} collective-permute-done((bf16[4,48,512]{2,1,0:T(8,128)(2,1)S(1)}, bf16[4,48,512]{2,1,0:T(8,128)(2,1)S(1)}, u32[]{:S(2)}, u32[]{:S(2)}) %collective-permute-start.8) | collective-permute-done | bytes 196640 | tf_op jit(solution)/shard_map/ppermute | solution.py:435
  57.0 0.5 collective-permute-done.9.refs_3_
  57.5 0.0 collective-permute-done.10.refs_5_
  57.5 0.9 %copy-done.6 = bf16[4,48,512]{2,1,0:T(8,128)(2,1)S(1)} copy-done((bf16[4,48,512]{2,1,0:T(8,128)(2,1)S(1)}, bf16[4,48,512]{2,1,0:T(8,128)(2,1)}, u32[]{:S(2)}) %copy-start.6) | copy-done | bytes 196632
  58.4 2.4 %near_products.1.near = f32[512,512]{1,0:T(8,128)S(1)} custom-call(s32[16]{0:T(128)S(1)} %copy-done.7, s32[16]{0:T(128)S(1)} %copy-done.8, bf16[1024,512]{1,0:T(8,128)(2,1)S(1)} %copy-done, bf16[4,48,512]{2,1,0:T(8,128)(2,1)S(1)} %pad_maximum_fusion.refs_0_, bf16[4,48,512]{2,1,0:T(8,128)(2,1)S(1)} %copy-done.6, ...), custom_call_target="tpu_custom_call" | custom-call | flops 1 | bytes 1 | tf_op jit(solution)/shard_map/near_products/pallas_call | solution.py:276
  60.8 0.0 copy-start.1
  60.8 1.6 %collective-permute-done.11.refs_3_ = bf16[256,512]{1,0:T(8,128)(2,1)S(1)} collective-permute-done((bf16[256,512]{1,0:T(8,128)(2,1)S(1)}, bf16[256,512]{1,0:T(8,128)(2,1)S(1)}, u32[]{:S(2)}, u32[]{:S(2)}) %collective-permute-start.11) | collective-permute-done | bytes 262176 | tf_op jit(solution)/shard_map/ppermute | solution.py:433
  62.4 0.8 %far_products.1 = (bf16[128,512]{1,0:T(8,128)(2,1)S(1)}, bf16[128,512]{1,0:T(8,128)(2,1)S(1)}, bf16[128,512]{1,0:T(8,128)(2,1)S(1)}, bf16[128,512]{1,0:T(8,128)(2,1)S(1)}) custom-call(f32[512,512]{1,0:T(8,128)S(1)} %near_products.1.near, bf16[256,512]{1,0:T(8,128)(2,1)S(1)} %collective-permute-done.refs_0_, ...), custom_call_target="tpu_custom_call" | custom-call | flops 1 | bytes 1 | tf_op jit(solution)/shard_map/far_products/pallas_call | solution.py:323
  63.3 0.1 collective-permute-start.12
  63.4 1.1 %collective-permute-start.13 = (bf16[128,512]{1,0:T(8,128)(2,1)S(1)}, bf16[128,512]{1,0:T(8,128)(2,1)S(1)}, u32[]{:S(2)}, u32[]{:S(2)}) collective-permute-start(bf16[128,512]{1,0:T(8,128)(2,1)S(1)} %get-tuple-element.54), channel_id=1, source_target_pairs={{0,4},{2,6},{4,0},{6,2},{1,5},{3,7},{5,1},{7,3},{8,12},{10,14},{12... | collective-permute-start | bytes 393224 | tf_op jit(solution)/shard_map/ppermute | solution.py:411
  64.4 2.4 %collective-permute-start.14 = (bf16[128,512]{1,0:T(8,128)(2,1)S(1)}, bf16[128,512]{1,0:T(8,128)(2,1)S(1)}, u32[]{:S(2)}, u32[]{:S(2)}) collective-permute-start(bf16[128,512]{1,0:T(8,128)(2,1)S(1)} %get-tuple-element.55), channel_id=1, source_target_pairs={{0,6},{2,4},{4,2},{6,0},{1,7},{3,5},{5,3},{7,1},{8,14},{10,12},{12... | collective-permute-start | bytes 393224 | tf_op jit(solution)/shard_map/ppermute | solution.py:411
  66.8 2.0 %collective-permute-done.12.refs_5_ = bf16[128,512]{1,0:T(8,128)(2,1)S(1)} collective-permute-done((bf16[128,512]{1,0:T(8,128)(2,1)S(1)}, bf16[128,512]{1,0:T(8,128)(2,1)S(1)}, u32[]{:S(2)}, u32[]{:S(2)}) %collective-permute-start.12) | collective-permute-done | bytes 131104 | tf_op jit(solution)/shard_map/ppermute | solution.py:411
  68.9 0.8 %collective-permute-done.13.refs_6_ = bf16[128,512]{1,0:T(8,128)(2,1)S(1)} collective-permute-done((bf16[128,512]{1,0:T(8,128)(2,1)S(1)}, bf16[128,512]{1,0:T(8,128)(2,1)S(1)}, u32[]{:S(2)}, u32[]{:S(2)}) %collective-permute-start.13) | collective-permute-done | bytes 131104 | tf_op jit(solution)/shard_map/ppermute | solution.py:411
  69.7 2.9 %collective-permute-done.14.refs_7_ = bf16[128,512]{1,0:T(8,128)(2,1)S(1)} collective-permute-done((bf16[128,512]{1,0:T(8,128)(2,1)S(1)}, bf16[128,512]{1,0:T(8,128)(2,1)S(1)}, u32[]{:S(2)}, u32[]{:S(2)}) %collective-permute-start.14) | collective-permute-done | bytes 131104 | tf_op jit(solution)/shard_map/ppermute | solution.py:411
  72.6 1.4 %finish_attention.1 = (bf16[128,4096]{1,0:T(8,128)(2,1)}, bf16[128,512]{1,0:T(8,128)(2,1)}) custom-call(f32[64,4096]{1,0:T(8,128)S(1)} %copy-done.1, f32[64,4096]{1,0:T(8,128)S(1)} %copy-done.2, bf16[2048,64]{1,0:T(8,128)(2,1)S(1)} %copy-done.3, bf16[2048,64]{1,0:T(8,128)(2,1)S(1)} %copy-done.4, bf16[128,512]{1,0:T(8,128)(2,1)S(1)} %get-tuple-element.52.refs_4_, ...), custom_call_target="tpu_custom_call" | custom-call | flops 1 | bytes 1 | tf_op jit(solution)/shard_map/finish_attention/pallas_call | solution.py:365
  (21 shorter events, 0.1 us)
Async XLA Ops:
  3.9 5.4 %copy-start.10 = (bf16[256,512]{1,0:T(8,128)(2,1)S(1)}, bf16[256,512]{1,0:T(8,128)(2,1)}, u32[]{:S(2)}) copy-start(bf16[256,512]{1,0:T(8,128)(2,1)} %get-tuple-element.32) | copy-start | bytes 786436
  3.9 8.0 %copy-start.14 = (bf16[48,512]{1,0:T(8,128)(2,1)S(1)}, bf16[48,512]{1,0:T(8,128)(2,1)}, u32[]{:S(2)}) copy-start(bf16[48,512]{1,0:T(8,128)(2,1)} %get-tuple-element.33) | copy-start | bytes 147460
  3.9 8.4 %copy-start.13 = (bf16[48,512]{1,0:T(8,128)(2,1)S(1)}, bf16[48,512]{1,0:T(8,128)(2,1)}, u32[]{:S(2)}) copy-start(bf16[48,512]{1,0:T(8,128)(2,1)} %get-tuple-element.34) | copy-start | bytes 147460
  3.9 12.4 %copy-start.12 = (bf16[48,512]{1,0:T(8,128)(2,1)S(1)}, bf16[48,512]{1,0:T(8,128)(2,1)}, u32[]{:S(2)}) copy-start(bf16[48,512]{1,0:T(8,128)(2,1)} %get-tuple-element.35) | copy-start | bytes 147460
  3.9 13.6 %copy-start.11 = (bf16[48,512]{1,0:T(8,128)(2,1)S(1)}, bf16[48,512]{1,0:T(8,128)(2,1)}, u32[]{:S(2)}) copy-start(bf16[48,512]{1,0:T(8,128)(2,1)} %get-tuple-element.36) | copy-start | bytes 147460
  3.9 48.3 %all-to-all-start = ((bf16[4,176,1024]{2,1,0:T(8,128)(2,1)}), bf16[4,176,1024]{2,1,0:T(8,128)(2,1)S(1)}, u32[]{:S(2)}, u32[]{:S(2)}) async-start(bf16[4,176,1024]{2,1,0:T(8,128)(2,1)} %get-tuple-element.29), calls=%async_computation | async-start | bytes 2883584 | tf_op jit(solution)/shard_map/all_to_all | solution.py:418
  9.3 30.6 %collective-permute-start = (bf16[256,512]{1,0:T(8,128)(2,1)S(1)}, bf16[256,512]{1,0:T(8,128)(2,1)S(1)}, u32[]{:S(2)}, u32[]{:S(2)}) collective-permute-start(bf16[256,512]{1,0:T(8,128)(2,1)S(1)} %copy-done.10), channel_id=1, source_target_pairs={{0,8},{8,0},{1,9},{9,1},{2,10},{10,2},{3,11},{11,3},{4,12},{12,4},... | collective-permute-start | bytes 786440 | tf_op jit(solution)/shard_map/ppermute | solution.py:420
  11.9 20.9 %collective-permute-start.1 = (bf16[48,512]{1,0:T(8,128)(2,1)S(1)}, bf16[48,512]{1,0:T(8,128)(2,1)S(1)}, u32[]{:S(2)}, u32[]{:S(2)}) collective-permute-start(bf16[48,512]{1,0:T(8,128)(2,1)S(1)} %copy-done.14), channel_id=1, source_target_pairs={{0,8},{2,10},{4,12},{6,14},{8,0},{10,2},{12,4},{14,6},{1,9},{3,11}... | collective-permute-start | bytes 147464 | tf_op jit(solution)/shard_map/ppermute | solution.py:415
  12.3 21.5 %collective-permute-start.2 = (bf16[48,512]{1,0:T(8,128)(2,1)S(1)}, bf16[48,512]{1,0:T(8,128)(2,1)S(1)}, u32[]{:S(2)}, u32[]{:S(2)}) collective-permute-start(bf16[48,512]{1,0:T(8,128)(2,1)S(1)} %copy-done.13), channel_id=1, source_target_pairs={{0,10},{2,8},{4,14},{6,12},{8,2},{10,0},{12,6},{14,4},{1,11},{3,9}... | collective-permute-start | bytes 147464 | tf_op jit(solution)/shard_map/ppermute | solution.py:415
  16.3 22.2 %collective-permute-start.3 = (bf16[48,512]{1,0:T(8,128)(2,1)S(1)}, bf16[48,512]{1,0:T(8,128)(2,1)S(1)}, u32[]{:S(2)}, u32[]{:S(2)}) collective-permute-start(bf16[48,512]{1,0:T(8,128)(2,1)S(1)} %copy-done.12), channel_id=1, source_target_pairs={{0,12},{2,14},{4,8},{6,10},{8,4},{10,6},{12,0},{14,2},{1,13},{3,15... | collective-permute-start | bytes 147464 | tf_op jit(solution)/shard_map/ppermute | solution.py:415
  17.5 23.9 %copy-start.9 = (bf16[256,512]{1,0:T(8,128)(2,1)S(1)}, bf16[256,512]{1,0:T(8,128)(2,1)}, u32[]{:S(2)}) copy-start(bf16[256,512]{1,0:T(8,128)(2,1)} %get-tuple-element.47) | copy-start | bytes 786436
  17.5 22.4 %collective-permute-start.4 = (bf16[48,512]{1,0:T(8,128)(2,1)S(1)}, bf16[48,512]{1,0:T(8,128)(2,1)S(1)}, u32[]{:S(2)}, u32[]{:S(2)}) collective-permute-start(bf16[48,512]{1,0:T(8,128)(2,1)S(1)} %copy-done.11), channel_id=1, source_target_pairs={{0,14},{2,12},{4,10},{6,8},{8,6},{10,4},{12,2},{14,0},{1,15},{3,13... | collective-permute-start | bytes 147464 | tf_op jit(solution)/shard_map/ppermute | solution.py:415
  39.9 12.3 %collective-permute-start.6 = (bf16[256,512]{1,0:T(8,128)(2,1)S(1)}, bf16[256,512]{1,0:T(8,128)(2,1)S(1)}, u32[]{:S(2)}, u32[]{:S(2)}) collective-permute-start(bf16[256,512]{1,0:T(8,128)(2,1)S(1)} %collective-permute-done.refs_0_), channel_id=1, source_target_pairs={{0,16},{16,0},{1,17},{17,1},{2,18},{18,2},{3,19},{19,3},{4,20},{20... | collective-permute-start | bytes 786440 | tf_op jit(solution)/shard_map/ppermute | solution.py:426
  41.4 10.8 %collective-permute-start.5 = (bf16[256,512]{1,0:T(8,128)(2,1)S(1)}, bf16[256,512]{1,0:T(8,128)(2,1)S(1)}, u32[]{:S(2)}, u32[]{:S(2)}) collective-permute-start(bf16[256,512]{1,0:T(8,128)(2,1)S(1)} %copy-done.9), channel_id=1, source_target_pairs={{0,8},{8,0},{1,9},{9,1},{2,10},{10,2},{3,11},{11,3},{4,12},{12,4},... | collective-permute-start | bytes 786440 | tf_op jit(solution)/shard_map/ppermute | solution.py:425
  41.5 16.0 %copy-start = (bf16[1024,512]{1,0:T(8,128)(2,1)S(1)}, bf16[1024,512]{1,0:T(8,128)(2,1)}, u32[]{:S(2)}) copy-start(bf16[1024,512]{1,0:T(8,128)(2,1)} %own_ref.1) | copy-start | bytes 3145732
  41.5 16.0 %copy-start.7 = (s32[16]{0:T(128)S(1)}, s32[16]{0:T(128)}, u32[]{:S(2)}) copy-start(s32[16]{0:T(128)} %position.1) | copy-start | bytes 196
  41.5 16.0 %copy-start.8 = (s32[16]{0:T(128)S(1)}, s32[16]{0:T(128)}, u32[]{:S(2)}) copy-start(s32[16]{0:T(128)} %adapter.1) | copy-start | bytes 196
  41.5 10.1 %collective-permute-start.7 = (bf16[4,48,512]{2,1,0:T(8,128)(2,1)S(1)}, bf16[4,48,512]{2,1,0:T(8,128)(2,1)S(1)}, u32[]{:S(2)}, u32[]{:S(2)}) collective-permute-start(bf16[4,48,512]{2,1,0:T(8,128)(2,1)S(1)} %pad_maximum_fusion.refs_0_), channel_id=1, source_target_pairs={{0,16},{16,0},{1,17},{17,1},{2,18},{18,2},{3,19},{19,3},{4,20},{20... | collective-permute-start | bytes 589832 | tf_op jit(solution)/shard_map/ppermute | solution.py:427
  51.6 0.7 copy-start.5
  52.3 5.2 %collective-permute-start.10 = (bf16[4,176,1024]{2,1,0:T(8,128)(2,1)S(1)}, bf16[4,176,1024]{2,1,0:T(8,128)(2,1)S(1)}, u32[]{:S(2)}, u32[]{:S(2)}) collective-permute-start(bf16[4,176,1024]{2,1,0:T(8,128)(2,1)S(1)} %all-to-all-done.refs_4_), channel_id=1, source_target_pairs={{0,1},{1,0},{2,3},{3,2},{4,5},{5,4},{6,7},{7,6},{8,9},{9,8},{10,11... | collective-permute-start | bytes 4325384 | tf_op jit(solution)/shard_map/ppermute | solution.py:436
  52.3 10.1 %collective-permute-start.11 = (bf16[256,512]{1,0:T(8,128)(2,1)S(1)}, bf16[256,512]{1,0:T(8,128)(2,1)S(1)}, u32[]{:S(2)}, u32[]{:S(2)}) collective-permute-start(bf16[256,512]{1,0:T(8,128)(2,1)S(1)} %collective-permute-done.5.refs_1_), channel_id=1, source_target_pairs={{0,16},{16,0},{1,17},{17,1},{2,18},{18,2},{3,19},{19,3},{4,20},{20... | collective-permute-start | bytes 786440 | tf_op jit(solution)/shard_map/ppermute | solution.py:433
  55.5 1.4 %collective-permute-start.8 = (bf16[4,48,512]{2,1,0:T(8,128)(2,1)S(1)}, bf16[4,48,512]{2,1,0:T(8,128)(2,1)S(1)}, u32[]{:S(2)}, u32[]{:S(2)}) collective-permute-start(bf16[4,48,512]{2,1,0:T(8,128)(2,1)S(1)} %pad_maximum_fusion.refs_0_), channel_id=1, source_target_pairs={{0,1},{1,0},{2,3},{3,2},{4,5},{5,4},{6,7},{7,6},{8,9},{9,8},{10,11... | collective-permute-start | bytes 589832 | tf_op jit(solution)/shard_map/ppermute | solution.py:435
  55.7 1.8 %collective-permute-start.9 = (bf16[4,48,512]{2,1,0:T(8,128)(2,1)}, bf16[4,48,512]{2,1,0:T(8,128)(2,1)S(1)}, u32[]{:S(2)}, u32[]{:S(2)}) collective-permute-start(bf16[4,48,512]{2,1,0:T(8,128)(2,1)} %copy-done.5), channel_id=1, source_target_pairs={{0,1},{1,0},{2,3},{3,2},{4,5},{5,4},{6,7},{7,6},{8,9},{9,8},{10,11... | collective-permute-start | bytes 589832 | tf_op jit(solution)/shard_map/ppermute | solution.py:435
  57.5 0.9 %copy-start.6 = (bf16[4,48,512]{2,1,0:T(8,128)(2,1)S(1)}, bf16[4,48,512]{2,1,0:T(8,128)(2,1)}, u32[]{:S(2)}) copy-start(bf16[4,48,512]{2,1,0:T(8,128)(2,1)} %copy-done.5) | copy-start | bytes 589828
  60.8 11.8 %copy-start.1 = (f32[64,4096]{1,0:T(8,128)S(1)}, f32[64,4096]{1,0:T(8,128)}, u32[]{:S(2)}) copy-start(f32[64,4096]{1,0:T(8,128)} %get-tuple-element.31.refs_0_) | copy-start | bytes 3145732
  60.8 11.8 %copy-start.2 = (f32[64,4096]{1,0:T(8,128)S(1)}, f32[64,4096]{1,0:T(8,128)}, u32[]{:S(2)}) copy-start(f32[64,4096]{1,0:T(8,128)} %get-tuple-element.44.refs_1_) | copy-start | bytes 3145732
  60.8 11.8 %copy-start.3 = (bf16[2048,64]{1,0:T(8,128)(2,1)S(1)}, bf16[2048,64]{1,0:T(8,128)(2,1)}, u32[]{:S(2)}) copy-start(bf16[2048,64]{1,0:T(8,128)(2,1)} %get-tuple-element.37.refs_2_) | copy-start | bytes 786436
  60.8 11.8 %copy-start.4 = (bf16[2048,64]{1,0:T(8,128)(2,1)S(1)}, bf16[2048,64]{1,0:T(8,128)(2,1)}, u32[]{:S(2)}) copy-start(bf16[2048,64]{1,0:T(8,128)(2,1)} %get-tuple-element.45.refs_3_) | copy-start | bytes 786436
  63.3 5.6 %collective-permute-start.12 = (bf16[128,512]{1,0:T(8,128)(2,1)S(1)}, bf16[128,512]{1,0:T(8,128)(2,1)S(1)}, u32[]{:S(2)}, u32[]{:S(2)}) collective-permute-start(bf16[128,512]{1,0:T(8,128)(2,1)S(1)} %get-tuple-element.53), channel_id=1, source_target_pairs={{0,2},{2,0},{4,6},{6,4},{1,3},{3,1},{5,7},{7,5},{8,10},{10,8},{12,... | collective-permute-start | bytes 393224 | tf_op jit(solution)/shard_map/ppermute | solution.py:411
  63.4 6.3 %collective-permute-start.13 = (bf16[128,512]{1,0:T(8,128)(2,1)S(1)}, bf16[128,512]{1,0:T(8,128)(2,1)S(1)}, u32[]{:S(2)}, u32[]{:S(2)}) collective-permute-start(bf16[128,512]{1,0:T(8,128)(2,1)S(1)} %get-tuple-element.54), channel_id=1, source_target_pairs={{0,4},{2,6},{4,0},{6,2},{1,5},{3,7},{5,1},{7,3},{8,12},{10,14},{12... | collective-permute-start | bytes 393224 | tf_op jit(solution)/shard_map/ppermute | solution.py:411
  64.4 8.2 %collective-permute-start.14 = (bf16[128,512]{1,0:T(8,128)(2,1)S(1)}, bf16[128,512]{1,0:T(8,128)(2,1)S(1)}, u32[]{:S(2)}, u32[]{:S(2)}) collective-permute-start(bf16[128,512]{1,0:T(8,128)(2,1)S(1)} %get-tuple-element.55), channel_id=1, source_target_pairs={{0,6},{2,4},{4,2},{6,0},{1,7},{3,5},{5,3},{7,1},{8,14},{10,12},{12... | collective-permute-start | bytes 393224 | tf_op jit(solution)/shard_map/ppermute | solution.py:411

commit v10 on v9

--- a/solution.py
+++ b/solution.py
@@ -141,33 +141,34 @@
     )(lengths, queries, fresh_keys, keys, values)
 
 
-def pack_kernel(x_hbm, d_hbm, u_hbm, w_hbm, tokens_out, *refs):
-    quads = tokens_out.shape[0]
-    maps_out, rows, sems = refs[:quads], refs[quads:-1], refs[-1]
+def pack_kernel(x_hbm, d_hbm, u_hbm, w_hbm, *refs):
+    quads = (len(refs) - 2) // 2
+    tokens_out, (early, late, sems) = refs[:quads], refs[-3:]
+    size = w_hbm.shape[0] // 2 - late.shape[0]
+    maps_out = [early.at[size:, :], *refs[quads:-3]]
     part, core, quad = lax.axis_index("parts") % 2, lax.axis_index("tensor"), lax.axis_index("quad")
     tokens, features = x_hbm.shape
     width, cols = w_hbm.shape
     ranks = d_hbm.shape[0]
-    step = maps_out[0].shape[1]
+    step = min(cols, width)
     mine = pl.ds(pl.multiple_of(part * RANK, RANK), RANK)
     copies = []
     for q, out in enumerate(maps_out):
         begin = core * features + (quad ^ q) * width
         for i, first in enumerate(range(0, width, step)):
             here = pl.ds(pl.multiple_of(begin + first, step), step)
-            copies.append((d_hbm.at[mine, here], out.at[i * RANK : (i + 1) * RANK, :]))
+            copies.append((d_hbm.at[mine, here], out.at[i * RANK : (i + 1) * RANK, :step]))
         for i, first in enumerate(range(0, cols, step)):
             row = width // step * RANK + i * RANK
-            copies.append((u_hbm.at[mine, first : first + step], out.at[row : row + RANK, :]))
+            copies.append((u_hbm.at[mine, first : first + step], out.at[row : row + RANK, :step]))
     begin = part * (width // 2)
-    for piece in rows:
-        size = piece.shape[0]
-        copies.append((w_hbm.at[pl.ds(pl.multiple_of(begin, RANK), size), :], piece))
-        begin = begin + size
-    for j in range(quads):
-        out = tokens_out.at[j]
-        copies.append((x_hbm.at[:, j * width : (j + 1) * width], out.at[:tokens, :]))
-        here = pl.ds(pl.multiple_of(core * features + j * width, width), width)
+    copies.append((w_hbm.at[pl.ds(pl.multiple_of(begin, RANK), size), :], early.at[:size, :]))
+    begin = begin + size
+    copies.append((w_hbm.at[pl.ds(pl.multiple_of(begin, RANK), late.shape[0]), :], late))
+    for q, out in enumerate(tokens_out):
+        here = pl.ds(pl.multiple_of((quad ^ q) * width, width), width)
+        copies.append((x_hbm.at[:, here], out.at[:tokens, :]))
+        here = pl.ds(pl.multiple_of(core * features + (quad ^ q) * width, width), width)
         copies.append((d_hbm.at[:, here], out.at[tokens : tokens + ranks, :]))
         for slot, first, row, col in up_places(cols, width):
             row += tokens + ranks
@@ -198,8 +199,9 @@
     kind = tokens.dtype
     pieces = (width + cols) // step
     first = width // 4
-    sizes = [(quads, tokens.shape[0] + ranks + RANK * (2 * cols // width), width)]
-    sizes += [(RANK * pieces, step)] * quads + [(first, cols), (width // 2 - first, cols)]
+    sizes = [(tokens.shape[0] + ranks + RANK * (2 * cols // width), width)] * quads
+    sizes += [(RANK * pieces, step)] * (quads - 1)
+    sizes += [(first + RANK * pieces, cols), (width // 2 - first, cols)]
     count = quads * (pieces + 2 + len(up_places(cols, width))) + 2
     return pl.pallas_call(
         pack_kernel,
@@ -246,13 +248,13 @@
     place = lax.broadcasted_iota(jnp.int32, (SPAN, us.shape[0]), 1)
     far = (place >= quads * ranks).astype(jnp.int32)
     index = place - far * (quads * ranks)
-    group = (wing ^ far) * quads + ((far * quad) ^ (index >> 5))
+    group = (wing ^ far) * quads + (quad ^ (index >> 5))
     which = 2 * group + (((index >> 4) & 1) ^ (far * part))
     spans = tokens // SPAN
     masked = []
     for q in range(quads):
         for i in range(spans):
-            slot = position[adapter[(wing * quads + q) * spans + i]]
+            slot = position[adapter[(wing * quads + (quad ^ q)) * spans + i]]
             row = (q * spans + i) * SPAN
             masked.append(jnp.where(which == slot, shrink[row : row + SPAN, :], 0.0))
     shrink = (jnp.concatenate(masked, axis=0) * ADAPTER_SCALE).astype(jnp.bfloat16)
@@ -290,19 +292,20 @@
 
 def far_kernel(tokens, quads, near, *refs):
     weights, (mine, theirs) = refs[:4], refs[4:6]
-    outs, (whole, total) = refs[6:-2], refs[-2:]
-    quad = lax.axis_index("quad")
+    outs, whole = refs[6:-1], refs[-1]
     part, core, wing = lax.axis_index("parts") % 2, lax.axis_index("tensor"), lax.axis_index("wing")
     for side in range(2):
         begin = (part if side == 0 else 1 - part) * (whole.shape[0] // 2)
-        for piece in weights[2 * side : 2 * side + 2]:
-            whole[pl.ds(pl.multiple_of(begin, RANK), piece.shape[0]), :] = piece[...]
-            begin = begin + piece.shape[0]
+        early, late = weights[2 * side : 2 * side + 2]
+        size = whole.shape[0] // 2 - late.shape[0]
+        whole[pl.ds(pl.multiple_of(begin, RANK), size), :] = early[:size, :]
+        whole[pl.ds(pl.multiple_of(begin + size, RANK), late.shape[0]), :] = late[...]
 
     def store(blocks):
         x = blocks[:, :tokens, :].reshape(near.shape[0], -1)
         product = (near[...] + dot(x, whole[...])).astype(jnp.bfloat16)
-        total[...] = product.reshape(total.shape)
+        for q, out in enumerate(outs):
+            out[...] = product[q * tokens : (q + 1) * tokens, :]
 
     @pl.when(core == wing)
     def _():
@@ -311,9 +314,6 @@
     @pl.when(core != wing)
     def _():
         store(mine)
-
-    for q, out in enumerate(outs):
-        out[...] = total[quad ^ q]
 
 
 def far_products(mine, theirs, near, weights, tokens):
@@ -325,10 +325,7 @@
         in_specs=[vmem] * (3 + len(weights)),
         out_specs=[vmem] * quads,
         out_shape=[jax.ShapeDtypeStruct((tokens, cols), jnp.bfloat16)] * quads,
-        scratch_shapes=[
-            pltpu.VMEM((width, cols), jnp.bfloat16),
-            pltpu.VMEM((quads, tokens, cols), jnp.bfloat16),
-        ],
+        scratch_shapes=[pltpu.VMEM((width, cols), jnp.bfloat16)],
         compiler_params=pltpu.CompilerParams(vmem_limit_bytes=48 * MIB if quads > 4 else 16 * MIB),
         cost_estimate=FREE,
         name="far_products",
@@ -414,22 +411,24 @@
         pairs = [(w * quads + j, (1 - w) * quads + (j ^ q)) for w in range(2) for j in range(quads)]
         return lax.ppermute(value, ("wing", "quad"), pairs)
 
-    message, *maps, early, late = pack(normed_inputs, downs, ups, value_matrix, quads)
-    mine = lax.all_to_all(message, "quad", 0, 0)
-    maps = [to_other_wing(each, q) for q, each in enumerate(maps)]
+    *blocks, early, late = pack(normed_inputs, downs, ups, value_matrix, quads)
+    mine = [to_quad(blocks[q], q) for q in range(1, quads)]
     early = lax.ppermute(early, "wing", SWAP)
-
-    attn = [attention(0, after(cache_length, message))]
+    maps = [to_other_wing(blocks[quads - 1 + q], q) for q in range(1, quads)]
+
+    attn = [attention(0, after(cache_length, blocks[0]))]
     early, *maps = lax.optimization_barrier((early, *maps, attn[0][1]))[:-1]
-    maps = jnp.stack(maps)
+    step = maps[0].shape[1]
+    maps = jnp.stack([early[early.shape[0] - maps[0].shape[0] :, :step], *maps])
     late = lax.ppermute(after(late, early), "wing", SWAP)
     early_other = lax.ppermute(early, "parts", parts_swap)
     maps_other = lax.ppermute(maps, "parts", parts_swap)
 
     attn.append(attention(1, after(cache_length, early, maps)))
-    late, mine, early_other, maps_other = lax.optimization_barrier(
-        (late, mine, early_other, maps_other, attn[1][1])
+    late, early_other, maps_other, *mine = lax.optimization_barrier(
+        (late, early_other, maps_other, *mine, attn[1][1])
     )[:-1]
+    mine = jnp.stack([blocks[0], *mine])
     late_other = lax.ppermute(late, "parts", parts_swap)
     maps_mine = (maps, maps_other)
     maps_theirs = [lax.ppermute(each, "tensor", SWAP) for each in maps_mine]

time: 74.4 us -> 72.3 us (0.972)
  waiting for transfers between devices: 18.6 us -> 24.2 us
  Pallas kernels: 28.5 us -> 23.4 us
  starting transfers between devices: 25 us -> 23.4 us
  local copies, waits for them, and re-layouts: 1.01 us -> 0.06 us
    ppermute x3 -> x6, waiting for transfers between devices: 5.76 us -> 13.9 us  [to_quad(): return lax.ppermute(value, 'quad', [(j, j ^ q) for j in range(quads)])]
    all_to_all x1 -> x0, starting transfers between devices: 5.39 us -> none  [on_device(): mine = lax.all_to_all(message, 'quad', 0, 0)]
    pallas_call x2, Pallas kernels: 20.6 us -> 15.6 us  [cache_attention(): pl.pallas_call(functools.partial(cache_kernel, span, first_head, kv_heads...]
    ppermute x3 -> x6, starting transfers between devices: 3.55 us -> 8.15 us  [to_quad(): return lax.ppermute(value, 'quad', [(j, j ^ q) for j in range(quads)])]
    ppermute x4 -> x3, waiting for transfers between devices: 9.2 us -> 6.08 us  [to_other_wing(): return lax.ppermute(value, ('wing', 'quad'), pairs)]
    ppermute x4 -> x3, starting transfers between devices: 7.65 us -> 4.9 us  [to_other_wing(): return lax.ppermute(value, ('wing', 'quad'), pairs)]
    ppermute x1, starting transfers between devices: 0.01 us -> 1.66 us  [on_device(): late = lax.ppermute(after(late, early), 'wing', SWAP)]
    ppermute x1, starting transfers between devices: 3.19 us -> 1.56 us  [on_device(): late_other = lax.ppermute(late, 'parts', parts_swap)]
  transfers between devices with their start and end apart: 16 -> 17, of which waited for: 11 -> 9; matrix products, arithmetic and copies ran while one was open for 0% -> 0% of each run, Pallas kernels for 31% -> 25%
where the time goes in v10:
time: 72.3 us; the launch traced here: 72.1 us
  waiting for transfers between devices  24.2 us (33%)
  Pallas kernels  23.4 us (32%)
  starting transfers between devices  23.4 us (32%)
  between operations  0.83 us (1%)
    pallas_call x2, Pallas kernels, cache_attention(): pl.pallas_call(functools.partial(cache_kernel, span, first_head, kv_heads...  15.6 us
    ppermute x6, waiting for transfers between devices, to_quad(): return lax.ppermute(value, 'quad', [(j, j ^ q) for j in range(quads)])  13.9 us
    ppermute x6, starting transfers between devices, to_quad(): return lax.ppermute(value, 'quad', [(j, j ^ q) for j in range(quads)])  8.15 us
    ppermute x3, waiting for transfers between devices, to_other_wing(): return lax.ppermute(value, ('wing', 'quad'), pairs)  6.08 us
    ppermute x3, starting transfers between devices, to_other_wing(): return lax.ppermute(value, ('wing', 'quad'), pairs)  4.9 us
    ppermute x1, starting transfers between devices, on_device(): early = lax.ppermute(early, 'wing', SWAP)  4.1 us
    pallas_call x1, Pallas kernels, pack(): pl.pallas_call(pack_kernel, in_specs=[hbm] * 4, out_specs=[vmem] * len(si...  3.23 us
    ppermute x1, waiting for transfers between devices, on_device(): late_other = lax.ppermute(late, 'parts', parts_swap)  2.5 us
  transfers between devices with their start and end apart: 17, of which 9 were waited for; matrix products, arithmetic and copies ran while one was open for 0% of the time, Pallas kernels for 25%

profile of v10, /device:TPU:0, one launch (start us, length us, event | category | flops | bytes accessed | tf_op | source)
XLA Modules:
  0.0 72.1 jit_solution(12235734572642131976)
XLA Ops:
  0.6 3.2 %pack.1 = (bf16[176,1024]{1,0:T(8,128)(2,1)}, bf16[176,1024]{1,0:T(8,128)(2,1)}, bf16[176,1024]{1,0:T(8,128)(2,1)}, bf16[176,1024]{1,0:T(8,128)(2,1)}, bf16[48,5...) custom-call(bf16[128,4096]{1,0:T(8,128)(2,1)} %x_hbm.1, ...), custom_call_target="tpu_custom_call" | custom-call | flops 1 | bytes 1 | tf_op jit(solution)/shard_map/pack/pallas_call | solution.py:206
  3.9 4.1 %collective-permute-start = (bf16[304,512]{1,0:T(8,128)(2,1)}, bf16[304,512]{1,0:T(8,128)(2,1)S(1)}, u32[]{:S(2)}, u32[]{:S(2)}) collective-permute-start(bf16[304,512]{1,0:T(8,128)(2,1)} %get-tuple-element.35), channel_id=1, source_target_pairs={{0,8},{8,0},{1,9},{9,1},{2,10},{10,2},{3,11},{11,3},{4,12},{12,4},... | collective-permute-start | bytes 933896 | tf_op jit(solution)/shard_map/ppermute | solution.py:416
  8.0 1.3 %collective-permute-start.1 = (bf16[48,512]{1,0:T(8,128)(2,1)}, bf16[48,512]{1,0:T(8,128)(2,1)S(1)}, u32[]{:S(2)}, u32[]{:S(2)}) collective-permute-start(bf16[48,512]{1,0:T(8,128)(2,1)} %get-tuple-element.36), channel_id=1, source_target_pairs={{0,10},{2,8},{4,14},{6,12},{8,2},{10,0},{12,6},{14,4},{1,11},{3,9}... | collective-permute-start | bytes 147464 | tf_op jit(solution)/shard_map/ppermute | solution.py:412
  9.3 3.6 %collective-permute-start.2 = (bf16[48,512]{1,0:T(8,128)(2,1)}, bf16[48,512]{1,0:T(8,128)(2,1)S(1)}, u32[]{:S(2)}, u32[]{:S(2)}) collective-permute-start(bf16[48,512]{1,0:T(8,128)(2,1)} %get-tuple-element.37), channel_id=1, source_target_pairs={{0,12},{2,14},{4,8},{6,10},{8,4},{10,6},{12,0},{14,2},{1,13},{3,15... | collective-permute-start | bytes 147464 | tf_op jit(solution)/shard_map/ppermute | solution.py:412
  12.9 0.0 collective-permute-start.3
  12.9 1.7 %collective-permute-start.7 = (bf16[176,1024]{1,0:T(8,128)(2,1)}, bf16[176,1024]{1,0:T(8,128)(2,1)S(1)}, u32[]{:S(2)}, u32[]{:S(2)}) collective-permute-start(bf16[176,1024]{1,0:T(8,128)(2,1)} %get-tuple-element.49), channel_id=1, source_target_pairs={{0,2},{2,0},{4,6},{6,4},{1,3},{3,1},{5,7},{7,5},{8,10},{10,8},{12,... | collective-permute-start | bytes 1081352 | tf_op jit(solution)/shard_map/ppermute | solution.py:408
  14.6 7.8 %cache_attention.2 = (f32[64,4096]{1,0:T(8,128)}, bf16[2048,64]{1,0:T(8,128)(2,1)}) custom-call(s32[2]{0:T(128)} %lens.1, bf16[128,4096]{1,0:T(8,128)(2,1)} %q_ref.3, bf16[128,512]{1,0:T(8,128)(2,1)} %fk_ref.3, bf16[2,2048,512]{2,1,0:T(8,128)(2,1)} %k_hbm.3, bf16[2,2048,512]{2,1,0:T(8,128)(2,1)} %v_hbm.3), custom_call_target="tpu_custom_call" | custom-call | flops 1 | bytes 1 | tf_op jit(solution)/shard_map/cache_attention/pallas_call | solution.py:118
  22.4 6.1 %collective-permute-done.1 = bf16[48,512]{1,0:T(8,128)(2,1)S(1)} collective-permute-done((bf16[48,512]{1,0:T(8,128)(2,1)}, bf16[48,512]{1,0:T(8,128)(2,1)S(1)}, u32[]{:S(2)}, u32[]{:S(2)}) %collective-permute-start.1) | collective-permute-done | bytes 49184 | tf_op jit(solution)/shard_map/ppermute | solution.py:412
  28.5 0.0 copy-done.9
  28.5 0.0 collective-permute-start.8
  28.5 0.0 collective-permute-done.2
  28.5 1.7 %collective-permute-start.9 = (bf16[176,1024]{1,0:T(8,128)(2,1)S(1)}, bf16[176,1024]{1,0:T(8,128)(2,1)S(1)}, u32[]{:S(2)}, u32[]{:S(2)}) collective-permute-start(bf16[176,1024]{1,0:T(8,128)(2,1)S(1)} %copy-done.8), channel_id=1, source_target_pairs={{0,6},{2,4},{4,2},{6,0},{1,7},{3,5},{5,3},{7,1},{8,14},{10,12},{12... | collective-permute-start | bytes 1081352 | tf_op jit(solution)/shard_map/ppermute | solution.py:408
  30.2 0.0 collective-permute-done.3
  30.2 0.0 collective-permute-done.refs_0_
  30.2 1.8 %collective-permute-start.5 = (bf16[304,512]{1,0:T(8,128)(2,1)S(1)}, bf16[304,512]{1,0:T(8,128)(2,1)S(1)}, u32[]{:S(2)}, u32[]{:S(2)}) collective-permute-start(bf16[304,512]{1,0:T(8,128)(2,1)S(1)} %collective-permute-done.refs_0_), channel_id=1, source_target_pairs={{0,16},{16,0},{1,17},{17,1},{2,18},{18,2},{3,19},{19,3},{4,20},{20... | collective-permute-start | bytes 933896 | tf_op jit(solution)/shard_map/ppermute | solution.py:424
  32.0 0.0 copy-done.10
  32.0 1.7 %collective-permute-start.4 = (bf16[256,512]{1,0:T(8,128)(2,1)S(1)}, bf16[256,512]{1,0:T(8,128)(2,1)S(1)}, u32[]{:S(2)}, u32[]{:S(2)}) collective-permute-start(bf16[256,512]{1,0:T(8,128)(2,1)S(1)} %copy-done.10), channel_id=1, source_target_pairs={{0,8},{8,0},{1,9},{9,1},{2,10},{10,2},{3,11},{11,3},{4,12},{12,4},... | collective-permute-start | bytes 786440 | tf_op jit(solution)/shard_map/ppermute | solution.py:423
  33.7 0.0 copy-start.7
  33.7 0.0 collective-permute-done.7
  33.7 0.6 collective-permute-start.6
  34.3 7.8 %cache_attention.3 = (f32[64,4096]{1,0:T(8,128)}, bf16[2048,64]{1,0:T(8,128)(2,1)}) custom-call(s32[2]{0:T(128)} %lens.1, bf16[128,4096]{1,0:T(8,128)(2,1)} %q_ref.3, bf16[128,512]{1,0:T(8,128)(2,1)} %fk_ref.3, bf16[2,2048,512]{2,1,0:T(8,128)(2,1)} %k_hbm.3, bf16[2,2048,512]{2,1,0:T(8,128)(2,1)} %v_hbm.3), custom_call_target="tpu_custom_call" | custom-call | flops 1 | bytes 1 | tf_op jit(solution)/shard_map/cache_attention/pallas_call | solution.py:118
  42.1 3.3 %collective-permute-done.8 = bf16[176,1024]{1,0:T(8,128)(2,1)S(1)} collective-permute-done((bf16[176,1024]{1,0:T(8,128)(2,1)S(1)}, bf16[176,1024]{1,0:T(8,128)(2,1)S(1)}, u32[]{:S(2)}, u32[]{:S(2)}) %collective-permute-start.8) | collective-permute-done | bytes 360480 | tf_op jit(solution)/shard_map/ppermute | solution.py:408
  45.5 4.7 %collective-permute-done.9 = bf16[176,1024]{1,0:T(8,128)(2,1)S(1)} collective-permute-done((bf16[176,1024]{1,0:T(8,128)(2,1)S(1)}, bf16[176,1024]{1,0:T(8,128)(2,1)S(1)}, u32[]{:S(2)}, u32[]{:S(2)}) %collective-permute-start.9) | collective-permute-done | bytes 360480 | tf_op jit(solution)/shard_map/ppermute | solution.py:408
  50.1 0.0 collective-permute-done.6.refs_1_
  50.1 0.0 collective-permute-done.4.refs_1_
  50.1 0.0 collective-permute-done.5.refs_2_
  50.2 0.0 copy-start
  50.2 0.0 copy-start.5
  50.2 0.0 copy-start.6
  50.2 0.2 pad_maximum_fusion.refs_4_
  50.4 0.1 collective-permute-start.12
  50.5 1.6 %collective-permute-start.13 = (bf16[256,512]{1,0:T(8,128)(2,1)S(1)}, bf16[256,512]{1,0:T(8,128)(2,1)S(1)}, u32[]{:S(2)}, u32[]{:S(2)}) collective-permute-start(bf16[256,512]{1,0:T(8,128)(2,1)S(1)} %collective-permute-done.4.refs_1_), channel_id=1, source_target_pairs={{0,16},{16,0},{1,17},{17,1},{2,18},{18,2},{3,19},{19,3},{4,20},{20... | collective-permute-start | bytes 786440 | tf_op jit(solution)/shard_map/ppermute | solution.py:432
  52.0 0.2 collective-permute-start.10
  52.2 0.3 collective-permute-start.11
  52.5 1.4 %collective-permute-done.10.refs_2_ = bf16[4,48,512]{2,1,0:T(8,128)(2,1)S(1)} collective-permute-done((bf16[4,48,512]{2,1,0:T(8,128)(2,1)S(1)}, bf16[4,48,512]{2,1,0:T(8,128)(2,1)S(1)}, u32[]{:S(2)}, u32[]{:S(2)}) %collective-permute-start.10) | collective-permute-done | bytes 196640 | tf_op jit(solution)/shard_map/ppermute | solution.py:434
  54.0 0.3 collective-permute-done.11.refs_3_
  54.2 0.0 collective-permute-done.12.refs_5_
  54.3 2.4 %near_products.1.near = f32[512,512]{1,0:T(8,128)S(1)} custom-call(s32[16]{0:T(128)S(1)} %copy-done.5, s32[16]{0:T(128)S(1)} %copy-done.6, bf16[1024,512]{1,0:T(8,128)(2,1)S(1)} %copy-done, bf16[4,48,512]{2,1,0:T(8,128)(2,1)S(1)} %pad_maximum_fusion.1.refs_0_, bf16[4,48,512]{2,1,0:T(8,128)(2,1)S(1)} %collective-permute-done.6.refs_1_, ...), custom_call_target="tpu_custom_call" | custom-call | flops 1 | bytes 1 | tf_op jit(solution)/shard_map/near_products/pallas_call | solution.py:278
  56.6 0.0 copy-start.1
  56.7 2.5 %collective-permute-done.13.refs_3_ = bf16[256,512]{1,0:T(8,128)(2,1)S(1)} collective-permute-done((bf16[256,512]{1,0:T(8,128)(2,1)S(1)}, bf16[256,512]{1,0:T(8,128)(2,1)S(1)}, u32[]{:S(2)}, u32[]{:S(2)}) %collective-permute-start.13) | collective-permute-done | bytes 262176 | tf_op jit(solution)/shard_map/ppermute | solution.py:432
  59.2 0.8 %far_products.1 = (bf16[128,512]{1,0:T(8,128)(2,1)S(1)}, bf16[128,512]{1,0:T(8,128)(2,1)S(1)}, bf16[128,512]{1,0:T(8,128)(2,1)S(1)}, bf16[128,512]{1,0:T(8,128)(2,1)S(1)}) custom-call(f32[512,512]{1,0:T(8,128)S(1)} %near_products.1.near, bf16[304,512]{1,0:T(8,128)(2,1)S(1)} %collective-permute-done.refs_0_, ...), custom_call_target="tpu_custom_call" | custom-call | flops 1 | bytes 1 | tf_op jit(solution)/shard_map/far_products/pallas_call | solution.py:323
  60.0 1.2 %collective-permute-start.14 = (bf16[128,512]{1,0:T(8,128)(2,1)S(1)}, bf16[128,512]{1,0:T(8,128)(2,1)S(1)}, u32[]{:S(2)}, u32[]{:S(2)}) collective-permute-start(bf16[128,512]{1,0:T(8,128)(2,1)S(1)} %get-tuple-element.59), channel_id=1, source_target_pairs={{0,2},{2,0},{4,6},{6,4},{1,3},{3,1},{5,7},{7,5},{8,10},{10,8},{12,... | collective-permute-start | bytes 393224 | tf_op jit(solution)/shard_map/ppermute | solution.py:408
  61.2 2.7 %collective-permute-start.15 = (bf16[128,512]{1,0:T(8,128)(2,1)S(1)}, bf16[128,512]{1,0:T(8,128)(2,1)S(1)}, u32[]{:S(2)}, u32[]{:S(2)}) collective-permute-start(bf16[128,512]{1,0:T(8,128)(2,1)S(1)} %get-tuple-element.60), channel_id=1, source_target_pairs={{0,4},{2,6},{4,0},{6,2},{1,5},{3,7},{5,1},{7,3},{8,12},{10,14},{12... | collective-permute-start | bytes 393224 | tf_op jit(solution)/shard_map/ppermute | solution.py:408
  63.8 1.0 %collective-permute-start.16 = (bf16[128,512]{1,0:T(8,128)(2,1)S(1)}, bf16[128,512]{1,0:T(8,128)(2,1)S(1)}, u32[]{:S(2)}, u32[]{:S(2)}) collective-permute-start(bf16[128,512]{1,0:T(8,128)(2,1)S(1)} %get-tuple-element.61), channel_id=1, source_target_pairs={{0,6},{2,4},{4,2},{6,0},{1,7},{3,5},{5,3},{7,1},{8,14},{10,12},{12... | collective-permute-start | bytes 393224 | tf_op jit(solution)/shard_map/ppermute | solution.py:408
  64.8 0.3 collective-permute-done.14.refs_5_
  65.1 2.4 %collective-permute-done.15.refs_6_ = bf16[128,512]{1,0:T(8,128)(2,1)S(1)} collective-permute-done((bf16[128,512]{1,0:T(8,128)(2,1)S(1)}, bf16[128,512]{1,0:T(8,128)(2,1)S(1)}, u32[]{:S(2)}, u32[]{:S(2)}) %collective-permute-start.15) | collective-permute-done | bytes 131104 | tf_op jit(solution)/shard_map/ppermute | solution.py:408
  67.5 3.1 %collective-permute-done.16.refs_7_ = bf16[128,512]{1,0:T(8,128)(2,1)S(1)} collective-permute-done((bf16[128,512]{1,0:T(8,128)(2,1)S(1)}, bf16[128,512]{1,0:T(8,128)(2,1)S(1)}, u32[]{:S(2)}, u32[]{:S(2)}) %collective-permute-start.16) | collective-permute-done | bytes 131104 | tf_op jit(solution)/shard_map/ppermute | solution.py:408
  70.6 1.4 %finish_attention.1 = (bf16[128,4096]{1,0:T(8,128)(2,1)}, bf16[128,512]{1,0:T(8,128)(2,1)}) custom-call(f32[64,4096]{1,0:T(8,128)S(1)} %copy-done.1, f32[64,4096]{1,0:T(8,128)S(1)} %copy-done.2, bf16[2048,64]{1,0:T(8,128)(2,1)S(1)} %copy-done.3, bf16[2048,64]{1,0:T(8,128)(2,1)S(1)} %copy-done.4, bf16[128,512]{1,0:T(8,128)(2,1)S(1)} %get-tuple-element.58.refs_4_, ...), custom_call_target="tpu_custom_call" | custom-call | flops 1 | bytes 1 | tf_op jit(solution)/shard_map/finish_attention/pallas_call | solution.py:362
  (17 shorter events, 0.1 us)
Async XLA Ops:
  3.9 26.3 %collective-permute-start = (bf16[304,512]{1,0:T(8,128)(2,1)}, bf16[304,512]{1,0:T(8,128)(2,1)S(1)}, u32[]{:S(2)}, u32[]{:S(2)}) collective-permute-start(bf16[304,512]{1,0:T(8,128)(2,1)} %get-tuple-element.35), channel_id=1, source_target_pairs={{0,8},{8,0},{1,9},{9,1},{2,10},{10,2},{3,11},{11,3},{4,12},{12,4},... | collective-permute-start | bytes 933896 | tf_op jit(solution)/shard_map/ppermute | solution.py:416
  8.0 20.5 %collective-permute-start.1 = (bf16[48,512]{1,0:T(8,128)(2,1)}, bf16[48,512]{1,0:T(8,128)(2,1)S(1)}, u32[]{:S(2)}, u32[]{:S(2)}) collective-permute-start(bf16[48,512]{1,0:T(8,128)(2,1)} %get-tuple-element.36), channel_id=1, source_target_pairs={{0,10},{2,8},{4,14},{6,12},{8,2},{10,0},{12,6},{14,4},{1,11},{3,9}... | collective-permute-start | bytes 147464 | tf_op jit(solution)/shard_map/ppermute | solution.py:412
  9.3 19.2 %collective-permute-start.2 = (bf16[48,512]{1,0:T(8,128)(2,1)}, bf16[48,512]{1,0:T(8,128)(2,1)S(1)}, u32[]{:S(2)}, u32[]{:S(2)}) collective-permute-start(bf16[48,512]{1,0:T(8,128)(2,1)} %get-tuple-element.37), channel_id=1, source_target_pairs={{0,12},{2,14},{4,8},{6,10},{8,4},{10,6},{12,0},{14,2},{1,13},{3,15... | collective-permute-start | bytes 147464 | tf_op jit(solution)/shard_map/ppermute | solution.py:412
  12.9 17.3 %collective-permute-start.3 = (bf16[48,512]{1,0:T(8,128)(2,1)}, bf16[48,512]{1,0:T(8,128)(2,1)S(1)}, u32[]{:S(2)}, u32[]{:S(2)}) collective-permute-start(bf16[48,512]{1,0:T(8,128)(2,1)} %get-tuple-element.38), channel_id=1, source_target_pairs={{0,14},{2,12},{4,10},{6,8},{8,6},{10,4},{12,2},{14,0},{1,15},{3,13... | collective-permute-start | bytes 147464 | tf_op jit(solution)/shard_map/ppermute | solution.py:412
  12.9 20.9 %collective-permute-start.7 = (bf16[176,1024]{1,0:T(8,128)(2,1)}, bf16[176,1024]{1,0:T(8,128)(2,1)S(1)}, u32[]{:S(2)}, u32[]{:S(2)}) collective-permute-start(bf16[176,1024]{1,0:T(8,128)(2,1)} %get-tuple-element.49), channel_id=1, source_target_pairs={{0,2},{2,0},{4,6},{6,4},{1,3},{3,1},{5,7},{7,5},{8,10},{10,8},{12,... | collective-permute-start | bytes 1081352 | tf_op jit(solution)/shard_map/ppermute | solution.py:408
  14.5 13.9 %copy-start.9 = (bf16[176,1024]{1,0:T(8,128)(2,1)S(1)}, bf16[176,1024]{1,0:T(8,128)(2,1)}, u32[]{:S(2)}) copy-start(bf16[176,1024]{1,0:T(8,128)(2,1)} %get-tuple-element.50) | copy-start | bytes 1081348
  14.5 13.9 %copy-start.8 = (bf16[176,1024]{1,0:T(8,128)(2,1)S(1)}, bf16[176,1024]{1,0:T(8,128)(2,1)}, u32[]{:S(2)}) copy-start(bf16[176,1024]{1,0:T(8,128)(2,1)} %get-tuple-element.51) | copy-start | bytes 1081348
  14.5 17.5 %copy-start.10 = (bf16[256,512]{1,0:T(8,128)(2,1)S(1)}, bf16[256,512]{1,0:T(8,128)(2,1)}, u32[]{:S(2)}) copy-start(bf16[256,512]{1,0:T(8,128)(2,1)} %get-tuple-element.48) | copy-start | bytes 786436
  28.5 17.0 %collective-permute-start.8 = (bf16[176,1024]{1,0:T(8,128)(2,1)S(1)}, bf16[176,1024]{1,0:T(8,128)(2,1)S(1)}, u32[]{:S(2)}, u32[]{:S(2)}) collective-permute-start(bf16[176,1024]{1,0:T(8,128)(2,1)S(1)} %copy-done.9), channel_id=1, source_target_pairs={{0,4},{2,6},{4,0},{6,2},{1,5},{3,7},{5,1},{7,3},{8,12},{10,14},{12... | collective-permute-start | bytes 1081352 | tf_op jit(solution)/shard_map/ppermute | solution.py:408
  28.5 21.6 %collective-permute-start.9 = (bf16[176,1024]{1,0:T(8,128)(2,1)S(1)}, bf16[176,1024]{1,0:T(8,128)(2,1)S(1)}, u32[]{:S(2)}, u32[]{:S(2)}) collective-permute-start(bf16[176,1024]{1,0:T(8,128)(2,1)S(1)} %copy-done.8), channel_id=1, source_target_pairs={{0,6},{2,4},{4,2},{6,0},{1,7},{3,5},{5,3},{7,1},{8,14},{10,12},{12... | collective-permute-start | bytes 1081352 | tf_op jit(solution)/shard_map/ppermute | solution.py:408
  30.2 20.0 %collective-permute-start.5 = (bf16[304,512]{1,0:T(8,128)(2,1)S(1)}, bf16[304,512]{1,0:T(8,128)(2,1)S(1)}, u32[]{:S(2)}, u32[]{:S(2)}) collective-permute-start(bf16[304,512]{1,0:T(8,128)(2,1)S(1)} %collective-permute-done.refs_0_), channel_id=1, source_target_pairs={{0,16},{16,0},{1,17},{17,1},{2,18},{18,2},{3,19},{19,3},{4,20},{20... | collective-permute-start | bytes 933896 | tf_op jit(solution)/shard_map/ppermute | solution.py:424
  32.0 18.1 %collective-permute-start.4 = (bf16[256,512]{1,0:T(8,128)(2,1)S(1)}, bf16[256,512]{1,0:T(8,128)(2,1)S(1)}, u32[]{:S(2)}, u32[]{:S(2)}) collective-permute-start(bf16[256,512]{1,0:T(8,128)(2,1)S(1)} %copy-done.10), channel_id=1, source_target_pairs={{0,8},{8,0},{1,9},{9,1},{2,10},{10,2},{3,11},{11,3},{4,12},{12,4},... | collective-permute-start | bytes 786440 | tf_op jit(solution)/shard_map/ppermute | solution.py:423
  33.7 16.4 %copy-start.7 = (bf16[176,1024]{1,0:T(8,128)(2,1)S(1)}, bf16[176,1024]{1,0:T(8,128)(2,1)}, u32[]{:S(2)}) copy-start(bf16[176,1024]{1,0:T(8,128)(2,1)} %get-tuple-element.32) | copy-start | bytes 1081348
  33.7 16.4 %collective-permute-start.6 = (bf16[4,48,512]{2,1,0:T(8,128)(2,1)S(1)}, bf16[4,48,512]{2,1,0:T(8,128)(2,1)S(1)}, u32[]{:S(2)}, u32[]{:S(2)}) collective-permute-start(bf16[4,48,512]{2,1,0:T(8,128)(2,1)S(1)} %pad_maximum_fusion.1.refs_0_), channel_id=1, source_target_pairs={{0,16},{16,0},{1,17},{17,1},{2,18},{18,2},{3,19},{19,3},{4,20},{20... | collective-permute-start | bytes 589832 | tf_op jit(solution)/shard_map/ppermute | solution.py:425
  50.2 4.1 %copy-start = (bf16[1024,512]{1,0:T(8,128)(2,1)S(1)}, bf16[1024,512]{1,0:T(8,128)(2,1)}, u32[]{:S(2)}) copy-start(bf16[1024,512]{1,0:T(8,128)(2,1)} %own_ref.1) | copy-start | bytes 3145732
  50.2 4.1 %copy-start.5 = (s32[16]{0:T(128)S(1)}, s32[16]{0:T(128)}, u32[]{:S(2)}) copy-start(s32[16]{0:T(128)} %position.1) | copy-start | bytes 196
  50.2 4.1 %copy-start.6 = (s32[16]{0:T(128)S(1)}, s32[16]{0:T(128)}, u32[]{:S(2)}) copy-start(s32[16]{0:T(128)} %adapter.1) | copy-start | bytes 196
  50.4 3.9 %collective-permute-start.12 = (bf16[4,176,1024]{2,1,0:T(8,128)(2,1)S(1)}, bf16[4,176,1024]{2,1,0:T(8,128)(2,1)S(1)}, u32[]{:S(2)}, u32[]{:S(2)}) collective-permute-start(bf16[4,176,1024]{2,1,0:T(8,128)(2,1)S(1)} %pad_maximum_fusion.refs_4_), channel_id=1, source_target_pairs={{0,1},{1,0},{2,3},{3,2},{4,5},{5,4},{6,7},{7,6},{8,9},{9,8},{10,11... | collective-permute-start | bytes 4325384 | tf_op jit(solution)/shard_map/ppermute | solution.py:435
  50.5 8.7 %collective-permute-start.13 = (bf16[256,512]{1,0:T(8,128)(2,1)S(1)}, bf16[256,512]{1,0:T(8,128)(2,1)S(1)}, u32[]{:S(2)}, u32[]{:S(2)}) collective-permute-start(bf16[256,512]{1,0:T(8,128)(2,1)S(1)} %collective-permute-done.4.refs_1_), channel_id=1, source_target_pairs={{0,16},{16,0},{1,17},{17,1},{2,18},{18,2},{3,19},{19,3},{4,20},{20... | collective-permute-start | bytes 786440 | tf_op jit(solution)/shard_map/ppermute | solution.py:432
  52.0 1.9 %collective-permute-start.10 = (bf16[4,48,512]{2,1,0:T(8,128)(2,1)S(1)}, bf16[4,48,512]{2,1,0:T(8,128)(2,1)S(1)}, u32[]{:S(2)}, u32[]{:S(2)}) collective-permute-start(bf16[4,48,512]{2,1,0:T(8,128)(2,1)S(1)} %pad_maximum_fusion.1.refs_0_), channel_id=1, source_target_pairs={{0,1},{1,0},{2,3},{3,2},{4,5},{5,4},{6,7},{7,6},{8,9},{9,8},{10,11... | collective-permute-start | bytes 589832 | tf_op jit(solution)/shard_map/ppermute | solution.py:434
  52.2 2.0 %collective-permute-start.11 = (bf16[4,48,512]{2,1,0:T(8,128)(2,1)S(1)}, bf16[4,48,512]{2,1,0:T(8,128)(2,1)S(1)}, u32[]{:S(2)}, u32[]{:S(2)}) collective-permute-start(bf16[4,48,512]{2,1,0:T(8,128)(2,1)S(1)} %collective-permute-done.6.refs_1_), channel_id=1, source_target_pairs={{0,1},{1,0},{2,3},{3,2},{4,5},{5,4},{6,7},{7,6},{8,9},{9,8},{10,11... | collective-permute-start | bytes 589832 | tf_op jit(solution)/shard_map/ppermute | solution.py:434
  56.6 14.0 %copy-start.1 = (f32[64,4096]{1,0:T(8,128)S(1)}, f32[64,4096]{1,0:T(8,128)}, u32[]{:S(2)}) copy-start(f32[64,4096]{1,0:T(8,128)} %get-tuple-element.34.refs_0_) | copy-start | bytes 3145732
  56.7 14.0 %copy-start.2 = (f32[64,4096]{1,0:T(8,128)S(1)}, f32[64,4096]{1,0:T(8,128)}, u32[]{:S(2)}) copy-start(f32[64,4096]{1,0:T(8,128)} %get-tuple-element.45.refs_1_) | copy-start | bytes 3145732
  56.7 14.0 %copy-start.3 = (bf16[2048,64]{1,0:T(8,128)(2,1)S(1)}, bf16[2048,64]{1,0:T(8,128)(2,1)}, u32[]{:S(2)}) copy-start(bf16[2048,64]{1,0:T(8,128)(2,1)} %get-tuple-element.39.refs_2_) | copy-start | bytes 786436
  56.7 14.0 %copy-start.4 = (bf16[2048,64]{1,0:T(8,128)(2,1)S(1)}, bf16[2048,64]{1,0:T(8,128)(2,1)}, u32[]{:S(2)}) copy-start(bf16[2048,64]{1,0:T(8,128)(2,1)} %get-tuple-element.46.refs_3_) | copy-start | bytes 786436
  60.0 5.1 %collective-permute-start.14 = (bf16[128,512]{1,0:T(8,128)(2,1)S(1)}, bf16[128,512]{1,0:T(8,128)(2,1)S(1)}, u32[]{:S(2)}, u32[]{:S(2)}) collective-permute-start(bf16[128,512]{1,0:T(8,128)(2,1)S(1)} %get-tuple-element.59), channel_id=1, source_target_pairs={{0,2},{2,0},{4,6},{6,4},{1,3},{3,1},{5,7},{7,5},{8,10},{10,8},{12,... | collective-permute-start | bytes 393224 | tf_op jit(solution)/shard_map/ppermute | solution.py:408
  61.2 6.4 %collective-permute-start.15 = (bf16[128,512]{1,0:T(8,128)(2,1)S(1)}, bf16[128,512]{1,0:T(8,128)(2,1)S(1)}, u32[]{:S(2)}, u32[]{:S(2)}) collective-permute-start(bf16[128,512]{1,0:T(8,128)(2,1)S(1)} %get-tuple-element.60), channel_id=1, source_target_pairs={{0,4},{2,6},{4,0},{6,2},{1,5},{3,7},{5,1},{7,3},{8,12},{10,14},{12... | collective-permute-start | bytes 393224 | tf_op jit(solution)/shard_map/ppermute | solution.py:408
  63.8 6.8 %collective-permute-start.16 = (bf16[128,512]{1,0:T(8,128)(2,1)S(1)}, bf16[128,512]{1,0:T(8,128)(2,1)S(1)}, u32[]{:S(2)}, u32[]{:S(2)}) collective-permute-start(bf16[128,512]{1,0:T(8,128)(2,1)S(1)} %get-tuple-element.61), channel_id=1, source_target_pairs={{0,6},{2,4},{4,2},{6,0},{1,7},{3,5},{5,3},{7,1},{8,14},{10,12},{12... | collective-permute-start | bytes 393224 | tf_op jit(solution)/shard_map/ppermute | solution.py:408

commit v11 on v10

--- a/solution.py
+++ b/solution.py
@@ -14,6 +14,7 @@
 SPAN = 64
 CHUNK = 512
 ONES = 16
+TILE = 128
 ADAPTER_SCALE = 2.0
 EXP2_SCALE = math.log2(math.e) / math.sqrt(HD)
 DEAD = -1e30
@@ -30,17 +31,18 @@
     return jnp.dot(a, b, preferred_element_type=jnp.float32)
 
 
-def cache_kernel(span, first_head, kv_heads, group_size, lens, q_ref, fk_ref, k_hbm, v_hbm, out_ref, pf_ref, qs, ks, vs, m_s, acc, sems):
+def cache_kernel(span, lens, q_ref, fk_ref, k_hbm, v_hbm, out_ref, pf_ref, qs, ks, vs, live, s_s, p_s, x_s, m_s, a_s, acc, sems):
     length = lens[span]
-    rows = group_size * SPAN
-    chunks, chunk, width = ks.shape
-    heads = slice(first_head * HD, first_head * HD + width)
+    chunks, chunk, _ = ks.shape
+    kv_heads, rows, _ = qs.shape
+    group_size = rows // SPAN
+    count = (length + chunk - 1) // chunk
 
     def copies(i):
-        live = pl.ds(pl.multiple_of(i * chunk, chunk), chunk)
+        slots = pl.ds(pl.multiple_of(i * chunk, chunk), chunk)
         return (
-            pltpu.make_async_copy(k_hbm.at[span, live, heads], ks.at[i], sems.at[0, i]),
-            pltpu.make_async_copy(v_hbm.at[span, live, heads], vs.at[i], sems.at[1, i]),
+            pltpu.make_async_copy(k_hbm.at[span, slots, :], ks.at[i], sems.at[0, i]),
+            pltpu.make_async_copy(v_hbm.at[span, slots, :], vs.at[i], sems.at[1, i]),
         )
 
     for i in range(chunks):
@@ -50,51 +52,78 @@
             for copy in copies(i):
                 copy.start()
 
+    def arrive(i):
+        for copy in copies(i):
+            copy.wait()
+        slot = i * chunk + lax.broadcasted_iota(jnp.int32, (ONES, chunk), 1)
+        live[i] = (slot < length).astype(jnp.float32).astype(jnp.bfloat16)
+
+        @pl.when((i + 1) * chunk > length)
+        def _():
+            dead = i * chunk + lax.broadcasted_iota(jnp.int32, ks.shape[1:], 0) >= length
+            keys = ks[i].astype(jnp.float32)
+            ks[i] = jnp.where(dead, keys[:1, :], keys).astype(jnp.bfloat16)
+            vs[i] = jnp.where(dead, 0.0, vs[i].astype(jnp.float32)).astype(jnp.bfloat16)
+
     def fresh_scores(k):
-        s = dot_last(fk_ref[span * SPAN : (span + 1) * SPAN, (first_head + k) * HD : (first_head + k + 1) * HD], qs[k])
+        s = dot_last(fk_ref[span * SPAN : (span + 1) * SPAN, k * HD : (k + 1) * HD], qs[k])
         key = lax.broadcasted_iota(jnp.int32, (SPAN, rows), 0)
         token = lax.broadcasted_iota(jnp.int32, (SPAN, rows), 1) % SPAN
         return jnp.where(key <= token, s, DEAD)
 
+    def tile_max(s):
+        return jnp.max(s.reshape(s.shape[0] // 8, 8, rows), axis=0)
+
+    def tiles(k):
+        return slice(k * HD, (k + 1) * HD)
+
     for k in range(kv_heads):
         for h in range(group_size):
-            col = ((first_head + k) * group_size + h) * HD
-            qs[k, h * SPAN : (h + 1) * SPAN, :] = q_ref[span * SPAN : (span + 1) * SPAN, col : col + HD]
+            qs[k, h * SPAN : (h + 1) * SPAN, :] = q_ref[
+                span * SPAN : (span + 1) * SPAN, (k * group_size + h) * HD : (k * group_size + h + 1) * HD
+            ]
         m_s[k] = jnp.max(fresh_scores(k), axis=0, keepdims=True)
+        a_s[k] = jnp.ones((1, rows), jnp.float32)
         acc[k] = jnp.zeros((HD + ONES, rows), jnp.float32)
-
-    ones = jnp.ones((ONES, chunk), jnp.bfloat16)
-
-    def add_chunk(i, masked):
-        for copy in copies(i):
-            copy.wait()
-
-        def scores(k):
-            s = dot_last(ks[i, :, k * HD : (k + 1) * HD], qs[k])
-            if masked:
-                slot = i * chunk + lax.broadcasted_iota(jnp.int32, (chunk, rows), 0)
-                s = jnp.where(slot < length, s, DEAD)
-            return s
-
-        s = scores(0)
+    p_s[1] = jnp.zeros((chunk, rows), jnp.bfloat16)
+    arrive(0)
+    s = dot_last(ks[0, :, :HD], qs[0])
+    s_s[0] = s
+    x_s[0] = tile_max(s)
+
+    def weighted(i, k, part, index):
+        return dot(jnp.concatenate([vs[i, part, tiles(k)].T, live[i, :, part]], axis=0), p_s[index, part, :])
+
+    @pl.loop(0, count)
+    def _(i):
+        @pl.when(i + 1 < count)
+        def _():
+            arrive(i + 1)
+
         for k in range(kv_heads):
-            later = scores(k + 1) if k + 1 < kv_heads else None
+            now, other = k % 2, 1 - k % 2
+            next_k, next_i = (k + 1) % kv_heads, i if k + 1 < kv_heads else jnp.minimum(i + 1, count - 1)
+            last_k, last_i = (k - 1) % kv_heads, i if k > 0 else jnp.maximum(i - 1, 0)
             before = m_s[k]
-            top = jnp.maximum(before, jnp.max(s, axis=0, keepdims=True))
+            top = jnp.maximum(before, jnp.max(x_s[now], axis=0, keepdims=True))
             m_s[k] = top
-            p = jnp.exp2((s - top) * EXP2_SCALE).astype(jnp.bfloat16)
-            alpha = jnp.exp2((before - top) * EXP2_SCALE)
-            values = jnp.concatenate([vs[i, :, k * HD : (k + 1) * HD].T, ones], axis=0)
-            acc[k] = acc[k] * alpha + dot(values, p)
-            s = later
-
-    @pl.loop(0, length // chunk)
-    def _(i):
-        add_chunk(i, False)
-
-    @pl.when(length % chunk != 0)
-    def _():
-        add_chunk(length // chunk, True)
+            highest, mixed = None, None
+            for j in range(0, chunk, TILE):
+                part = slice(j, j + TILE)
+                s = dot_last(ks[next_i, part, tiles(next_k)], qs[next_k])
+                s_s[other, part, :] = s
+                high = tile_max(s)
+                highest = high if highest is None else jnp.maximum(highest, high)
+                p_s[now, part, :] = jnp.exp2((s_s[now, part, :] - top) * EXP2_SCALE).astype(jnp.bfloat16)
+                if (j // TILE) % 2 == 1:
+                    product = weighted(last_i, last_k, slice(j - TILE, j + TILE), other)
+                    mixed = product if mixed is None else mixed + product
+            x_s[other] = highest
+            acc[last_k] = acc[last_k] * a_s[last_k] + mixed
+            a_s[k] = jnp.exp2((before - top) * EXP2_SCALE)
+
+    last = kv_heads - 1
+    acc[last] = acc[last] * a_s[last] + weighted(count - 1, last, slice(0, chunk), last % 2)
 
     for k in range(kv_heads):
         p = jnp.exp2((fresh_scores(k) - m_s[k]) * EXP2_SCALE)
@@ -106,37 +135,38 @@
             out_ref[:, col : col + HD] = mixed[h * SPAN : (h + 1) * SPAN, :]
 
 
-def cache_attention(span, first_head, kv_heads, hides, queries, fresh_keys, keys, values, lengths):
-    slots = keys.shape[1]
-    group_size = queries.shape[1] // keys.shape[2]
-    width = kv_heads * HD
+def cache_attention(span, queries, fresh_keys, keys, values, lengths):
+    slots, width = keys.shape[1:]
+    kv_heads = width // HD
+    group_size = queries.shape[1] // width
     rows = group_size * SPAN
     chunk = min(CHUNK, slots)
     chunks = slots // chunk
     vmem = pl.BlockSpec(memory_space=pltpu.VMEM)
     hbm = pl.BlockSpec(memory_space=pltpu.HBM)
     return pl.pallas_call(
-        functools.partial(cache_kernel, span, first_head, kv_heads, group_size),
+        functools.partial(cache_kernel, span),
         in_specs=[pl.BlockSpec(memory_space=pltpu.SMEM), vmem, vmem, hbm, hbm],
         out_specs=[vmem, vmem],
         scratch_shapes=[
             pltpu.VMEM((kv_heads, rows, HD), jnp.bfloat16),
             pltpu.VMEM((chunks, chunk, width), jnp.bfloat16),
             pltpu.VMEM((chunks, chunk, width), jnp.bfloat16),
+            pltpu.VMEM((chunks, ONES, chunk), jnp.bfloat16),
+            pltpu.VMEM((2, chunk, rows), jnp.float32),
+            pltpu.VMEM((2, chunk, rows), jnp.bfloat16),
+            pltpu.VMEM((2, 8, rows), jnp.float32),
+            pltpu.VMEM((kv_heads, 1, rows), jnp.float32),
             pltpu.VMEM((kv_heads, 1, rows), jnp.float32),
             pltpu.VMEM((kv_heads, HD + ONES, rows), jnp.float32),
             pltpu.SemaphoreType.DMA((2, chunks)),
         ],
         out_shape=[
-            jax.ShapeDtypeStruct((SPAN, group_size * width), jnp.float32),
+            jax.ShapeDtypeStruct((SPAN, queries.shape[1]), jnp.float32),
             jax.ShapeDtypeStruct((kv_heads * rows, SPAN), jnp.bfloat16),
         ],
         compiler_params=pltpu.CompilerParams(vmem_limit_bytes=57 * MIB),
-        cost_estimate=pl.CostEstimate(
-            flops=4 * rows * slots * width, bytes_accessed=4 * slots * width, transcendentals=0
-        )
-        if hides
-        else FREE,
+        cost_estimate=FREE,
         name="cache_attention",
     )(lengths, queries, fresh_keys, keys, values)
 
@@ -393,13 +423,8 @@
     ups = adapter_up_weight.reshape(-1, cols)
 
     kv_heads = cols // HD
-    kv_heads = cols // HD
-    pieces = [(0, 0, kv_heads), (1, 0, kv_heads)]
-
-    def attention(piece, lengths):
-        return cache_attention(
-            *pieces[piece], False, queries, incoming_keys, stored_keys, stored_values, lengths
-        )
+    def attention(span, lengths):
+        return cache_attention(span, queries, incoming_keys, stored_keys, stored_values, lengths)
 
     def after(value, *others):
         return lax.optimization_barrier((value, *others))[0]
@@ -412,7 +437,8 @@
         return lax.ppermute(value, ("wing", "quad"), pairs)
 
     *blocks, early, late = pack(normed_inputs, downs, ups, value_matrix, quads)
-    mine = [to_quad(blocks[q], q) for q in range(1, quads)]
+    order = [*range(quads // 2, quads), *range(1, quads // 2)]
+    mine = [to_quad(blocks[q], q) for q in order]
     early = lax.ppermute(early, "wing", SWAP)
     maps = [to_other_wing(blocks[quads - 1 + q], q) for q in range(1, quads)]
 
@@ -428,7 +454,7 @@
     late, early_other, maps_other, *mine = lax.optimization_barrier(
         (late, early_other, maps_other, *mine, attn[1][1])
     )[:-1]
-    mine = jnp.stack([blocks[0], *mine])
+    mine = jnp.stack([blocks[0]] + [mine[order.index(q)] for q in range(1, quads)])
     late_other = lax.ppermute(late, "parts", parts_swap)
     maps_mine = (maps, maps_other)
     maps_theirs = [lax.ppermute(each, "tensor", SWAP) for each in maps_mine]
@@ -441,7 +467,7 @@
     products = far_products(mine, theirs, near, (early, late, early_other, late_other), tokens)
     parts = [products[0]] + [to_quad(products[q], q) for q in range(1, quads)]
     mixed, fresh_probs = zip(*attn)
-    attended, incoming_values = finish([piece[:2] for piece in pieces], mixed, fresh_probs, parts, q_width)
+    attended, incoming_values = finish([(0, 0), (1, 0)], mixed, fresh_probs, parts, q_width)
     return (attended, incoming_values)
 
 

time: 72.3 us -> 70 us (0.968)
  the two profiles are of different devices: /device:TPU:0 before, /device:TPU:16 now
where the time goes in v11:
time: 70 us; the launch traced here: 69 us
  starting transfers between devices  28 us (40%)
  Pallas kernels  25.6 us (37%)
  waiting for transfers between devices  14.2 us (20%)
  between operations  0.86 us (1%)
    pallas_call x2, Pallas kernels, cache_attention(): pl.pallas_call(functools.partial(cache_kernel, span), in_specs=[pl.BlockS...  17.8 us
    ppermute x6, starting transfers between devices, to_quad(): return lax.ppermute(value, 'quad', [(j, j ^ q) for j in range(quads)])  12 us
    ppermute x6, waiting for transfers between devices, to_quad(): return lax.ppermute(value, 'quad', [(j, j ^ q) for j in range(quads)])  10.3 us
    ppermute x3, starting transfers between devices, to_other_wing(): return lax.ppermute(value, ('wing', 'quad'), pairs)  5.84 us
    ppermute x1, starting transfers between devices, on_device(): late_other = lax.ppermute(late, 'parts', parts_swap)  4.76 us
    pallas_call x1, Pallas kernels, pack(): pl.pallas_call(pack_kernel, in_specs=[hbm] * 4, out_specs=[vmem] * len(si...  3.23 us
    ppermute x1, starting transfers between devices, on_device(): maps_other = lax.ppermute(maps, 'parts', parts_swap)  3.18 us
    ppermute x1, waiting for transfers between devices, on_device(): late_other = lax.ppermute(late, 'parts', parts_swap)  2.71 us
  transfers between devices with their start and end apart: 17, of which 7 were waited for; matrix products, arithmetic and copies ran while one was open for 0% of the time, Pallas kernels for 29%

profile of v11, /device:TPU:16, one launch (start us, length us, event | category | flops | bytes accessed | tf_op | source)
XLA Modules:
  0.0 69.0 jit_solution(4413208160965480135)
XLA Ops:
  0.6 3.2 %pack.1 = (bf16[176,1024]{1,0:T(8,128)(2,1)}, bf16[176,1024]{1,0:T(8,128)(2,1)}, bf16[176,1024]{1,0:T(8,128)(2,1)}, bf16[176,1024]{1,0:T(8,128)(2,1)}, bf16[48,5...) custom-call(bf16[128,4096]{1,0:T(8,128)(2,1)} %x_hbm.1, ...), custom_call_target="tpu_custom_call" | custom-call | flops 1 | bytes 1 | tf_op jit(solution)/shard_map/pack/pallas_call | solution.py:236
  3.9 0.1 collective-permute-start
  3.9 3.9 %collective-permute-start.1 = (bf16[48,512]{1,0:T(8,128)(2,1)}, bf16[48,512]{1,0:T(8,128)(2,1)S(1)}, u32[]{:S(2)}, u32[]{:S(2)}) collective-permute-start(bf16[48,512]{1,0:T(8,128)(2,1)} %get-tuple-element.36), channel_id=1, source_target_pairs={{0,10},{2,8},{4,14},{6,12},{8,2},{10,0},{12,6},{14,4},{1,11},{3,9}... | collective-permute-start | bytes 147464 | tf_op jit(solution)/shard_map/ppermute | solution.py:437
  7.8 0.4 collective-permute-start.2
  8.3 1.5 %collective-permute-start.3 = (bf16[48,512]{1,0:T(8,128)(2,1)}, bf16[48,512]{1,0:T(8,128)(2,1)S(1)}, u32[]{:S(2)}, u32[]{:S(2)}) collective-permute-start(bf16[48,512]{1,0:T(8,128)(2,1)} %get-tuple-element.38), channel_id=1, source_target_pairs={{0,14},{2,12},{4,10},{6,8},{8,6},{10,4},{12,2},{14,0},{1,15},{3,13... | collective-permute-start | bytes 147464 | tf_op jit(solution)/shard_map/ppermute | solution.py:437
  9.8 3.4 %collective-permute-start.7 = (bf16[176,1024]{1,0:T(8,128)(2,1)}, bf16[176,1024]{1,0:T(8,128)(2,1)S(1)}, u32[]{:S(2)}, u32[]{:S(2)}) collective-permute-start(bf16[176,1024]{1,0:T(8,128)(2,1)} %get-tuple-element.49), channel_id=1, source_target_pairs={{0,4},{2,6},{4,0},{6,2},{1,5},{3,7},{5,1},{7,3},{8,12},{10,14},{12... | collective-permute-start | bytes 1081352 | tf_op jit(solution)/shard_map/ppermute | solution.py:433
  13.2 11.3 %cache_attention.2 = (f32[64,4096]{1,0:T(8,128)}, bf16[2048,64]{1,0:T(8,128)(2,1)}) custom-call(s32[2]{0:T(128)} %lens.1, bf16[128,4096]{1,0:T(8,128)(2,1)} %q_ref.3, bf16[128,512]{1,0:T(8,128)(2,1)} %fk_ref.3, bf16[2,2048,512]{2,1,0:T(8,128)(2,1)} %k_hbm.3, bf16[2,2048,512]{2,1,0:T(8,128)(2,1)} %v_hbm.3), custom_call_target="tpu_custom_call" | custom-call | flops 1 | bytes 1 | tf_op jit(solution)/shard_map/cache_attention/pallas_call | solution.py:147
  24.5 0.0 collective-permute-done.1
  24.5 0.0 copy-done.9
  24.5 3.0 %collective-permute-start.8 = (bf16[176,1024]{1,0:T(8,128)(2,1)S(1)}, bf16[176,1024]{1,0:T(8,128)(2,1)S(1)}, u32[]{:S(2)}, u32[]{:S(2)}) collective-permute-start(bf16[176,1024]{1,0:T(8,128)(2,1)S(1)} %copy-done.9), channel_id=1, source_target_pairs={{0,6},{2,4},{4,2},{6,0},{1,7},{3,5},{5,3},{7,1},{8,14},{10,12},{12... | collective-permute-start | bytes 1081352 | tf_op jit(solution)/shard_map/ppermute | solution.py:433
  27.5 0.0 collective-permute-done.2
  27.5 1.5 %collective-permute-start.9 = (bf16[176,1024]{1,0:T(8,128)(2,1)S(1)}, bf16[176,1024]{1,0:T(8,128)(2,1)S(1)}, u32[]{:S(2)}, u32[]{:S(2)}) collective-permute-start(bf16[176,1024]{1,0:T(8,128)(2,1)S(1)} %copy-done.8), channel_id=1, source_target_pairs={{0,2},{2,0},{4,6},{6,4},{1,3},{3,1},{5,7},{7,5},{8,10},{10,8},{12,... | collective-permute-start | bytes 1081352 | tf_op jit(solution)/shard_map/ppermute | solution.py:433
  29.1 0.0 collective-permute-done.3
  29.1 0.0 collective-permute-done.refs_0_
  29.1 1.6 %collective-permute-start.5 = (bf16[304,512]{1,0:T(8,128)(2,1)S(1)}, bf16[304,512]{1,0:T(8,128)(2,1)S(1)}, u32[]{:S(2)}, u32[]{:S(2)}) collective-permute-start(bf16[304,512]{1,0:T(8,128)(2,1)S(1)} %collective-permute-done.refs_0_), channel_id=1, source_target_pairs={{0,16},{16,0},{1,17},{17,1},{2,18},{18,2},{3,19},{19,3},{4,20},{20... | collective-permute-start | bytes 933896 | tf_op jit(solution)/shard_map/ppermute | solution.py:450
  30.6 0.0 collective-permute-start.4
  30.7 4.4 %collective-permute-done.7 = bf16[176,1024]{1,0:T(8,128)(2,1)S(1)} collective-permute-done((bf16[176,1024]{1,0:T(8,128)(2,1)}, bf16[176,1024]{1,0:T(8,128)(2,1)S(1)}, u32[]{:S(2)}, u32[]{:S(2)}) %collective-permute-start.7) | collective-permute-done | bytes 360480 | tf_op jit(solution)/shard_map/ppermute | solution.py:433
  35.1 3.2 %collective-permute-start.6 = (bf16[4,48,512]{2,1,0:T(8,128)(2,1)S(1)}, bf16[4,48,512]{2,1,0:T(8,128)(2,1)S(1)}, u32[]{:S(2)}, u32[]{:S(2)}) collective-permute-start(bf16[4,48,512]{2,1,0:T(8,128)(2,1)S(1)} %pad_maximum_fusion.1.refs_0_), channel_id=1, source_target_pairs={{0,16},{16,0},{1,17},{17,1},{2,18},{18,2},{3,19},{19,3},{4,20},{20... | collective-permute-start | bytes 589832 | tf_op jit(solution)/shard_map/ppermute | solution.py:451
  38.3 6.5 %cache_attention.3 = (f32[64,4096]{1,0:T(8,128)}, bf16[2048,64]{1,0:T(8,128)(2,1)}) custom-call(s32[2]{0:T(128)} %lens.1, bf16[128,4096]{1,0:T(8,128)(2,1)} %q_ref.3, bf16[128,512]{1,0:T(8,128)(2,1)} %fk_ref.3, bf16[2,2048,512]{2,1,0:T(8,128)(2,1)} %k_hbm.3, bf16[2,2048,512]{2,1,0:T(8,128)(2,1)} %v_hbm.3), custom_call_target="tpu_custom_call" | custom-call | flops 1 | bytes 1 | tf_op jit(solution)/shard_map/cache_attention/pallas_call | solution.py:147
  44.8 0.0 collective-permute-done.8
  44.8 0.0 collective-permute-done.9
  44.8 0.0 collective-permute-done.6.refs_1_
  44.8 0.0 collective-permute-done.4.refs_1_
  44.8 0.0 collective-permute-done.5.refs_2_
  44.8 0.0 copy-done.7
  44.8 0.0 copy-start
  44.9 0.0 copy-start.5
  44.9 0.0 copy-start.6
  44.9 0.2 pad_maximum_fusion.refs_4_
  45.1 0.1 collective-permute-start.12
  45.1 4.8 %collective-permute-start.13 = (bf16[256,512]{1,0:T(8,128)(2,1)S(1)}, bf16[256,512]{1,0:T(8,128)(2,1)S(1)}, u32[]{:S(2)}, u32[]{:S(2)}) collective-permute-start(bf16[256,512]{1,0:T(8,128)(2,1)S(1)} %collective-permute-done.4.refs_1_), channel_id=1, source_target_pairs={{0,16},{16,0},{1,17},{17,1},{2,18},{18,2},{3,19},{19,3},{4,20},{20... | collective-permute-start | bytes 786440 | tf_op jit(solution)/shard_map/ppermute | solution.py:458
  49.9 0.2 collective-permute-start.10
  50.1 0.3 collective-permute-start.11
  50.4 0.9 %collective-permute-done.10.refs_2_ = bf16[4,48,512]{2,1,0:T(8,128)(2,1)S(1)} collective-permute-done((bf16[4,48,512]{2,1,0:T(8,128)(2,1)S(1)}, bf16[4,48,512]{2,1,0:T(8,128)(2,1)S(1)}, u32[]{:S(2)}, u32[]{:S(2)}) %collective-permute-start.10) | collective-permute-done | bytes 196640 | tf_op jit(solution)/shard_map/ppermute | solution.py:460
  51.3 0.3 collective-permute-done.11.refs_3_
  51.6 0.0 collective-permute-done.12.refs_5_
  51.6 0.0 copy-done.6
  51.7 2.4 %near_products.1.near = f32[512,512]{1,0:T(8,128)S(1)} custom-call(s32[16]{0:T(128)S(1)} %copy-done.5, s32[16]{0:T(128)S(1)} %copy-done.6, bf16[1024,512]{1,0:T(8,128)(2,1)S(1)} %copy-done, bf16[4,48,512]{2,1,0:T(8,128)(2,1)S(1)} %pad_maximum_fusion.1.refs_0_, bf16[4,48,512]{2,1,0:T(8,128)(2,1)S(1)} %collective-permute-done.6.refs_1_, ...), custom_call_target="tpu_custom_call" | custom-call | flops 1 | bytes 1 | tf_op jit(solution)/shard_map/near_products/pallas_call | solution.py:308
  54.1 0.0 copy-start.1
  54.1 2.7 %collective-permute-done.13.refs_3_ = bf16[256,512]{1,0:T(8,128)(2,1)S(1)} collective-permute-done((bf16[256,512]{1,0:T(8,128)(2,1)S(1)}, bf16[256,512]{1,0:T(8,128)(2,1)S(1)}, u32[]{:S(2)}, u32[]{:S(2)}) %collective-permute-start.13) | collective-permute-done | bytes 262176 | tf_op jit(solution)/shard_map/ppermute | solution.py:458
  56.8 0.8 %far_products.1 = (bf16[128,512]{1,0:T(8,128)(2,1)S(1)}, bf16[128,512]{1,0:T(8,128)(2,1)S(1)}, bf16[128,512]{1,0:T(8,128)(2,1)S(1)}, bf16[128,512]{1,0:T(8,128)(2,1)S(1)}) custom-call(f32[512,512]{1,0:T(8,128)S(1)} %near_products.1.near, bf16[304,512]{1,0:T(8,128)(2,1)S(1)} %collective-permute-done.refs_0_, ...), custom_call_target="tpu_custom_call" | custom-call | flops 1 | bytes 1 | tf_op jit(solution)/shard_map/far_products/pallas_call | solution.py:353
  57.6 0.6 collective-permute-start.14
  58.2 2.1 %collective-permute-start.15 = (bf16[128,512]{1,0:T(8,128)(2,1)S(1)}, bf16[128,512]{1,0:T(8,128)(2,1)S(1)}, u32[]{:S(2)}, u32[]{:S(2)}) collective-permute-start(bf16[128,512]{1,0:T(8,128)(2,1)S(1)} %get-tuple-element.60), channel_id=1, source_target_pairs={{0,4},{2,6},{4,0},{6,2},{1,5},{3,7},{5,1},{7,3},{8,12},{10,14},{12... | collective-permute-start | bytes 393224 | tf_op jit(solution)/shard_map/ppermute | solution.py:433
  60.3 1.4 %collective-permute-start.16 = (bf16[128,512]{1,0:T(8,128)(2,1)S(1)}, bf16[128,512]{1,0:T(8,128)(2,1)S(1)}, u32[]{:S(2)}, u32[]{:S(2)}) collective-permute-start(bf16[128,512]{1,0:T(8,128)(2,1)S(1)} %get-tuple-element.61), channel_id=1, source_target_pairs={{0,6},{2,4},{4,2},{6,0},{1,7},{3,5},{5,3},{7,1},{8,14},{10,12},{12... | collective-permute-start | bytes 393224 | tf_op jit(solution)/shard_map/ppermute | solution.py:433
  61.7 1.2 %collective-permute-done.14.refs_5_ = bf16[128,512]{1,0:T(8,128)(2,1)S(1)} collective-permute-done((bf16[128,512]{1,0:T(8,128)(2,1)S(1)}, bf16[128,512]{1,0:T(8,128)(2,1)S(1)}, u32[]{:S(2)}, u32[]{:S(2)}) %collective-permute-start.14) | collective-permute-done | bytes 131104 | tf_op jit(solution)/shard_map/ppermute | solution.py:433
  62.9 1.3 %collective-permute-done.15.refs_6_ = bf16[128,512]{1,0:T(8,128)(2,1)S(1)} collective-permute-done((bf16[128,512]{1,0:T(8,128)(2,1)S(1)}, bf16[128,512]{1,0:T(8,128)(2,1)S(1)}, u32[]{:S(2)}, u32[]{:S(2)}) %collective-permute-start.15) | collective-permute-done | bytes 131104 | tf_op jit(solution)/shard_map/ppermute | solution.py:433
  64.2 3.3 %collective-permute-done.16.refs_7_ = bf16[128,512]{1,0:T(8,128)(2,1)S(1)} collective-permute-done((bf16[128,512]{1,0:T(8,128)(2,1)S(1)}, bf16[128,512]{1,0:T(8,128)(2,1)S(1)}, u32[]{:S(2)}, u32[]{:S(2)}) %collective-permute-start.16) | collective-permute-done | bytes 131104 | tf_op jit(solution)/shard_map/ppermute | solution.py:433
  67.6 1.4 %finish_attention.1 = (bf16[128,4096]{1,0:T(8,128)(2,1)}, bf16[128,512]{1,0:T(8,128)(2,1)}) custom-call(f32[64,4096]{1,0:T(8,128)S(1)} %copy-done.1, f32[64,4096]{1,0:T(8,128)S(1)} %copy-done.2, bf16[2048,64]{1,0:T(8,128)(2,1)S(1)} %copy-done.3, bf16[2048,64]{1,0:T(8,128)(2,1)S(1)} %copy-done.4, bf16[128,512]{1,0:T(8,128)(2,1)S(1)} %get-tuple-element.58.refs_4_, ...), custom_call_target="tpu_custom_call" | custom-call | flops 1 | bytes 1 | tf_op jit(solution)/shard_map/finish_attention/pallas_call | solution.py:392
  (17 shorter events, 0.1 us)
Async XLA Ops:
  3.9 25.2 %collective-permute-start = (bf16[304,512]{1,0:T(8,128)(2,1)}, bf16[304,512]{1,0:T(8,128)(2,1)S(1)}, u32[]{:S(2)}, u32[]{:S(2)}) collective-permute-start(bf16[304,512]{1,0:T(8,128)(2,1)} %get-tuple-element.35), channel_id=1, source_target_pairs={{0,8},{8,0},{1,9},{9,1},{2,10},{10,2},{3,11},{11,3},{4,12},{12,4},... | collective-permute-start | bytes 933896 | tf_op jit(solution)/shard_map/ppermute | solution.py:442
  3.9 20.5 %collective-permute-start.1 = (bf16[48,512]{1,0:T(8,128)(2,1)}, bf16[48,512]{1,0:T(8,128)(2,1)S(1)}, u32[]{:S(2)}, u32[]{:S(2)}) collective-permute-start(bf16[48,512]{1,0:T(8,128)(2,1)} %get-tuple-element.36), channel_id=1, source_target_pairs={{0,10},{2,8},{4,14},{6,12},{8,2},{10,0},{12,6},{14,4},{1,11},{3,9}... | collective-permute-start | bytes 147464 | tf_op jit(solution)/shard_map/ppermute | solution.py:437
  7.8 19.7 %collective-permute-start.2 = (bf16[48,512]{1,0:T(8,128)(2,1)}, bf16[48,512]{1,0:T(8,128)(2,1)S(1)}, u32[]{:S(2)}, u32[]{:S(2)}) collective-permute-start(bf16[48,512]{1,0:T(8,128)(2,1)} %get-tuple-element.37), channel_id=1, source_target_pairs={{0,12},{2,14},{4,8},{6,10},{8,4},{10,6},{12,0},{14,2},{1,13},{3,15... | collective-permute-start | bytes 147464 | tf_op jit(solution)/shard_map/ppermute | solution.py:437
  8.3 20.8 %collective-permute-start.3 = (bf16[48,512]{1,0:T(8,128)(2,1)}, bf16[48,512]{1,0:T(8,128)(2,1)S(1)}, u32[]{:S(2)}, u32[]{:S(2)}) collective-permute-start(bf16[48,512]{1,0:T(8,128)(2,1)} %get-tuple-element.38), channel_id=1, source_target_pairs={{0,14},{2,12},{4,10},{6,8},{8,6},{10,4},{12,2},{14,0},{1,15},{3,13... | collective-permute-start | bytes 147464 | tf_op jit(solution)/shard_map/ppermute | solution.py:437
  9.8 25.3 %collective-permute-start.7 = (bf16[176,1024]{1,0:T(8,128)(2,1)}, bf16[176,1024]{1,0:T(8,128)(2,1)S(1)}, u32[]{:S(2)}, u32[]{:S(2)}) collective-permute-start(bf16[176,1024]{1,0:T(8,128)(2,1)} %get-tuple-element.49), channel_id=1, source_target_pairs={{0,4},{2,6},{4,0},{6,2},{1,5},{3,7},{5,1},{7,3},{8,12},{10,14},{12... | collective-permute-start | bytes 1081352 | tf_op jit(solution)/shard_map/ppermute | solution.py:433
  13.2 11.3 %copy-start.9 = (bf16[176,1024]{1,0:T(8,128)(2,1)S(1)}, bf16[176,1024]{1,0:T(8,128)(2,1)}, u32[]{:S(2)}) copy-start(bf16[176,1024]{1,0:T(8,128)(2,1)} %get-tuple-element.50) | copy-start | bytes 1081348
  13.2 14.4 %copy-start.8 = (bf16[176,1024]{1,0:T(8,128)(2,1)S(1)}, bf16[176,1024]{1,0:T(8,128)(2,1)}, u32[]{:S(2)}) copy-start(bf16[176,1024]{1,0:T(8,128)(2,1)} %get-tuple-element.51) | copy-start | bytes 1081348
  13.2 17.5 %copy-start.10 = (bf16[256,512]{1,0:T(8,128)(2,1)S(1)}, bf16[256,512]{1,0:T(8,128)(2,1)}, u32[]{:S(2)}) copy-start(bf16[256,512]{1,0:T(8,128)(2,1)} %get-tuple-element.48) | copy-start | bytes 786436
  24.5 20.3 %collective-permute-start.8 = (bf16[176,1024]{1,0:T(8,128)(2,1)S(1)}, bf16[176,1024]{1,0:T(8,128)(2,1)S(1)}, u32[]{:S(2)}, u32[]{:S(2)}) collective-permute-start(bf16[176,1024]{1,0:T(8,128)(2,1)S(1)} %copy-done.9), channel_id=1, source_target_pairs={{0,6},{2,4},{4,2},{6,0},{1,7},{3,5},{5,3},{7,1},{8,14},{10,12},{12... | collective-permute-start | bytes 1081352 | tf_op jit(solution)/shard_map/ppermute | solution.py:433
  27.5 17.3 %collective-permute-start.9 = (bf16[176,1024]{1,0:T(8,128)(2,1)S(1)}, bf16[176,1024]{1,0:T(8,128)(2,1)S(1)}, u32[]{:S(2)}, u32[]{:S(2)}) collective-permute-start(bf16[176,1024]{1,0:T(8,128)(2,1)S(1)} %copy-done.8), channel_id=1, source_target_pairs={{0,2},{2,0},{4,6},{6,4},{1,3},{3,1},{5,7},{7,5},{8,10},{10,8},{12,... | collective-permute-start | bytes 1081352 | tf_op jit(solution)/shard_map/ppermute | solution.py:433
  29.1 15.8 %collective-permute-start.5 = (bf16[304,512]{1,0:T(8,128)(2,1)S(1)}, bf16[304,512]{1,0:T(8,128)(2,1)S(1)}, u32[]{:S(2)}, u32[]{:S(2)}) collective-permute-start(bf16[304,512]{1,0:T(8,128)(2,1)S(1)} %collective-permute-done.refs_0_), channel_id=1, source_target_pairs={{0,16},{16,0},{1,17},{17,1},{2,18},{18,2},{3,19},{19,3},{4,20},{20... | collective-permute-start | bytes 933896 | tf_op jit(solution)/shard_map/ppermute | solution.py:450
  30.6 14.2 %collective-permute-start.4 = (bf16[256,512]{1,0:T(8,128)(2,1)S(1)}, bf16[256,512]{1,0:T(8,128)(2,1)S(1)}, u32[]{:S(2)}, u32[]{:S(2)}) collective-permute-start(bf16[256,512]{1,0:T(8,128)(2,1)S(1)} %copy-done.10), channel_id=1, source_target_pairs={{0,8},{8,0},{1,9},{9,1},{2,10},{10,2},{3,11},{11,3},{4,12},{12,4},... | collective-permute-start | bytes 786440 | tf_op jit(solution)/shard_map/ppermute | solution.py:449
  30.7 14.2 %copy-start.7 = (bf16[176,1024]{1,0:T(8,128)(2,1)S(1)}, bf16[176,1024]{1,0:T(8,128)(2,1)}, u32[]{:S(2)}) copy-start(bf16[176,1024]{1,0:T(8,128)(2,1)} %get-tuple-element.32) | copy-start | bytes 1081348
  35.1 9.7 %collective-permute-start.6 = (bf16[4,48,512]{2,1,0:T(8,128)(2,1)S(1)}, bf16[4,48,512]{2,1,0:T(8,128)(2,1)S(1)}, u32[]{:S(2)}, u32[]{:S(2)}) collective-permute-start(bf16[4,48,512]{2,1,0:T(8,128)(2,1)S(1)} %pad_maximum_fusion.1.refs_0_), channel_id=1, source_target_pairs={{0,16},{16,0},{1,17},{17,1},{2,18},{18,2},{3,19},{19,3},{4,20},{20... | collective-permute-start | bytes 589832 | tf_op jit(solution)/shard_map/ppermute | solution.py:451
  44.8 6.8 %copy-start = (bf16[1024,512]{1,0:T(8,128)(2,1)S(1)}, bf16[1024,512]{1,0:T(8,128)(2,1)}, u32[]{:S(2)}) copy-start(bf16[1024,512]{1,0:T(8,128)(2,1)} %own_ref.1) | copy-start | bytes 3145732
  44.9 6.8 %copy-start.5 = (s32[16]{0:T(128)S(1)}, s32[16]{0:T(128)}, u32[]{:S(2)}) copy-start(s32[16]{0:T(128)} %position.1) | copy-start | bytes 196
  44.9 6.8 %copy-start.6 = (s32[16]{0:T(128)S(1)}, s32[16]{0:T(128)}, u32[]{:S(2)}) copy-start(s32[16]{0:T(128)} %adapter.1) | copy-start | bytes 196
  45.1 6.6 %collective-permute-start.12 = (bf16[4,176,1024]{2,1,0:T(8,128)(2,1)S(1)}, bf16[4,176,1024]{2,1,0:T(8,128)(2,1)S(1)}, u32[]{:S(2)}, u32[]{:S(2)}) collective-permute-start(bf16[4,176,1024]{2,1,0:T(8,128)(2,1)S(1)} %pad_maximum_fusion.refs_4_), channel_id=1, source_target_pairs={{0,1},{1,0},{2,3},{3,2},{4,5},{5,4},{6,7},{7,6},{8,9},{9,8},{10,11... | collective-permute-start | bytes 4325384 | tf_op jit(solution)/shard_map/ppermute | solution.py:461
  45.1 11.7 %collective-permute-start.13 = (bf16[256,512]{1,0:T(8,128)(2,1)S(1)}, bf16[256,512]{1,0:T(8,128)(2,1)S(1)}, u32[]{:S(2)}, u32[]{:S(2)}) collective-permute-start(bf16[256,512]{1,0:T(8,128)(2,1)S(1)} %collective-permute-done.4.refs_1_), channel_id=1, source_target_pairs={{0,16},{16,0},{1,17},{17,1},{2,18},{18,2},{3,19},{19,3},{4,20},{20... | collective-permute-start | bytes 786440 | tf_op jit(solution)/shard_map/ppermute | solution.py:458
  49.9 1.4 %collective-permute-start.10 = (bf16[4,48,512]{2,1,0:T(8,128)(2,1)S(1)}, bf16[4,48,512]{2,1,0:T(8,128)(2,1)S(1)}, u32[]{:S(2)}, u32[]{:S(2)}) collective-permute-start(bf16[4,48,512]{2,1,0:T(8,128)(2,1)S(1)} %pad_maximum_fusion.1.refs_0_), channel_id=1, source_target_pairs={{0,1},{1,0},{2,3},{3,2},{4,5},{5,4},{6,7},{7,6},{8,9},{9,8},{10,11... | collective-permute-start | bytes 589832 | tf_op jit(solution)/shard_map/ppermute | solution.py:460
  50.1 1.6 %collective-permute-start.11 = (bf16[4,48,512]{2,1,0:T(8,128)(2,1)S(1)}, bf16[4,48,512]{2,1,0:T(8,128)(2,1)S(1)}, u32[]{:S(2)}, u32[]{:S(2)}) collective-permute-start(bf16[4,48,512]{2,1,0:T(8,128)(2,1)S(1)} %collective-permute-done.6.refs_1_), channel_id=1, source_target_pairs={{0,1},{1,0},{2,3},{3,2},{4,5},{5,4},{6,7},{7,6},{8,9},{9,8},{10,11... | collective-permute-start | bytes 589832 | tf_op jit(solution)/shard_map/ppermute | solution.py:460
  54.1 13.5 %copy-start.1 = (f32[64,4096]{1,0:T(8,128)S(1)}, f32[64,4096]{1,0:T(8,128)}, u32[]{:S(2)}) copy-start(f32[64,4096]{1,0:T(8,128)} %get-tuple-element.34.refs_0_) | copy-start | bytes 3145732
  54.1 13.5 %copy-start.2 = (f32[64,4096]{1,0:T(8,128)S(1)}, f32[64,4096]{1,0:T(8,128)}, u32[]{:S(2)}) copy-start(f32[64,4096]{1,0:T(8,128)} %get-tuple-element.45.refs_1_) | copy-start | bytes 3145732
  54.1 13.5 %copy-start.3 = (bf16[2048,64]{1,0:T(8,128)(2,1)S(1)}, bf16[2048,64]{1,0:T(8,128)(2,1)}, u32[]{:S(2)}) copy-start(bf16[2048,64]{1,0:T(8,128)(2,1)} %get-tuple-element.39.refs_2_) | copy-start | bytes 786436
  54.1 13.5 %copy-start.4 = (bf16[2048,64]{1,0:T(8,128)(2,1)S(1)}, bf16[2048,64]{1,0:T(8,128)(2,1)}, u32[]{:S(2)}) copy-start(bf16[2048,64]{1,0:T(8,128)(2,1)} %get-tuple-element.46.refs_3_) | copy-start | bytes 786436
  57.6 5.3 %collective-permute-start.14 = (bf16[128,512]{1,0:T(8,128)(2,1)S(1)}, bf16[128,512]{1,0:T(8,128)(2,1)S(1)}, u32[]{:S(2)}, u32[]{:S(2)}) collective-permute-start(bf16[128,512]{1,0:T(8,128)(2,1)S(1)} %get-tuple-element.59), channel_id=1, source_target_pairs={{0,2},{2,0},{4,6},{6,4},{1,3},{3,1},{5,7},{7,5},{8,10},{10,8},{12,... | collective-permute-start | bytes 393224 | tf_op jit(solution)/shard_map/ppermute | solution.py:433
  58.2 6.0 %collective-permute-start.15 = (bf16[128,512]{1,0:T(8,128)(2,1)S(1)}, bf16[128,512]{1,0:T(8,128)(2,1)S(1)}, u32[]{:S(2)}, u32[]{:S(2)}) collective-permute-start(bf16[128,512]{1,0:T(8,128)(2,1)S(1)} %get-tuple-element.60), channel_id=1, source_target_pairs={{0,4},{2,6},{4,0},{6,2},{1,5},{3,7},{5,1},{7,3},{8,12},{10,14},{12... | collective-permute-start | bytes 393224 | tf_op jit(solution)/shard_map/ppermute | solution.py:433
  60.3 7.2 %collective-permute-start.16 = (bf16[128,512]{1,0:T(8,128)(2,1)S(1)}, bf16[128,512]{1,0:T(8,128)(2,1)S(1)}, u32[]{:S(2)}, u32[]{:S(2)}) collective-permute-start(bf16[128,512]{1,0:T(8,128)(2,1)S(1)} %get-tuple-element.61), channel_id=1, source_target_pairs={{0,6},{2,4},{4,2},{6,0},{1,7},{3,5},{5,3},{7,1},{8,14},{10,12},{12... | collective-permute-start | bytes 393224 | tf_op jit(solution)/shard_map/ppermute | solution.py:433

commit v12 on v11

--- a/solution.py
+++ b/solution.py
@@ -31,42 +31,60 @@
     return jnp.dot(a, b, preferred_element_type=jnp.float32)
 
 
-def cache_kernel(span, lens, q_ref, fk_ref, k_hbm, v_hbm, out_ref, pf_ref, qs, ks, vs, live, s_s, p_s, x_s, m_s, a_s, acc, sems):
+def span_of(order, lens):
+    longer = (lens[1] > lens[0]).astype(jnp.int32)
+    return longer if order == 0 else 1 - longer
+
+
+def cache_kernel(order, lens, q_hbm, fk_hbm, k_hbm, v_hbm, out_hbm, pf_hbm, qs, ks, vs, live, s_s, p_s, x_s, m_s, a_s, acc, q_s, fk_s, out_s, pf_s, sems, io_sems):
+    span = span_of(order, lens)
     length = lens[span]
     chunks, chunk, _ = ks.shape
     kv_heads, rows, _ = qs.shape
     group_size = rows // SPAN
     count = (length + chunk - 1) // chunk
-
-    def copies(i):
+    mine = pl.ds(pl.multiple_of(span * SPAN, SPAN), SPAN)
+
+    def copy_in(side, i):
         slots = pl.ds(pl.multiple_of(i * chunk, chunk), chunk)
-        return (
-            pltpu.make_async_copy(k_hbm.at[span, slots, :], ks.at[i], sems.at[0, i]),
-            pltpu.make_async_copy(v_hbm.at[span, slots, :], vs.at[i], sems.at[1, i]),
-        )
-
+        source, target = ((k_hbm, ks), (v_hbm, vs))[side]
+        return pltpu.make_async_copy(source.at[span, slots, :], target.at[i], sems.at[side, i])
+
+    small = [
+        pltpu.make_async_copy(q_hbm.at[mine, :], q_s, io_sems.at[0]),
+        pltpu.make_async_copy(fk_hbm.at[mine, :], fk_s, io_sems.at[1]),
+    ]
+    for copy in small:
+        copy.start()
     for i in range(chunks):
 
         @pl.when(i * chunk < length)
         def _():
-            for copy in copies(i):
-                copy.start()
-
-    def arrive(i):
-        for copy in copies(i):
-            copy.wait()
+            copy_in(0, i).start()
+            copy_in(1, i).start()
+
+    def dead_slots(i):
+        return i * chunk + lax.broadcasted_iota(jnp.int32, ks.shape[1:], 0) >= length
+
+    def arrive_keys(i):
+        copy_in(0, i).wait()
+
+        @pl.when((i + 1) * chunk > length)
+        def _():
+            keys = ks[i].astype(jnp.float32)
+            ks[i] = jnp.where(dead_slots(i), keys[:1, :], keys).astype(jnp.bfloat16)
+
+    def arrive_values(i):
+        copy_in(1, i).wait()
         slot = i * chunk + lax.broadcasted_iota(jnp.int32, (ONES, chunk), 1)
         live[i] = (slot < length).astype(jnp.float32).astype(jnp.bfloat16)
 
         @pl.when((i + 1) * chunk > length)
         def _():
-            dead = i * chunk + lax.broadcasted_iota(jnp.int32, ks.shape[1:], 0) >= length
-            keys = ks[i].astype(jnp.float32)
-            ks[i] = jnp.where(dead, keys[:1, :], keys).astype(jnp.bfloat16)
-            vs[i] = jnp.where(dead, 0.0, vs[i].astype(jnp.float32)).astype(jnp.bfloat16)
+            vs[i] = jnp.where(dead_slots(i), 0.0, vs[i].astype(jnp.float32)).astype(jnp.bfloat16)
 
     def fresh_scores(k):
-        s = dot_last(fk_ref[span * SPAN : (span + 1) * SPAN, k * HD : (k + 1) * HD], qs[k])
+        s = dot_last(fk_s[:, k * HD : (k + 1) * HD], qs[k])
         key = lax.broadcasted_iota(jnp.int32, (SPAN, rows), 0)
         token = lax.broadcasted_iota(jnp.int32, (SPAN, rows), 1) % SPAN
         return jnp.where(key <= token, s, DEAD)
@@ -77,16 +95,16 @@
     def tiles(k):
         return slice(k * HD, (k + 1) * HD)
 
+    for copy in small:
+        copy.wait()
     for k in range(kv_heads):
         for h in range(group_size):
-            qs[k, h * SPAN : (h + 1) * SPAN, :] = q_ref[
-                span * SPAN : (span + 1) * SPAN, (k * group_size + h) * HD : (k * group_size + h + 1) * HD
-            ]
+            qs[k, h * SPAN : (h + 1) * SPAN, :] = q_s[:, tiles(k * group_size + h)]
         m_s[k] = jnp.max(fresh_scores(k), axis=0, keepdims=True)
         a_s[k] = jnp.ones((1, rows), jnp.float32)
         acc[k] = jnp.zeros((HD + ONES, rows), jnp.float32)
     p_s[1] = jnp.zeros((chunk, rows), jnp.bfloat16)
-    arrive(0)
+    arrive_keys(0)
     s = dot_last(ks[0, :, :HD], qs[0])
     s_s[0] = s
     x_s[0] = tile_max(s)
@@ -96,9 +114,11 @@
 
     @pl.loop(0, count)
     def _(i):
+        arrive_values(i)
+
         @pl.when(i + 1 < count)
         def _():
-            arrive(i + 1)
+            arrive_keys(i + 1)
 
         for k in range(kv_heads):
             now, other = k % 2, 1 - k % 2
@@ -125,29 +145,39 @@
     last = kv_heads - 1
     acc[last] = acc[last] * a_s[last] + weighted(count - 1, last, slice(0, chunk), last % 2)
 
+    leaving = []
     for k in range(kv_heads):
         p = jnp.exp2((fresh_scores(k) - m_s[k]) * EXP2_SCALE)
         inverse = 1.0 / (acc[k, HD : HD + 1, :] + jnp.sum(p, axis=0, keepdims=True))
-        pf_ref[k * rows : (k + 1) * rows, :] = (p * inverse).T.astype(jnp.bfloat16)
-        mixed = (acc[k, :HD, :] * inverse).T
+        p_s[0, (k % 2) * SPAN : (k % 2 + 1) * SPAN, :] = (p * inverse).astype(jnp.bfloat16)
+        mixed = (acc[k, :HD, :] * inverse).T.astype(jnp.bfloat16)
         for h in range(group_size):
-            col = (k * group_size + h) * HD
-            out_ref[:, col : col + HD] = mixed[h * SPAN : (h + 1) * SPAN, :]
-
-
-def cache_attention(span, queries, fresh_keys, keys, values, lengths):
+            out_s[:, tiles(k * group_size + h)] = mixed[h * SPAN : (h + 1) * SPAN, :]
+        here = slice(k * group_size * HD, (k + 1) * group_size * HD)
+        leaving.append(pltpu.make_async_copy(out_s.at[:, here], out_hbm.at[:, here], io_sems.at[2 + k]))
+        leaving[-1].start()
+        if k % 2 == 1:
+            pf_s[k // 2] = p_s[0, : 2 * SPAN, :].T
+    leaving.append(pltpu.make_async_copy(pf_s, pf_hbm, io_sems.at[2 + kv_heads]))
+    leaving[-1].start()
+    for copy in leaving:
+        copy.wait()
+
+
+def cache_attention(order, queries, fresh_keys, keys, values, lengths):
     slots, width = keys.shape[1:]
     kv_heads = width // HD
     group_size = queries.shape[1] // width
     rows = group_size * SPAN
     chunk = min(CHUNK, slots)
     chunks = slots // chunk
-    vmem = pl.BlockSpec(memory_space=pltpu.VMEM)
     hbm = pl.BlockSpec(memory_space=pltpu.HBM)
+    result = (SPAN, queries.shape[1])
+    weights = (kv_heads // 2, rows, 2 * SPAN)
     return pl.pallas_call(
-        functools.partial(cache_kernel, span),
-        in_specs=[pl.BlockSpec(memory_space=pltpu.SMEM), vmem, vmem, hbm, hbm],
-        out_specs=[vmem, vmem],
+        functools.partial(cache_kernel, order),
+        in_specs=[pl.BlockSpec(memory_space=pltpu.SMEM)] + [hbm] * 4,
+        out_specs=[hbm] * 2,
         scratch_shapes=[
             pltpu.VMEM((kv_heads, rows, HD), jnp.bfloat16),
             pltpu.VMEM((chunks, chunk, width), jnp.bfloat16),
@@ -159,11 +189,16 @@
             pltpu.VMEM((kv_heads, 1, rows), jnp.float32),
             pltpu.VMEM((kv_heads, 1, rows), jnp.float32),
             pltpu.VMEM((kv_heads, HD + ONES, rows), jnp.float32),
+            pltpu.VMEM(result, jnp.bfloat16),
+            pltpu.VMEM((SPAN, width), jnp.bfloat16),
+            pltpu.VMEM(result, jnp.bfloat16),
+            pltpu.VMEM(weights, jnp.bfloat16),
             pltpu.SemaphoreType.DMA((2, chunks)),
+            pltpu.SemaphoreType.DMA((3 + kv_heads,)),
         ],
         out_shape=[
-            jax.ShapeDtypeStruct((SPAN, queries.shape[1]), jnp.float32),
-            jax.ShapeDtypeStruct((kv_heads * rows, SPAN), jnp.bfloat16),
+            jax.ShapeDtypeStruct(result, jnp.bfloat16),
+            jax.ShapeDtypeStruct(weights, jnp.bfloat16),
         ],
         compiler_params=pltpu.CompilerParams(vmem_limit_bytes=57 * MIB),
         cost_estimate=FREE,
@@ -362,36 +397,40 @@
     )(near, *weights, mine, theirs)
 
 
-def finish_kernel(places, *refs):
-    count = len(places)
+def finish_kernel(spans, lens, *refs):
     out_ref, values_ref = refs[-2:]
-    mixed, probs, parts = refs[:count], refs[count : 2 * count], refs[2 * count : -2]
+    mixed, probs, parts = refs[:spans], refs[spans : 2 * spans], refs[2 * spans : -2]
     total = parts[0][...].astype(jnp.float32)
     for part in parts[1:]:
         total = total + part[...].astype(jnp.float32)
-    total = total.astype(jnp.bfloat16)
-    values_ref[...] = total
-    for (span, head), mix, prob in zip(places, mixed, probs):
-        rows = slice(span * SPAN, (span + 1) * SPAN)
-        group_size = out_ref.shape[1] // total.shape[1]
-        queries = group_size * SPAN
-        for k in range(prob.shape[0] // queries):
-            values = total[rows, (head + k) * HD : (head + k + 1) * HD]
-            fresh = dot(prob[k * queries : (k + 1) * queries, :], values)
-            for h in range(group_size):
-                here = slice((k * group_size + h) * HD, (k * group_size + h + 1) * HD)
-                col = ((head + k) * group_size + h) * HD
-                out_ref[rows, col : col + HD] = (
-                    mix[:, here] + fresh[h * SPAN : (h + 1) * SPAN, :]
-                ).astype(jnp.bfloat16)
-
-
-def finish(places, mixed, fresh_probs, parts, q_width):
+    values_ref[...] = total.astype(jnp.bfloat16)
+    none = jnp.zeros((SPAN, HD), jnp.bfloat16)
+    group_size = out_ref.shape[1] // values_ref.shape[1]
+    for order in range(spans):
+        span = span_of(order, lens)
+        rows = pl.ds(pl.multiple_of(span * SPAN, SPAN), SPAN)
+        for pair in range(probs[order].shape[0]):
+            left = values_ref[rows, 2 * pair * HD : (2 * pair + 1) * HD]
+            right = values_ref[rows, (2 * pair + 1) * HD : (2 * pair + 2) * HD]
+            both = jnp.concatenate(
+                [jnp.concatenate([left, none], axis=1), jnp.concatenate([none, right], axis=1)], axis=0
+            )
+            fresh = dot(probs[order][pair], both)
+            for side in range(2):
+                for h in range(group_size):
+                    col = ((2 * pair + side) * group_size + h) * HD
+                    added = fresh[h * SPAN : (h + 1) * SPAN, side * HD : (side + 1) * HD]
+                    before = mixed[order][:, col : col + HD].astype(jnp.float32)
+                    out_ref[rows, col : col + HD] = (before + added).astype(jnp.bfloat16)
+
+
+def finish(lengths, mixed, fresh_probs, parts, q_width):
     tokens, cols = parts[0].shape
     vmem = pl.BlockSpec(memory_space=pltpu.VMEM)
+    smem = pl.BlockSpec(memory_space=pltpu.SMEM)
     return pl.pallas_call(
-        functools.partial(finish_kernel, places),
-        in_specs=[vmem] * (len(parts) + 2 * len(mixed)),
+        functools.partial(finish_kernel, len(mixed)),
+        in_specs=[smem] + [vmem] * (len(parts) + 2 * len(mixed)),
         out_specs=[vmem] * 2,
         out_shape=[
             jax.ShapeDtypeStruct((tokens, q_width), jnp.bfloat16),
@@ -400,7 +439,7 @@
         compiler_params=pltpu.CompilerParams(vmem_limit_bytes=16 * MIB),
         cost_estimate=FREE,
         name="finish_attention",
-    )(*mixed, *fresh_probs, *parts)
+    )(lengths, *mixed, *fresh_probs, *parts)
 
 
 def on_device(
@@ -423,8 +462,8 @@
     ups = adapter_up_weight.reshape(-1, cols)
 
     kv_heads = cols // HD
-    def attention(span, lengths):
-        return cache_attention(span, queries, incoming_keys, stored_keys, stored_values, lengths)
+    def attention(order, lengths):
+        return cache_attention(order, queries, incoming_keys, stored_keys, stored_values, lengths)
 
     def after(value, *others):
         return lax.optimization_barrier((value, *others))[0]
@@ -467,7 +506,7 @@
     products = far_products(mine, theirs, near, (early, late, early_other, late_other), tokens)
     parts = [products[0]] + [to_quad(products[q], q) for q in range(1, quads)]
     mixed, fresh_probs = zip(*attn)
-    attended, incoming_values = finish([(0, 0), (1, 0)], mixed, fresh_probs, parts, q_width)
+    attended, incoming_values = finish(cache_length, mixed, fresh_probs, parts, q_width)
     return (attended, incoming_values)
 
 

time: 70 us -> 71.1 us (1.016)
  the two profiles are of different devices: /device:TPU:16 before, /device:TPU:0 now
where the time goes in v12:
time: 71.1 us; the launch traced here: 71 us
  Pallas kernels  30.1 us (42%)
  starting transfers between devices  24.8 us (35%)
  waiting for transfers between devices  14.9 us (21%)
  between operations  0.85 us (1%)
    pallas_call x2, Pallas kernels, cache_attention(): pl.pallas_call(functools.partial(cache_kernel, order), in_specs=[pl.Block...  21.7 us
    ppermute x6, starting transfers between devices, to_quad(): return lax.ppermute(value, 'quad', [(j, j ^ q) for j in range(quads)])  7.52 us
    ppermute x6, waiting for transfers between devices, to_quad(): return lax.ppermute(value, 'quad', [(j, j ^ q) for j in range(quads)])  6.41 us
    ppermute x3, starting transfers between devices, to_other_wing(): return lax.ppermute(value, ('wing', 'quad'), pairs)  4.9 us
    ppermute x1, starting transfers between devices, on_device(): early = lax.ppermute(early, 'wing', SWAP)  4.1 us
    ppermute x1, starting transfers between devices, on_device(): late = lax.ppermute(after(late, early), 'wing', SWAP)  3.96 us
    ppermute x3, waiting for transfers between devices, to_other_wing(): return lax.ppermute(value, ('wing', 'quad'), pairs)  3.89 us
    pallas_call x1, Pallas kernels, pack(): pl.pallas_call(pack_kernel, in_specs=[hbm] * 4, out_specs=[vmem] * len(si...  3.22 us
  transfers between devices with their start and end apart: 17, of which 9 were waited for; matrix products, arithmetic and copies ran while one was open for 0% of the time, Pallas kernels for 34%

profile of v12, /device:TPU:0, one launch (start us, length us, event | category | flops | bytes accessed | tf_op | source)
XLA Modules:
  0.0 71.0 jit_solution(8211290057948700198)
XLA Ops:
  0.6 3.2 %pack.1 = (bf16[176,1024]{1,0:T(8,128)(2,1)}, bf16[176,1024]{1,0:T(8,128)(2,1)}, bf16[176,1024]{1,0:T(8,128)(2,1)}, bf16[176,1024]{1,0:T(8,128)(2,1)}, bf16[48,5...) custom-call(bf16[128,4096]{1,0:T(8,128)(2,1)} %x_hbm.1, ...), custom_call_target="tpu_custom_call" | custom-call | flops 1 | bytes 1 | tf_op jit(solution)/shard_map/pack/pallas_call | solution.py:271
  3.9 4.1 %collective-permute-start = (bf16[304,512]{1,0:T(8,128)(2,1)}, bf16[304,512]{1,0:T(8,128)(2,1)S(1)}, u32[]{:S(2)}, u32[]{:S(2)}) collective-permute-start(bf16[304,512]{1,0:T(8,128)(2,1)} %get-tuple-element.35), channel_id=1, source_target_pairs={{0,8},{8,0},{1,9},{9,1},{2,10},{10,2},{3,11},{11,3},{4,12},{12,4},... | collective-permute-start | bytes 933896 | tf_op jit(solution)/shard_map/ppermute | solution.py:481
  8.0 1.3 %collective-permute-start.1 = (bf16[48,512]{1,0:T(8,128)(2,1)}, bf16[48,512]{1,0:T(8,128)(2,1)S(1)}, u32[]{:S(2)}, u32[]{:S(2)}) collective-permute-start(bf16[48,512]{1,0:T(8,128)(2,1)} %get-tuple-element.36), channel_id=1, source_target_pairs={{0,10},{2,8},{4,14},{6,12},{8,2},{10,0},{12,6},{14,4},{1,11},{3,9}... | collective-permute-start | bytes 147464 | tf_op jit(solution)/shard_map/ppermute | solution.py:476
  9.3 3.6 %collective-permute-start.2 = (bf16[48,512]{1,0:T(8,128)(2,1)}, bf16[48,512]{1,0:T(8,128)(2,1)S(1)}, u32[]{:S(2)}, u32[]{:S(2)}) collective-permute-start(bf16[48,512]{1,0:T(8,128)(2,1)} %get-tuple-element.37), channel_id=1, source_target_pairs={{0,12},{2,14},{4,8},{6,10},{8,4},{10,6},{12,0},{14,2},{1,13},{3,15... | collective-permute-start | bytes 147464 | tf_op jit(solution)/shard_map/ppermute | solution.py:476
  12.9 0.0 collective-permute-start.3
  12.9 0.0 collective-permute-start.7
  12.9 0.0 copy-start.9
  12.9 0.0 copy-start.11
  12.9 11.7 %cache_attention.2 = (bf16[64,4096]{1,0:T(8,128)(2,1)}, bf16[2,512,128]{2,1,0:T(8,128)(2,1)}) custom-call(s32[2]{0:T(128)} %lens.3, bf16[128,4096]{1,0:T(8,128)(2,1)} %q_hbm.3, bf16[128,512]{1,0:T(8,128)(2,1)} %fk_hbm.3, bf16[2,2048,512]{2,1,0:T(8,128)(2,1)} %k_hbm.3, bf16[2,2048,512]{2,1,0:T(8,128)(2,1)} %v_hbm.3), custom_call_target="tpu_custom_call" | custom-call | flops 1 | bytes 1 | tf_op jit(solution)/shard_map/cache_attention/pallas_call | solution.py:177
  24.6 3.9 %collective-permute-done.1 = bf16[48,512]{1,0:T(8,128)(2,1)S(1)} collective-permute-done((bf16[48,512]{1,0:T(8,128)(2,1)}, bf16[48,512]{1,0:T(8,128)(2,1)S(1)}, u32[]{:S(2)}, u32[]{:S(2)}) %collective-permute-start.1) | collective-permute-done | bytes 49184 | tf_op jit(solution)/shard_map/ppermute | solution.py:476
  28.5 0.0 collective-permute-start.8
  28.5 0.0 collective-permute-done.2
  28.5 0.3 collective-permute-start.9
  28.9 0.0 collective-permute-done.3
  28.9 0.0 collective-permute-done.refs_0_
  28.9 1.8 %collective-permute-start.5 = (bf16[304,512]{1,0:T(8,128)(2,1)S(1)}, bf16[304,512]{1,0:T(8,128)(2,1)S(1)}, u32[]{:S(2)}, u32[]{:S(2)}) collective-permute-start(bf16[304,512]{1,0:T(8,128)(2,1)S(1)} %collective-permute-done.refs_0_), channel_id=1, source_target_pairs={{0,16},{16,0},{1,17},{17,1},{2,18},{18,2},{3,19},{19,3},{4,20},{20... | collective-permute-start | bytes 933896 | tf_op jit(solution)/shard_map/ppermute | solution.py:489
  30.7 4.0 %collective-permute-start.4 = (bf16[256,512]{1,0:T(8,128)(2,1)S(1)}, bf16[256,512]{1,0:T(8,128)(2,1)S(1)}, u32[]{:S(2)}, u32[]{:S(2)}) collective-permute-start(bf16[256,512]{1,0:T(8,128)(2,1)S(1)} %copy-done.11), channel_id=1, source_target_pairs={{0,8},{8,0},{1,9},{9,1},{2,10},{10,2},{3,11},{11,3},{4,12},{12,4},... | collective-permute-start | bytes 786440 | tf_op jit(solution)/shard_map/ppermute | solution.py:488
  34.7 0.0 collective-permute-done.7
  34.7 0.6 collective-permute-start.6
  35.3 9.9 %cache_attention.3 = (bf16[64,4096]{1,0:T(8,128)(2,1)}, bf16[2,512,128]{2,1,0:T(8,128)(2,1)}) custom-call(s32[2]{0:T(128)} %lens.3, bf16[128,4096]{1,0:T(8,128)(2,1)} %q_hbm.3, bf16[128,512]{1,0:T(8,128)(2,1)} %fk_hbm.3, bf16[2,2048,512]{2,1,0:T(8,128)(2,1)} %k_hbm.3, bf16[2,2048,512]{2,1,0:T(8,128)(2,1)} %v_hbm.3), custom_call_target="tpu_custom_call" | custom-call | flops 1 | bytes 1 | tf_op jit(solution)/shard_map/cache_attention/pallas_call | solution.py:177
  45.3 0.0 collective-permute-done.8
  45.3 0.4 collective-permute-done.9
  45.6 0.0 collective-permute-done.6.refs_1_
  45.6 0.2 collective-permute-done.4.refs_1_
  45.9 0.0 collective-permute-done.5.refs_2_
  45.9 0.0 copy-start.6
  45.9 0.0 copy-start.7
  45.9 0.2 pad_maximum_fusion.refs_4_
  46.1 0.1 collective-permute-start.12
  46.2 1.4 %collective-permute-start.13 = (bf16[256,512]{1,0:T(8,128)(2,1)S(1)}, bf16[256,512]{1,0:T(8,128)(2,1)S(1)}, u32[]{:S(2)}, u32[]{:S(2)}) collective-permute-start(bf16[256,512]{1,0:T(8,128)(2,1)S(1)} %collective-permute-done.4.refs_1_), channel_id=1, source_target_pairs={{0,16},{16,0},{1,17},{17,1},{2,18},{18,2},{3,19},{19,3},{4,20},{20... | collective-permute-start | bytes 786440 | tf_op jit(solution)/shard_map/ppermute | solution.py:497
  47.5 0.2 collective-permute-start.10
  47.7 0.3 collective-permute-start.11
  48.0 1.6 %collective-permute-done.10.refs_2_ = bf16[4,48,512]{2,1,0:T(8,128)(2,1)S(1)} collective-permute-done((bf16[4,48,512]{2,1,0:T(8,128)(2,1)S(1)}, bf16[4,48,512]{2,1,0:T(8,128)(2,1)S(1)}, u32[]{:S(2)}, u32[]{:S(2)}) %collective-permute-start.10) | collective-permute-done | bytes 196640 | tf_op jit(solution)/shard_map/ppermute | solution.py:499
  49.7 0.3 collective-permute-done.11.refs_3_
  49.9 0.0 collective-permute-done.12.refs_5_
  50.0 0.0 copy-done.6
  50.0 2.4 %near_products.1.near = f32[512,512]{1,0:T(8,128)S(1)} custom-call(s32[16]{0:T(128)S(1)} %copy-done.6, s32[16]{0:T(128)S(1)} %copy-done.7, bf16[1024,512]{1,0:T(8,128)(2,1)S(1)} %copy-done, bf16[4,48,512]{2,1,0:T(8,128)(2,1)S(1)} %pad_maximum_fusion.1.refs_0_, bf16[4,48,512]{2,1,0:T(8,128)(2,1)S(1)} %collective-permute-done.6.refs_1_, ...), custom_call_target="tpu_custom_call" | custom-call | flops 1 | bytes 1 | tf_op jit(solution)/shard_map/near_products/pallas_call | solution.py:343
  52.3 0.0 copy-start.1
  52.4 0.0 copy-start.5
  52.4 2.5 %collective-permute-done.13.refs_3_ = bf16[256,512]{1,0:T(8,128)(2,1)S(1)} collective-permute-done((bf16[256,512]{1,0:T(8,128)(2,1)S(1)}, bf16[256,512]{1,0:T(8,128)(2,1)S(1)}, u32[]{:S(2)}, u32[]{:S(2)}) %collective-permute-start.13) | collective-permute-done | bytes 262176 | tf_op jit(solution)/shard_map/ppermute | solution.py:497
  54.9 0.8 %far_products.1 = (bf16[128,512]{1,0:T(8,128)(2,1)S(1)}, bf16[128,512]{1,0:T(8,128)(2,1)S(1)}, bf16[128,512]{1,0:T(8,128)(2,1)S(1)}, bf16[128,512]{1,0:T(8,128)(2,1)S(1)}) custom-call(f32[512,512]{1,0:T(8,128)S(1)} %near_products.1.near, bf16[304,512]{1,0:T(8,128)(2,1)S(1)} %collective-permute-done.refs_0_, ...), custom_call_target="tpu_custom_call" | custom-call | flops 1 | bytes 1 | tf_op jit(solution)/shard_map/far_products/pallas_call | solution.py:388
  55.7 5.7 %collective-permute-start.14 = (bf16[128,512]{1,0:T(8,128)(2,1)S(1)}, bf16[128,512]{1,0:T(8,128)(2,1)S(1)}, u32[]{:S(2)}, u32[]{:S(2)}) collective-permute-start(bf16[128,512]{1,0:T(8,128)(2,1)S(1)} %get-tuple-element.59), channel_id=1, source_target_pairs={{0,2},{2,0},{4,6},{6,4},{1,3},{3,1},{5,7},{7,5},{8,10},{10,8},{12,... | collective-permute-start | bytes 393224 | tf_op jit(solution)/shard_map/ppermute | solution.py:472
  61.4 0.0 collective-permute-start.15
  61.4 1.5 %collective-permute-start.16 = (bf16[128,512]{1,0:T(8,128)(2,1)S(1)}, bf16[128,512]{1,0:T(8,128)(2,1)S(1)}, u32[]{:S(2)}, u32[]{:S(2)}) collective-permute-start(bf16[128,512]{1,0:T(8,128)(2,1)S(1)} %get-tuple-element.61), channel_id=1, source_target_pairs={{0,6},{2,4},{4,2},{6,0},{1,7},{3,5},{5,3},{7,1},{8,14},{10,12},{12... | collective-permute-start | bytes 393224 | tf_op jit(solution)/shard_map/ppermute | solution.py:472
  62.9 2.0 %collective-permute-done.14.refs_5_ = bf16[128,512]{1,0:T(8,128)(2,1)S(1)} collective-permute-done((bf16[128,512]{1,0:T(8,128)(2,1)S(1)}, bf16[128,512]{1,0:T(8,128)(2,1)S(1)}, u32[]{:S(2)}, u32[]{:S(2)}) %collective-permute-start.14) | collective-permute-done | bytes 131104 | tf_op jit(solution)/shard_map/ppermute | solution.py:472
  64.9 2.9 %collective-permute-done.15.refs_6_ = bf16[128,512]{1,0:T(8,128)(2,1)S(1)} collective-permute-done((bf16[128,512]{1,0:T(8,128)(2,1)S(1)}, bf16[128,512]{1,0:T(8,128)(2,1)S(1)}, u32[]{:S(2)}, u32[]{:S(2)}) %collective-permute-start.15) | collective-permute-done | bytes 131104 | tf_op jit(solution)/shard_map/ppermute | solution.py:472
  67.7 1.2 %collective-permute-done.16.refs_7_ = bf16[128,512]{1,0:T(8,128)(2,1)S(1)} collective-permute-done((bf16[128,512]{1,0:T(8,128)(2,1)S(1)}, bf16[128,512]{1,0:T(8,128)(2,1)S(1)}, u32[]{:S(2)}, u32[]{:S(2)}) %collective-permute-start.16) | collective-permute-done | bytes 131104 | tf_op jit(solution)/shard_map/ppermute | solution.py:472
  69.0 2.0 %finish_attention.1 = (bf16[128,4096]{1,0:T(8,128)(2,1)}, bf16[128,512]{1,0:T(8,128)(2,1)}) custom-call(s32[2]{0:T(128)S(1)} %copy-done.5, bf16[64,4096]{1,0:T(8,128)(2,1)S(1)} %copy-done.1, bf16[64,4096]{1,0:T(8,128)(2,1)S(1)} %copy-done.2, bf16[2,512,128]{2,1,0:T(8,128)(2,1)S(1)} %copy-done.3, bf16[2,512,128]{2,1,0:T(8,128)(2,1)S(1)} %copy-done.4, ...), custom_call_target="tpu_custom_call" | custom-call | flops 1 | bytes 1 | tf_op jit(solution)/shard_map/finish_attention/pallas_call | solution.py:431
  (19 shorter events, 0.1 us)
Async XLA Ops:
  3.9 25.0 %collective-permute-start = (bf16[304,512]{1,0:T(8,128)(2,1)}, bf16[304,512]{1,0:T(8,128)(2,1)S(1)}, u32[]{:S(2)}, u32[]{:S(2)}) collective-permute-start(bf16[304,512]{1,0:T(8,128)(2,1)} %get-tuple-element.35), channel_id=1, source_target_pairs={{0,8},{8,0},{1,9},{9,1},{2,10},{10,2},{3,11},{11,3},{4,12},{12,4},... | collective-permute-start | bytes 933896 | tf_op jit(solution)/shard_map/ppermute | solution.py:481
  8.0 20.6 %collective-permute-start.1 = (bf16[48,512]{1,0:T(8,128)(2,1)}, bf16[48,512]{1,0:T(8,128)(2,1)S(1)}, u32[]{:S(2)}, u32[]{:S(2)}) collective-permute-start(bf16[48,512]{1,0:T(8,128)(2,1)} %get-tuple-element.36), channel_id=1, source_target_pairs={{0,10},{2,8},{4,14},{6,12},{8,2},{10,0},{12,6},{14,4},{1,11},{3,9}... | collective-permute-start | bytes 147464 | tf_op jit(solution)/shard_map/ppermute | solution.py:476
  9.3 19.3 %collective-permute-start.2 = (bf16[48,512]{1,0:T(8,128)(2,1)}, bf16[48,512]{1,0:T(8,128)(2,1)S(1)}, u32[]{:S(2)}, u32[]{:S(2)}) collective-permute-start(bf16[48,512]{1,0:T(8,128)(2,1)} %get-tuple-element.37), channel_id=1, source_target_pairs={{0,12},{2,14},{4,8},{6,10},{8,4},{10,6},{12,0},{14,2},{1,13},{3,15... | collective-permute-start | bytes 147464 | tf_op jit(solution)/shard_map/ppermute | solution.py:476
  12.9 16.0 %collective-permute-start.3 = (bf16[48,512]{1,0:T(8,128)(2,1)}, bf16[48,512]{1,0:T(8,128)(2,1)S(1)}, u32[]{:S(2)}, u32[]{:S(2)}) collective-permute-start(bf16[48,512]{1,0:T(8,128)(2,1)} %get-tuple-element.38), channel_id=1, source_target_pairs={{0,14},{2,12},{4,10},{6,8},{8,6},{10,4},{12,2},{14,0},{1,15},{3,13... | collective-permute-start | bytes 147464 | tf_op jit(solution)/shard_map/ppermute | solution.py:476
  12.9 21.8 %collective-permute-start.7 = (bf16[176,1024]{1,0:T(8,128)(2,1)}, bf16[176,1024]{1,0:T(8,128)(2,1)S(1)}, u32[]{:S(2)}, u32[]{:S(2)}) collective-permute-start(bf16[176,1024]{1,0:T(8,128)(2,1)} %get-tuple-element.49), channel_id=1, source_target_pairs={{0,4},{2,6},{4,0},{6,2},{1,5},{3,7},{5,1},{7,3},{8,12},{10,14},{12... | collective-permute-start | bytes 1081352 | tf_op jit(solution)/shard_map/ppermute | solution.py:472
  12.9 15.7 %copy-start.10 = (bf16[176,1024]{1,0:T(8,128)(2,1)S(1)}, bf16[176,1024]{1,0:T(8,128)(2,1)}, u32[]{:S(2)}) copy-start(bf16[176,1024]{1,0:T(8,128)(2,1)} %get-tuple-element.50) | copy-start | bytes 1081348
  12.9 15.7 %copy-start.9 = (bf16[176,1024]{1,0:T(8,128)(2,1)S(1)}, bf16[176,1024]{1,0:T(8,128)(2,1)}, u32[]{:S(2)}) copy-start(bf16[176,1024]{1,0:T(8,128)(2,1)} %get-tuple-element.51) | copy-start | bytes 1081348
  12.9 17.8 %copy-start.11 = (bf16[256,512]{1,0:T(8,128)(2,1)S(1)}, bf16[256,512]{1,0:T(8,128)(2,1)}, u32[]{:S(2)}) copy-start(bf16[256,512]{1,0:T(8,128)(2,1)} %get-tuple-element.48) | copy-start | bytes 786436
  28.5 16.7 %collective-permute-start.8 = (bf16[176,1024]{1,0:T(8,128)(2,1)S(1)}, bf16[176,1024]{1,0:T(8,128)(2,1)S(1)}, u32[]{:S(2)}, u32[]{:S(2)}) collective-permute-start(bf16[176,1024]{1,0:T(8,128)(2,1)S(1)} %copy-done.10), channel_id=1, source_target_pairs={{0,6},{2,4},{4,2},{6,0},{1,7},{3,5},{5,3},{7,1},{8,14},{10,12},{12... | collective-permute-start | bytes 1081352 | tf_op jit(solution)/shard_map/ppermute | solution.py:472
  28.5 17.1 %collective-permute-start.9 = (bf16[176,1024]{1,0:T(8,128)(2,1)S(1)}, bf16[176,1024]{1,0:T(8,128)(2,1)S(1)}, u32[]{:S(2)}, u32[]{:S(2)}) collective-permute-start(bf16[176,1024]{1,0:T(8,128)(2,1)S(1)} %copy-done.9), channel_id=1, source_target_pairs={{0,2},{2,0},{4,6},{6,4},{1,3},{3,1},{5,7},{7,5},{8,10},{10,8},{12,... | collective-permute-start | bytes 1081352 | tf_op jit(solution)/shard_map/ppermute | solution.py:472
  28.9 17.0 %collective-permute-start.5 = (bf16[304,512]{1,0:T(8,128)(2,1)S(1)}, bf16[304,512]{1,0:T(8,128)(2,1)S(1)}, u32[]{:S(2)}, u32[]{:S(2)}) collective-permute-start(bf16[304,512]{1,0:T(8,128)(2,1)S(1)} %collective-permute-done.refs_0_), channel_id=1, source_target_pairs={{0,16},{16,0},{1,17},{17,1},{2,18},{18,2},{3,19},{19,3},{4,20},{20... | collective-permute-start | bytes 933896 | tf_op jit(solution)/shard_map/ppermute | solution.py:489
  30.7 15.2 %collective-permute-start.4 = (bf16[256,512]{1,0:T(8,128)(2,1)S(1)}, bf16[256,512]{1,0:T(8,128)(2,1)S(1)}, u32[]{:S(2)}, u32[]{:S(2)}) collective-permute-start(bf16[256,512]{1,0:T(8,128)(2,1)S(1)} %copy-done.11), channel_id=1, source_target_pairs={{0,8},{8,0},{1,9},{9,1},{2,10},{10,2},{3,11},{11,3},{4,12},{12,4},... | collective-permute-start | bytes 786440 | tf_op jit(solution)/shard_map/ppermute | solution.py:488
  34.7 11.2 %copy-start.8 = (bf16[176,1024]{1,0:T(8,128)(2,1)S(1)}, bf16[176,1024]{1,0:T(8,128)(2,1)}, u32[]{:S(2)}) copy-start(bf16[176,1024]{1,0:T(8,128)(2,1)} %get-tuple-element.32) | copy-start | bytes 1081348
  34.7 10.9 %collective-permute-start.6 = (bf16[4,48,512]{2,1,0:T(8,128)(2,1)S(1)}, bf16[4,48,512]{2,1,0:T(8,128)(2,1)S(1)}, u32[]{:S(2)}, u32[]{:S(2)}) collective-permute-start(bf16[4,48,512]{2,1,0:T(8,128)(2,1)S(1)} %pad_maximum_fusion.1.refs_0_), channel_id=1, source_target_pairs={{0,16},{16,0},{1,17},{17,1},{2,18},{18,2},{3,19},{19,3},{4,20},{20... | collective-permute-start | bytes 589832 | tf_op jit(solution)/shard_map/ppermute | solution.py:490
  45.9 4.1 %copy-start = (bf16[1024,512]{1,0:T(8,128)(2,1)S(1)}, bf16[1024,512]{1,0:T(8,128)(2,1)}, u32[]{:S(2)}) copy-start(bf16[1024,512]{1,0:T(8,128)(2,1)} %own_ref.1) | copy-start | bytes 3145732
  45.9 4.1 %copy-start.6 = (s32[16]{0:T(128)S(1)}, s32[16]{0:T(128)}, u32[]{:S(2)}) copy-start(s32[16]{0:T(128)} %position.1) | copy-start | bytes 196
  45.9 4.1 %copy-start.7 = (s32[16]{0:T(128)S(1)}, s32[16]{0:T(128)}, u32[]{:S(2)}) copy-start(s32[16]{0:T(128)} %adapter.1) | copy-start | bytes 196
  46.1 3.9 %collective-permute-start.12 = (bf16[4,176,1024]{2,1,0:T(8,128)(2,1)S(1)}, bf16[4,176,1024]{2,1,0:T(8,128)(2,1)S(1)}, u32[]{:S(2)}, u32[]{:S(2)}) collective-permute-start(bf16[4,176,1024]{2,1,0:T(8,128)(2,1)S(1)} %pad_maximum_fusion.refs_4_), channel_id=1, source_target_pairs={{0,1},{1,0},{2,3},{3,2},{4,5},{5,4},{6,7},{7,6},{8,9},{9,8},{10,11... | collective-permute-start | bytes 4325384 | tf_op jit(solution)/shard_map/ppermute | solution.py:500
  46.2 8.7 %collective-permute-start.13 = (bf16[256,512]{1,0:T(8,128)(2,1)S(1)}, bf16[256,512]{1,0:T(8,128)(2,1)S(1)}, u32[]{:S(2)}, u32[]{:S(2)}) collective-permute-start(bf16[256,512]{1,0:T(8,128)(2,1)S(1)} %collective-permute-done.4.refs_1_), channel_id=1, source_target_pairs={{0,16},{16,0},{1,17},{17,1},{2,18},{18,2},{3,19},{19,3},{4,20},{20... | collective-permute-start | bytes 786440 | tf_op jit(solution)/shard_map/ppermute | solution.py:497
  47.5 2.1 %collective-permute-start.10 = (bf16[4,48,512]{2,1,0:T(8,128)(2,1)S(1)}, bf16[4,48,512]{2,1,0:T(8,128)(2,1)S(1)}, u32[]{:S(2)}, u32[]{:S(2)}) collective-permute-start(bf16[4,48,512]{2,1,0:T(8,128)(2,1)S(1)} %pad_maximum_fusion.1.refs_0_), channel_id=1, source_target_pairs={{0,1},{1,0},{2,3},{3,2},{4,5},{5,4},{6,7},{7,6},{8,9},{9,8},{10,11... | collective-permute-start | bytes 589832 | tf_op jit(solution)/shard_map/ppermute | solution.py:499
  47.7 2.2 %collective-permute-start.11 = (bf16[4,48,512]{2,1,0:T(8,128)(2,1)S(1)}, bf16[4,48,512]{2,1,0:T(8,128)(2,1)S(1)}, u32[]{:S(2)}, u32[]{:S(2)}) collective-permute-start(bf16[4,48,512]{2,1,0:T(8,128)(2,1)S(1)} %collective-permute-done.6.refs_1_), channel_id=1, source_target_pairs={{0,1},{1,0},{2,3},{3,2},{4,5},{5,4},{6,7},{7,6},{8,9},{9,8},{10,11... | collective-permute-start | bytes 589832 | tf_op jit(solution)/shard_map/ppermute | solution.py:499
  52.3 16.6 %copy-start.1 = (bf16[64,4096]{1,0:T(8,128)(2,1)S(1)}, bf16[64,4096]{1,0:T(8,128)(2,1)}, u32[]{:S(2)}) copy-start(bf16[64,4096]{1,0:T(8,128)(2,1)} %get-tuple-element.34.refs_0_) | copy-start | bytes 1572868
  52.4 16.6 %copy-start.2 = (bf16[64,4096]{1,0:T(8,128)(2,1)S(1)}, bf16[64,4096]{1,0:T(8,128)(2,1)}, u32[]{:S(2)}) copy-start(bf16[64,4096]{1,0:T(8,128)(2,1)} %get-tuple-element.45.refs_1_) | copy-start | bytes 1572868
  52.4 16.6 %copy-start.3 = (bf16[2,512,128]{2,1,0:T(8,128)(2,1)S(1)}, bf16[2,512,128]{2,1,0:T(8,128)(2,1)}, u32[]{:S(2)}) copy-start(bf16[2,512,128]{2,1,0:T(8,128)(2,1)} %get-tuple-element.39.refs_2_) | copy-start | bytes 786436
  52.4 16.6 %copy-start.4 = (bf16[2,512,128]{2,1,0:T(8,128)(2,1)S(1)}, bf16[2,512,128]{2,1,0:T(8,128)(2,1)}, u32[]{:S(2)}) copy-start(bf16[2,512,128]{2,1,0:T(8,128)(2,1)} %get-tuple-element.46.refs_3_) | copy-start | bytes 786436
  52.4 16.6 %copy-start.5 = (s32[2]{0:T(128)S(1)}, s32[2]{0:T(128)}, u32[]{:S(2)}) copy-start(s32[2]{0:T(128)} %lens.3) | copy-start | bytes 28
  55.7 9.2 %collective-permute-start.14 = (bf16[128,512]{1,0:T(8,128)(2,1)S(1)}, bf16[128,512]{1,0:T(8,128)(2,1)S(1)}, u32[]{:S(2)}, u32[]{:S(2)}) collective-permute-start(bf16[128,512]{1,0:T(8,128)(2,1)S(1)} %get-tuple-element.59), channel_id=1, source_target_pairs={{0,2},{2,0},{4,6},{6,4},{1,3},{3,1},{5,7},{7,5},{8,10},{10,8},{12,... | collective-permute-start | bytes 393224 | tf_op jit(solution)/shard_map/ppermute | solution.py:472
  61.4 6.4 %collective-permute-start.15 = (bf16[128,512]{1,0:T(8,128)(2,1)S(1)}, bf16[128,512]{1,0:T(8,128)(2,1)S(1)}, u32[]{:S(2)}, u32[]{:S(2)}) collective-permute-start(bf16[128,512]{1,0:T(8,128)(2,1)S(1)} %get-tuple-element.60), channel_id=1, source_target_pairs={{0,4},{2,6},{4,0},{6,2},{1,5},{3,7},{5,1},{7,3},{8,12},{10,14},{12... | collective-permute-start | bytes 393224 | tf_op jit(solution)/shard_map/ppermute | solution.py:472
  61.4 7.6 %collective-permute-start.16 = (bf16[128,512]{1,0:T(8,128)(2,1)S(1)}, bf16[128,512]{1,0:T(8,128)(2,1)S(1)}, u32[]{:S(2)}, u32[]{:S(2)}) collective-permute-start(bf16[128,512]{1,0:T(8,128)(2,1)S(1)} %get-tuple-element.61), channel_id=1, source_target_pairs={{0,6},{2,4},{4,2},{6,0},{1,7},{3,5},{5,3},{7,1},{8,14},{10,12},{12... | collective-permute-start | bytes 393224 | tf_op jit(solution)/shard_map/ppermute | solution.py:472

commit v13 on v12

--- a/solution.py
+++ b/solution.py
@@ -56,12 +56,7 @@
     ]
     for copy in small:
         copy.start()
-    for i in range(chunks):
-
-        @pl.when(i * chunk < length)
-        def _():
-            copy_in(0, i).start()
-            copy_in(1, i).start()
+    copy_in(0, 0).start()
 
     def dead_slots(i):
         return i * chunk + lax.broadcasted_iota(jnp.int32, ks.shape[1:], 0) >= length
@@ -97,6 +92,7 @@
 
     for copy in small:
         copy.wait()
+    copy_in(1, 0).start()
     for k in range(kv_heads):
         for h in range(group_size):
             qs[k, h * SPAN : (h + 1) * SPAN, :] = q_s[:, tiles(k * group_size + h)]
@@ -105,6 +101,13 @@
         acc[k] = jnp.zeros((HD + ONES, rows), jnp.float32)
     p_s[1] = jnp.zeros((chunk, rows), jnp.bfloat16)
     arrive_keys(0)
+    for i in range(1, chunks):
+
+        @pl.when(i * chunk < length)
+        def _():
+            copy_in(0, i).start()
+            copy_in(1, i).start()
+
     s = dot_last(ks[0, :, :HD], qs[0])
     s_s[0] = s
     x_s[0] = tile_max(s)
@@ -206,31 +209,68 @@
     )(lengths, queries, fresh_keys, keys, values)
 
 
-def pack_kernel(x_hbm, d_hbm, u_hbm, w_hbm, *refs):
-    quads = (len(refs) - 2) // 2
-    tokens_out, (early, late, sems) = refs[:quads], refs[-3:]
-    size = w_hbm.shape[0] // 2 - late.shape[0]
-    maps_out = [early.at[size:, :], *refs[quads:-3]]
+def run_copies(copies, sems):
+    copies = [pltpu.make_async_copy(src, dst, sems.at[i]) for i, (src, dst) in enumerate(copies)]
+    for copy in copies:
+        copy.start()
+    for copy in copies:
+        copy.wait()
+
+
+def cross_kernel(d_hbm, u_hbm, w_hbm, early, late, *refs):
+    maps_out, sems = [early, *refs[:-1]], refs[-1]
     part, core, quad = lax.axis_index("parts") % 2, lax.axis_index("tensor"), lax.axis_index("quad")
+    width, cols = w_hbm.shape
+    step = min(cols, width)
+    size = width // 2 - late.shape[0]
+    mine = pl.ds(pl.multiple_of(part * RANK, RANK), RANK)
+    begin = part * (width // 2)
+    copies = [
+        (w_hbm.at[pl.ds(pl.multiple_of(begin, RANK), size), :], early.at[:size, :]),
+        (w_hbm.at[pl.ds(pl.multiple_of(begin + size, RANK), late.shape[0]), :], late),
+    ]
+    for q, out in enumerate(maps_out):
+        base = size if q == 0 else 0
+        begin = core * (d_hbm.shape[1] // 2) + (quad ^ q) * width
+        sources = [
+            d_hbm.at[mine, pl.ds(pl.multiple_of(begin + first, step), step)] for first in range(0, width, step)
+        ]
+        sources += [u_hbm.at[mine, first : first + step] for first in range(0, cols, step)]
+        for i, source in enumerate(sources):
+            copies.append((source, out.at[base + i * RANK : base + (i + 1) * RANK, :step]))
+    run_copies(copies, sems)
+
+
+def cross_pack(downs, ups, weights, quads):
+    vmem = pl.BlockSpec(memory_space=pltpu.VMEM)
+    hbm = pl.BlockSpec(memory_space=pltpu.HBM)
+    width, cols = weights.shape
+    step = min(cols, width)
+    pieces = (width + cols) // step
+    first = width // 2 * 13 // 32 // RANK * RANK
+    sizes = [(first + RANK * pieces, cols), (width // 2 - first, cols)]
+    sizes += [(RANK * pieces, step)] * (quads - 1)
+    return pl.pallas_call(
+        cross_kernel,
+        in_specs=[hbm] * 3,
+        out_specs=[vmem] * len(sizes),
+        out_shape=[jax.ShapeDtypeStruct(size, weights.dtype) for size in sizes],
+        scratch_shapes=[pltpu.SemaphoreType.DMA((quads * pieces + 2,))],
+        compiler_params=pltpu.CompilerParams(vmem_limit_bytes=57 * MIB),
+        cost_estimate=FREE,
+        name="cross_pack",
+    )(downs, ups, weights)
+
+
+def quad_kernel(x_hbm, d_hbm, u_hbm, *refs):
+    outs, sems = refs[:-1], refs[-1]
+    core, quad = lax.axis_index("tensor"), lax.axis_index("quad")
     tokens, features = x_hbm.shape
-    width, cols = w_hbm.shape
-    ranks = d_hbm.shape[0]
+    ranks, cols = u_hbm.shape
+    width = outs[0].shape[1]
     step = min(cols, width)
-    mine = pl.ds(pl.multiple_of(part * RANK, RANK), RANK)
     copies = []
-    for q, out in enumerate(maps_out):
-        begin = core * features + (quad ^ q) * width
-        for i, first in enumerate(range(0, width, step)):
-            here = pl.ds(pl.multiple_of(begin + first, step), step)
-            copies.append((d_hbm.at[mine, here], out.at[i * RANK : (i + 1) * RANK, :step]))
-        for i, first in enumerate(range(0, cols, step)):
-            row = width // step * RANK + i * RANK
-            copies.append((u_hbm.at[mine, first : first + step], out.at[row : row + RANK, :step]))
-    begin = part * (width // 2)
-    copies.append((w_hbm.at[pl.ds(pl.multiple_of(begin, RANK), size), :], early.at[:size, :]))
-    begin = begin + size
-    copies.append((w_hbm.at[pl.ds(pl.multiple_of(begin, RANK), late.shape[0]), :], late))
-    for q, out in enumerate(tokens_out):
+    for q, out in enumerate(outs):
         here = pl.ds(pl.multiple_of((quad ^ q) * width, width), width)
         copies.append((x_hbm.at[:, here], out.at[:tokens, :]))
         here = pl.ds(pl.multiple_of(core * features + (quad ^ q) * width, width), width)
@@ -239,11 +279,7 @@
             row += tokens + ranks
             up = u_hbm.at[slot * RANK : (slot + 1) * RANK, first : first + step]
             copies.append((up, out.at[row : row + RANK, col : col + step]))
-    copies = [pltpu.make_async_copy(src, dst, sems.at[i]) for i, (src, dst) in enumerate(copies)]
-    for copy in copies:
-        copy.start()
-    for copy in copies:
-        copy.wait()
+    run_copies(copies, sems)
 
 
 def up_places(cols, width):
@@ -255,29 +291,22 @@
     ]
 
 
-def pack(tokens, downs, ups, weights, quads):
+def quad_pack(tokens, downs, ups, width, quads):
     vmem = pl.BlockSpec(memory_space=pltpu.VMEM)
     hbm = pl.BlockSpec(memory_space=pltpu.HBM)
     ranks, cols = ups.shape
-    width = weights.shape[0]
-    step = min(cols, width)
-    kind = tokens.dtype
-    pieces = (width + cols) // step
-    first = width // 4
-    sizes = [(tokens.shape[0] + ranks + RANK * (2 * cols // width), width)] * quads
-    sizes += [(RANK * pieces, step)] * (quads - 1)
-    sizes += [(first + RANK * pieces, cols), (width // 2 - first, cols)]
-    count = quads * (pieces + 2 + len(up_places(cols, width))) + 2
+    block = (tokens.shape[0] + ranks + RANK * (2 * cols // width), width)
+    count = quads * (2 + len(up_places(cols, width)))
     return pl.pallas_call(
-        pack_kernel,
-        in_specs=[hbm] * 4,
-        out_specs=[vmem] * len(sizes),
-        out_shape=[jax.ShapeDtypeStruct(size, kind) for size in sizes],
+        quad_kernel,
+        in_specs=[hbm] * 3,
+        out_specs=[vmem] * quads,
+        out_shape=[jax.ShapeDtypeStruct(block, tokens.dtype)] * quads,
         scratch_shapes=[pltpu.SemaphoreType.DMA((count,))],
         compiler_params=pltpu.CompilerParams(vmem_limit_bytes=57 * MIB),
         cost_estimate=FREE,
-        name="pack",
-    )(tokens, downs, ups, weights)
+        name="quad_pack",
+    )(tokens, downs, ups)
 
 
 def near_kernel(tokens, quads, position, adapter, own_ref, *refs):
@@ -475,11 +504,12 @@
         pairs = [(w * quads + j, (1 - w) * quads + (j ^ q)) for w in range(2) for j in range(quads)]
         return lax.ppermute(value, ("wing", "quad"), pairs)
 
-    *blocks, early, late = pack(normed_inputs, downs, ups, value_matrix, quads)
+    early, late, *maps = cross_pack(downs, ups, value_matrix, quads)
+    blocks = quad_pack(after(normed_inputs, early), downs, ups, width, quads)
     order = [*range(quads // 2, quads), *range(1, quads // 2)]
     mine = [to_quad(blocks[q], q) for q in order]
     early = lax.ppermute(early, "wing", SWAP)
-    maps = [to_other_wing(blocks[quads - 1 + q], q) for q in range(1, quads)]
+    maps = [to_other_wing(each, q + 1) for q, each in enumerate(maps)]
 
     attn = [attention(0, after(cache_length, blocks[0]))]
     early, *maps = lax.optimization_barrier((early, *maps, attn[0][1]))[:-1]

time: 71.1 us -> 68.3 us (0.961)
  starting transfers between devices: 24.8 us -> 22.8 us
  waiting for transfers between devices: 14.9 us -> 13 us
  Pallas kernels: 30.1 us -> 31.1 us
    ppermute x3, waiting for transfers between devices: 3.89 us -> 0.01 us  [to_other_wing(): return lax.ppermute(value, ('wing', 'quad'), pairs)]
    ppermute x1, starting transfers between devices: 3.96 us -> 2.28 us  [on_device(): late = lax.ppermute(after(late, early), 'wing', SWAP)]
    pallas_call x1 -> x2, Pallas kernels: 3.22 us -> 4.71 us  [the longest x1 2.6 us: quad_pack(): pl.pallas_call(quad_kernel, in_specs=[hbm] * 3, out_specs=[vmem] * quads,...]
    ppermute x1, waiting for transfers between devices: 2.49 us -> 3.61 us  [on_device(): late_other = lax.ppermute(late, 'parts', parts_swap)]
    ppermute x6, waiting for transfers between devices: 6.41 us -> 7.33 us  [to_quad(): return lax.ppermute(value, 'quad', [(j, j ^ q) for j in range(quads)])]
  transfers between devices with their start and end apart: 17 -> 17, of which waited for: 9 -> 9; matrix products, arithmetic and copies ran while one was open for 0% -> 0% of each run, Pallas kernels for 34% -> 39%
where the time goes in v13:
time: 68.3 us; the launch traced here: 67.9 us
  Pallas kernels  31.1 us (46%)
  starting transfers between devices  22.8 us (33%)
  waiting for transfers between devices  13 us (19%)
  between operations  0.86 us (1%)
    pallas_call x2, Pallas kernels, cache_attention(): pl.pallas_call(functools.partial(cache_kernel, order), in_specs=[pl.Block...  21.2 us
    ppermute x6, waiting for transfers between devices, to_quad(): return lax.ppermute(value, 'quad', [(j, j ^ q) for j in range(quads)])  7.33 us
    ppermute x6, starting transfers between devices, to_quad(): return lax.ppermute(value, 'quad', [(j, j ^ q) for j in range(quads)])  7.13 us
    ppermute x3, starting transfers between devices, to_other_wing(): return lax.ppermute(value, ('wing', 'quad'), pairs)  4.9 us
    ppermute x1, starting transfers between devices, on_device(): early = lax.ppermute(early, 'wing', SWAP)  4.1 us
    ppermute x1, waiting for transfers between devices, on_device(): late_other = lax.ppermute(late, 'parts', parts_swap)  3.61 us
    pallas_call x1, Pallas kernels, quad_pack(): pl.pallas_call(quad_kernel, in_specs=[hbm] * 3, out_specs=[vmem] * quads,...  2.6 us
    pallas_call x1, Pallas kernels, near_products(): pl.pallas_call(functools.partial(near_kernel, tokens, quads), in_specs=[s...  2.37 us
  transfers between devices with their start and end apart: 17, of which 9 were waited for; matrix products, arithmetic and copies ran while one was open for 0% of the time, Pallas kernels for 39%

profile of v13, /device:TPU:0, one launch (start us, length us, event | category | flops | bytes accessed | tf_op | source)
XLA Modules:
  0.0 67.9 jit_solution(11815967324637890284)
XLA Ops:
  0.6 2.1 %cross_pack.1 = (bf16[256,512]{1,0:T(8,128)(2,1)}, bf16[304,512]{1,0:T(8,128)(2,1)}, bf16[48,512]{1,0:T(8,128)(2,1)}, bf16[48,512]{1,0:T(8,128)(2,1)}, bf16[48,512]{1,0:T(8,128)(2,1)}) custom-call(bf16[32,8192]{1,0:T(8,128)(2,1)} %bitcast.11, bf16[32,512]{1,0:T(8,128)(2,1)} %bitcast.17, bf16[1024,512]{1,0:T(8,128)(2,1)} %own_ref.1), custom_call_target="tpu_custom_call" | custom-call | flops 1 | bytes 1 | tf_op jit(solution)/shard_map/cross_pack/pallas_call | solution.py:253
  2.7 4.1 %collective-permute-start = (bf16[256,512]{1,0:T(8,128)(2,1)}, bf16[256,512]{1,0:T(8,128)(2,1)S(1)}, u32[]{:S(2)}, u32[]{:S(2)}) collective-permute-start(bf16[256,512]{1,0:T(8,128)(2,1)} %get-tuple-element.33), channel_id=1, source_target_pairs={{0,8},{8,0},{1,9},{9,1},{2,10},{10,2},{3,11},{11,3},{4,12},{12,4},... | collective-permute-start | bytes 786440 | tf_op jit(solution)/shard_map/ppermute | solution.py:511
  6.8 1.3 %collective-permute-start.1 = (bf16[48,512]{1,0:T(8,128)(2,1)}, bf16[48,512]{1,0:T(8,128)(2,1)S(1)}, u32[]{:S(2)}, u32[]{:S(2)}) collective-permute-start(bf16[48,512]{1,0:T(8,128)(2,1)} %get-tuple-element.38), channel_id=1, source_target_pairs={{0,10},{2,8},{4,14},{6,12},{8,2},{10,0},{12,6},{14,4},{1,11},{3,9}... | collective-permute-start | bytes 147464 | tf_op jit(solution)/shard_map/ppermute | solution.py:505
  8.1 3.6 %collective-permute-start.2 = (bf16[48,512]{1,0:T(8,128)(2,1)}, bf16[48,512]{1,0:T(8,128)(2,1)S(1)}, u32[]{:S(2)}, u32[]{:S(2)}) collective-permute-start(bf16[48,512]{1,0:T(8,128)(2,1)} %get-tuple-element.39), channel_id=1, source_target_pairs={{0,12},{2,14},{4,8},{6,10},{8,4},{10,6},{12,0},{14,2},{1,13},{3,15... | collective-permute-start | bytes 147464 | tf_op jit(solution)/shard_map/ppermute | solution.py:505
  11.7 0.0 collective-permute-start.3
  11.7 2.6 %quad_pack.1 = (bf16[176,1024]{1,0:T(8,128)(2,1)}, bf16[176,1024]{1,0:T(8,128)(2,1)}, bf16[176,1024]{1,0:T(8,128)(2,1)}, bf16[176,1024]{1,0:T(8,128)(2,1)}) custom-call(bf16[128,4096]{1,0:T(8,128)(2,1)} %x_hbm, bf16[32,8192]{1,0:T(8,128)(2,1)} %bitcast.12, bf16[32,512]{1,0:T(8,128)(2,1)} %bitcast.18), custom_call_target="tpu_custom_call" | custom-call | flops 1 | bytes 1 | tf_op jit(solution)/shard_map/quad_pack/pallas_call | solution.py:300
  14.3 0.1 collective-permute-start.7
  14.5 11.5 %cache_attention.2 = (bf16[64,4096]{1,0:T(8,128)(2,1)}, bf16[2,512,128]{2,1,0:T(8,128)(2,1)}) custom-call(s32[2]{0:T(128)} %lens.3, bf16[128,4096]{1,0:T(8,128)(2,1)} %q_hbm.3, bf16[128,512]{1,0:T(8,128)(2,1)} %fk_hbm.3, bf16[2,2048,512]{2,1,0:T(8,128)(2,1)} %k_hbm.3, bf16[2,2048,512]{2,1,0:T(8,128)(2,1)} %v_hbm.3), custom_call_target="tpu_custom_call" | custom-call | flops 1 | bytes 1 | tf_op jit(solution)/shard_map/cache_attention/pallas_call | solution.py:180
  25.9 0.0 collective-permute-done.1
  25.9 2.9 %collective-permute-start.8 = (bf16[176,1024]{1,0:T(8,128)(2,1)S(1)}, bf16[176,1024]{1,0:T(8,128)(2,1)S(1)}, u32[]{:S(2)}, u32[]{:S(2)}) collective-permute-start(bf16[176,1024]{1,0:T(8,128)(2,1)S(1)} %copy-done.10), channel_id=1, source_target_pairs={{0,6},{2,4},{4,2},{6,0},{1,7},{3,5},{5,3},{7,1},{8,14},{10,12},{12... | collective-permute-start | bytes 1081352 | tf_op jit(solution)/shard_map/ppermute | solution.py:501
  28.9 0.0 collective-permute-done.2
  28.9 0.0 copy-done.9
  28.9 0.6 collective-permute-start.9
  29.5 0.0 collective-permute-done.3
  29.5 0.0 collective-permute-done.refs_0_
  29.5 1.7 %collective-permute-start.5 = (bf16[256,512]{1,0:T(8,128)(2,1)S(1)}, bf16[256,512]{1,0:T(8,128)(2,1)S(1)}, u32[]{:S(2)}, u32[]{:S(2)}) collective-permute-start(bf16[256,512]{1,0:T(8,128)(2,1)S(1)} %collective-permute-done.refs_0_), channel_id=1, source_target_pairs={{0,16},{16,0},{1,17},{17,1},{2,18},{18,2},{3,19},{19,3},{4,20},{20... | collective-permute-start | bytes 786440 | tf_op jit(solution)/shard_map/ppermute | solution.py:519
  31.2 2.3 %collective-permute-start.4 = (bf16[304,512]{1,0:T(8,128)(2,1)S(1)}, bf16[304,512]{1,0:T(8,128)(2,1)S(1)}, u32[]{:S(2)}, u32[]{:S(2)}) collective-permute-start(bf16[304,512]{1,0:T(8,128)(2,1)S(1)} %copy-done.11), channel_id=1, source_target_pairs={{0,8},{8,0},{1,9},{9,1},{2,10},{10,2},{3,11},{11,3},{4,12},{12,4},... | collective-permute-start | bytes 933896 | tf_op jit(solution)/shard_map/ppermute | solution.py:518
  33.5 0.0 collective-permute-done.7
  33.5 0.2 collective-permute-start.6
  33.7 9.8 %cache_attention.3 = (bf16[64,4096]{1,0:T(8,128)(2,1)}, bf16[2,512,128]{2,1,0:T(8,128)(2,1)}) custom-call(s32[2]{0:T(128)} %lens.3, bf16[128,4096]{1,0:T(8,128)(2,1)} %q_hbm.3, bf16[128,512]{1,0:T(8,128)(2,1)} %fk_hbm.3, bf16[2,2048,512]{2,1,0:T(8,128)(2,1)} %k_hbm.3, bf16[2,2048,512]{2,1,0:T(8,128)(2,1)} %v_hbm.3), custom_call_target="tpu_custom_call" | custom-call | flops 1 | bytes 1 | tf_op jit(solution)/shard_map/cache_attention/pallas_call | solution.py:180
  43.5 1.1 %collective-permute-done.8 = bf16[176,1024]{1,0:T(8,128)(2,1)S(1)} collective-permute-done((bf16[176,1024]{1,0:T(8,128)(2,1)S(1)}, bf16[176,1024]{1,0:T(8,128)(2,1)S(1)}, u32[]{:S(2)}, u32[]{:S(2)}) %collective-permute-start.8) | collective-permute-done | bytes 360480 | tf_op jit(solution)/shard_map/ppermute | solution.py:501
  44.5 0.6 collective-permute-done.9
  45.2 0.0 collective-permute-done.6.refs_1_
  45.2 0.0 collective-permute-done.5.refs_2_
  45.2 0.6 collective-permute-done.4.refs_1_
  45.8 0.2 pad_maximum_fusion.refs_4_
  46.0 0.1 collective-permute-start.12
  46.1 1.9 %collective-permute-start.13 = (bf16[304,512]{1,0:T(8,128)(2,1)S(1)}, bf16[304,512]{1,0:T(8,128)(2,1)S(1)}, u32[]{:S(2)}, u32[]{:S(2)}) collective-permute-start(bf16[304,512]{1,0:T(8,128)(2,1)S(1)} %collective-permute-done.4.refs_1_), channel_id=1, source_target_pairs={{0,16},{16,0},{1,17},{17,1},{2,18},{18,2},{3,19},{19,3},{4,20},{20... | collective-permute-start | bytes 933896 | tf_op jit(solution)/shard_map/ppermute | solution.py:527
  47.9 0.2 collective-permute-start.10
  48.1 0.3 collective-permute-start.11
  48.5 1.1 %collective-permute-done.10.refs_2_ = bf16[4,48,512]{2,1,0:T(8,128)(2,1)S(1)} collective-permute-done((bf16[4,48,512]{2,1,0:T(8,128)(2,1)S(1)}, bf16[4,48,512]{2,1,0:T(8,128)(2,1)S(1)}, u32[]{:S(2)}, u32[]{:S(2)}) %collective-permute-start.10) | collective-permute-done | bytes 196640 | tf_op jit(solution)/shard_map/ppermute | solution.py:529
  49.6 0.3 collective-permute-done.11.refs_3_
  49.8 0.0 collective-permute-done.12.refs_5_
  49.8 0.0 copy-done
  49.9 2.4 %near_products.1.near = f32[512,512]{1,0:T(8,128)S(1)} custom-call(s32[16]{0:T(128)S(1)} %copy-done.6, s32[16]{0:T(128)S(1)} %copy-done.7, bf16[1024,512]{1,0:T(8,128)(2,1)S(1)} %copy-done, bf16[4,48,512]{2,1,0:T(8,128)(2,1)S(1)} %pad_maximum_fusion.1.refs_0_, bf16[4,48,512]{2,1,0:T(8,128)(2,1)S(1)} %collective-permute-done.6.refs_1_, ...), custom_call_target="tpu_custom_call" | custom-call | flops 1 | bytes 1 | tf_op jit(solution)/shard_map/near_products/pallas_call | solution.py:372
  52.2 0.0 copy-start.1
  52.3 0.0 copy-start.5
  52.3 3.6 %collective-permute-done.13.refs_3_ = bf16[304,512]{1,0:T(8,128)(2,1)S(1)} collective-permute-done((bf16[304,512]{1,0:T(8,128)(2,1)S(1)}, bf16[304,512]{1,0:T(8,128)(2,1)S(1)}, u32[]{:S(2)}, u32[]{:S(2)}) %collective-permute-start.13) | collective-permute-done | bytes 311328 | tf_op jit(solution)/shard_map/ppermute | solution.py:527
  55.9 0.8 %far_products.1 = (bf16[128,512]{1,0:T(8,128)(2,1)S(1)}, bf16[128,512]{1,0:T(8,128)(2,1)S(1)}, bf16[128,512]{1,0:T(8,128)(2,1)S(1)}, bf16[128,512]{1,0:T(8,128)(2,1)S(1)}) custom-call(f32[512,512]{1,0:T(8,128)S(1)} %near_products.1.near, bf16[256,512]{1,0:T(8,128)(2,1)S(1)} %collective-permute-done.refs_0_, ...), custom_call_target="tpu_custom_call" | custom-call | flops 1 | bytes 1 | tf_op jit(solution)/shard_map/far_products/pallas_call | solution.py:417
  56.7 1.2 %collective-permute-start.14 = (bf16[128,512]{1,0:T(8,128)(2,1)S(1)}, bf16[128,512]{1,0:T(8,128)(2,1)S(1)}, u32[]{:S(2)}, u32[]{:S(2)}) collective-permute-start(bf16[128,512]{1,0:T(8,128)(2,1)S(1)} %get-tuple-element.61), channel_id=1, source_target_pairs={{0,2},{2,0},{4,6},{6,4},{1,3},{3,1},{5,7},{7,5},{8,10},{10,8},{12,... | collective-permute-start | bytes 393224 | tf_op jit(solution)/shard_map/ppermute | solution.py:501
  57.9 0.9 %collective-permute-start.15 = (bf16[128,512]{1,0:T(8,128)(2,1)S(1)}, bf16[128,512]{1,0:T(8,128)(2,1)S(1)}, u32[]{:S(2)}, u32[]{:S(2)}) collective-permute-start(bf16[128,512]{1,0:T(8,128)(2,1)S(1)} %get-tuple-element.62), channel_id=1, source_target_pairs={{0,4},{2,6},{4,0},{6,2},{1,5},{3,7},{5,1},{7,3},{8,12},{10,14},{12... | collective-permute-start | bytes 393224 | tf_op jit(solution)/shard_map/ppermute | solution.py:501
  58.8 1.4 %collective-permute-start.16 = (bf16[128,512]{1,0:T(8,128)(2,1)S(1)}, bf16[128,512]{1,0:T(8,128)(2,1)S(1)}, u32[]{:S(2)}, u32[]{:S(2)}) collective-permute-start(bf16[128,512]{1,0:T(8,128)(2,1)S(1)} %get-tuple-element.63), channel_id=1, source_target_pairs={{0,6},{2,4},{4,2},{6,0},{1,7},{3,5},{5,3},{7,1},{8,14},{10,12},{12... | collective-permute-start | bytes 393224 | tf_op jit(solution)/shard_map/ppermute | solution.py:501
  60.3 2.0 %collective-permute-done.14.refs_5_ = bf16[128,512]{1,0:T(8,128)(2,1)S(1)} collective-permute-done((bf16[128,512]{1,0:T(8,128)(2,1)S(1)}, bf16[128,512]{1,0:T(8,128)(2,1)S(1)}, u32[]{:S(2)}, u32[]{:S(2)}) %collective-permute-start.14) | collective-permute-done | bytes 131104 | tf_op jit(solution)/shard_map/ppermute | solution.py:501
  62.3 1.8 %collective-permute-done.15.refs_6_ = bf16[128,512]{1,0:T(8,128)(2,1)S(1)} collective-permute-done((bf16[128,512]{1,0:T(8,128)(2,1)S(1)}, bf16[128,512]{1,0:T(8,128)(2,1)S(1)}, u32[]{:S(2)}, u32[]{:S(2)}) %collective-permute-start.15) | collective-permute-done | bytes 131104 | tf_op jit(solution)/shard_map/ppermute | solution.py:501
  64.1 1.8 %collective-permute-done.16.refs_7_ = bf16[128,512]{1,0:T(8,128)(2,1)S(1)} collective-permute-done((bf16[128,512]{1,0:T(8,128)(2,1)S(1)}, bf16[128,512]{1,0:T(8,128)(2,1)S(1)}, u32[]{:S(2)}, u32[]{:S(2)}) %collective-permute-start.16) | collective-permute-done | bytes 131104 | tf_op jit(solution)/shard_map/ppermute | solution.py:501
  65.9 0.0 copy-done.4
  65.9 0.0 copy-done.5
  65.9 2.0 %finish_attention.1 = (bf16[128,4096]{1,0:T(8,128)(2,1)}, bf16[128,512]{1,0:T(8,128)(2,1)}) custom-call(s32[2]{0:T(128)S(1)} %copy-done.5, bf16[64,4096]{1,0:T(8,128)(2,1)S(1)} %copy-done.1, bf16[64,4096]{1,0:T(8,128)(2,1)S(1)} %copy-done.2, bf16[2,512,128]{2,1,0:T(8,128)(2,1)S(1)} %copy-done.3, bf16[2,512,128]{2,1,0:T(8,128)(2,1)S(1)} %copy-done.4, ...), custom_call_target="tpu_custom_call" | custom-call | flops 1 | bytes 1 | tf_op jit(solution)/shard_map/finish_attention/pallas_call | solution.py:460
  (20 shorter events, 0.1 us)
Async XLA Ops:
  2.7 26.7 %collective-permute-start = (bf16[256,512]{1,0:T(8,128)(2,1)}, bf16[256,512]{1,0:T(8,128)(2,1)S(1)}, u32[]{:S(2)}, u32[]{:S(2)}) collective-permute-start(bf16[256,512]{1,0:T(8,128)(2,1)} %get-tuple-element.33), channel_id=1, source_target_pairs={{0,8},{8,0},{1,9},{9,1},{2,10},{10,2},{3,11},{11,3},{4,12},{12,4},... | collective-permute-start | bytes 786440 | tf_op jit(solution)/shard_map/ppermute | solution.py:511
  6.8 19.1 %collective-permute-start.1 = (bf16[48,512]{1,0:T(8,128)(2,1)}, bf16[48,512]{1,0:T(8,128)(2,1)S(1)}, u32[]{:S(2)}, u32[]{:S(2)}) collective-permute-start(bf16[48,512]{1,0:T(8,128)(2,1)} %get-tuple-element.38), channel_id=1, source_target_pairs={{0,10},{2,8},{4,14},{6,12},{8,2},{10,0},{12,6},{14,4},{1,11},{3,9}... | collective-permute-start | bytes 147464 | tf_op jit(solution)/shard_map/ppermute | solution.py:505
  8.1 20.8 %collective-permute-start.2 = (bf16[48,512]{1,0:T(8,128)(2,1)}, bf16[48,512]{1,0:T(8,128)(2,1)S(1)}, u32[]{:S(2)}, u32[]{:S(2)}) collective-permute-start(bf16[48,512]{1,0:T(8,128)(2,1)} %get-tuple-element.39), channel_id=1, source_target_pairs={{0,12},{2,14},{4,8},{6,10},{8,4},{10,6},{12,0},{14,2},{1,13},{3,15... | collective-permute-start | bytes 147464 | tf_op jit(solution)/shard_map/ppermute | solution.py:505
  11.7 17.7 %collective-permute-start.3 = (bf16[48,512]{1,0:T(8,128)(2,1)}, bf16[48,512]{1,0:T(8,128)(2,1)S(1)}, u32[]{:S(2)}, u32[]{:S(2)}) collective-permute-start(bf16[48,512]{1,0:T(8,128)(2,1)} %get-tuple-element.40), channel_id=1, source_target_pairs={{0,14},{2,12},{4,10},{6,8},{8,6},{10,4},{12,2},{14,0},{1,15},{3,13... | collective-permute-start | bytes 147464 | tf_op jit(solution)/shard_map/ppermute | solution.py:505
  14.3 19.2 %collective-permute-start.7 = (bf16[176,1024]{1,0:T(8,128)(2,1)}, bf16[176,1024]{1,0:T(8,128)(2,1)S(1)}, u32[]{:S(2)}, u32[]{:S(2)}) collective-permute-start(bf16[176,1024]{1,0:T(8,128)(2,1)} %get-tuple-element.51), channel_id=1, source_target_pairs={{0,4},{2,6},{4,0},{6,2},{1,5},{3,7},{5,1},{7,3},{8,12},{10,14},{12... | collective-permute-start | bytes 1081352 | tf_op jit(solution)/shard_map/ppermute | solution.py:501
  14.4 11.5 %copy-start.10 = (bf16[176,1024]{1,0:T(8,128)(2,1)S(1)}, bf16[176,1024]{1,0:T(8,128)(2,1)}, u32[]{:S(2)}) copy-start(bf16[176,1024]{1,0:T(8,128)(2,1)} %get-tuple-element.52) | copy-start | bytes 1081348
  14.4 14.5 %copy-start.9 = (bf16[176,1024]{1,0:T(8,128)(2,1)S(1)}, bf16[176,1024]{1,0:T(8,128)(2,1)}, u32[]{:S(2)}) copy-start(bf16[176,1024]{1,0:T(8,128)(2,1)} %get-tuple-element.53) | copy-start | bytes 1081348
  14.4 16.7 %copy-start.11 = (bf16[304,512]{1,0:T(8,128)(2,1)S(1)}, bf16[304,512]{1,0:T(8,128)(2,1)}, u32[]{:S(2)}) copy-start(bf16[304,512]{1,0:T(8,128)(2,1)} %get-tuple-element.50) | copy-start | bytes 933892
  25.9 18.6 %collective-permute-start.8 = (bf16[176,1024]{1,0:T(8,128)(2,1)S(1)}, bf16[176,1024]{1,0:T(8,128)(2,1)S(1)}, u32[]{:S(2)}, u32[]{:S(2)}) collective-permute-start(bf16[176,1024]{1,0:T(8,128)(2,1)S(1)} %copy-done.10), channel_id=1, source_target_pairs={{0,6},{2,4},{4,2},{6,0},{1,7},{3,5},{5,3},{7,1},{8,14},{10,12},{12... | collective-permute-start | bytes 1081352 | tf_op jit(solution)/shard_map/ppermute | solution.py:501
  28.9 16.3 %collective-permute-start.9 = (bf16[176,1024]{1,0:T(8,128)(2,1)S(1)}, bf16[176,1024]{1,0:T(8,128)(2,1)S(1)}, u32[]{:S(2)}, u32[]{:S(2)}) collective-permute-start(bf16[176,1024]{1,0:T(8,128)(2,1)S(1)} %copy-done.9), channel_id=1, source_target_pairs={{0,2},{2,0},{4,6},{6,4},{1,3},{3,1},{5,7},{7,5},{8,10},{10,8},{12,... | collective-permute-start | bytes 1081352 | tf_op jit(solution)/shard_map/ppermute | solution.py:501
  29.5 15.7 %collective-permute-start.5 = (bf16[256,512]{1,0:T(8,128)(2,1)S(1)}, bf16[256,512]{1,0:T(8,128)(2,1)S(1)}, u32[]{:S(2)}, u32[]{:S(2)}) collective-permute-start(bf16[256,512]{1,0:T(8,128)(2,1)S(1)} %collective-permute-done.refs_0_), channel_id=1, source_target_pairs={{0,16},{16,0},{1,17},{17,1},{2,18},{18,2},{3,19},{19,3},{4,20},{20... | collective-permute-start | bytes 786440 | tf_op jit(solution)/shard_map/ppermute | solution.py:519
  31.2 14.6 %collective-permute-start.4 = (bf16[304,512]{1,0:T(8,128)(2,1)S(1)}, bf16[304,512]{1,0:T(8,128)(2,1)S(1)}, u32[]{:S(2)}, u32[]{:S(2)}) collective-permute-start(bf16[304,512]{1,0:T(8,128)(2,1)S(1)} %copy-done.11), channel_id=1, source_target_pairs={{0,8},{8,0},{1,9},{9,1},{2,10},{10,2},{3,11},{11,3},{4,12},{12,4},... | collective-permute-start | bytes 933896 | tf_op jit(solution)/shard_map/ppermute | solution.py:518
  33.5 12.3 %copy-start.8 = (bf16[176,1024]{1,0:T(8,128)(2,1)S(1)}, bf16[176,1024]{1,0:T(8,128)(2,1)}, u32[]{:S(2)}) copy-start(bf16[176,1024]{1,0:T(8,128)(2,1)} %get-tuple-element.35) | copy-start | bytes 1081348
  33.5 11.6 %collective-permute-start.6 = (bf16[4,48,512]{2,1,0:T(8,128)(2,1)S(1)}, bf16[4,48,512]{2,1,0:T(8,128)(2,1)S(1)}, u32[]{:S(2)}, u32[]{:S(2)}) collective-permute-start(bf16[4,48,512]{2,1,0:T(8,128)(2,1)S(1)} %pad_maximum_fusion.1.refs_0_), channel_id=1, source_target_pairs={{0,16},{16,0},{1,17},{17,1},{2,18},{18,2},{3,19},{19,3},{4,20},{20... | collective-permute-start | bytes 589832 | tf_op jit(solution)/shard_map/ppermute | solution.py:520
  45.8 4.1 %copy-start = (bf16[1024,512]{1,0:T(8,128)(2,1)S(1)}, bf16[1024,512]{1,0:T(8,128)(2,1)}, u32[]{:S(2)}) copy-start(bf16[1024,512]{1,0:T(8,128)(2,1)} %own_ref.1) | copy-start | bytes 3145732
  45.8 4.1 %copy-start.6 = (s32[16]{0:T(128)S(1)}, s32[16]{0:T(128)}, u32[]{:S(2)}) copy-start(s32[16]{0:T(128)} %position.1) | copy-start | bytes 196
  45.8 4.1 %copy-start.7 = (s32[16]{0:T(128)S(1)}, s32[16]{0:T(128)}, u32[]{:S(2)}) copy-start(s32[16]{0:T(128)} %adapter.1) | copy-start | bytes 196
  46.0 3.9 %collective-permute-start.12 = (bf16[4,176,1024]{2,1,0:T(8,128)(2,1)S(1)}, bf16[4,176,1024]{2,1,0:T(8,128)(2,1)S(1)}, u32[]{:S(2)}, u32[]{:S(2)}) collective-permute-start(bf16[4,176,1024]{2,1,0:T(8,128)(2,1)S(1)} %pad_maximum_fusion.refs_4_), channel_id=1, source_target_pairs={{0,1},{1,0},{2,3},{3,2},{4,5},{5,4},{6,7},{7,6},{8,9},{9,8},{10,11... | collective-permute-start | bytes 4325384 | tf_op jit(solution)/shard_map/ppermute | solution.py:530
  46.1 9.8 %collective-permute-start.13 = (bf16[304,512]{1,0:T(8,128)(2,1)S(1)}, bf16[304,512]{1,0:T(8,128)(2,1)S(1)}, u32[]{:S(2)}, u32[]{:S(2)}) collective-permute-start(bf16[304,512]{1,0:T(8,128)(2,1)S(1)} %collective-permute-done.4.refs_1_), channel_id=1, source_target_pairs={{0,16},{16,0},{1,17},{17,1},{2,18},{18,2},{3,19},{19,3},{4,20},{20... | collective-permute-start | bytes 933896 | tf_op jit(solution)/shard_map/ppermute | solution.py:527
  47.9 1.6 %collective-permute-start.10 = (bf16[4,48,512]{2,1,0:T(8,128)(2,1)S(1)}, bf16[4,48,512]{2,1,0:T(8,128)(2,1)S(1)}, u32[]{:S(2)}, u32[]{:S(2)}) collective-permute-start(bf16[4,48,512]{2,1,0:T(8,128)(2,1)S(1)} %pad_maximum_fusion.1.refs_0_), channel_id=1, source_target_pairs={{0,1},{1,0},{2,3},{3,2},{4,5},{5,4},{6,7},{7,6},{8,9},{9,8},{10,11... | collective-permute-start | bytes 589832 | tf_op jit(solution)/shard_map/ppermute | solution.py:529
  48.1 1.7 %collective-permute-start.11 = (bf16[4,48,512]{2,1,0:T(8,128)(2,1)S(1)}, bf16[4,48,512]{2,1,0:T(8,128)(2,1)S(1)}, u32[]{:S(2)}, u32[]{:S(2)}) collective-permute-start(bf16[4,48,512]{2,1,0:T(8,128)(2,1)S(1)} %collective-permute-done.6.refs_1_), channel_id=1, source_target_pairs={{0,1},{1,0},{2,3},{3,2},{4,5},{5,4},{6,7},{7,6},{8,9},{9,8},{10,11... | collective-permute-start | bytes 589832 | tf_op jit(solution)/shard_map/ppermute | solution.py:529
  52.2 13.6 %copy-start.1 = (bf16[64,4096]{1,0:T(8,128)(2,1)S(1)}, bf16[64,4096]{1,0:T(8,128)(2,1)}, u32[]{:S(2)}) copy-start(bf16[64,4096]{1,0:T(8,128)(2,1)} %get-tuple-element.37.refs_0_) | copy-start | bytes 1572868
  52.3 13.6 %copy-start.2 = (bf16[64,4096]{1,0:T(8,128)(2,1)S(1)}, bf16[64,4096]{1,0:T(8,128)(2,1)}, u32[]{:S(2)}) copy-start(bf16[64,4096]{1,0:T(8,128)(2,1)} %get-tuple-element.47.refs_1_) | copy-start | bytes 1572868
  52.3 13.6 %copy-start.3 = (bf16[2,512,128]{2,1,0:T(8,128)(2,1)S(1)}, bf16[2,512,128]{2,1,0:T(8,128)(2,1)}, u32[]{:S(2)}) copy-start(bf16[2,512,128]{2,1,0:T(8,128)(2,1)} %get-tuple-element.41.refs_2_) | copy-start | bytes 786436
  52.3 13.6 %copy-start.4 = (bf16[2,512,128]{2,1,0:T(8,128)(2,1)S(1)}, bf16[2,512,128]{2,1,0:T(8,128)(2,1)}, u32[]{:S(2)}) copy-start(bf16[2,512,128]{2,1,0:T(8,128)(2,1)} %get-tuple-element.48.refs_3_) | copy-start | bytes 786436
  52.3 13.6 %copy-start.5 = (s32[2]{0:T(128)S(1)}, s32[2]{0:T(128)}, u32[]{:S(2)}) copy-start(s32[2]{0:T(128)} %lens.3) | copy-start | bytes 28
  56.7 5.6 %collective-permute-start.14 = (bf16[128,512]{1,0:T(8,128)(2,1)S(1)}, bf16[128,512]{1,0:T(8,128)(2,1)S(1)}, u32[]{:S(2)}, u32[]{:S(2)}) collective-permute-start(bf16[128,512]{1,0:T(8,128)(2,1)S(1)} %get-tuple-element.61), channel_id=1, source_target_pairs={{0,2},{2,0},{4,6},{6,4},{1,3},{3,1},{5,7},{7,5},{8,10},{10,8},{12,... | collective-permute-start | bytes 393224 | tf_op jit(solution)/shard_map/ppermute | solution.py:501
  57.9 6.2 %collective-permute-start.15 = (bf16[128,512]{1,0:T(8,128)(2,1)S(1)}, bf16[128,512]{1,0:T(8,128)(2,1)S(1)}, u32[]{:S(2)}, u32[]{:S(2)}) collective-permute-start(bf16[128,512]{1,0:T(8,128)(2,1)S(1)} %get-tuple-element.62), channel_id=1, source_target_pairs={{0,4},{2,6},{4,0},{6,2},{1,5},{3,7},{5,1},{7,3},{8,12},{10,14},{12... | collective-permute-start | bytes 393224 | tf_op jit(solution)/shard_map/ppermute | solution.py:501
  58.8 7.0 %collective-permute-start.16 = (bf16[128,512]{1,0:T(8,128)(2,1)S(1)}, bf16[128,512]{1,0:T(8,128)(2,1)S(1)}, u32[]{:S(2)}, u32[]{:S(2)}) collective-permute-start(bf16[128,512]{1,0:T(8,128)(2,1)S(1)} %get-tuple-element.63), channel_id=1, source_target_pairs={{0,6},{2,4},{4,2},{6,0},{1,7},{3,5},{5,3},{7,1},{8,14},{10,12},{12... | collective-permute-start | bytes 393224 | tf_op jit(solution)/shard_map/ppermute | solution.py:501

commit v14 on v12

--- a/solution.py
+++ b/solution.py
@@ -56,12 +56,7 @@
     ]
     for copy in small:
         copy.start()
-    for i in range(chunks):
-
-        @pl.when(i * chunk < length)
-        def _():
-            copy_in(0, i).start()
-            copy_in(1, i).start()
+    copy_in(0, 0).start()
 
     def dead_slots(i):
         return i * chunk + lax.broadcasted_iota(jnp.int32, ks.shape[1:], 0) >= length
@@ -97,6 +92,7 @@
 
     for copy in small:
         copy.wait()
+    copy_in(1, 0).start()
     for k in range(kv_heads):
         for h in range(group_size):
             qs[k, h * SPAN : (h + 1) * SPAN, :] = q_s[:, tiles(k * group_size + h)]
@@ -105,6 +101,13 @@
         acc[k] = jnp.zeros((HD + ONES, rows), jnp.float32)
     p_s[1] = jnp.zeros((chunk, rows), jnp.bfloat16)
     arrive_keys(0)
+    for i in range(1, chunks):
+
+        @pl.when(i * chunk < length)
+        def _():
+            copy_in(0, i).start()
+            copy_in(1, i).start()
+
     s = dot_last(ks[0, :, :HD], qs[0])
     s_s[0] = s
     x_s[0] = tile_max(s)
@@ -206,35 +209,37 @@
     )(lengths, queries, fresh_keys, keys, values)
 
 
-def pack_kernel(x_hbm, d_hbm, u_hbm, w_hbm, *refs):
-    quads = (len(refs) - 2) // 2
-    tokens_out, (early, late, sems) = refs[:quads], refs[-3:]
-    size = w_hbm.shape[0] // 2 - late.shape[0]
-    maps_out = [early.at[size:, :], *refs[quads:-3]]
+def pack_kernel(x_hbm, d_hbm, u_hbm, w_hbm, early, late, *refs):
+    sems = refs[-1]
+    quads = len(refs) // 2
+    maps_out, tokens_out = [early, *refs[: quads - 1]], refs[quads - 1 : -1]
     part, core, quad = lax.axis_index("parts") % 2, lax.axis_index("tensor"), lax.axis_index("quad")
+    width, cols = w_hbm.shape
     tokens, features = x_hbm.shape
-    width, cols = w_hbm.shape
-    ranks = d_hbm.shape[0]
+    ranks = u_hbm.shape[0]
     step = min(cols, width)
+    size = width // 2 - late.shape[0]
     mine = pl.ds(pl.multiple_of(part * RANK, RANK), RANK)
-    copies = []
-    for q, out in enumerate(maps_out):
-        begin = core * features + (quad ^ q) * width
-        for i, first in enumerate(range(0, width, step)):
-            here = pl.ds(pl.multiple_of(begin + first, step), step)
-            copies.append((d_hbm.at[mine, here], out.at[i * RANK : (i + 1) * RANK, :step]))
-        for i, first in enumerate(range(0, cols, step)):
-            row = width // step * RANK + i * RANK
-            copies.append((u_hbm.at[mine, first : first + step], out.at[row : row + RANK, :step]))
     begin = part * (width // 2)
-    copies.append((w_hbm.at[pl.ds(pl.multiple_of(begin, RANK), size), :], early.at[:size, :]))
-    begin = begin + size
-    copies.append((w_hbm.at[pl.ds(pl.multiple_of(begin, RANK), late.shape[0]), :], late))
+    copies = [
+        (w_hbm.at[pl.ds(pl.multiple_of(begin, RANK), size), :], early.at[:size, :]),
+        (w_hbm.at[pl.ds(pl.multiple_of(begin + size, RANK), late.shape[0]), :], late),
+    ]
     for q, out in enumerate(tokens_out):
         here = pl.ds(pl.multiple_of((quad ^ q) * width, width), width)
         copies.append((x_hbm.at[:, here], out.at[:tokens, :]))
         here = pl.ds(pl.multiple_of(core * features + (quad ^ q) * width, width), width)
         copies.append((d_hbm.at[:, here], out.at[tokens : tokens + ranks, :]))
+    for q, out in enumerate(maps_out):
+        base = size if q == 0 else 0
+        begin = core * features + (quad ^ q) * width
+        sources = [
+            d_hbm.at[mine, pl.ds(pl.multiple_of(begin + first, step), step)] for first in range(0, width, step)
+        ]
+        sources += [u_hbm.at[mine, first : first + step] for first in range(0, cols, step)]
+        for i, source in enumerate(sources):
+            copies.append((source, out.at[base + i * RANK : base + (i + 1) * RANK, :step]))
+    for out in tokens_out:
         for slot, first, row, col in up_places(cols, width):
             row += tokens + ranks
             up = u_hbm.at[slot * RANK : (slot + 1) * RANK, first : first + step]
@@ -246,6 +251,29 @@
         copy.wait()
 
 
+def pack(tokens, downs, ups, weights, quads):
+    hbm = pl.BlockSpec(memory_space=pltpu.HBM)
+    ranks, cols = ups.shape
+    width = weights.shape[0]
+    step = min(cols, width)
+    pieces = (width + cols) // step
+    first = width // 2 * 9 // 32 // RANK * RANK
+    sizes = [(first + RANK * pieces, cols), (width // 2 - first, cols)]
+    sizes += [(RANK * pieces, step)] * (quads - 1)
+    sizes += [(tokens.shape[0] + ranks + RANK * (2 * cols // width), width)] * quads
+    count = 2 + quads * (2 + pieces + len(up_places(cols, width)))
+    return pl.pallas_call(
+        pack_kernel,
+        in_specs=[hbm] * 4,
+        out_specs=[hbm] * len(sizes),
+        out_shape=[jax.ShapeDtypeStruct(size, tokens.dtype) for size in sizes],
+        scratch_shapes=[pltpu.SemaphoreType.DMA((count,))],
+        compiler_params=pltpu.CompilerParams(vmem_limit_bytes=57 * MIB),
+        cost_estimate=FREE,
+        name="pack",
+    )(tokens, downs, ups, weights)
+
+
 def up_places(cols, width):
     step = min(cols, width)
     return [
@@ -253,31 +281,6 @@
         for slot in range(2)
         for first in range(0, cols, step)
     ]
-
-
-def pack(tokens, downs, ups, weights, quads):
-    vmem = pl.BlockSpec(memory_space=pltpu.VMEM)
-    hbm = pl.BlockSpec(memory_space=pltpu.HBM)
-    ranks, cols = ups.shape
-    width = weights.shape[0]
-    step = min(cols, width)
-    kind = tokens.dtype
-    pieces = (width + cols) // step
-    first = width // 4
-    sizes = [(tokens.shape[0] + ranks + RANK * (2 * cols // width), width)] * quads
-    sizes += [(RANK * pieces, step)] * (quads - 1)
-    sizes += [(first + RANK * pieces, cols), (width // 2 - first, cols)]
-    count = quads * (pieces + 2 + len(up_places(cols, width))) + 2
-    return pl.pallas_call(
-        pack_kernel,
-        in_specs=[hbm] * 4,
-        out_specs=[vmem] * len(sizes),
-        out_shape=[jax.ShapeDtypeStruct(size, kind) for size in sizes],
-        scratch_shapes=[pltpu.SemaphoreType.DMA((count,))],
-        compiler_params=pltpu.CompilerParams(vmem_limit_bytes=57 * MIB),
-        cost_estimate=FREE,
-        name="pack",
-    )(tokens, downs, ups, weights)
 
 
 def near_kernel(tokens, quads, position, adapter, own_ref, *refs):
@@ -475,17 +478,18 @@
         pairs = [(w * quads + j, (1 - w) * quads + (j ^ q)) for w in range(2) for j in range(quads)]
         return lax.ppermute(value, ("wing", "quad"), pairs)
 
-    *blocks, early, late = pack(normed_inputs, downs, ups, value_matrix, quads)
+    early, late, *blocks = pack(normed_inputs, downs, ups, value_matrix, quads)
+    maps, blocks = blocks[: quads - 1], blocks[quads - 1 :]
     order = [*range(quads // 2, quads), *range(1, quads // 2)]
     mine = [to_quad(blocks[q], q) for q in order]
     early = lax.ppermute(early, "wing", SWAP)
-    maps = [to_other_wing(blocks[quads - 1 + q], q) for q in range(1, quads)]
+    maps = [to_other_wing(each, q + 1) for q, each in enumerate(maps)]
 
     attn = [attention(0, after(cache_length, blocks[0]))]
     early, *maps = lax.optimization_barrier((early, *maps, attn[0][1]))[:-1]
     step = maps[0].shape[1]
     maps = jnp.stack([early[early.shape[0] - maps[0].shape[0] :, :step], *maps])
-    late = lax.ppermute(after(late, early), "wing", SWAP)
+    late = lax.ppermute(after(late, attn[0][1]), "wing", SWAP)
     early_other = lax.ppermute(early, "parts", parts_swap)
     maps_other = lax.ppermute(maps, "parts", parts_swap)
 

time: 71.1 us -> 133 us (1.87)
  Pallas kernels: 30.1 us -> 88.6 us
  waiting for transfers between devices: 14.9 us -> 20.1 us
    pallas_call x1, Pallas kernels: 3.22 us -> 66.9 us  [pack(): pl.pallas_call(pack_kernel, in_specs=[hbm] * 4, out_specs=[hbm] * len(siz...]
    pallas_call x2, Pallas kernels: 21.7 us -> 16.5 us  [cache_attention(): pl.pallas_call(functools.partial(cache_kernel, order), in_specs=[pl.Block...]
    ppermute x6, waiting for transfers between devices: 6.41 us -> 11 us  [to_quad(): return lax.ppermute(value, 'quad', [(j, j ^ q) for j in range(quads)])]
    ppermute x1, waiting for transfers between devices: 2.49 us -> 4.96 us  [on_device(): late_other = lax.ppermute(late, 'parts', parts_swap)]
    ppermute x6, starting transfers between devices: 7.52 us -> 5.15 us  [to_quad(): return lax.ppermute(value, 'quad', [(j, j ^ q) for j in range(quads)])]
    ppermute x3, waiting for transfers between devices: 3.89 us -> 2.43 us  [to_other_wing(): return lax.ppermute(value, ('wing', 'quad'), pairs)]
  transfers between devices with their start and end apart: 17 -> 17, of which waited for: 9 -> 8; matrix products, arithmetic and copies ran while one was open for 0% -> 0% of each run, Pallas kernels for 34% -> 14%
where the time goes in v14:
time: 133 us
  Pallas kernels  88.6 us (67%)
  starting transfers between devices  23.6 us (18%)
  waiting for transfers between devices  20.1 us (15%)
    pallas_call x1, Pallas kernels, pack(): pl.pallas_call(pack_kernel, in_specs=[hbm] * 4, out_specs=[hbm] * len(siz...  66.9 us
    pallas_call x2, Pallas kernels, cache_attention(): pl.pallas_call(functools.partial(cache_kernel, order), in_specs=[pl.Block...  16.5 us
    ppermute x6, waiting for transfers between devices, to_quad(): return lax.ppermute(value, 'quad', [(j, j ^ q) for j in range(quads)])  11 us
    ppermute x6, starting transfers between devices, to_quad(): return lax.ppermute(value, 'quad', [(j, j ^ q) for j in range(quads)])  5.15 us
    ppermute x1, starting transfers between devices, on_device(): late = lax.ppermute(after(late, attn[0][1]), 'wing', SWAP)  5.12 us
    ppermute x1, waiting for transfers between devices, on_device(): late_other = lax.ppermute(late, 'parts', parts_swap)  4.96 us
    ppermute x3, starting transfers between devices, to_other_wing(): return lax.ppermute(value, ('wing', 'quad'), pairs)  4.9 us
    ppermute x1, starting transfers between devices, on_device(): early = lax.ppermute(early, 'wing', SWAP)  4.1 us
  transfers between devices with their start and end apart: 17, of which 8 were waited for; matrix products, arithmetic and copies ran while one was open for 0% of the time, Pallas kernels for 14%

profile of v14, /device:TPU:0, one launch (start us, length us, event | category | flops | bytes accessed | tf_op | source)
XLA Modules:
  0.0 133.3 jit_solution(7885694294412367738)
XLA Ops:
  0.6 66.9 %pack.1 = (bf16[192,512]{1,0:T(8,128)(2,1)}, bf16[368,512]{1,0:T(8,128)(2,1)}, bf16[48,512]{1,0:T(8,128)(2,1)}, bf16[48,512]{1,0:T(8,128)(2,1)}, bf16[48,512]{1,...) custom-call(bf16[128,4096]{1,0:T(8,128)(2,1)} %x_hbm.1, ...), custom_call_target="tpu_custom_call" | custom-call | flops 1 | bytes 1 | tf_op jit(solution)/shard_map/pack/pallas_call | solution.py:265
  67.5 4.1 %collective-permute-start = (bf16[192,512]{1,0:T(8,128)(2,1)}, bf16[192,512]{1,0:T(8,128)(2,1)S(1)}, u32[]{:S(2)}, u32[]{:S(2)}) collective-permute-start(bf16[192,512]{1,0:T(8,128)(2,1)} %get-tuple-element.35), channel_id=1, source_target_pairs={{0,8},{8,0},{1,9},{9,1},{2,10},{10,2},{3,11},{11,3},{4,12},{12,4},... | collective-permute-start | bytes 589832 | tf_op jit(solution)/shard_map/ppermute | solution.py:485
  71.6 1.3 collective-permute-start.1
  72.9 3.6 %collective-permute-start.2 = (bf16[48,512]{1,0:T(8,128)(2,1)}, bf16[48,512]{1,0:T(8,128)(2,1)S(1)}, u32[]{:S(2)}, u32[]{:S(2)}) collective-permute-start(bf16[48,512]{1,0:T(8,128)(2,1)} %get-tuple-element.37), channel_id=1, source_target_pairs={{0,12},{2,14},{4,8},{6,10},{8,4},{10,6},{12,0},{14,2},{1,13},{3,15... | collective-permute-start | bytes 147464 | tf_op jit(solution)/shard_map/ppermute | solution.py:479
  76.5 0.0 collective-permute-start.3
  76.5 0.0 collective-permute-start.7
  76.6 8.3 %cache_attention.2 = (bf16[64,4096]{1,0:T(8,128)(2,1)}, bf16[2,512,128]{2,1,0:T(8,128)(2,1)}) custom-call(s32[2]{0:T(128)} %lens.3, bf16[128,4096]{1,0:T(8,128)(2,1)} %q_hbm.3, bf16[128,512]{1,0:T(8,128)(2,1)} %fk_hbm.3, bf16[2,2048,512]{2,1,0:T(8,128)(2,1)} %k_hbm.3, bf16[2,2048,512]{2,1,0:T(8,128)(2,1)} %v_hbm.3), custom_call_target="tpu_custom_call" | custom-call | flops 1 | bytes 1 | tf_op jit(solution)/shard_map/cache_attention/pallas_call | solution.py:180
  84.9 2.4 %collective-permute-done.1 = bf16[48,512]{1,0:T(8,128)(2,1)S(1)} collective-permute-done((bf16[48,512]{1,0:T(8,128)(2,1)}, bf16[48,512]{1,0:T(8,128)(2,1)S(1)}, u32[]{:S(2)}, u32[]{:S(2)}) %collective-permute-start.1) | collective-permute-done | bytes 49184 | tf_op jit(solution)/shard_map/ppermute | solution.py:479
  87.3 0.0 copy-done.9
  87.3 5.1 %collective-permute-start.4 = (bf16[368,512]{1,0:T(8,128)(2,1)S(1)}, bf16[368,512]{1,0:T(8,128)(2,1)S(1)}, u32[]{:S(2)}, u32[]{:S(2)}) collective-permute-start(bf16[368,512]{1,0:T(8,128)(2,1)S(1)} %copy-done.9), channel_id=1, source_target_pairs={{0,8},{8,0},{1,9},{9,1},{2,10},{10,2},{3,11},{11,3},{4,12},{12,4},... | collective-permute-start | bytes 1130504 | tf_op jit(solution)/shard_map/ppermute | solution.py:492
  92.4 0.0 collective-permute-done.2
  92.4 0.0 collective-permute-start.8
  92.4 0.0 collective-permute-done.3
  92.4 0.0 copy-done.10
  92.4 1.6 %collective-permute-start.9 = (bf16[176,1024]{1,0:T(8,128)(2,1)S(1)}, bf16[176,1024]{1,0:T(8,128)(2,1)S(1)}, u32[]{:S(2)}, u32[]{:S(2)}) collective-permute-start(bf16[176,1024]{1,0:T(8,128)(2,1)S(1)} %copy-done.10), channel_id=1, source_target_pairs={{0,2},{2,0},{4,6},{6,4},{1,3},{3,1},{5,7},{7,5},{8,10},{10,8},{12,... | collective-permute-start | bytes 1081352 | tf_op jit(solution)/shard_map/ppermute | solution.py:475
  94.0 0.0 collective-permute-done.refs_0_
  94.0 1.6 %collective-permute-start.5 = (bf16[192,512]{1,0:T(8,128)(2,1)S(1)}, bf16[192,512]{1,0:T(8,128)(2,1)S(1)}, u32[]{:S(2)}, u32[]{:S(2)}) collective-permute-start(bf16[192,512]{1,0:T(8,128)(2,1)S(1)} %collective-permute-done.refs_0_), channel_id=1, source_target_pairs={{0,16},{16,0},{1,17},{17,1},{2,18},{18,2},{3,19},{19,3},{4,20},{20... | collective-permute-start | bytes 589832 | tf_op jit(solution)/shard_map/ppermute | solution.py:493
  95.6 0.0 collective-permute-done.7
  95.7 0.6 collective-permute-start.6
  96.3 8.2 %cache_attention.3 = (bf16[64,4096]{1,0:T(8,128)(2,1)}, bf16[2,512,128]{2,1,0:T(8,128)(2,1)}) custom-call(s32[2]{0:T(128)} %lens.3, bf16[128,4096]{1,0:T(8,128)(2,1)} %q_hbm.3, bf16[128,512]{1,0:T(8,128)(2,1)} %fk_hbm.3, bf16[2,2048,512]{2,1,0:T(8,128)(2,1)} %k_hbm.3, bf16[2,2048,512]{2,1,0:T(8,128)(2,1)} %v_hbm.3), custom_call_target="tpu_custom_call" | custom-call | flops 1 | bytes 1 | tf_op jit(solution)/shard_map/cache_attention/pallas_call | solution.py:180
  104.4 5.4 %collective-permute-done.8 = bf16[176,1024]{1,0:T(8,128)(2,1)S(1)} collective-permute-done((bf16[176,1024]{1,0:T(8,128)(2,1)S(1)}, bf16[176,1024]{1,0:T(8,128)(2,1)S(1)}, u32[]{:S(2)}, u32[]{:S(2)}) %collective-permute-start.8) | collective-permute-done | bytes 360480 | tf_op jit(solution)/shard_map/ppermute | solution.py:475
  109.8 0.0 collective-permute-done.9
  109.8 0.0 collective-permute-done.4.refs_1_
  109.8 0.0 collective-permute-done.5.refs_2_
  109.8 0.0 collective-permute-done.6.refs_1_
  109.9 0.0 copy-start
  109.9 0.0 copy-start.6
  109.9 0.0 copy-start.7
  109.9 0.2 pad_maximum_fusion.refs_4_
  110.1 0.1 collective-permute-start.12
  110.2 1.6 %collective-permute-start.13 = (bf16[368,512]{1,0:T(8,128)(2,1)S(1)}, bf16[368,512]{1,0:T(8,128)(2,1)S(1)}, u32[]{:S(2)}, u32[]{:S(2)}) collective-permute-start(bf16[368,512]{1,0:T(8,128)(2,1)S(1)} %collective-permute-done.4.refs_1_), channel_id=1, source_target_pairs={{0,16},{16,0},{1,17},{17,1},{2,18},{18,2},{3,19},{19,3},{4,20},{20... | collective-permute-start | bytes 1130504 | tf_op jit(solution)/shard_map/ppermute | solution.py:501
  111.7 0.2 collective-permute-start.10
  111.9 0.3 collective-permute-start.11
  112.2 1.4 %collective-permute-done.10.refs_2_ = bf16[4,48,512]{2,1,0:T(8,128)(2,1)S(1)} collective-permute-done((bf16[4,48,512]{2,1,0:T(8,128)(2,1)S(1)}, bf16[4,48,512]{2,1,0:T(8,128)(2,1)S(1)}, u32[]{:S(2)}, u32[]{:S(2)}) %collective-permute-start.10) | collective-permute-done | bytes 196640 | tf_op jit(solution)/shard_map/ppermute | solution.py:503
  113.7 0.3 collective-permute-done.11.refs_3_
  113.9 0.0 collective-permute-done.12.refs_5_
  114.0 2.4 %near_products.1.near = f32[512,512]{1,0:T(8,128)S(1)} custom-call(s32[16]{0:T(128)S(1)} %copy-done.6, s32[16]{0:T(128)S(1)} %copy-done.7, bf16[1024,512]{1,0:T(8,128)(2,1)S(1)} %copy-done, bf16[4,48,512]{2,1,0:T(8,128)(2,1)S(1)} %pad_maximum_fusion.1.refs_0_, bf16[4,48,512]{2,1,0:T(8,128)(2,1)S(1)} %collective-permute-done.6.refs_1_, ...), custom_call_target="tpu_custom_call" | custom-call | flops 1 | bytes 1 | tf_op jit(solution)/shard_map/near_products/pallas_call | solution.py:346
  116.3 0.0 copy-start.1
  116.4 0.0 copy-start.5
  116.4 5.0 %collective-permute-done.13.refs_3_ = bf16[368,512]{1,0:T(8,128)(2,1)S(1)} collective-permute-done((bf16[368,512]{1,0:T(8,128)(2,1)S(1)}, bf16[368,512]{1,0:T(8,128)(2,1)S(1)}, u32[]{:S(2)}, u32[]{:S(2)}) %collective-permute-start.13) | collective-permute-done | bytes 376864 | tf_op jit(solution)/shard_map/ppermute | solution.py:501
  121.3 0.8 far_products.1
  122.2 1.6 %collective-permute-start.14 = (bf16[128,512]{1,0:T(8,128)(2,1)S(1)}, bf16[128,512]{1,0:T(8,128)(2,1)S(1)}, u32[]{:S(2)}, u32[]{:S(2)}) collective-permute-start(bf16[128,512]{1,0:T(8,128)(2,1)S(1)} %get-tuple-element.59), channel_id=1, source_target_pairs={{0,2},{2,0},{4,6},{6,4},{1,3},{3,1},{5,7},{7,5},{8,10},{10,8},{12,... | collective-permute-start | bytes 393224 | tf_op jit(solution)/shard_map/ppermute | solution.py:475
  123.7 0.5 collective-permute-start.15
  124.2 1.5 %collective-permute-start.16 = (bf16[128,512]{1,0:T(8,128)(2,1)S(1)}, bf16[128,512]{1,0:T(8,128)(2,1)S(1)}, u32[]{:S(2)}, u32[]{:S(2)}) collective-permute-start(bf16[128,512]{1,0:T(8,128)(2,1)S(1)} %get-tuple-element.61), channel_id=1, source_target_pairs={{0,6},{2,4},{4,2},{6,0},{1,7},{3,5},{5,3},{7,1},{8,14},{10,12},{12... | collective-permute-start | bytes 393224 | tf_op jit(solution)/shard_map/ppermute | solution.py:475
  125.7 2.0 %collective-permute-done.14.refs_5_ = bf16[128,512]{1,0:T(8,128)(2,1)S(1)} collective-permute-done((bf16[128,512]{1,0:T(8,128)(2,1)S(1)}, bf16[128,512]{1,0:T(8,128)(2,1)S(1)}, u32[]{:S(2)}, u32[]{:S(2)}) %collective-permute-start.14) | collective-permute-done | bytes 131104 | tf_op jit(solution)/shard_map/ppermute | solution.py:475
  127.8 2.2 %collective-permute-done.15.refs_6_ = bf16[128,512]{1,0:T(8,128)(2,1)S(1)} collective-permute-done((bf16[128,512]{1,0:T(8,128)(2,1)S(1)}, bf16[128,512]{1,0:T(8,128)(2,1)S(1)}, u32[]{:S(2)}, u32[]{:S(2)}) %collective-permute-start.15) | collective-permute-done | bytes 131104 | tf_op jit(solution)/shard_map/ppermute | solution.py:475
  129.9 1.4 %collective-permute-done.16.refs_7_ = bf16[128,512]{1,0:T(8,128)(2,1)S(1)} collective-permute-done((bf16[128,512]{1,0:T(8,128)(2,1)S(1)}, bf16[128,512]{1,0:T(8,128)(2,1)S(1)}, u32[]{:S(2)}, u32[]{:S(2)}) %collective-permute-start.16) | collective-permute-done | bytes 131104 | tf_op jit(solution)/shard_map/ppermute | solution.py:475
  131.3 2.0 %finish_attention.1 = (bf16[128,4096]{1,0:T(8,128)(2,1)}, bf16[128,512]{1,0:T(8,128)(2,1)}) custom-call(s32[2]{0:T(128)S(1)} %copy-done.5, bf16[64,4096]{1,0:T(8,128)(2,1)S(1)} %copy-done.1, bf16[64,4096]{1,0:T(8,128)(2,1)S(1)} %copy-done.2, bf16[2,512,128]{2,1,0:T(8,128)(2,1)S(1)} %copy-done.3, bf16[2,512,128]{2,1,0:T(8,128)(2,1)S(1)} %copy-done.4, ...), custom_call_target="tpu_custom_call" | custom-call | flops 1 | bytes 1 | tf_op jit(solution)/shard_map/finish_attention/pallas_call | solution.py:434
  (19 shorter events, 0.1 us)
Async XLA Ops:
  67.5 26.5 %collective-permute-start = (bf16[192,512]{1,0:T(8,128)(2,1)}, bf16[192,512]{1,0:T(8,128)(2,1)S(1)}, u32[]{:S(2)}, u32[]{:S(2)}) collective-permute-start(bf16[192,512]{1,0:T(8,128)(2,1)} %get-tuple-element.35), channel_id=1, source_target_pairs={{0,8},{8,0},{1,9},{9,1},{2,10},{10,2},{3,11},{11,3},{4,12},{12,4},... | collective-permute-start | bytes 589832 | tf_op jit(solution)/shard_map/ppermute | solution.py:485
  71.6 15.6 %collective-permute-start.1 = (bf16[48,512]{1,0:T(8,128)(2,1)}, bf16[48,512]{1,0:T(8,128)(2,1)S(1)}, u32[]{:S(2)}, u32[]{:S(2)}) collective-permute-start(bf16[48,512]{1,0:T(8,128)(2,1)} %get-tuple-element.36), channel_id=1, source_target_pairs={{0,10},{2,8},{4,14},{6,12},{8,2},{10,0},{12,6},{14,4},{1,11},{3,9}... | collective-permute-start | bytes 147464 | tf_op jit(solution)/shard_map/ppermute | solution.py:479
  72.9 19.5 %collective-permute-start.2 = (bf16[48,512]{1,0:T(8,128)(2,1)}, bf16[48,512]{1,0:T(8,128)(2,1)S(1)}, u32[]{:S(2)}, u32[]{:S(2)}) collective-permute-start(bf16[48,512]{1,0:T(8,128)(2,1)} %get-tuple-element.37), channel_id=1, source_target_pairs={{0,12},{2,14},{4,8},{6,10},{8,4},{10,6},{12,0},{14,2},{1,13},{3,15... | collective-permute-start | bytes 147464 | tf_op jit(solution)/shard_map/ppermute | solution.py:479
  76.5 15.9 %collective-permute-start.3 = (bf16[48,512]{1,0:T(8,128)(2,1)}, bf16[48,512]{1,0:T(8,128)(2,1)S(1)}, u32[]{:S(2)}, u32[]{:S(2)}) collective-permute-start(bf16[48,512]{1,0:T(8,128)(2,1)} %get-tuple-element.38), channel_id=1, source_target_pairs={{0,14},{2,12},{4,10},{6,8},{8,6},{10,4},{12,2},{14,0},{1,15},{3,13... | collective-permute-start | bytes 147464 | tf_op jit(solution)/shard_map/ppermute | solution.py:479
  76.5 19.1 %collective-permute-start.7 = (bf16[176,1024]{1,0:T(8,128)(2,1)}, bf16[176,1024]{1,0:T(8,128)(2,1)S(1)}, u32[]{:S(2)}, u32[]{:S(2)}) collective-permute-start(bf16[176,1024]{1,0:T(8,128)(2,1)} %get-tuple-element.49), channel_id=1, source_target_pairs={{0,4},{2,6},{4,0},{6,2},{1,5},{3,7},{5,1},{7,3},{8,12},{10,14},{12... | collective-permute-start | bytes 1081352 | tf_op jit(solution)/shard_map/ppermute | solution.py:475
  76.5 10.8 %copy-start.9 = (bf16[368,512]{1,0:T(8,128)(2,1)S(1)}, bf16[368,512]{1,0:T(8,128)(2,1)}, u32[]{:S(2)}) copy-start(bf16[368,512]{1,0:T(8,128)(2,1)} %get-tuple-element.48) | copy-start | bytes 1130500
  76.5 15.9 %copy-start.11 = (bf16[176,1024]{1,0:T(8,128)(2,1)S(1)}, bf16[176,1024]{1,0:T(8,128)(2,1)}, u32[]{:S(2)}) copy-start(bf16[176,1024]{1,0:T(8,128)(2,1)} %get-tuple-element.50) | copy-start | bytes 1081348
  76.6 15.9 %copy-start.10 = (bf16[176,1024]{1,0:T(8,128)(2,1)S(1)}, bf16[176,1024]{1,0:T(8,128)(2,1)}, u32[]{:S(2)}) copy-start(bf16[176,1024]{1,0:T(8,128)(2,1)} %get-tuple-element.51) | copy-start | bytes 1081348
  87.3 22.5 %collective-permute-start.4 = (bf16[368,512]{1,0:T(8,128)(2,1)S(1)}, bf16[368,512]{1,0:T(8,128)(2,1)S(1)}, u32[]{:S(2)}, u32[]{:S(2)}) collective-permute-start(bf16[368,512]{1,0:T(8,128)(2,1)S(1)} %copy-done.9), channel_id=1, source_target_pairs={{0,8},{8,0},{1,9},{9,1},{2,10},{10,2},{3,11},{11,3},{4,12},{12,4},... | collective-permute-start | bytes 1130504 | tf_op jit(solution)/shard_map/ppermute | solution.py:492
  92.4 17.4 %collective-permute-start.8 = (bf16[176,1024]{1,0:T(8,128)(2,1)S(1)}, bf16[176,1024]{1,0:T(8,128)(2,1)S(1)}, u32[]{:S(2)}, u32[]{:S(2)}) collective-permute-start(bf16[176,1024]{1,0:T(8,128)(2,1)S(1)} %copy-done.11), channel_id=1, source_target_pairs={{0,6},{2,4},{4,2},{6,0},{1,7},{3,5},{5,3},{7,1},{8,14},{10,12},{12... | collective-permute-start | bytes 1081352 | tf_op jit(solution)/shard_map/ppermute | solution.py:475
  92.4 17.4 %collective-permute-start.9 = (bf16[176,1024]{1,0:T(8,128)(2,1)S(1)}, bf16[176,1024]{1,0:T(8,128)(2,1)S(1)}, u32[]{:S(2)}, u32[]{:S(2)}) collective-permute-start(bf16[176,1024]{1,0:T(8,128)(2,1)S(1)} %copy-done.10), channel_id=1, source_target_pairs={{0,2},{2,0},{4,6},{6,4},{1,3},{3,1},{5,7},{7,5},{8,10},{10,8},{12,... | collective-permute-start | bytes 1081352 | tf_op jit(solution)/shard_map/ppermute | solution.py:475
  94.0 15.8 %collective-permute-start.5 = (bf16[192,512]{1,0:T(8,128)(2,1)S(1)}, bf16[192,512]{1,0:T(8,128)(2,1)S(1)}, u32[]{:S(2)}, u32[]{:S(2)}) collective-permute-start(bf16[192,512]{1,0:T(8,128)(2,1)S(1)} %collective-permute-done.refs_0_), channel_id=1, source_target_pairs={{0,16},{16,0},{1,17},{17,1},{2,18},{18,2},{3,19},{19,3},{4,20},{20... | collective-permute-start | bytes 589832 | tf_op jit(solution)/shard_map/ppermute | solution.py:493
  95.6 14.2 %copy-start.8 = (bf16[176,1024]{1,0:T(8,128)(2,1)S(1)}, bf16[176,1024]{1,0:T(8,128)(2,1)}, u32[]{:S(2)}) copy-start(bf16[176,1024]{1,0:T(8,128)(2,1)} %get-tuple-element.32) | copy-start | bytes 1081348
  95.7 14.2 %collective-permute-start.6 = (bf16[4,48,512]{2,1,0:T(8,128)(2,1)S(1)}, bf16[4,48,512]{2,1,0:T(8,128)(2,1)S(1)}, u32[]{:S(2)}, u32[]{:S(2)}) collective-permute-start(bf16[4,48,512]{2,1,0:T(8,128)(2,1)S(1)} %pad_maximum_fusion.1.refs_0_), channel_id=1, source_target_pairs={{0,16},{16,0},{1,17},{17,1},{2,18},{18,2},{3,19},{19,3},{4,20},{20... | collective-permute-start | bytes 589832 | tf_op jit(solution)/shard_map/ppermute | solution.py:494
  109.9 4.1 %copy-start = (bf16[1024,512]{1,0:T(8,128)(2,1)S(1)}, bf16[1024,512]{1,0:T(8,128)(2,1)}, u32[]{:S(2)}) copy-start(bf16[1024,512]{1,0:T(8,128)(2,1)} %own_ref.1) | copy-start | bytes 3145732
  109.9 4.1 %copy-start.6 = (s32[16]{0:T(128)S(1)}, s32[16]{0:T(128)}, u32[]{:S(2)}) copy-start(s32[16]{0:T(128)} %position.1) | copy-start | bytes 196
  109.9 4.1 %copy-start.7 = (s32[16]{0:T(128)S(1)}, s32[16]{0:T(128)}, u32[]{:S(2)}) copy-start(s32[16]{0:T(128)} %adapter.1) | copy-start | bytes 196
  110.1 3.9 %collective-permute-start.12 = (bf16[4,176,1024]{2,1,0:T(8,128)(2,1)S(1)}, bf16[4,176,1024]{2,1,0:T(8,128)(2,1)S(1)}, u32[]{:S(2)}, u32[]{:S(2)}) collective-permute-start(bf16[4,176,1024]{2,1,0:T(8,128)(2,1)S(1)} %pad_maximum_fusion.refs_4_), channel_id=1, source_target_pairs={{0,1},{1,0},{2,3},{3,2},{4,5},{5,4},{6,7},{7,6},{8,9},{9,8},{10,11... | collective-permute-start | bytes 4325384 | tf_op jit(solution)/shard_map/ppermute | solution.py:504
  110.2 11.2 %collective-permute-start.13 = (bf16[368,512]{1,0:T(8,128)(2,1)S(1)}, bf16[368,512]{1,0:T(8,128)(2,1)S(1)}, u32[]{:S(2)}, u32[]{:S(2)}) collective-permute-start(bf16[368,512]{1,0:T(8,128)(2,1)S(1)} %collective-permute-done.4.refs_1_), channel_id=1, source_target_pairs={{0,16},{16,0},{1,17},{17,1},{2,18},{18,2},{3,19},{19,3},{4,20},{20... | collective-permute-start | bytes 1130504 | tf_op jit(solution)/shard_map/ppermute | solution.py:501
  111.7 1.9 %collective-permute-start.10 = (bf16[4,48,512]{2,1,0:T(8,128)(2,1)S(1)}, bf16[4,48,512]{2,1,0:T(8,128)(2,1)S(1)}, u32[]{:S(2)}, u32[]{:S(2)}) collective-permute-start(bf16[4,48,512]{2,1,0:T(8,128)(2,1)S(1)} %pad_maximum_fusion.1.refs_0_), channel_id=1, source_target_pairs={{0,1},{1,0},{2,3},{3,2},{4,5},{5,4},{6,7},{7,6},{8,9},{9,8},{10,11... | collective-permute-start | bytes 589832 | tf_op jit(solution)/shard_map/ppermute | solution.py:503
  111.9 2.1 %collective-permute-start.11 = (bf16[4,48,512]{2,1,0:T(8,128)(2,1)S(1)}, bf16[4,48,512]{2,1,0:T(8,128)(2,1)S(1)}, u32[]{:S(2)}, u32[]{:S(2)}) collective-permute-start(bf16[4,48,512]{2,1,0:T(8,128)(2,1)S(1)} %collective-permute-done.6.refs_1_), channel_id=1, source_target_pairs={{0,1},{1,0},{2,3},{3,2},{4,5},{5,4},{6,7},{7,6},{8,9},{9,8},{10,11... | collective-permute-start | bytes 589832 | tf_op jit(solution)/shard_map/ppermute | solution.py:503
  116.3 14.9 %copy-start.1 = (bf16[64,4096]{1,0:T(8,128)(2,1)S(1)}, bf16[64,4096]{1,0:T(8,128)(2,1)}, u32[]{:S(2)}) copy-start(bf16[64,4096]{1,0:T(8,128)(2,1)} %get-tuple-element.34.refs_0_) | copy-start | bytes 1572868
  116.3 14.9 %copy-start.2 = (bf16[64,4096]{1,0:T(8,128)(2,1)S(1)}, bf16[64,4096]{1,0:T(8,128)(2,1)}, u32[]{:S(2)}) copy-start(bf16[64,4096]{1,0:T(8,128)(2,1)} %get-tuple-element.45.refs_1_) | copy-start | bytes 1572868
  116.4 14.9 %copy-start.3 = (bf16[2,512,128]{2,1,0:T(8,128)(2,1)S(1)}, bf16[2,512,128]{2,1,0:T(8,128)(2,1)}, u32[]{:S(2)}) copy-start(bf16[2,512,128]{2,1,0:T(8,128)(2,1)} %get-tuple-element.39.refs_2_) | copy-start | bytes 786436
  116.4 14.9 %copy-start.4 = (bf16[2,512,128]{2,1,0:T(8,128)(2,1)S(1)}, bf16[2,512,128]{2,1,0:T(8,128)(2,1)}, u32[]{:S(2)}) copy-start(bf16[2,512,128]{2,1,0:T(8,128)(2,1)} %get-tuple-element.46.refs_3_) | copy-start | bytes 786436
  116.4 14.9 %copy-start.5 = (s32[2]{0:T(128)S(1)}, s32[2]{0:T(128)}, u32[]{:S(2)}) copy-start(s32[2]{0:T(128)} %lens.3) | copy-start | bytes 28
  122.2 5.6 %collective-permute-start.14 = (bf16[128,512]{1,0:T(8,128)(2,1)S(1)}, bf16[128,512]{1,0:T(8,128)(2,1)S(1)}, u32[]{:S(2)}, u32[]{:S(2)}) collective-permute-start(bf16[128,512]{1,0:T(8,128)(2,1)S(1)} %get-tuple-element.59), channel_id=1, source_target_pairs={{0,2},{2,0},{4,6},{6,4},{1,3},{3,1},{5,7},{7,5},{8,10},{10,8},{12,... | collective-permute-start | bytes 393224 | tf_op jit(solution)/shard_map/ppermute | solution.py:475
  123.7 6.2 %collective-permute-start.15 = (bf16[128,512]{1,0:T(8,128)(2,1)S(1)}, bf16[128,512]{1,0:T(8,128)(2,1)S(1)}, u32[]{:S(2)}, u32[]{:S(2)}) collective-permute-start(bf16[128,512]{1,0:T(8,128)(2,1)S(1)} %get-tuple-element.60), channel_id=1, source_target_pairs={{0,4},{2,6},{4,0},{6,2},{1,5},{3,7},{5,1},{7,3},{8,12},{10,14},{12... | collective-permute-start | bytes 393224 | tf_op jit(solution)/shard_map/ppermute | solution.py:475
  124.2 7.0 %collective-permute-start.16 = (bf16[128,512]{1,0:T(8,128)(2,1)S(1)}, bf16[128,512]{1,0:T(8,128)(2,1)S(1)}, u32[]{:S(2)}, u32[]{:S(2)}) collective-permute-start(bf16[128,512]{1,0:T(8,128)(2,1)S(1)} %get-tuple-element.61), channel_id=1, source_target_pairs={{0,6},{2,4},{4,2},{6,0},{1,7},{3,5},{5,3},{7,1},{8,14},{10,12},{12... | collective-permute-start | bytes 393224 | tf_op jit(solution)/shard_map/ppermute | solution.py:475

commit v15 on v13

--- a/solution.py
+++ b/solution.py
@@ -247,7 +247,7 @@
     width, cols = weights.shape
     step = min(cols, width)
     pieces = (width + cols) // step
-    first = width // 2 * 13 // 32 // RANK * RANK
+    first = width // 2 * 15 // 32 // RANK * RANK
     sizes = [(first + RANK * pieces, cols), (width // 2 - first, cols)]
     sizes += [(RANK * pieces, step)] * (quads - 1)
     return pl.pallas_call(
@@ -427,14 +427,16 @@
 
 
 def finish_kernel(spans, lens, *refs):
-    out_ref, values_ref = refs[-2:]
-    mixed, probs, parts = refs[:spans], refs[spans : 2 * spans], refs[2 * spans : -2]
+    out_hbm, values_ref, out_s, sems = refs[-4:]
+    mixed, probs, parts = refs[:spans], refs[spans : 2 * spans], refs[2 * spans : -4]
     total = parts[0][...].astype(jnp.float32)
     for part in parts[1:]:
         total = total + part[...].astype(jnp.float32)
     values_ref[...] = total.astype(jnp.bfloat16)
     none = jnp.zeros((SPAN, HD), jnp.bfloat16)
-    group_size = out_ref.shape[1] // values_ref.shape[1]
+    group_size = out_hbm.shape[1] // values_ref.shape[1]
+    pair_width = 2 * group_size * HD
+    leaving = []
     for order in range(spans):
         span = span_of(order, lens)
         rows = pl.ds(pl.multiple_of(span * SPAN, SPAN), SPAN)
@@ -450,7 +452,14 @@
                     col = ((2 * pair + side) * group_size + h) * HD
                     added = fresh[h * SPAN : (h + 1) * SPAN, side * HD : (side + 1) * HD]
                     before = mixed[order][:, col : col + HD].astype(jnp.float32)
-                    out_ref[rows, col : col + HD] = (before + added).astype(jnp.bfloat16)
+                    out_s[order, :, col : col + HD] = (before + added).astype(jnp.bfloat16)
+            here = slice(pair * pair_width, (pair + 1) * pair_width)
+            leaving.append(
+                pltpu.make_async_copy(out_s.at[order, :, here], out_hbm.at[rows, here], sems.at[order, pair])
+            )
+            leaving[-1].start()
+    for copy in leaving:
+        copy.wait()
 
 
 def finish(lengths, mixed, fresh_probs, parts, q_width):
@@ -460,10 +469,14 @@
     return pl.pallas_call(
         functools.partial(finish_kernel, len(mixed)),
         in_specs=[smem] + [vmem] * (len(parts) + 2 * len(mixed)),
-        out_specs=[vmem] * 2,
+        out_specs=[pl.BlockSpec(memory_space=pl.ANY), vmem],
         out_shape=[
             jax.ShapeDtypeStruct((tokens, q_width), jnp.bfloat16),
             jax.ShapeDtypeStruct((tokens, cols), jnp.bfloat16),
+        ],
+        scratch_shapes=[
+            pltpu.VMEM((len(mixed), *mixed[0].shape), jnp.bfloat16),
+            pltpu.SemaphoreType.DMA((len(mixed), fresh_probs[0].shape[0])),
         ],
         compiler_params=pltpu.CompilerParams(vmem_limit_bytes=16 * MIB),
         cost_estimate=FREE,

time: 68.3 us -> 72.6 us (1.063)
  starting transfers between devices: 22.8 us -> 30.7 us
  Pallas kernels: 31.1 us -> 24.8 us
  waiting for transfers between devices: 13 us -> 15 us
    pallas_call x2, Pallas kernels: 21.2 us -> 14.3 us  [cache_attention(): pl.pallas_call(functools.partial(cache_kernel, order), in_specs=[pl.Block...]
    ppermute x1, starting transfers between devices: 0.15 us -> 6.22 us  [on_device(): maps_other = lax.ppermute(maps, 'parts', parts_swap)]
    ppermute x3, waiting for transfers between devices: 0.01 us -> 3.96 us  [to_other_wing(): return lax.ppermute(value, ('wing', 'quad'), pairs)]
    ppermute x6, starting transfers between devices: 7.13 us -> 9.11 us  [to_quad(): return lax.ppermute(value, 'quad', [(j, j ^ q) for j in range(quads)])]
    ppermute x6, waiting for transfers between devices: 7.33 us -> 6.44 us  [to_quad(): return lax.ppermute(value, 'quad', [(j, j ^ q) for j in range(quads)])]
    ppermute x1, waiting for transfers between devices: 3.61 us -> 2.84 us  [on_device(): late_other = lax.ppermute(late, 'parts', parts_swap)]
  transfers between devices with their start and end apart: 17 -> 17, of which waited for: 9 -> 8; matrix products, arithmetic and copies ran while one was open for 0% -> 0% of each run, Pallas kernels for 39% -> 27%
where the time goes in v15:
time: 72.6 us; the launch traced here: 71.6 us
  starting transfers between devices  30.7 us (42%)
  Pallas kernels  24.8 us (34%)
  waiting for transfers between devices  15 us (21%)
  between operations  0.88 us (1%)
    pallas_call x2, Pallas kernels, cache_attention(): pl.pallas_call(functools.partial(cache_kernel, order), in_specs=[pl.Block...  14.3 us
    ppermute x6, starting transfers between devices, to_quad(): return lax.ppermute(value, 'quad', [(j, j ^ q) for j in range(quads)])  9.11 us
    ppermute x6, waiting for transfers between devices, to_quad(): return lax.ppermute(value, 'quad', [(j, j ^ q) for j in range(quads)])  6.44 us
    ppermute x1, starting transfers between devices, on_device(): maps_other = lax.ppermute(maps, 'parts', parts_swap)  6.22 us
    ppermute x3, starting transfers between devices, to_other_wing(): return lax.ppermute(value, ('wing', 'quad'), pairs)  4.9 us
    ppermute x1, starting transfers between devices, on_device(): early = lax.ppermute(early, 'wing', SWAP)  4.1 us
    ppermute x3, waiting for transfers between devices, to_other_wing(): return lax.ppermute(value, ('wing', 'quad'), pairs)  3.96 us
    ppermute x1, waiting for transfers between devices, on_device(): late_other = lax.ppermute(late, 'parts', parts_swap)  2.84 us
  transfers between devices with their start and end apart: 17, of which 8 were waited for; matrix products, arithmetic and copies ran while one was open for 0% of the time, Pallas kernels for 27%

profile of v15, /device:TPU:0, one launch (start us, length us, event | category | flops | bytes accessed | tf_op | source)
XLA Modules:
  0.0 71.6 jit_solution(13589072350906028261)
XLA Ops:
  0.6 2.1 %cross_pack.1 = (bf16[288,512]{1,0:T(8,128)(2,1)}, bf16[272,512]{1,0:T(8,128)(2,1)}, bf16[48,512]{1,0:T(8,128)(2,1)}, bf16[48,512]{1,0:T(8,128)(2,1)}, bf16[48,512]{1,0:T(8,128)(2,1)}) custom-call(bf16[32,8192]{1,0:T(8,128)(2,1)} %bitcast.11, bf16[32,512]{1,0:T(8,128)(2,1)} %bitcast.17, bf16[1024,512]{1,0:T(8,128)(2,1)} %own_ref.1), custom_call_target="tpu_custom_call" | custom-call | flops 1 | bytes 1 | tf_op jit(solution)/shard_map/cross_pack/pallas_call | solution.py:253
  2.7 4.1 %collective-permute-start = (bf16[288,512]{1,0:T(8,128)(2,1)}, bf16[288,512]{1,0:T(8,128)(2,1)S(1)}, u32[]{:S(2)}, u32[]{:S(2)}) collective-permute-start(bf16[288,512]{1,0:T(8,128)(2,1)} %get-tuple-element.33), channel_id=1, source_target_pairs={{0,8},{8,0},{1,9},{9,1},{2,10},{10,2},{3,11},{11,3},{4,12},{12,4},... | collective-permute-start | bytes 884744 | tf_op jit(solution)/shard_map/ppermute | solution.py:524
  6.8 1.3 %collective-permute-start.1 = (bf16[48,512]{1,0:T(8,128)(2,1)}, bf16[48,512]{1,0:T(8,128)(2,1)S(1)}, u32[]{:S(2)}, u32[]{:S(2)}) collective-permute-start(bf16[48,512]{1,0:T(8,128)(2,1)} %get-tuple-element.38), channel_id=1, source_target_pairs={{0,10},{2,8},{4,14},{6,12},{8,2},{10,0},{12,6},{14,4},{1,11},{3,9}... | collective-permute-start | bytes 147464 | tf_op jit(solution)/shard_map/ppermute | solution.py:518
  8.1 3.6 %collective-permute-start.2 = (bf16[48,512]{1,0:T(8,128)(2,1)}, bf16[48,512]{1,0:T(8,128)(2,1)S(1)}, u32[]{:S(2)}, u32[]{:S(2)}) collective-permute-start(bf16[48,512]{1,0:T(8,128)(2,1)} %get-tuple-element.39), channel_id=1, source_target_pairs={{0,12},{2,14},{4,8},{6,10},{8,4},{10,6},{12,0},{14,2},{1,13},{3,15... | collective-permute-start | bytes 147464 | tf_op jit(solution)/shard_map/ppermute | solution.py:518
  11.7 0.0 collective-permute-start.3
  11.7 2.6 %quad_pack.1 = (bf16[176,1024]{1,0:T(8,128)(2,1)}, bf16[176,1024]{1,0:T(8,128)(2,1)}, bf16[176,1024]{1,0:T(8,128)(2,1)}, bf16[176,1024]{1,0:T(8,128)(2,1)}) custom-call(bf16[128,4096]{1,0:T(8,128)(2,1)} %x_hbm, bf16[32,8192]{1,0:T(8,128)(2,1)} %bitcast.12, bf16[32,512]{1,0:T(8,128)(2,1)} %bitcast.18), custom_call_target="tpu_custom_call" | custom-call | flops 1 | bytes 1 | tf_op jit(solution)/shard_map/quad_pack/pallas_call | solution.py:300
  14.4 0.1 collective-permute-start.7
  14.5 8.3 %cache_attention.2 = (bf16[64,4096]{1,0:T(8,128)(2,1)}, bf16[2,512,128]{2,1,0:T(8,128)(2,1)}) custom-call(s32[2]{0:T(128)} %lens.3, bf16[128,4096]{1,0:T(8,128)(2,1)} %q_hbm.3, bf16[128,512]{1,0:T(8,128)(2,1)} %fk_hbm.3, bf16[2,2048,512]{2,1,0:T(8,128)(2,1)} %k_hbm.3, bf16[2,2048,512]{2,1,0:T(8,128)(2,1)} %v_hbm.3), custom_call_target="tpu_custom_call" | custom-call | flops 1 | bytes 1 | tf_op jit(solution)/shard_map/cache_attention/pallas_call | solution.py:180
  22.8 4.0 %collective-permute-done.1 = bf16[48,512]{1,0:T(8,128)(2,1)S(1)} collective-permute-done((bf16[48,512]{1,0:T(8,128)(2,1)}, bf16[48,512]{1,0:T(8,128)(2,1)S(1)}, u32[]{:S(2)}, u32[]{:S(2)}) %collective-permute-start.1) | collective-permute-done | bytes 49184 | tf_op jit(solution)/shard_map/ppermute | solution.py:518
  26.7 0.8 %collective-permute-start.8 = (bf16[176,1024]{1,0:T(8,128)(2,1)S(1)}, bf16[176,1024]{1,0:T(8,128)(2,1)S(1)}, u32[]{:S(2)}, u32[]{:S(2)}) collective-permute-start(bf16[176,1024]{1,0:T(8,128)(2,1)S(1)} %copy-done.10), channel_id=1, source_target_pairs={{0,6},{2,4},{4,2},{6,0},{1,7},{3,5},{5,3},{7,1},{8,14},{10,12},{12... | collective-permute-start | bytes 1081352 | tf_op jit(solution)/shard_map/ppermute | solution.py:514
  27.5 0.0 collective-permute-done.2
  27.5 1.7 %collective-permute-start.9 = (bf16[176,1024]{1,0:T(8,128)(2,1)S(1)}, bf16[176,1024]{1,0:T(8,128)(2,1)S(1)}, u32[]{:S(2)}, u32[]{:S(2)}) collective-permute-start(bf16[176,1024]{1,0:T(8,128)(2,1)S(1)} %copy-done.9), channel_id=1, source_target_pairs={{0,2},{2,0},{4,6},{6,4},{1,3},{3,1},{5,7},{7,5},{8,10},{10,8},{12,... | collective-permute-start | bytes 1081352 | tf_op jit(solution)/shard_map/ppermute | solution.py:514
  29.2 0.0 collective-permute-done.3
  29.2 0.0 collective-permute-done.refs_0_
  29.3 1.9 %collective-permute-start.5 = (bf16[288,512]{1,0:T(8,128)(2,1)S(1)}, bf16[288,512]{1,0:T(8,128)(2,1)S(1)}, u32[]{:S(2)}, u32[]{:S(2)}) collective-permute-start(bf16[288,512]{1,0:T(8,128)(2,1)S(1)} %collective-permute-done.refs_0_), channel_id=1, source_target_pairs={{0,16},{16,0},{1,17},{17,1},{2,18},{18,2},{3,19},{19,3},{4,20},{20... | collective-permute-start | bytes 884744 | tf_op jit(solution)/shard_map/ppermute | solution.py:532
  31.2 2.3 %collective-permute-start.4 = (bf16[272,512]{1,0:T(8,128)(2,1)S(1)}, bf16[272,512]{1,0:T(8,128)(2,1)S(1)}, u32[]{:S(2)}, u32[]{:S(2)}) collective-permute-start(bf16[272,512]{1,0:T(8,128)(2,1)S(1)} %copy-done.11), channel_id=1, source_target_pairs={{0,8},{8,0},{1,9},{9,1},{2,10},{10,2},{3,11},{11,3},{4,12},{12,4},... | collective-permute-start | bytes 835592 | tf_op jit(solution)/shard_map/ppermute | solution.py:531
  33.5 0.0 copy-start.8
  33.5 0.0 collective-permute-done.7
  33.5 6.2 %collective-permute-start.6 = (bf16[4,48,512]{2,1,0:T(8,128)(2,1)S(1)}, bf16[4,48,512]{2,1,0:T(8,128)(2,1)S(1)}, u32[]{:S(2)}, u32[]{:S(2)}) collective-permute-start(bf16[4,48,512]{2,1,0:T(8,128)(2,1)S(1)} %pad_maximum_fusion.1.refs_0_), channel_id=1, source_target_pairs={{0,16},{16,0},{1,17},{17,1},{2,18},{18,2},{3,19},{19,3},{4,20},{20... | collective-permute-start | bytes 589832 | tf_op jit(solution)/shard_map/ppermute | solution.py:533
  39.8 6.0 %cache_attention.3 = (bf16[64,4096]{1,0:T(8,128)(2,1)}, bf16[2,512,128]{2,1,0:T(8,128)(2,1)}) custom-call(s32[2]{0:T(128)} %lens.3, bf16[128,4096]{1,0:T(8,128)(2,1)} %q_hbm.3, bf16[128,512]{1,0:T(8,128)(2,1)} %fk_hbm.3, bf16[2,2048,512]{2,1,0:T(8,128)(2,1)} %k_hbm.3, bf16[2,2048,512]{2,1,0:T(8,128)(2,1)} %v_hbm.3), custom_call_target="tpu_custom_call" | custom-call | flops 1 | bytes 1 | tf_op jit(solution)/shard_map/cache_attention/pallas_call | solution.py:180
  45.8 0.6 collective-permute-done.8
  46.4 0.0 collective-permute-done.9
  46.4 0.0 collective-permute-done.6.refs_1_
  46.4 0.0 collective-permute-done.4.refs_1_
  46.4 0.0 collective-permute-done.5.refs_2_
  46.4 0.0 copy-start
  46.5 0.0 copy-start.6
  46.5 0.0 copy-start.7
  46.5 0.2 pad_maximum_fusion.refs_4_
  46.7 0.1 collective-permute-start.12
  46.7 1.6 %collective-permute-start.13 = (bf16[272,512]{1,0:T(8,128)(2,1)S(1)}, bf16[272,512]{1,0:T(8,128)(2,1)S(1)}, u32[]{:S(2)}, u32[]{:S(2)}) collective-permute-start(bf16[272,512]{1,0:T(8,128)(2,1)S(1)} %collective-permute-done.4.refs_1_), channel_id=1, source_target_pairs={{0,16},{16,0},{1,17},{17,1},{2,18},{18,2},{3,19},{19,3},{4,20},{20... | collective-permute-start | bytes 835592 | tf_op jit(solution)/shard_map/ppermute | solution.py:540
  48.3 0.2 collective-permute-start.10
  48.5 0.3 collective-permute-start.11
  48.8 1.4 %collective-permute-done.10.refs_2_ = bf16[4,48,512]{2,1,0:T(8,128)(2,1)S(1)} collective-permute-done((bf16[4,48,512]{2,1,0:T(8,128)(2,1)S(1)}, bf16[4,48,512]{2,1,0:T(8,128)(2,1)S(1)}, u32[]{:S(2)}, u32[]{:S(2)}) %collective-permute-start.10) | collective-permute-done | bytes 196640 | tf_op jit(solution)/shard_map/ppermute | solution.py:542
  50.2 0.3 collective-permute-done.11.refs_3_
  50.5 0.0 collective-permute-done.12.refs_5_
  50.5 2.4 %near_products.1.near = f32[512,512]{1,0:T(8,128)S(1)} custom-call(s32[16]{0:T(128)S(1)} %copy-done.6, s32[16]{0:T(128)S(1)} %copy-done.7, bf16[1024,512]{1,0:T(8,128)(2,1)S(1)} %copy-done, bf16[4,48,512]{2,1,0:T(8,128)(2,1)S(1)} %pad_maximum_fusion.1.refs_0_, bf16[4,48,512]{2,1,0:T(8,128)(2,1)S(1)} %collective-permute-done.6.refs_1_, ...), custom_call_target="tpu_custom_call" | custom-call | flops 1 | bytes 1 | tf_op jit(solution)/shard_map/near_products/pallas_call | solution.py:372
  52.9 0.0 copy-start.1
  53.0 0.0 copy-start.5
  53.0 2.8 %collective-permute-done.13.refs_3_ = bf16[272,512]{1,0:T(8,128)(2,1)S(1)} collective-permute-done((bf16[272,512]{1,0:T(8,128)(2,1)S(1)}, bf16[272,512]{1,0:T(8,128)(2,1)S(1)}, u32[]{:S(2)}, u32[]{:S(2)}) %collective-permute-start.13) | collective-permute-done | bytes 278560 | tf_op jit(solution)/shard_map/ppermute | solution.py:540
  55.8 0.8 %far_products.1 = (bf16[128,512]{1,0:T(8,128)(2,1)S(1)}, bf16[128,512]{1,0:T(8,128)(2,1)S(1)}, bf16[128,512]{1,0:T(8,128)(2,1)S(1)}, bf16[128,512]{1,0:T(8,128)(2,1)S(1)}) custom-call(f32[512,512]{1,0:T(8,128)S(1)} %near_products.1.near, bf16[288,512]{1,0:T(8,128)(2,1)S(1)} %collective-permute-done.refs_0_, ...), custom_call_target="tpu_custom_call" | custom-call | flops 1 | bytes 1 | tf_op jit(solution)/shard_map/far_products/pallas_call | solution.py:417
  56.6 5.0 %collective-permute-start.14 = (bf16[128,512]{1,0:T(8,128)(2,1)S(1)}, bf16[128,512]{1,0:T(8,128)(2,1)S(1)}, u32[]{:S(2)}, u32[]{:S(2)}) collective-permute-start(bf16[128,512]{1,0:T(8,128)(2,1)S(1)} %get-tuple-element.61), channel_id=1, source_target_pairs={{0,2},{2,0},{4,6},{6,4},{1,3},{3,1},{5,7},{7,5},{8,10},{10,8},{12,... | collective-permute-start | bytes 393224 | tf_op jit(solution)/shard_map/ppermute | solution.py:514
  61.6 0.0 collective-permute-start.15
  61.6 1.5 %collective-permute-start.16 = (bf16[128,512]{1,0:T(8,128)(2,1)S(1)}, bf16[128,512]{1,0:T(8,128)(2,1)S(1)}, u32[]{:S(2)}, u32[]{:S(2)}) collective-permute-start(bf16[128,512]{1,0:T(8,128)(2,1)S(1)} %get-tuple-element.63), channel_id=1, source_target_pairs={{0,6},{2,4},{4,2},{6,0},{1,7},{3,5},{5,3},{7,1},{8,14},{10,12},{12... | collective-permute-start | bytes 393224 | tf_op jit(solution)/shard_map/ppermute | solution.py:514
  63.1 1.9 %collective-permute-done.14.refs_5_ = bf16[128,512]{1,0:T(8,128)(2,1)S(1)} collective-permute-done((bf16[128,512]{1,0:T(8,128)(2,1)S(1)}, bf16[128,512]{1,0:T(8,128)(2,1)S(1)}, u32[]{:S(2)}, u32[]{:S(2)}) %collective-permute-start.14) | collective-permute-done | bytes 131104 | tf_op jit(solution)/shard_map/ppermute | solution.py:514
  65.0 2.8 %collective-permute-done.15.refs_6_ = bf16[128,512]{1,0:T(8,128)(2,1)S(1)} collective-permute-done((bf16[128,512]{1,0:T(8,128)(2,1)S(1)}, bf16[128,512]{1,0:T(8,128)(2,1)S(1)}, u32[]{:S(2)}, u32[]{:S(2)}) %collective-permute-start.15) | collective-permute-done | bytes 131104 | tf_op jit(solution)/shard_map/ppermute | solution.py:514
  67.8 1.2 %collective-permute-done.16.refs_7_ = bf16[128,512]{1,0:T(8,128)(2,1)S(1)} collective-permute-done((bf16[128,512]{1,0:T(8,128)(2,1)S(1)}, bf16[128,512]{1,0:T(8,128)(2,1)S(1)}, u32[]{:S(2)}, u32[]{:S(2)}) %collective-permute-start.16) | collective-permute-done | bytes 131104 | tf_op jit(solution)/shard_map/ppermute | solution.py:514
  69.0 2.6 %finish_attention.1 = (bf16[128,4096]{1,0:T(8,128)(2,1)}, bf16[128,512]{1,0:T(8,128)(2,1)}) custom-call(s32[2]{0:T(128)S(1)} %copy-done.5, bf16[64,4096]{1,0:T(8,128)(2,1)S(1)} %copy-done.1, bf16[64,4096]{1,0:T(8,128)(2,1)S(1)} %copy-done.2, bf16[2,512,128]{2,1,0:T(8,128)(2,1)S(1)} %copy-done.3, bf16[2,512,128]{2,1,0:T(8,128)(2,1)S(1)} %copy-done.4, ...), custom_call_target="tpu_custom_call" | custom-call | flops 1 | bytes 1 | tf_op jit(solution)/shard_map/finish_attention/pallas_call | solution.py:469
  (20 shorter events, 0.1 us)
Async XLA Ops:
  2.7 26.5 %collective-permute-start = (bf16[288,512]{1,0:T(8,128)(2,1)}, bf16[288,512]{1,0:T(8,128)(2,1)S(1)}, u32[]{:S(2)}, u32[]{:S(2)}) collective-permute-start(bf16[288,512]{1,0:T(8,128)(2,1)} %get-tuple-element.33), channel_id=1, source_target_pairs={{0,8},{8,0},{1,9},{9,1},{2,10},{10,2},{3,11},{11,3},{4,12},{12,4},... | collective-permute-start | bytes 884744 | tf_op jit(solution)/shard_map/ppermute | solution.py:524
  6.8 19.9 %collective-permute-start.1 = (bf16[48,512]{1,0:T(8,128)(2,1)}, bf16[48,512]{1,0:T(8,128)(2,1)S(1)}, u32[]{:S(2)}, u32[]{:S(2)}) collective-permute-start(bf16[48,512]{1,0:T(8,128)(2,1)} %get-tuple-element.38), channel_id=1, source_target_pairs={{0,10},{2,8},{4,14},{6,12},{8,2},{10,0},{12,6},{14,4},{1,11},{3,9}... | collective-permute-start | bytes 147464 | tf_op jit(solution)/shard_map/ppermute | solution.py:518
  8.1 19.4 %collective-permute-start.2 = (bf16[48,512]{1,0:T(8,128)(2,1)}, bf16[48,512]{1,0:T(8,128)(2,1)S(1)}, u32[]{:S(2)}, u32[]{:S(2)}) collective-permute-start(bf16[48,512]{1,0:T(8,128)(2,1)} %get-tuple-element.39), channel_id=1, source_target_pairs={{0,12},{2,14},{4,8},{6,10},{8,4},{10,6},{12,0},{14,2},{1,13},{3,15... | collective-permute-start | bytes 147464 | tf_op jit(solution)/shard_map/ppermute | solution.py:518
  11.7 17.5 %collective-permute-start.3 = (bf16[48,512]{1,0:T(8,128)(2,1)}, bf16[48,512]{1,0:T(8,128)(2,1)S(1)}, u32[]{:S(2)}, u32[]{:S(2)}) collective-permute-start(bf16[48,512]{1,0:T(8,128)(2,1)} %get-tuple-element.40), channel_id=1, source_target_pairs={{0,14},{2,12},{4,10},{6,8},{8,6},{10,4},{12,2},{14,0},{1,15},{3,13... | collective-permute-start | bytes 147464 | tf_op jit(solution)/shard_map/ppermute | solution.py:518
  14.4 19.2 %collective-permute-start.7 = (bf16[176,1024]{1,0:T(8,128)(2,1)}, bf16[176,1024]{1,0:T(8,128)(2,1)S(1)}, u32[]{:S(2)}, u32[]{:S(2)}) collective-permute-start(bf16[176,1024]{1,0:T(8,128)(2,1)} %get-tuple-element.51), channel_id=1, source_target_pairs={{0,4},{2,6},{4,0},{6,2},{1,5},{3,7},{5,1},{7,3},{8,12},{10,14},{12... | collective-permute-start | bytes 1081352 | tf_op jit(solution)/shard_map/ppermute | solution.py:514
  14.4 12.3 %copy-start.10 = (bf16[176,1024]{1,0:T(8,128)(2,1)S(1)}, bf16[176,1024]{1,0:T(8,128)(2,1)}, u32[]{:S(2)}) copy-start(bf16[176,1024]{1,0:T(8,128)(2,1)} %get-tuple-element.52) | copy-start | bytes 1081348
  14.4 13.1 %copy-start.9 = (bf16[176,1024]{1,0:T(8,128)(2,1)S(1)}, bf16[176,1024]{1,0:T(8,128)(2,1)}, u32[]{:S(2)}) copy-start(bf16[176,1024]{1,0:T(8,128)(2,1)} %get-tuple-element.53) | copy-start | bytes 1081348
  14.4 16.7 %copy-start.11 = (bf16[272,512]{1,0:T(8,128)(2,1)S(1)}, bf16[272,512]{1,0:T(8,128)(2,1)}, u32[]{:S(2)}) copy-start(bf16[272,512]{1,0:T(8,128)(2,1)} %get-tuple-element.50) | copy-start | bytes 835588
  26.7 19.7 %collective-permute-start.8 = (bf16[176,1024]{1,0:T(8,128)(2,1)S(1)}, bf16[176,1024]{1,0:T(8,128)(2,1)S(1)}, u32[]{:S(2)}, u32[]{:S(2)}) collective-permute-start(bf16[176,1024]{1,0:T(8,128)(2,1)S(1)} %copy-done.10), channel_id=1, source_target_pairs={{0,6},{2,4},{4,2},{6,0},{1,7},{3,5},{5,3},{7,1},{8,14},{10,12},{12... | collective-permute-start | bytes 1081352 | tf_op jit(solution)/shard_map/ppermute | solution.py:514
  27.5 18.9 %collective-permute-start.9 = (bf16[176,1024]{1,0:T(8,128)(2,1)S(1)}, bf16[176,1024]{1,0:T(8,128)(2,1)S(1)}, u32[]{:S(2)}, u32[]{:S(2)}) collective-permute-start(bf16[176,1024]{1,0:T(8,128)(2,1)S(1)} %copy-done.9), channel_id=1, source_target_pairs={{0,2},{2,0},{4,6},{6,4},{1,3},{3,1},{5,7},{7,5},{8,10},{10,8},{12,... | collective-permute-start | bytes 1081352 | tf_op jit(solution)/shard_map/ppermute | solution.py:514
  29.3 17.2 %collective-permute-start.5 = (bf16[288,512]{1,0:T(8,128)(2,1)S(1)}, bf16[288,512]{1,0:T(8,128)(2,1)S(1)}, u32[]{:S(2)}, u32[]{:S(2)}) collective-permute-start(bf16[288,512]{1,0:T(8,128)(2,1)S(1)} %collective-permute-done.refs_0_), channel_id=1, source_target_pairs={{0,16},{16,0},{1,17},{17,1},{2,18},{18,2},{3,19},{19,3},{4,20},{20... | collective-permute-start | bytes 884744 | tf_op jit(solution)/shard_map/ppermute | solution.py:532
  31.2 15.2 %collective-permute-start.4 = (bf16[272,512]{1,0:T(8,128)(2,1)S(1)}, bf16[272,512]{1,0:T(8,128)(2,1)S(1)}, u32[]{:S(2)}, u32[]{:S(2)}) collective-permute-start(bf16[272,512]{1,0:T(8,128)(2,1)S(1)} %copy-done.11), channel_id=1, source_target_pairs={{0,8},{8,0},{1,9},{9,1},{2,10},{10,2},{3,11},{11,3},{4,12},{12,4},... | collective-permute-start | bytes 835592 | tf_op jit(solution)/shard_map/ppermute | solution.py:531
  33.5 12.9 %copy-start.8 = (bf16[176,1024]{1,0:T(8,128)(2,1)S(1)}, bf16[176,1024]{1,0:T(8,128)(2,1)}, u32[]{:S(2)}) copy-start(bf16[176,1024]{1,0:T(8,128)(2,1)} %get-tuple-element.35) | copy-start | bytes 1081348
  33.5 12.9 %collective-permute-start.6 = (bf16[4,48,512]{2,1,0:T(8,128)(2,1)S(1)}, bf16[4,48,512]{2,1,0:T(8,128)(2,1)S(1)}, u32[]{:S(2)}, u32[]{:S(2)}) collective-permute-start(bf16[4,48,512]{2,1,0:T(8,128)(2,1)S(1)} %pad_maximum_fusion.1.refs_0_), channel_id=1, source_target_pairs={{0,16},{16,0},{1,17},{17,1},{2,18},{18,2},{3,19},{19,3},{4,20},{20... | collective-permute-start | bytes 589832 | tf_op jit(solution)/shard_map/ppermute | solution.py:533
  46.4 4.1 %copy-start = (bf16[1024,512]{1,0:T(8,128)(2,1)S(1)}, bf16[1024,512]{1,0:T(8,128)(2,1)}, u32[]{:S(2)}) copy-start(bf16[1024,512]{1,0:T(8,128)(2,1)} %own_ref.1) | copy-start | bytes 3145732
  46.5 4.1 %copy-start.6 = (s32[16]{0:T(128)S(1)}, s32[16]{0:T(128)}, u32[]{:S(2)}) copy-start(s32[16]{0:T(128)} %position.1) | copy-start | bytes 196
  46.5 4.1 %copy-start.7 = (s32[16]{0:T(128)S(1)}, s32[16]{0:T(128)}, u32[]{:S(2)}) copy-start(s32[16]{0:T(128)} %adapter.1) | copy-start | bytes 196
  46.7 3.9 %collective-permute-start.12 = (bf16[4,176,1024]{2,1,0:T(8,128)(2,1)S(1)}, bf16[4,176,1024]{2,1,0:T(8,128)(2,1)S(1)}, u32[]{:S(2)}, u32[]{:S(2)}) collective-permute-start(bf16[4,176,1024]{2,1,0:T(8,128)(2,1)S(1)} %pad_maximum_fusion.refs_4_), channel_id=1, source_target_pairs={{0,1},{1,0},{2,3},{3,2},{4,5},{5,4},{6,7},{7,6},{8,9},{9,8},{10,11... | collective-permute-start | bytes 4325384 | tf_op jit(solution)/shard_map/ppermute | solution.py:543
  46.7 9.1 %collective-permute-start.13 = (bf16[272,512]{1,0:T(8,128)(2,1)S(1)}, bf16[272,512]{1,0:T(8,128)(2,1)S(1)}, u32[]{:S(2)}, u32[]{:S(2)}) collective-permute-start(bf16[272,512]{1,0:T(8,128)(2,1)S(1)} %collective-permute-done.4.refs_1_), channel_id=1, source_target_pairs={{0,16},{16,0},{1,17},{17,1},{2,18},{18,2},{3,19},{19,3},{4,20},{20... | collective-permute-start | bytes 835592 | tf_op jit(solution)/shard_map/ppermute | solution.py:540
  48.3 1.9 %collective-permute-start.10 = (bf16[4,48,512]{2,1,0:T(8,128)(2,1)S(1)}, bf16[4,48,512]{2,1,0:T(8,128)(2,1)S(1)}, u32[]{:S(2)}, u32[]{:S(2)}) collective-permute-start(bf16[4,48,512]{2,1,0:T(8,128)(2,1)S(1)} %pad_maximum_fusion.1.refs_0_), channel_id=1, source_target_pairs={{0,1},{1,0},{2,3},{3,2},{4,5},{5,4},{6,7},{7,6},{8,9},{9,8},{10,11... | collective-permute-start | bytes 589832 | tf_op jit(solution)/shard_map/ppermute | solution.py:542
  48.5 2.0 %collective-permute-start.11 = (bf16[4,48,512]{2,1,0:T(8,128)(2,1)S(1)}, bf16[4,48,512]{2,1,0:T(8,128)(2,1)S(1)}, u32[]{:S(2)}, u32[]{:S(2)}) collective-permute-start(bf16[4,48,512]{2,1,0:T(8,128)(2,1)S(1)} %collective-permute-done.6.refs_1_), channel_id=1, source_target_pairs={{0,1},{1,0},{2,3},{3,2},{4,5},{5,4},{6,7},{7,6},{8,9},{9,8},{10,11... | collective-permute-start | bytes 589832 | tf_op jit(solution)/shard_map/ppermute | solution.py:542
  52.9 16.1 %copy-start.1 = (bf16[64,4096]{1,0:T(8,128)(2,1)S(1)}, bf16[64,4096]{1,0:T(8,128)(2,1)}, u32[]{:S(2)}) copy-start(bf16[64,4096]{1,0:T(8,128)(2,1)} %get-tuple-element.37.refs_0_) | copy-start | bytes 1572868
  52.9 16.1 %copy-start.2 = (bf16[64,4096]{1,0:T(8,128)(2,1)S(1)}, bf16[64,4096]{1,0:T(8,128)(2,1)}, u32[]{:S(2)}) copy-start(bf16[64,4096]{1,0:T(8,128)(2,1)} %get-tuple-element.47.refs_1_) | copy-start | bytes 1572868
  52.9 16.0 %copy-start.3 = (bf16[2,512,128]{2,1,0:T(8,128)(2,1)S(1)}, bf16[2,512,128]{2,1,0:T(8,128)(2,1)}, u32[]{:S(2)}) copy-start(bf16[2,512,128]{2,1,0:T(8,128)(2,1)} %get-tuple-element.41.refs_2_) | copy-start | bytes 786436
  53.0 16.0 %copy-start.4 = (bf16[2,512,128]{2,1,0:T(8,128)(2,1)S(1)}, bf16[2,512,128]{2,1,0:T(8,128)(2,1)}, u32[]{:S(2)}) copy-start(bf16[2,512,128]{2,1,0:T(8,128)(2,1)} %get-tuple-element.48.refs_3_) | copy-start | bytes 786436
  53.0 16.0 %copy-start.5 = (s32[2]{0:T(128)S(1)}, s32[2]{0:T(128)}, u32[]{:S(2)}) copy-start(s32[2]{0:T(128)} %lens.3) | copy-start | bytes 28
  56.6 8.4 %collective-permute-start.14 = (bf16[128,512]{1,0:T(8,128)(2,1)S(1)}, bf16[128,512]{1,0:T(8,128)(2,1)S(1)}, u32[]{:S(2)}, u32[]{:S(2)}) collective-permute-start(bf16[128,512]{1,0:T(8,128)(2,1)S(1)} %get-tuple-element.61), channel_id=1, source_target_pairs={{0,2},{2,0},{4,6},{6,4},{1,3},{3,1},{5,7},{7,5},{8,10},{10,8},{12,... | collective-permute-start | bytes 393224 | tf_op jit(solution)/shard_map/ppermute | solution.py:514
  61.6 6.2 %collective-permute-start.15 = (bf16[128,512]{1,0:T(8,128)(2,1)S(1)}, bf16[128,512]{1,0:T(8,128)(2,1)S(1)}, u32[]{:S(2)}, u32[]{:S(2)}) collective-permute-start(bf16[128,512]{1,0:T(8,128)(2,1)S(1)} %get-tuple-element.62), channel_id=1, source_target_pairs={{0,4},{2,6},{4,0},{6,2},{1,5},{3,7},{5,1},{7,3},{8,12},{10,14},{12... | collective-permute-start | bytes 393224 | tf_op jit(solution)/shard_map/ppermute | solution.py:514
  61.6 7.4 %collective-permute-start.16 = (bf16[128,512]{1,0:T(8,128)(2,1)S(1)}, bf16[128,512]{1,0:T(8,128)(2,1)S(1)}, u32[]{:S(2)}, u32[]{:S(2)}) collective-permute-start(bf16[128,512]{1,0:T(8,128)(2,1)S(1)} %get-tuple-element.63), channel_id=1, source_target_pairs={{0,6},{2,4},{4,2},{6,0},{1,7},{3,5},{5,3},{7,1},{8,14},{10,12},{12... | collective-permute-start | bytes 393224 | tf_op jit(solution)/shard_map/ppermute | solution.py:514

commit v16 on v13

--- a/solution.py
+++ b/solution.py
@@ -153,7 +153,7 @@
         p = jnp.exp2((fresh_scores(k) - m_s[k]) * EXP2_SCALE)
         inverse = 1.0 / (acc[k, HD : HD + 1, :] + jnp.sum(p, axis=0, keepdims=True))
         p_s[0, (k % 2) * SPAN : (k % 2 + 1) * SPAN, :] = (p * inverse).astype(jnp.bfloat16)
-        mixed = (acc[k, :HD, :] * inverse).T.astype(jnp.bfloat16)
+        mixed = (acc[k, :HD, :] * inverse).astype(jnp.bfloat16).T
         for h in range(group_size):
             out_s[:, tiles(k * group_size + h)] = mixed[h * SPAN : (h + 1) * SPAN, :]
         here = slice(k * group_size * HD, (k + 1) * group_size * HD)
@@ -534,7 +534,7 @@
         mine, theirs, maps_mine, maps_theirs, value_matrix, adapter_position, span_adapter_index, tokens
     )
     products = far_products(mine, theirs, near, (early, late, early_other, late_other), tokens)
-    parts = [products[0]] + [to_quad(products[q], q) for q in range(1, quads)]
+    parts = [products[0]] + [to_quad(products[q], q) for q in range(quads - 1, 0, -1)]
     mixed, fresh_probs = zip(*attn)
     attended, incoming_values = finish(cache_length, mixed, fresh_probs, parts, q_width)
     return (attended, incoming_values)

time: 68.3 us -> 68 us (level)
  Pallas kernels: 31.1 us -> 24.2 us
  waiting for transfers between devices: 13 us -> 19.2 us
    pallas_call x2, Pallas kernels: 21.2 us -> 14.3 us  [cache_attention(): pl.pallas_call(functools.partial(cache_kernel, order), in_specs=[pl.Block...]
    ppermute x6, waiting for transfers between devices: 7.33 us -> 11.3 us  [to_quad(): return lax.ppermute(value, 'quad', [(j, j ^ q) for j in range(quads)])]
    ppermute x3, waiting for transfers between devices: 0.01 us -> 2.61 us  [to_other_wing(): return lax.ppermute(value, ('wing', 'quad'), pairs)]
    ppermute x1, starting transfers between devices: 2.28 us -> 3.74 us  [on_device(): late = lax.ppermute(after(late, early), 'wing', SWAP)]
    ppermute x1, starting transfers between devices: 1.72 us -> 0.46 us  [on_device(): early_other = lax.ppermute(early, 'parts', parts_swap)]
  transfers between devices with their start and end apart: 17 -> 17, of which waited for: 9 -> 8; matrix products, arithmetic and copies ran while one was open for 0% -> 0% of each run, Pallas kernels for 39% -> 28%
where the time goes in v16:
time: 68 us; the launch traced here: 67.9 us
  Pallas kernels  24.2 us (36%)
  starting transfers between devices  23.3 us (34%)
  waiting for transfers between devices  19.2 us (28%)
  between operations  0.9 us (1%)
    pallas_call x2, Pallas kernels, cache_attention(): pl.pallas_call(functools.partial(cache_kernel, order), in_specs=[pl.Block...  14.3 us
    ppermute x6, waiting for transfers between devices, to_quad(): return lax.ppermute(value, 'quad', [(j, j ^ q) for j in range(quads)])  11.3 us
    ppermute x6, starting transfers between devices, to_quad(): return lax.ppermute(value, 'quad', [(j, j ^ q) for j in range(quads)])  7.37 us
    ppermute x3, starting transfers between devices, to_other_wing(): return lax.ppermute(value, ('wing', 'quad'), pairs)  4.9 us
    ppermute x1, starting transfers between devices, on_device(): early = lax.ppermute(early, 'wing', SWAP)  4.1 us
    ppermute x1, starting transfers between devices, on_device(): late = lax.ppermute(after(late, early), 'wing', SWAP)  3.74 us
    ppermute x1, waiting for transfers between devices, on_device(): late_other = lax.ppermute(late, 'parts', parts_swap)  3.55 us
    ppermute x3, waiting for transfers between devices, to_other_wing(): return lax.ppermute(value, ('wing', 'quad'), pairs)  2.61 us
  transfers between devices with their start and end apart: 17, of which 8 were waited for; matrix products, arithmetic and copies ran while one was open for 0% of the time, Pallas kernels for 28%

profile of v16, /device:TPU:0, one launch (start us, length us, event | category | flops | bytes accessed | tf_op | source)
XLA Modules:
  0.0 67.9 jit_solution(17483474048786173829)
XLA Ops:
  0.6 2.1 %cross_pack.1 = (bf16[256,512]{1,0:T(8,128)(2,1)}, bf16[304,512]{1,0:T(8,128)(2,1)}, bf16[48,512]{1,0:T(8,128)(2,1)}, bf16[48,512]{1,0:T(8,128)(2,1)}, bf16[48,512]{1,0:T(8,128)(2,1)}) custom-call(bf16[32,8192]{1,0:T(8,128)(2,1)} %bitcast.11, bf16[32,512]{1,0:T(8,128)(2,1)} %bitcast.17, bf16[1024,512]{1,0:T(8,128)(2,1)} %own_ref.1), custom_call_target="tpu_custom_call" | custom-call | flops 1 | bytes 1 | tf_op jit(solution)/shard_map/cross_pack/pallas_call | solution.py:253
  2.7 4.1 %collective-permute-start = (bf16[256,512]{1,0:T(8,128)(2,1)}, bf16[256,512]{1,0:T(8,128)(2,1)S(1)}, u32[]{:S(2)}, u32[]{:S(2)}) collective-permute-start(bf16[256,512]{1,0:T(8,128)(2,1)} %get-tuple-element.33), channel_id=1, source_target_pairs={{0,8},{8,0},{1,9},{9,1},{2,10},{10,2},{3,11},{11,3},{4,12},{12,4},... | collective-permute-start | bytes 786440 | tf_op jit(solution)/shard_map/ppermute | solution.py:511
  6.8 1.3 %collective-permute-start.1 = (bf16[48,512]{1,0:T(8,128)(2,1)}, bf16[48,512]{1,0:T(8,128)(2,1)S(1)}, u32[]{:S(2)}, u32[]{:S(2)}) collective-permute-start(bf16[48,512]{1,0:T(8,128)(2,1)} %get-tuple-element.38), channel_id=1, source_target_pairs={{0,10},{2,8},{4,14},{6,12},{8,2},{10,0},{12,6},{14,4},{1,11},{3,9}... | collective-permute-start | bytes 147464 | tf_op jit(solution)/shard_map/ppermute | solution.py:505
  8.1 3.6 %collective-permute-start.2 = (bf16[48,512]{1,0:T(8,128)(2,1)}, bf16[48,512]{1,0:T(8,128)(2,1)S(1)}, u32[]{:S(2)}, u32[]{:S(2)}) collective-permute-start(bf16[48,512]{1,0:T(8,128)(2,1)} %get-tuple-element.39), channel_id=1, source_target_pairs={{0,12},{2,14},{4,8},{6,10},{8,4},{10,6},{12,0},{14,2},{1,13},{3,15... | collective-permute-start | bytes 147464 | tf_op jit(solution)/shard_map/ppermute | solution.py:505
  11.7 0.0 collective-permute-start.3
  11.7 2.6 %quad_pack.1 = (bf16[176,1024]{1,0:T(8,128)(2,1)}, bf16[176,1024]{1,0:T(8,128)(2,1)}, bf16[176,1024]{1,0:T(8,128)(2,1)}, bf16[176,1024]{1,0:T(8,128)(2,1)}) custom-call(bf16[128,4096]{1,0:T(8,128)(2,1)} %x_hbm, bf16[32,8192]{1,0:T(8,128)(2,1)} %bitcast.12, bf16[32,512]{1,0:T(8,128)(2,1)} %bitcast.18), custom_call_target="tpu_custom_call" | custom-call | flops 1 | bytes 1 | tf_op jit(solution)/shard_map/quad_pack/pallas_call | solution.py:300
  14.3 0.1 collective-permute-start.7
  14.5 8.2 %cache_attention.2 = (bf16[64,4096]{1,0:T(8,128)(2,1)}, bf16[2,512,128]{2,1,0:T(8,128)(2,1)}) custom-call(s32[2]{0:T(128)} %lens.3, bf16[128,4096]{1,0:T(8,128)(2,1)} %q_hbm.3, bf16[128,512]{1,0:T(8,128)(2,1)} %fk_hbm.3, bf16[2,2048,512]{2,1,0:T(8,128)(2,1)} %k_hbm.3, bf16[2,2048,512]{2,1,0:T(8,128)(2,1)} %v_hbm.3), custom_call_target="tpu_custom_call" | custom-call | flops 1 | bytes 1 | tf_op jit(solution)/shard_map/cache_attention/pallas_call | solution.py:180
  22.7 2.6 %collective-permute-done.1 = bf16[48,512]{1,0:T(8,128)(2,1)S(1)} collective-permute-done((bf16[48,512]{1,0:T(8,128)(2,1)}, bf16[48,512]{1,0:T(8,128)(2,1)S(1)}, u32[]{:S(2)}, u32[]{:S(2)}) %collective-permute-start.1) | collective-permute-done | bytes 49184 | tf_op jit(solution)/shard_map/ppermute | solution.py:505
  25.3 3.7 %collective-permute-start.8 = (bf16[176,1024]{1,0:T(8,128)(2,1)S(1)}, bf16[176,1024]{1,0:T(8,128)(2,1)S(1)}, u32[]{:S(2)}, u32[]{:S(2)}) collective-permute-start(bf16[176,1024]{1,0:T(8,128)(2,1)S(1)} %copy-done.10), channel_id=1, source_target_pairs={{0,6},{2,4},{4,2},{6,0},{1,7},{3,5},{5,3},{7,1},{8,14},{10,12},{12... | collective-permute-start | bytes 1081352 | tf_op jit(solution)/shard_map/ppermute | solution.py:501
  29.0 0.0 collective-permute-done.2
  29.1 0.0 collective-permute-start.9
  29.1 0.0 collective-permute-done.3
  29.1 0.0 collective-permute-done.refs_0_
  29.1 0.5 collective-permute-start.5
  29.6 3.7 %collective-permute-start.4 = (bf16[304,512]{1,0:T(8,128)(2,1)S(1)}, bf16[304,512]{1,0:T(8,128)(2,1)S(1)}, u32[]{:S(2)}, u32[]{:S(2)}) collective-permute-start(bf16[304,512]{1,0:T(8,128)(2,1)S(1)} %copy-done.11), channel_id=1, source_target_pairs={{0,8},{8,0},{1,9},{9,1},{2,10},{10,2},{3,11},{11,3},{4,12},{12,4},... | collective-permute-start | bytes 933896 | tf_op jit(solution)/shard_map/ppermute | solution.py:518
  33.3 0.0 collective-permute-done.7
  33.3 0.6 collective-permute-start.6
  34.0 6.0 %cache_attention.3 = (bf16[64,4096]{1,0:T(8,128)(2,1)}, bf16[2,512,128]{2,1,0:T(8,128)(2,1)}) custom-call(s32[2]{0:T(128)} %lens.3, bf16[128,4096]{1,0:T(8,128)(2,1)} %q_hbm.3, bf16[128,512]{1,0:T(8,128)(2,1)} %fk_hbm.3, bf16[2,2048,512]{2,1,0:T(8,128)(2,1)} %k_hbm.3, bf16[2,2048,512]{2,1,0:T(8,128)(2,1)} %v_hbm.3), custom_call_target="tpu_custom_call" | custom-call | flops 1 | bytes 1 | tf_op jit(solution)/shard_map/cache_attention/pallas_call | solution.py:180
  40.0 6.0 %collective-permute-done.8 = bf16[176,1024]{1,0:T(8,128)(2,1)S(1)} collective-permute-done((bf16[176,1024]{1,0:T(8,128)(2,1)S(1)}, bf16[176,1024]{1,0:T(8,128)(2,1)S(1)}, u32[]{:S(2)}, u32[]{:S(2)}) %collective-permute-start.8) | collective-permute-done | bytes 360480 | tf_op jit(solution)/shard_map/ppermute | solution.py:501
  46.1 0.0 collective-permute-done.9
  46.1 0.0 collective-permute-done.6.refs_1_
  46.1 0.0 collective-permute-done.5.refs_2_
  46.1 0.0 collective-permute-done.4.refs_1_
  46.1 0.0 copy-start
  46.1 0.0 copy-start.6
  46.1 0.0 copy-start.7
  46.1 0.2 pad_maximum_fusion.refs_4_
  46.3 0.1 collective-permute-start.12
  46.4 1.6 %collective-permute-start.13 = (bf16[304,512]{1,0:T(8,128)(2,1)S(1)}, bf16[304,512]{1,0:T(8,128)(2,1)S(1)}, u32[]{:S(2)}, u32[]{:S(2)}) collective-permute-start(bf16[304,512]{1,0:T(8,128)(2,1)S(1)} %collective-permute-done.4.refs_1_), channel_id=1, source_target_pairs={{0,16},{16,0},{1,17},{17,1},{2,18},{18,2},{3,19},{19,3},{4,20},{20... | collective-permute-start | bytes 933896 | tf_op jit(solution)/shard_map/ppermute | solution.py:527
  47.9 0.2 collective-permute-start.10
  48.1 0.3 collective-permute-start.11
  48.5 1.4 %collective-permute-done.10.refs_2_ = bf16[4,48,512]{2,1,0:T(8,128)(2,1)S(1)} collective-permute-done((bf16[4,48,512]{2,1,0:T(8,128)(2,1)S(1)}, bf16[4,48,512]{2,1,0:T(8,128)(2,1)S(1)}, u32[]{:S(2)}, u32[]{:S(2)}) %collective-permute-start.10) | collective-permute-done | bytes 196640 | tf_op jit(solution)/shard_map/ppermute | solution.py:529
  49.9 0.3 collective-permute-done.11.refs_3_
  50.2 0.0 collective-permute-done.12.refs_5_
  50.2 0.0 copy-done.7
  50.2 2.4 %near_products.1.near = f32[512,512]{1,0:T(8,128)S(1)} custom-call(s32[16]{0:T(128)S(1)} %copy-done.6, s32[16]{0:T(128)S(1)} %copy-done.7, bf16[1024,512]{1,0:T(8,128)(2,1)S(1)} %copy-done, bf16[4,48,512]{2,1,0:T(8,128)(2,1)S(1)} %pad_maximum_fusion.1.refs_0_, bf16[4,48,512]{2,1,0:T(8,128)(2,1)S(1)} %collective-permute-done.6.refs_1_, ...), custom_call_target="tpu_custom_call" | custom-call | flops 1 | bytes 1 | tf_op jit(solution)/shard_map/near_products/pallas_call | solution.py:372
  52.6 0.0 copy-start.1
  52.6 0.0 copy-start.5
  52.6 3.5 %collective-permute-done.13.refs_3_ = bf16[304,512]{1,0:T(8,128)(2,1)S(1)} collective-permute-done((bf16[304,512]{1,0:T(8,128)(2,1)S(1)}, bf16[304,512]{1,0:T(8,128)(2,1)S(1)}, u32[]{:S(2)}, u32[]{:S(2)}) %collective-permute-start.13) | collective-permute-done | bytes 311328 | tf_op jit(solution)/shard_map/ppermute | solution.py:527
  56.2 0.8 %far_products.1 = (bf16[128,512]{1,0:T(8,128)(2,1)S(1)}, bf16[128,512]{1,0:T(8,128)(2,1)S(1)}, bf16[128,512]{1,0:T(8,128)(2,1)S(1)}, bf16[128,512]{1,0:T(8,128)(2,1)S(1)}) custom-call(f32[512,512]{1,0:T(8,128)S(1)} %near_products.1.near, bf16[256,512]{1,0:T(8,128)(2,1)S(1)} %collective-permute-done.refs_0_, ...), custom_call_target="tpu_custom_call" | custom-call | flops 1 | bytes 1 | tf_op jit(solution)/shard_map/far_products/pallas_call | solution.py:417
  57.0 2.0 %collective-permute-start.14 = (bf16[128,512]{1,0:T(8,128)(2,1)S(1)}, bf16[128,512]{1,0:T(8,128)(2,1)S(1)}, u32[]{:S(2)}, u32[]{:S(2)}) collective-permute-start(bf16[128,512]{1,0:T(8,128)(2,1)S(1)} %get-tuple-element.61), channel_id=1, source_target_pairs={{0,6},{2,4},{4,2},{6,0},{1,7},{3,5},{5,3},{7,1},{8,14},{10,12},{12... | collective-permute-start | bytes 393224 | tf_op jit(solution)/shard_map/ppermute | solution.py:501
  59.0 0.0 collective-permute-start.15
  59.0 1.5 %collective-permute-start.16 = (bf16[128,512]{1,0:T(8,128)(2,1)S(1)}, bf16[128,512]{1,0:T(8,128)(2,1)S(1)}, u32[]{:S(2)}, u32[]{:S(2)}) collective-permute-start(bf16[128,512]{1,0:T(8,128)(2,1)S(1)} %get-tuple-element.63), channel_id=1, source_target_pairs={{0,2},{2,0},{4,6},{6,4},{1,3},{3,1},{5,7},{7,5},{8,10},{10,8},{12,... | collective-permute-start | bytes 393224 | tf_op jit(solution)/shard_map/ppermute | solution.py:501
  60.5 3.8 %collective-permute-done.14.refs_5_ = bf16[128,512]{1,0:T(8,128)(2,1)S(1)} collective-permute-done((bf16[128,512]{1,0:T(8,128)(2,1)S(1)}, bf16[128,512]{1,0:T(8,128)(2,1)S(1)}, u32[]{:S(2)}, u32[]{:S(2)}) %collective-permute-start.14) | collective-permute-done | bytes 131104 | tf_op jit(solution)/shard_map/ppermute | solution.py:501
  64.4 0.5 collective-permute-done.15.refs_6_
  64.9 0.9 %collective-permute-done.16.refs_7_ = bf16[128,512]{1,0:T(8,128)(2,1)S(1)} collective-permute-done((bf16[128,512]{1,0:T(8,128)(2,1)S(1)}, bf16[128,512]{1,0:T(8,128)(2,1)S(1)}, u32[]{:S(2)}, u32[]{:S(2)}) %collective-permute-start.16) | collective-permute-done | bytes 131104 | tf_op jit(solution)/shard_map/ppermute | solution.py:501
  65.8 2.0 %finish_attention.1 = (bf16[128,4096]{1,0:T(8,128)(2,1)}, bf16[128,512]{1,0:T(8,128)(2,1)}) custom-call(s32[2]{0:T(128)S(1)} %copy-done.5, bf16[64,4096]{1,0:T(8,128)(2,1)S(1)} %copy-done.1, bf16[64,4096]{1,0:T(8,128)(2,1)S(1)} %copy-done.2, bf16[2,512,128]{2,1,0:T(8,128)(2,1)S(1)} %copy-done.3, bf16[2,512,128]{2,1,0:T(8,128)(2,1)S(1)} %copy-done.4, ...), custom_call_target="tpu_custom_call" | custom-call | flops 1 | bytes 1 | tf_op jit(solution)/shard_map/finish_attention/pallas_call | solution.py:460
  (20 shorter events, 0.1 us)
Async XLA Ops:
  2.7 26.3 %collective-permute-start = (bf16[256,512]{1,0:T(8,128)(2,1)}, bf16[256,512]{1,0:T(8,128)(2,1)S(1)}, u32[]{:S(2)}, u32[]{:S(2)}) collective-permute-start(bf16[256,512]{1,0:T(8,128)(2,1)} %get-tuple-element.33), channel_id=1, source_target_pairs={{0,8},{8,0},{1,9},{9,1},{2,10},{10,2},{3,11},{11,3},{4,12},{12,4},... | collective-permute-start | bytes 786440 | tf_op jit(solution)/shard_map/ppermute | solution.py:511
  6.8 18.5 %collective-permute-start.1 = (bf16[48,512]{1,0:T(8,128)(2,1)}, bf16[48,512]{1,0:T(8,128)(2,1)S(1)}, u32[]{:S(2)}, u32[]{:S(2)}) collective-permute-start(bf16[48,512]{1,0:T(8,128)(2,1)} %get-tuple-element.38), channel_id=1, source_target_pairs={{0,10},{2,8},{4,14},{6,12},{8,2},{10,0},{12,6},{14,4},{1,11},{3,9}... | collective-permute-start | bytes 147464 | tf_op jit(solution)/shard_map/ppermute | solution.py:505
  8.1 20.9 %collective-permute-start.2 = (bf16[48,512]{1,0:T(8,128)(2,1)}, bf16[48,512]{1,0:T(8,128)(2,1)S(1)}, u32[]{:S(2)}, u32[]{:S(2)}) collective-permute-start(bf16[48,512]{1,0:T(8,128)(2,1)} %get-tuple-element.39), channel_id=1, source_target_pairs={{0,12},{2,14},{4,8},{6,10},{8,4},{10,6},{12,0},{14,2},{1,13},{3,15... | collective-permute-start | bytes 147464 | tf_op jit(solution)/shard_map/ppermute | solution.py:505
  11.7 17.3 %collective-permute-start.3 = (bf16[48,512]{1,0:T(8,128)(2,1)}, bf16[48,512]{1,0:T(8,128)(2,1)S(1)}, u32[]{:S(2)}, u32[]{:S(2)}) collective-permute-start(bf16[48,512]{1,0:T(8,128)(2,1)} %get-tuple-element.40), channel_id=1, source_target_pairs={{0,14},{2,12},{4,10},{6,8},{8,6},{10,4},{12,2},{14,0},{1,15},{3,13... | collective-permute-start | bytes 147464 | tf_op jit(solution)/shard_map/ppermute | solution.py:505
  14.3 19.0 %collective-permute-start.7 = (bf16[176,1024]{1,0:T(8,128)(2,1)}, bf16[176,1024]{1,0:T(8,128)(2,1)S(1)}, u32[]{:S(2)}, u32[]{:S(2)}) collective-permute-start(bf16[176,1024]{1,0:T(8,128)(2,1)} %get-tuple-element.51), channel_id=1, source_target_pairs={{0,4},{2,6},{4,0},{6,2},{1,5},{3,7},{5,1},{7,3},{8,12},{10,14},{12... | collective-permute-start | bytes 1081352 | tf_op jit(solution)/shard_map/ppermute | solution.py:501
  14.4 10.9 %copy-start.10 = (bf16[176,1024]{1,0:T(8,128)(2,1)S(1)}, bf16[176,1024]{1,0:T(8,128)(2,1)}, u32[]{:S(2)}) copy-start(bf16[176,1024]{1,0:T(8,128)(2,1)} %get-tuple-element.52) | copy-start | bytes 1081348
  14.4 14.6 %copy-start.9 = (bf16[176,1024]{1,0:T(8,128)(2,1)S(1)}, bf16[176,1024]{1,0:T(8,128)(2,1)}, u32[]{:S(2)}) copy-start(bf16[176,1024]{1,0:T(8,128)(2,1)} %get-tuple-element.53) | copy-start | bytes 1081348
  14.4 15.1 %copy-start.11 = (bf16[304,512]{1,0:T(8,128)(2,1)S(1)}, bf16[304,512]{1,0:T(8,128)(2,1)}, u32[]{:S(2)}) copy-start(bf16[304,512]{1,0:T(8,128)(2,1)} %get-tuple-element.50) | copy-start | bytes 933892
  25.3 20.8 %collective-permute-start.8 = (bf16[176,1024]{1,0:T(8,128)(2,1)S(1)}, bf16[176,1024]{1,0:T(8,128)(2,1)S(1)}, u32[]{:S(2)}, u32[]{:S(2)}) collective-permute-start(bf16[176,1024]{1,0:T(8,128)(2,1)S(1)} %copy-done.10), channel_id=1, source_target_pairs={{0,6},{2,4},{4,2},{6,0},{1,7},{3,5},{5,3},{7,1},{8,14},{10,12},{12... | collective-permute-start | bytes 1081352 | tf_op jit(solution)/shard_map/ppermute | solution.py:501
  29.1 17.0 %collective-permute-start.9 = (bf16[176,1024]{1,0:T(8,128)(2,1)S(1)}, bf16[176,1024]{1,0:T(8,128)(2,1)S(1)}, u32[]{:S(2)}, u32[]{:S(2)}) collective-permute-start(bf16[176,1024]{1,0:T(8,128)(2,1)S(1)} %copy-done.9), channel_id=1, source_target_pairs={{0,2},{2,0},{4,6},{6,4},{1,3},{3,1},{5,7},{7,5},{8,10},{10,8},{12,... | collective-permute-start | bytes 1081352 | tf_op jit(solution)/shard_map/ppermute | solution.py:501
  29.1 17.0 %collective-permute-start.5 = (bf16[256,512]{1,0:T(8,128)(2,1)S(1)}, bf16[256,512]{1,0:T(8,128)(2,1)S(1)}, u32[]{:S(2)}, u32[]{:S(2)}) collective-permute-start(bf16[256,512]{1,0:T(8,128)(2,1)S(1)} %collective-permute-done.refs_0_), channel_id=1, source_target_pairs={{0,16},{16,0},{1,17},{17,1},{2,18},{18,2},{3,19},{19,3},{4,20},{20... | collective-permute-start | bytes 786440 | tf_op jit(solution)/shard_map/ppermute | solution.py:519
  29.6 16.5 %collective-permute-start.4 = (bf16[304,512]{1,0:T(8,128)(2,1)S(1)}, bf16[304,512]{1,0:T(8,128)(2,1)S(1)}, u32[]{:S(2)}, u32[]{:S(2)}) collective-permute-start(bf16[304,512]{1,0:T(8,128)(2,1)S(1)} %copy-done.11), channel_id=1, source_target_pairs={{0,8},{8,0},{1,9},{9,1},{2,10},{10,2},{3,11},{11,3},{4,12},{12,4},... | collective-permute-start | bytes 933896 | tf_op jit(solution)/shard_map/ppermute | solution.py:518
  33.3 12.8 %copy-start.8 = (bf16[176,1024]{1,0:T(8,128)(2,1)S(1)}, bf16[176,1024]{1,0:T(8,128)(2,1)}, u32[]{:S(2)}) copy-start(bf16[176,1024]{1,0:T(8,128)(2,1)} %get-tuple-element.35) | copy-start | bytes 1081348
  33.3 12.7 %collective-permute-start.6 = (bf16[4,48,512]{2,1,0:T(8,128)(2,1)S(1)}, bf16[4,48,512]{2,1,0:T(8,128)(2,1)S(1)}, u32[]{:S(2)}, u32[]{:S(2)}) collective-permute-start(bf16[4,48,512]{2,1,0:T(8,128)(2,1)S(1)} %pad_maximum_fusion.1.refs_0_), channel_id=1, source_target_pairs={{0,16},{16,0},{1,17},{17,1},{2,18},{18,2},{3,19},{19,3},{4,20},{20... | collective-permute-start | bytes 589832 | tf_op jit(solution)/shard_map/ppermute | solution.py:520
  46.1 4.1 %copy-start = (bf16[1024,512]{1,0:T(8,128)(2,1)S(1)}, bf16[1024,512]{1,0:T(8,128)(2,1)}, u32[]{:S(2)}) copy-start(bf16[1024,512]{1,0:T(8,128)(2,1)} %own_ref.1) | copy-start | bytes 3145732
  46.1 4.1 %copy-start.6 = (s32[16]{0:T(128)S(1)}, s32[16]{0:T(128)}, u32[]{:S(2)}) copy-start(s32[16]{0:T(128)} %position.1) | copy-start | bytes 196
  46.1 4.1 %copy-start.7 = (s32[16]{0:T(128)S(1)}, s32[16]{0:T(128)}, u32[]{:S(2)}) copy-start(s32[16]{0:T(128)} %adapter.1) | copy-start | bytes 196
  46.3 3.9 %collective-permute-start.12 = (bf16[4,176,1024]{2,1,0:T(8,128)(2,1)S(1)}, bf16[4,176,1024]{2,1,0:T(8,128)(2,1)S(1)}, u32[]{:S(2)}, u32[]{:S(2)}) collective-permute-start(bf16[4,176,1024]{2,1,0:T(8,128)(2,1)S(1)} %pad_maximum_fusion.refs_4_), channel_id=1, source_target_pairs={{0,1},{1,0},{2,3},{3,2},{4,5},{5,4},{6,7},{7,6},{8,9},{9,8},{10,11... | collective-permute-start | bytes 4325384 | tf_op jit(solution)/shard_map/ppermute | solution.py:530
  46.4 9.8 %collective-permute-start.13 = (bf16[304,512]{1,0:T(8,128)(2,1)S(1)}, bf16[304,512]{1,0:T(8,128)(2,1)S(1)}, u32[]{:S(2)}, u32[]{:S(2)}) collective-permute-start(bf16[304,512]{1,0:T(8,128)(2,1)S(1)} %collective-permute-done.4.refs_1_), channel_id=1, source_target_pairs={{0,16},{16,0},{1,17},{17,1},{2,18},{18,2},{3,19},{19,3},{4,20},{20... | collective-permute-start | bytes 933896 | tf_op jit(solution)/shard_map/ppermute | solution.py:527
  47.9 1.9 %collective-permute-start.10 = (bf16[4,48,512]{2,1,0:T(8,128)(2,1)S(1)}, bf16[4,48,512]{2,1,0:T(8,128)(2,1)S(1)}, u32[]{:S(2)}, u32[]{:S(2)}) collective-permute-start(bf16[4,48,512]{2,1,0:T(8,128)(2,1)S(1)} %pad_maximum_fusion.1.refs_0_), channel_id=1, source_target_pairs={{0,1},{1,0},{2,3},{3,2},{4,5},{5,4},{6,7},{7,6},{8,9},{9,8},{10,11... | collective-permute-start | bytes 589832 | tf_op jit(solution)/shard_map/ppermute | solution.py:529
  48.1 2.0 %collective-permute-start.11 = (bf16[4,48,512]{2,1,0:T(8,128)(2,1)S(1)}, bf16[4,48,512]{2,1,0:T(8,128)(2,1)S(1)}, u32[]{:S(2)}, u32[]{:S(2)}) collective-permute-start(bf16[4,48,512]{2,1,0:T(8,128)(2,1)S(1)} %collective-permute-done.6.refs_1_), channel_id=1, source_target_pairs={{0,1},{1,0},{2,3},{3,2},{4,5},{5,4},{6,7},{7,6},{8,9},{9,8},{10,11... | collective-permute-start | bytes 589832 | tf_op jit(solution)/shard_map/ppermute | solution.py:529
  52.6 13.2 %copy-start.1 = (bf16[64,4096]{1,0:T(8,128)(2,1)S(1)}, bf16[64,4096]{1,0:T(8,128)(2,1)}, u32[]{:S(2)}) copy-start(bf16[64,4096]{1,0:T(8,128)(2,1)} %get-tuple-element.37.refs_0_) | copy-start | bytes 1572868
  52.6 13.2 %copy-start.2 = (bf16[64,4096]{1,0:T(8,128)(2,1)S(1)}, bf16[64,4096]{1,0:T(8,128)(2,1)}, u32[]{:S(2)}) copy-start(bf16[64,4096]{1,0:T(8,128)(2,1)} %get-tuple-element.47.refs_1_) | copy-start | bytes 1572868
  52.6 13.2 %copy-start.3 = (bf16[2,512,128]{2,1,0:T(8,128)(2,1)S(1)}, bf16[2,512,128]{2,1,0:T(8,128)(2,1)}, u32[]{:S(2)}) copy-start(bf16[2,512,128]{2,1,0:T(8,128)(2,1)} %get-tuple-element.41.refs_2_) | copy-start | bytes 786436
  52.6 13.2 %copy-start.4 = (bf16[2,512,128]{2,1,0:T(8,128)(2,1)S(1)}, bf16[2,512,128]{2,1,0:T(8,128)(2,1)}, u32[]{:S(2)}) copy-start(bf16[2,512,128]{2,1,0:T(8,128)(2,1)} %get-tuple-element.48.refs_3_) | copy-start | bytes 786436
  52.6 13.2 %copy-start.5 = (s32[2]{0:T(128)S(1)}, s32[2]{0:T(128)}, u32[]{:S(2)}) copy-start(s32[2]{0:T(128)} %lens.3) | copy-start | bytes 28
  57.0 7.4 %collective-permute-start.14 = (bf16[128,512]{1,0:T(8,128)(2,1)S(1)}, bf16[128,512]{1,0:T(8,128)(2,1)S(1)}, u32[]{:S(2)}, u32[]{:S(2)}) collective-permute-start(bf16[128,512]{1,0:T(8,128)(2,1)S(1)} %get-tuple-element.61), channel_id=1, source_target_pairs={{0,6},{2,4},{4,2},{6,0},{1,7},{3,5},{5,3},{7,1},{8,14},{10,12},{12... | collective-permute-start | bytes 393224 | tf_op jit(solution)/shard_map/ppermute | solution.py:501
  59.0 5.9 %collective-permute-start.15 = (bf16[128,512]{1,0:T(8,128)(2,1)S(1)}, bf16[128,512]{1,0:T(8,128)(2,1)S(1)}, u32[]{:S(2)}, u32[]{:S(2)}) collective-permute-start(bf16[128,512]{1,0:T(8,128)(2,1)S(1)} %get-tuple-element.62), channel_id=1, source_target_pairs={{0,4},{2,6},{4,0},{6,2},{1,5},{3,7},{5,1},{7,3},{8,12},{10,14},{12... | collective-permute-start | bytes 393224 | tf_op jit(solution)/shard_map/ppermute | solution.py:501
  59.0 6.8 %collective-permute-start.16 = (bf16[128,512]{1,0:T(8,128)(2,1)S(1)}, bf16[128,512]{1,0:T(8,128)(2,1)S(1)}, u32[]{:S(2)}, u32[]{:S(2)}) collective-permute-start(bf16[128,512]{1,0:T(8,128)(2,1)S(1)} %get-tuple-element.63), channel_id=1, source_target_pairs={{0,2},{2,0},{4,6},{6,4},{1,3},{3,1},{5,7},{7,5},{8,10},{10,8},{12,... | collective-permute-start | bytes 393224 | tf_op jit(solution)/shard_map/ppermute | solution.py:501

commit v17 on v16

--- a/solution.py
+++ b/solution.py
@@ -247,7 +247,7 @@
     width, cols = weights.shape
     step = min(cols, width)
     pieces = (width + cols) // step
-    first = width // 2 * 13 // 32 // RANK * RANK
+    first = width // 2 * 14 // 32 // RANK * RANK
     sizes = [(first + RANK * pieces, cols), (width // 2 - first, cols)]
     sizes += [(RANK * pieces, step)] * (quads - 1)
     return pl.pallas_call(
@@ -506,7 +506,7 @@
 
     early, late, *maps = cross_pack(downs, ups, value_matrix, quads)
     blocks = quad_pack(after(normed_inputs, early), downs, ups, width, quads)
-    order = [*range(quads // 2, quads), *range(1, quads // 2)]
+    order = list(range(quads - 1, 0, -1))
     mine = [to_quad(blocks[q], q) for q in order]
     early = lax.ppermute(early, "wing", SWAP)
     maps = [to_other_wing(each, q + 1) for q, each in enumerate(maps)]

time: 68 us -> 71.3 us (1.049)
  starting transfers between devices: 23.3 us -> 33.5 us
  waiting for transfers between devices: 19.2 us -> 13 us
    ppermute x1, starting transfers between devices: 0.62 us -> 6.51 us  [on_device(): maps_other = lax.ppermute(maps, 'parts', parts_swap)]
    ppermute x6, waiting for transfers between devices: 11.3 us -> 5.85 us  [to_quad(): return lax.ppermute(value, 'quad', [(j, j ^ q) for j in range(quads)])]
    ppermute x6, starting transfers between devices: 7.37 us -> 11.3 us  [to_quad(): return lax.ppermute(value, 'quad', [(j, j ^ q) for j in range(quads)])]
    ppermute x1, starting transfers between devices: 3.74 us -> 2.24 us  [on_device(): late = lax.ppermute(after(late, early), 'wing', SWAP)]
    ppermute x1, starting transfers between devices: 0.46 us -> 1.71 us  [on_device(): early_other = lax.ppermute(early, 'parts', parts_swap)]
  transfers between devices with their start and end apart: 17 -> 17, of which waited for: 8 -> 5; matrix products, arithmetic and copies ran while one was open for 0% -> 0% of each run, Pallas kernels for 28% -> 27%
where the time goes in v17:
time: 71.3 us; the launch traced here: 71.8 us
  starting transfers between devices  33.5 us (47%)
  Pallas kernels  24.2 us (34%)
  waiting for transfers between devices  13 us (18%)
  between operations  0.89 us (1%)
    pallas_call x2, Pallas kernels, cache_attention(): pl.pallas_call(functools.partial(cache_kernel, order), in_specs=[pl.Block...  14.3 us
    ppermute x6, starting transfers between devices, to_quad(): return lax.ppermute(value, 'quad', [(j, j ^ q) for j in range(quads)])  11.3 us
    ppermute x1, starting transfers between devices, on_device(): maps_other = lax.ppermute(maps, 'parts', parts_swap)  6.51 us
    ppermute x6, waiting for transfers between devices, to_quad(): return lax.ppermute(value, 'quad', [(j, j ^ q) for j in range(quads)])  5.85 us
    ppermute x3, starting transfers between devices, to_other_wing(): return lax.ppermute(value, ('wing', 'quad'), pairs)  4.9 us
    ppermute x1, starting transfers between devices, on_device(): early = lax.ppermute(early, 'wing', SWAP)  4.1 us
    ppermute x1, waiting for transfers between devices, on_device(): late_other = lax.ppermute(late, 'parts', parts_swap)  3.42 us
    pallas_call x1, Pallas kernels, quad_pack(): pl.pallas_call(quad_kernel, in_specs=[hbm] * 3, out_specs=[vmem] * quads,...  2.59 us
  transfers between devices with their start and end apart: 17, of which 5 were waited for; matrix products, arithmetic and copies ran while one was open for 0% of the time, Pallas kernels for 27%

profile of v17, /device:TPU:0, one launch (start us, length us, event | category | flops | bytes accessed | tf_op | source)
XLA Modules:
  0.0 71.8 jit_solution(4260609893573337015)
XLA Ops:
  0.6 2.1 %cross_pack.1 = (bf16[272,512]{1,0:T(8,128)(2,1)}, bf16[288,512]{1,0:T(8,128)(2,1)}, bf16[48,512]{1,0:T(8,128)(2,1)}, bf16[48,512]{1,0:T(8,128)(2,1)}, bf16[48,512]{1,0:T(8,128)(2,1)}) custom-call(bf16[32,8192]{1,0:T(8,128)(2,1)} %bitcast.11, bf16[32,512]{1,0:T(8,128)(2,1)} %bitcast.17, bf16[1024,512]{1,0:T(8,128)(2,1)} %own_ref.1), custom_call_target="tpu_custom_call" | custom-call | flops 1 | bytes 1 | tf_op jit(solution)/shard_map/cross_pack/pallas_call | solution.py:253
  2.7 4.1 %collective-permute-start = (bf16[272,512]{1,0:T(8,128)(2,1)}, bf16[272,512]{1,0:T(8,128)(2,1)S(1)}, u32[]{:S(2)}, u32[]{:S(2)}) collective-permute-start(bf16[272,512]{1,0:T(8,128)(2,1)} %get-tuple-element.33), channel_id=1, source_target_pairs={{0,8},{8,0},{1,9},{9,1},{2,10},{10,2},{3,11},{11,3},{4,12},{12,4},... | collective-permute-start | bytes 835592 | tf_op jit(solution)/shard_map/ppermute | solution.py:511
  6.8 1.3 %collective-permute-start.1 = (bf16[48,512]{1,0:T(8,128)(2,1)}, bf16[48,512]{1,0:T(8,128)(2,1)S(1)}, u32[]{:S(2)}, u32[]{:S(2)}) collective-permute-start(bf16[48,512]{1,0:T(8,128)(2,1)} %get-tuple-element.38), channel_id=1, source_target_pairs={{0,10},{2,8},{4,14},{6,12},{8,2},{10,0},{12,6},{14,4},{1,11},{3,9}... | collective-permute-start | bytes 147464 | tf_op jit(solution)/shard_map/ppermute | solution.py:505
  8.1 3.6 %collective-permute-start.2 = (bf16[48,512]{1,0:T(8,128)(2,1)}, bf16[48,512]{1,0:T(8,128)(2,1)S(1)}, u32[]{:S(2)}, u32[]{:S(2)}) collective-permute-start(bf16[48,512]{1,0:T(8,128)(2,1)} %get-tuple-element.39), channel_id=1, source_target_pairs={{0,12},{2,14},{4,8},{6,10},{8,4},{10,6},{12,0},{14,2},{1,13},{3,15... | collective-permute-start | bytes 147464 | tf_op jit(solution)/shard_map/ppermute | solution.py:505
  11.7 0.0 collective-permute-start.3
  11.7 2.6 %quad_pack.1 = (bf16[176,1024]{1,0:T(8,128)(2,1)}, bf16[176,1024]{1,0:T(8,128)(2,1)}, bf16[176,1024]{1,0:T(8,128)(2,1)}, bf16[176,1024]{1,0:T(8,128)(2,1)}) custom-call(bf16[128,4096]{1,0:T(8,128)(2,1)} %x_hbm, bf16[32,8192]{1,0:T(8,128)(2,1)} %bitcast.12, bf16[32,512]{1,0:T(8,128)(2,1)} %bitcast.18), custom_call_target="tpu_custom_call" | custom-call | flops 1 | bytes 1 | tf_op jit(solution)/shard_map/quad_pack/pallas_call | solution.py:300
  14.3 1.0 %collective-permute-start.7 = (bf16[176,1024]{1,0:T(8,128)(2,1)}, bf16[176,1024]{1,0:T(8,128)(2,1)S(1)}, u32[]{:S(2)}, u32[]{:S(2)}) collective-permute-start(bf16[176,1024]{1,0:T(8,128)(2,1)} %get-tuple-element.51), channel_id=1, source_target_pairs={{0,6},{2,4},{4,2},{6,0},{1,7},{3,5},{5,3},{7,1},{8,14},{10,12},{12... | collective-permute-start | bytes 1081352 | tf_op jit(solution)/shard_map/ppermute | solution.py:501
  15.3 8.2 %cache_attention.2 = (bf16[64,4096]{1,0:T(8,128)(2,1)}, bf16[2,512,128]{2,1,0:T(8,128)(2,1)}) custom-call(s32[2]{0:T(128)} %lens.3, bf16[128,4096]{1,0:T(8,128)(2,1)} %q_hbm.3, bf16[128,512]{1,0:T(8,128)(2,1)} %fk_hbm.3, bf16[2,2048,512]{2,1,0:T(8,128)(2,1)} %k_hbm.3, bf16[2,2048,512]{2,1,0:T(8,128)(2,1)} %v_hbm.3), custom_call_target="tpu_custom_call" | custom-call | flops 1 | bytes 1 | tf_op jit(solution)/shard_map/cache_attention/pallas_call | solution.py:180
  23.5 2.5 %collective-permute-done.1 = bf16[48,512]{1,0:T(8,128)(2,1)S(1)} collective-permute-done((bf16[48,512]{1,0:T(8,128)(2,1)}, bf16[48,512]{1,0:T(8,128)(2,1)S(1)}, u32[]{:S(2)}, u32[]{:S(2)}) %collective-permute-start.1) | collective-permute-done | bytes 49184 | tf_op jit(solution)/shard_map/ppermute | solution.py:505
  26.0 0.0 copy-done.10
  26.0 0.0 collective-permute-start.8
  26.0 0.0 collective-permute-done.2
  26.0 3.4 %collective-permute-start.9 = (bf16[176,1024]{1,0:T(8,128)(2,1)S(1)}, bf16[176,1024]{1,0:T(8,128)(2,1)S(1)}, u32[]{:S(2)}, u32[]{:S(2)}) collective-permute-start(bf16[176,1024]{1,0:T(8,128)(2,1)S(1)} %copy-done.9), channel_id=1, source_target_pairs={{0,2},{2,0},{4,6},{6,4},{1,3},{3,1},{5,7},{7,5},{8,10},{10,8},{12,... | collective-permute-start | bytes 1081352 | tf_op jit(solution)/shard_map/ppermute | solution.py:501
  29.4 0.0 collective-permute-done.3
  29.4 0.0 collective-permute-done.refs_0_
  29.4 1.7 %collective-permute-start.5 = (bf16[272,512]{1,0:T(8,128)(2,1)S(1)}, bf16[272,512]{1,0:T(8,128)(2,1)S(1)}, u32[]{:S(2)}, u32[]{:S(2)}) collective-permute-start(bf16[272,512]{1,0:T(8,128)(2,1)S(1)} %collective-permute-done.refs_0_), channel_id=1, source_target_pairs={{0,16},{16,0},{1,17},{17,1},{2,18},{18,2},{3,19},{19,3},{4,20},{20... | collective-permute-start | bytes 835592 | tf_op jit(solution)/shard_map/ppermute | solution.py:519
  31.1 2.2 %collective-permute-start.4 = (bf16[288,512]{1,0:T(8,128)(2,1)S(1)}, bf16[288,512]{1,0:T(8,128)(2,1)S(1)}, u32[]{:S(2)}, u32[]{:S(2)}) collective-permute-start(bf16[288,512]{1,0:T(8,128)(2,1)S(1)} %copy-done.11), channel_id=1, source_target_pairs={{0,8},{8,0},{1,9},{9,1},{2,10},{10,2},{3,11},{11,3},{4,12},{12,4},... | collective-permute-start | bytes 884744 | tf_op jit(solution)/shard_map/ppermute | solution.py:518
  33.4 0.0 collective-permute-done.7
  33.4 6.5 %collective-permute-start.6 = (bf16[4,48,512]{2,1,0:T(8,128)(2,1)S(1)}, bf16[4,48,512]{2,1,0:T(8,128)(2,1)S(1)}, u32[]{:S(2)}, u32[]{:S(2)}) collective-permute-start(bf16[4,48,512]{2,1,0:T(8,128)(2,1)S(1)} %pad_maximum_fusion.1.refs_0_), channel_id=1, source_target_pairs={{0,16},{16,0},{1,17},{17,1},{2,18},{18,2},{3,19},{19,3},{4,20},{20... | collective-permute-start | bytes 589832 | tf_op jit(solution)/shard_map/ppermute | solution.py:520
  39.9 6.0 %cache_attention.3 = (bf16[64,4096]{1,0:T(8,128)(2,1)}, bf16[2,512,128]{2,1,0:T(8,128)(2,1)}) custom-call(s32[2]{0:T(128)} %lens.3, bf16[128,4096]{1,0:T(8,128)(2,1)} %q_hbm.3, bf16[128,512]{1,0:T(8,128)(2,1)} %fk_hbm.3, bf16[2,2048,512]{2,1,0:T(8,128)(2,1)} %k_hbm.3, bf16[2,2048,512]{2,1,0:T(8,128)(2,1)} %v_hbm.3), custom_call_target="tpu_custom_call" | custom-call | flops 1 | bytes 1 | tf_op jit(solution)/shard_map/cache_attention/pallas_call | solution.py:180
  46.0 0.0 collective-permute-done.8
  46.0 0.0 collective-permute-done.9
  46.0 0.0 collective-permute-done.6.refs_1_
  46.0 0.0 collective-permute-done.5.refs_2_
  46.0 0.0 collective-permute-done.4.refs_1_
  46.0 0.0 copy-start
  46.0 0.0 copy-start.6
  46.1 0.0 copy-start.7
  46.1 0.2 pad_maximum_fusion.refs_4_
  46.3 0.1 collective-permute-start.12
  46.3 2.2 %collective-permute-start.13 = (bf16[288,512]{1,0:T(8,128)(2,1)S(1)}, bf16[288,512]{1,0:T(8,128)(2,1)S(1)}, u32[]{:S(2)}, u32[]{:S(2)}) collective-permute-start(bf16[288,512]{1,0:T(8,128)(2,1)S(1)} %collective-permute-done.4.refs_1_), channel_id=1, source_target_pairs={{0,16},{16,0},{1,17},{17,1},{2,18},{18,2},{3,19},{19,3},{4,20},{20... | collective-permute-start | bytes 884744 | tf_op jit(solution)/shard_map/ppermute | solution.py:527
  48.5 0.2 collective-permute-start.10
  48.7 0.3 collective-permute-start.11
  49.0 0.9 %collective-permute-done.10.refs_2_ = bf16[4,48,512]{2,1,0:T(8,128)(2,1)S(1)} collective-permute-done((bf16[4,48,512]{2,1,0:T(8,128)(2,1)S(1)}, bf16[4,48,512]{2,1,0:T(8,128)(2,1)S(1)}, u32[]{:S(2)}, u32[]{:S(2)}) %collective-permute-start.10) | collective-permute-done | bytes 196640 | tf_op jit(solution)/shard_map/ppermute | solution.py:529
  50.0 0.3 collective-permute-done.11.refs_3_
  50.2 0.0 collective-permute-done.12.refs_5_
  50.3 2.4 %near_products.1.near = f32[512,512]{1,0:T(8,128)S(1)} custom-call(s32[16]{0:T(128)S(1)} %copy-done.6, s32[16]{0:T(128)S(1)} %copy-done.7, bf16[1024,512]{1,0:T(8,128)(2,1)S(1)} %copy-done, bf16[4,48,512]{2,1,0:T(8,128)(2,1)S(1)} %pad_maximum_fusion.1.refs_0_, bf16[4,48,512]{2,1,0:T(8,128)(2,1)S(1)} %collective-permute-done.6.refs_1_, ...), custom_call_target="tpu_custom_call" | custom-call | flops 1 | bytes 1 | tf_op jit(solution)/shard_map/near_products/pallas_call | solution.py:372
  52.6 0.0 copy-start.1
  52.7 0.0 copy-start.5
  52.7 3.4 %collective-permute-done.13.refs_3_ = bf16[288,512]{1,0:T(8,128)(2,1)S(1)} collective-permute-done((bf16[288,512]{1,0:T(8,128)(2,1)S(1)}, bf16[288,512]{1,0:T(8,128)(2,1)S(1)}, u32[]{:S(2)}, u32[]{:S(2)}) %collective-permute-start.13) | collective-permute-done | bytes 294944 | tf_op jit(solution)/shard_map/ppermute | solution.py:527
  56.1 0.8 %far_products.1 = (bf16[128,512]{1,0:T(8,128)(2,1)S(1)}, bf16[128,512]{1,0:T(8,128)(2,1)S(1)}, bf16[128,512]{1,0:T(8,128)(2,1)S(1)}, bf16[128,512]{1,0:T(8,128)(2,1)S(1)}) custom-call(f32[512,512]{1,0:T(8,128)S(1)} %near_products.1.near, bf16[272,512]{1,0:T(8,128)(2,1)S(1)} %collective-permute-done.refs_0_, ...), custom_call_target="tpu_custom_call" | custom-call | flops 1 | bytes 1 | tf_op jit(solution)/shard_map/far_products/pallas_call | solution.py:417
  56.9 1.0 %collective-permute-start.14 = (bf16[128,512]{1,0:T(8,128)(2,1)S(1)}, bf16[128,512]{1,0:T(8,128)(2,1)S(1)}, u32[]{:S(2)}, u32[]{:S(2)}) collective-permute-start(bf16[128,512]{1,0:T(8,128)(2,1)S(1)} %get-tuple-element.61), channel_id=1, source_target_pairs={{0,6},{2,4},{4,2},{6,0},{1,7},{3,5},{5,3},{7,1},{8,14},{10,12},{12... | collective-permute-start | bytes 393224 | tf_op jit(solution)/shard_map/ppermute | solution.py:501
  57.9 6.0 %collective-permute-start.15 = (bf16[128,512]{1,0:T(8,128)(2,1)S(1)}, bf16[128,512]{1,0:T(8,128)(2,1)S(1)}, u32[]{:S(2)}, u32[]{:S(2)}) collective-permute-start(bf16[128,512]{1,0:T(8,128)(2,1)S(1)} %get-tuple-element.62), channel_id=1, source_target_pairs={{0,4},{2,6},{4,0},{6,2},{1,5},{3,7},{5,1},{7,3},{8,12},{10,14},{12... | collective-permute-start | bytes 393224 | tf_op jit(solution)/shard_map/ppermute | solution.py:501
  63.9 0.0 collective-permute-start.16
  63.9 0.0 collective-permute-done.14.refs_5_
  63.9 5.8 %collective-permute-done.15.refs_6_ = bf16[128,512]{1,0:T(8,128)(2,1)S(1)} collective-permute-done((bf16[128,512]{1,0:T(8,128)(2,1)S(1)}, bf16[128,512]{1,0:T(8,128)(2,1)S(1)}, u32[]{:S(2)}, u32[]{:S(2)}) %collective-permute-start.15) | collective-permute-done | bytes 131104 | tf_op jit(solution)/shard_map/ppermute | solution.py:501
  69.7 0.0 collective-permute-done.16.refs_7_
  69.8 2.0 %finish_attention.1 = (bf16[128,4096]{1,0:T(8,128)(2,1)}, bf16[128,512]{1,0:T(8,128)(2,1)}) custom-call(s32[2]{0:T(128)S(1)} %copy-done.5, bf16[64,4096]{1,0:T(8,128)(2,1)S(1)} %copy-done.1, bf16[64,4096]{1,0:T(8,128)(2,1)S(1)} %copy-done.2, bf16[2,512,128]{2,1,0:T(8,128)(2,1)S(1)} %copy-done.3, bf16[2,512,128]{2,1,0:T(8,128)(2,1)S(1)} %copy-done.4, ...), custom_call_target="tpu_custom_call" | custom-call | flops 1 | bytes 1 | tf_op jit(solution)/shard_map/finish_attention/pallas_call | solution.py:460
  (20 shorter events, 0.1 us)
Async XLA Ops:
  2.7 26.7 %collective-permute-start = (bf16[272,512]{1,0:T(8,128)(2,1)}, bf16[272,512]{1,0:T(8,128)(2,1)S(1)}, u32[]{:S(2)}, u32[]{:S(2)}) collective-permute-start(bf16[272,512]{1,0:T(8,128)(2,1)} %get-tuple-element.33), channel_id=1, source_target_pairs={{0,8},{8,0},{1,9},{9,1},{2,10},{10,2},{3,11},{11,3},{4,12},{12,4},... | collective-permute-start | bytes 835592 | tf_op jit(solution)/shard_map/ppermute | solution.py:511
  6.8 19.2 %collective-permute-start.1 = (bf16[48,512]{1,0:T(8,128)(2,1)}, bf16[48,512]{1,0:T(8,128)(2,1)S(1)}, u32[]{:S(2)}, u32[]{:S(2)}) collective-permute-start(bf16[48,512]{1,0:T(8,128)(2,1)} %get-tuple-element.38), channel_id=1, source_target_pairs={{0,10},{2,8},{4,14},{6,12},{8,2},{10,0},{12,6},{14,4},{1,11},{3,9}... | collective-permute-start | bytes 147464 | tf_op jit(solution)/shard_map/ppermute | solution.py:505
  8.1 17.9 %collective-permute-start.2 = (bf16[48,512]{1,0:T(8,128)(2,1)}, bf16[48,512]{1,0:T(8,128)(2,1)S(1)}, u32[]{:S(2)}, u32[]{:S(2)}) collective-permute-start(bf16[48,512]{1,0:T(8,128)(2,1)} %get-tuple-element.39), channel_id=1, source_target_pairs={{0,12},{2,14},{4,8},{6,10},{8,4},{10,6},{12,0},{14,2},{1,13},{3,15... | collective-permute-start | bytes 147464 | tf_op jit(solution)/shard_map/ppermute | solution.py:505
  11.7 17.7 %collective-permute-start.3 = (bf16[48,512]{1,0:T(8,128)(2,1)}, bf16[48,512]{1,0:T(8,128)(2,1)S(1)}, u32[]{:S(2)}, u32[]{:S(2)}) collective-permute-start(bf16[48,512]{1,0:T(8,128)(2,1)} %get-tuple-element.40), channel_id=1, source_target_pairs={{0,14},{2,12},{4,10},{6,8},{8,6},{10,4},{12,2},{14,0},{1,15},{3,13... | collective-permute-start | bytes 147464 | tf_op jit(solution)/shard_map/ppermute | solution.py:505
  14.3 19.1 %collective-permute-start.7 = (bf16[176,1024]{1,0:T(8,128)(2,1)}, bf16[176,1024]{1,0:T(8,128)(2,1)S(1)}, u32[]{:S(2)}, u32[]{:S(2)}) collective-permute-start(bf16[176,1024]{1,0:T(8,128)(2,1)} %get-tuple-element.51), channel_id=1, source_target_pairs={{0,6},{2,4},{4,2},{6,0},{1,7},{3,5},{5,3},{7,1},{8,14},{10,12},{12... | collective-permute-start | bytes 1081352 | tf_op jit(solution)/shard_map/ppermute | solution.py:501
  15.3 10.7 %copy-start.10 = (bf16[176,1024]{1,0:T(8,128)(2,1)S(1)}, bf16[176,1024]{1,0:T(8,128)(2,1)}, u32[]{:S(2)}) copy-start(bf16[176,1024]{1,0:T(8,128)(2,1)} %get-tuple-element.52) | copy-start | bytes 1081348
  15.3 10.7 %copy-start.9 = (bf16[176,1024]{1,0:T(8,128)(2,1)S(1)}, bf16[176,1024]{1,0:T(8,128)(2,1)}, u32[]{:S(2)}) copy-start(bf16[176,1024]{1,0:T(8,128)(2,1)} %get-tuple-element.53) | copy-start | bytes 1081348
  15.3 15.8 %copy-start.11 = (bf16[288,512]{1,0:T(8,128)(2,1)S(1)}, bf16[288,512]{1,0:T(8,128)(2,1)}, u32[]{:S(2)}) copy-start(bf16[288,512]{1,0:T(8,128)(2,1)} %get-tuple-element.50) | copy-start | bytes 884740
  26.0 20.0 %collective-permute-start.8 = (bf16[176,1024]{1,0:T(8,128)(2,1)S(1)}, bf16[176,1024]{1,0:T(8,128)(2,1)S(1)}, u32[]{:S(2)}, u32[]{:S(2)}) collective-permute-start(bf16[176,1024]{1,0:T(8,128)(2,1)S(1)} %copy-done.10), channel_id=1, source_target_pairs={{0,4},{2,6},{4,0},{6,2},{1,5},{3,7},{5,1},{7,3},{8,12},{10,14},{12... | collective-permute-start | bytes 1081352 | tf_op jit(solution)/shard_map/ppermute | solution.py:501
  26.0 20.0 %collective-permute-start.9 = (bf16[176,1024]{1,0:T(8,128)(2,1)S(1)}, bf16[176,1024]{1,0:T(8,128)(2,1)S(1)}, u32[]{:S(2)}, u32[]{:S(2)}) collective-permute-start(bf16[176,1024]{1,0:T(8,128)(2,1)S(1)} %copy-done.9), channel_id=1, source_target_pairs={{0,2},{2,0},{4,6},{6,4},{1,3},{3,1},{5,7},{7,5},{8,10},{10,8},{12,... | collective-permute-start | bytes 1081352 | tf_op jit(solution)/shard_map/ppermute | solution.py:501
  29.4 16.6 %collective-permute-start.5 = (bf16[272,512]{1,0:T(8,128)(2,1)S(1)}, bf16[272,512]{1,0:T(8,128)(2,1)S(1)}, u32[]{:S(2)}, u32[]{:S(2)}) collective-permute-start(bf16[272,512]{1,0:T(8,128)(2,1)S(1)} %collective-permute-done.refs_0_), channel_id=1, source_target_pairs={{0,16},{16,0},{1,17},{17,1},{2,18},{18,2},{3,19},{19,3},{4,20},{20... | collective-permute-start | bytes 835592 | tf_op jit(solution)/shard_map/ppermute | solution.py:519
  31.1 14.9 %collective-permute-start.4 = (bf16[288,512]{1,0:T(8,128)(2,1)S(1)}, bf16[288,512]{1,0:T(8,128)(2,1)S(1)}, u32[]{:S(2)}, u32[]{:S(2)}) collective-permute-start(bf16[288,512]{1,0:T(8,128)(2,1)S(1)} %copy-done.11), channel_id=1, source_target_pairs={{0,8},{8,0},{1,9},{9,1},{2,10},{10,2},{3,11},{11,3},{4,12},{12,4},... | collective-permute-start | bytes 884744 | tf_op jit(solution)/shard_map/ppermute | solution.py:518
  33.4 12.6 %copy-start.8 = (bf16[176,1024]{1,0:T(8,128)(2,1)S(1)}, bf16[176,1024]{1,0:T(8,128)(2,1)}, u32[]{:S(2)}) copy-start(bf16[176,1024]{1,0:T(8,128)(2,1)} %get-tuple-element.35) | copy-start | bytes 1081348
  33.4 12.6 %collective-permute-start.6 = (bf16[4,48,512]{2,1,0:T(8,128)(2,1)S(1)}, bf16[4,48,512]{2,1,0:T(8,128)(2,1)S(1)}, u32[]{:S(2)}, u32[]{:S(2)}) collective-permute-start(bf16[4,48,512]{2,1,0:T(8,128)(2,1)S(1)} %pad_maximum_fusion.1.refs_0_), channel_id=1, source_target_pairs={{0,16},{16,0},{1,17},{17,1},{2,18},{18,2},{3,19},{19,3},{4,20},{20... | collective-permute-start | bytes 589832 | tf_op jit(solution)/shard_map/ppermute | solution.py:520
  46.0 4.2 %copy-start = (bf16[1024,512]{1,0:T(8,128)(2,1)S(1)}, bf16[1024,512]{1,0:T(8,128)(2,1)}, u32[]{:S(2)}) copy-start(bf16[1024,512]{1,0:T(8,128)(2,1)} %own_ref.1) | copy-start | bytes 3145732
  46.0 4.2 %copy-start.6 = (s32[16]{0:T(128)S(1)}, s32[16]{0:T(128)}, u32[]{:S(2)}) copy-start(s32[16]{0:T(128)} %position.1) | copy-start | bytes 196
  46.1 4.2 %copy-start.7 = (s32[16]{0:T(128)S(1)}, s32[16]{0:T(128)}, u32[]{:S(2)}) copy-start(s32[16]{0:T(128)} %adapter.1) | copy-start | bytes 196
  46.3 4.0 %collective-permute-start.12 = (bf16[4,176,1024]{2,1,0:T(8,128)(2,1)S(1)}, bf16[4,176,1024]{2,1,0:T(8,128)(2,1)S(1)}, u32[]{:S(2)}, u32[]{:S(2)}) collective-permute-start(bf16[4,176,1024]{2,1,0:T(8,128)(2,1)S(1)} %pad_maximum_fusion.refs_4_), channel_id=1, source_target_pairs={{0,1},{1,0},{2,3},{3,2},{4,5},{5,4},{6,7},{7,6},{8,9},{9,8},{10,11... | collective-permute-start | bytes 4325384 | tf_op jit(solution)/shard_map/ppermute | solution.py:530
  46.3 9.8 %collective-permute-start.13 = (bf16[288,512]{1,0:T(8,128)(2,1)S(1)}, bf16[288,512]{1,0:T(8,128)(2,1)S(1)}, u32[]{:S(2)}, u32[]{:S(2)}) collective-permute-start(bf16[288,512]{1,0:T(8,128)(2,1)S(1)} %collective-permute-done.4.refs_1_), channel_id=1, source_target_pairs={{0,16},{16,0},{1,17},{17,1},{2,18},{18,2},{3,19},{19,3},{4,20},{20... | collective-permute-start | bytes 884744 | tf_op jit(solution)/shard_map/ppermute | solution.py:527
  48.5 1.4 %collective-permute-start.10 = (bf16[4,48,512]{2,1,0:T(8,128)(2,1)S(1)}, bf16[4,48,512]{2,1,0:T(8,128)(2,1)S(1)}, u32[]{:S(2)}, u32[]{:S(2)}) collective-permute-start(bf16[4,48,512]{2,1,0:T(8,128)(2,1)S(1)} %pad_maximum_fusion.1.refs_0_), channel_id=1, source_target_pairs={{0,1},{1,0},{2,3},{3,2},{4,5},{5,4},{6,7},{7,6},{8,9},{9,8},{10,11... | collective-permute-start | bytes 589832 | tf_op jit(solution)/shard_map/ppermute | solution.py:529
  48.7 1.6 %collective-permute-start.11 = (bf16[4,48,512]{2,1,0:T(8,128)(2,1)S(1)}, bf16[4,48,512]{2,1,0:T(8,128)(2,1)S(1)}, u32[]{:S(2)}, u32[]{:S(2)}) collective-permute-start(bf16[4,48,512]{2,1,0:T(8,128)(2,1)S(1)} %collective-permute-done.6.refs_1_), channel_id=1, source_target_pairs={{0,1},{1,0},{2,3},{3,2},{4,5},{5,4},{6,7},{7,6},{8,9},{9,8},{10,11... | collective-permute-start | bytes 589832 | tf_op jit(solution)/shard_map/ppermute | solution.py:529
  52.6 17.1 %copy-start.1 = (bf16[64,4096]{1,0:T(8,128)(2,1)S(1)}, bf16[64,4096]{1,0:T(8,128)(2,1)}, u32[]{:S(2)}) copy-start(bf16[64,4096]{1,0:T(8,128)(2,1)} %get-tuple-element.37.refs_0_) | copy-start | bytes 1572868
  52.7 17.1 %copy-start.2 = (bf16[64,4096]{1,0:T(8,128)(2,1)S(1)}, bf16[64,4096]{1,0:T(8,128)(2,1)}, u32[]{:S(2)}) copy-start(bf16[64,4096]{1,0:T(8,128)(2,1)} %get-tuple-element.47.refs_1_) | copy-start | bytes 1572868
  52.7 17.1 %copy-start.3 = (bf16[2,512,128]{2,1,0:T(8,128)(2,1)S(1)}, bf16[2,512,128]{2,1,0:T(8,128)(2,1)}, u32[]{:S(2)}) copy-start(bf16[2,512,128]{2,1,0:T(8,128)(2,1)} %get-tuple-element.41.refs_2_) | copy-start | bytes 786436
  52.7 17.1 %copy-start.4 = (bf16[2,512,128]{2,1,0:T(8,128)(2,1)S(1)}, bf16[2,512,128]{2,1,0:T(8,128)(2,1)}, u32[]{:S(2)}) copy-start(bf16[2,512,128]{2,1,0:T(8,128)(2,1)} %get-tuple-element.48.refs_3_) | copy-start | bytes 786436
  52.7 17.1 %copy-start.5 = (s32[2]{0:T(128)S(1)}, s32[2]{0:T(128)}, u32[]{:S(2)}) copy-start(s32[2]{0:T(128)} %lens.3) | copy-start | bytes 28
  56.9 7.0 %collective-permute-start.14 = (bf16[128,512]{1,0:T(8,128)(2,1)S(1)}, bf16[128,512]{1,0:T(8,128)(2,1)S(1)}, u32[]{:S(2)}, u32[]{:S(2)}) collective-permute-start(bf16[128,512]{1,0:T(8,128)(2,1)S(1)} %get-tuple-element.61), channel_id=1, source_target_pairs={{0,6},{2,4},{4,2},{6,0},{1,7},{3,5},{5,3},{7,1},{8,14},{10,12},{12... | collective-permute-start | bytes 393224 | tf_op jit(solution)/shard_map/ppermute | solution.py:501
  57.9 11.8 %collective-permute-start.15 = (bf16[128,512]{1,0:T(8,128)(2,1)S(1)}, bf16[128,512]{1,0:T(8,128)(2,1)S(1)}, u32[]{:S(2)}, u32[]{:S(2)}) collective-permute-start(bf16[128,512]{1,0:T(8,128)(2,1)S(1)} %get-tuple-element.62), channel_id=1, source_target_pairs={{0,4},{2,6},{4,0},{6,2},{1,5},{3,7},{5,1},{7,3},{8,12},{10,14},{12... | collective-permute-start | bytes 393224 | tf_op jit(solution)/shard_map/ppermute | solution.py:501
  63.9 5.8 %collective-permute-start.16 = (bf16[128,512]{1,0:T(8,128)(2,1)S(1)}, bf16[128,512]{1,0:T(8,128)(2,1)S(1)}, u32[]{:S(2)}, u32[]{:S(2)}) collective-permute-start(bf16[128,512]{1,0:T(8,128)(2,1)S(1)} %get-tuple-element.63), channel_id=1, source_target_pairs={{0,2},{2,0},{4,6},{6,4},{1,3},{3,1},{5,7},{7,5},{8,10},{10,8},{12,... | collective-permute-start | bytes 393224 | tf_op jit(solution)/shard_map/ppermute | solution.py:501
